TPU v7x, 32 devices: a whole 2x2x4 slice. The times are simulated.
32 devices in a mesh: sec: 2 (over core), dev: 16 (over z, y, x).
Axes of the slice: x: 2, y: 2, z: 4, core: 2. Of those that a mesh axis runs over, the one named last changes fastest.
Arguments:
- raw_pixels: float32 [2, 32, 512, 512], P(None, ('sec', 'dev')), may hold values from -8 to 8
- flat_field: float32 [32, 512, 512], P(('sec', 'dev')), may hold values from 0.5 to 1.5
- bias_rows: float32 [2, 32, 512], P(None, ('sec', 'dev')), may hold values from -6 to 6
- psf_taps: float32 [2, 1, 2, 41], replicated, may hold values from -1 to 1
- term_weights: float32 [2, 32, 1], P(None, ('sec', 'dev')), may hold values from -5 to 5
- warp_shift: float32 [2, 32, 2], P(None, ('sec', 'dev')), may hold values from -3 to 3
- warp_scale: float32 [2, 32, 2], P(None, ('sec', 'dev')), may hold values from 0.97 to 1.03
- owner_of: int32 [1024, 1], P(('sec', 'dev')), may hold values from 0 to 31; in each aligned block of 32 rows (0 to 31, 32 to 63, ...) at most 2 rows name the same one
- patch_slot: int32 [1024, 1], P(('sec', 'dev')), may hold values from 0 to 3
- weight_index: int32 [1024, 1], P(('sec', 'dev')), may hold values from 0 to 15
- weight_table: float32 [16], replicated, may hold values from 0.3 to 3
- detect_taps: float32 [2, 41], replicated, may hold values from -1 to 1
Outputs:
- coadd: float32 [4096, 512], P(('sec', 'dev'))
- detection: float32 [4096, 512], P(('sec', 'dev'))
Inputs may be any that keep to these rules, and one draw needn't show every extreme that they name: `owner_of`: among the 32 rows of one slab no owner is named more than 2 times, a bound that some block reaches.
All inputs are finite; a program needn't handle non-finite values.
Results may differ from a plain program's by a relative error of at most 0.01.
Values may be sent and summed in bfloat16 or wider, within the bound.
No kernel may reach another device: no remote copies, remote signals or barrier semaphores. Data moves between devices by JAX's collectives and lax.ppermute only.
A program may use at most 128 MiB of HBM per device.

v0:
```python
import jax
import jax.numpy as jnp
from jax import lax
from jax.sharding import PartitionSpec as P

P_SIZE = 128
CAP = 2
PATCH_DEV = 4


def extended_2(block, sides, width):
    for axis, dim in sides:
        count = lax.axis_size(axis)
        forward = [(i, i + 1) for i in range(count - 1)]
        backward = [(target, source) for source, target in forward]
        low = lax.ppermute(
            lax.slice_in_dim(block, block.shape[dim] - width, None, axis=dim), axis, forward
        )
        high = lax.ppermute(lax.slice_in_dim(block, 0, width, axis=dim), axis, backward)
        block = jnp.concatenate([low, block, high], axis=dim)
    return block


def band_matrix(tap_values, out_count, in_count, leading):
    out_pos = jnp.arange(out_count, dtype=jnp.int32)
    in_pos = jnp.arange(in_count, dtype=jnp.int32)
    offset = in_pos[None, :] - out_pos[:, None] + leading
    matrix = jnp.zeros((out_count, in_count), jnp.float32)
    for tap_index in range(tap_values.shape[0]):
        matrix = matrix + jnp.where(offset == tap_index, tap_values[tap_index], 0.0)
    return matrix


def blocked_interpolation(shift_value, scale_value, length, side):
    block_count = length // side
    centre = (length - 1) / 2.0
    out_pos = jnp.arange(length).astype(jnp.float32).reshape(block_count, side)
    source = scale_value * (out_pos - centre) + centre + shift_value
    starts = (jnp.arange(block_count).astype(jnp.float32) - 1.0) * side
    in_pos = starts[:, None] + jnp.arange(3 * side).astype(jnp.float32)[None, :]
    return jnp.maximum(0.0, 1.0 - jnp.abs(in_pos[:, None, :] - source[:, :, None]))


def column_windows(image, side):
    row_count, col_count = image.shape
    block_count = col_count // side
    padded = jnp.pad(image, ((0, 0), (side, side))).reshape(row_count, block_count + 2, side)
    return jnp.concatenate((padded[:, :-2], padded[:, 1:-1], padded[:, 2:]), axis=2)


def row_windows(image, side):
    row_count, col_count = image.shape
    block_count = row_count // side
    padded = jnp.pad(image, ((side, side), (0, 0))).reshape(block_count + 2, side, col_count)
    return jnp.concatenate((padded[:-2], padded[1:-1], padded[2:]), axis=1)


def contract_last_float(left, right):
    return lax.dot_general(
        left,
        right,
        (((1,), (1,)), ((), ())),
        precision=lax.Precision.HIGHEST,
        preferred_element_type=jnp.float32,
    )


def warp_visit(
    raw_visit, flat_slab, bias_visit, taps_visit, weights_visit, shift_visit, scale_visit
):
    row_count, col_count = raw_visit.shape
    half_width = taps_visit.shape[2] // 2
    exposure = ((raw_visit - bias_visit[:, None]) * flat_slab).astype(jnp.bfloat16)
    exposure_windows = column_windows(exposure, P_SIZE)
    across_taps = taps_visit[0, 1].astype(jnp.bfloat16).astype(jnp.float32)
    down_taps = taps_visit[0, 0].astype(jnp.bfloat16).astype(jnp.float32)
    across_band = band_matrix(across_taps, P_SIZE, 3 * P_SIZE, half_width - P_SIZE).astype(
        jnp.bfloat16
    )
    down_band = band_matrix(down_taps, P_SIZE, 3 * P_SIZE, half_width - P_SIZE).astype(jnp.bfloat16)
    smoothed = jnp.einsum(
        "rbw,ow->rbo", exposure_windows, across_band, preferred_element_type=jnp.float32
    )
    smoothed = smoothed.reshape(row_count, col_count).astype(jnp.bfloat16)
    along = jnp.einsum(
        "ow,bwc->boc", down_band, row_windows(smoothed, P_SIZE), preferred_element_type=jnp.float32
    )
    matched = weights_visit[0] * along.reshape(row_count, col_count)
    matched = matched.astype(jnp.bfloat16)
    warp_cols = blocked_interpolation(shift_visit[1], scale_visit[1], col_count, P_SIZE).astype(
        jnp.bfloat16
    )
    warp_rows = blocked_interpolation(shift_visit[0], scale_visit[0], row_count, P_SIZE).astype(
        jnp.bfloat16
    )
    half_warped = jnp.einsum(
        "rbw,bow->rbo",
        column_windows(matched, P_SIZE),
        warp_cols,
        preferred_element_type=jnp.float32,
    )
    half_warped = half_warped.reshape(row_count, col_count).astype(jnp.bfloat16)
    warped = jnp.einsum(
        "bow,bwc->boc",
        warp_rows,
        row_windows(half_warped, P_SIZE),
        preferred_element_type=jnp.float32,
    )
    return warped.reshape(row_count, col_count).astype(jnp.bfloat16)


def cut_blocks(image, side):
    row_blocks = image.shape[0] // side
    col_blocks = image.shape[1] // side
    shaped = image.reshape(row_blocks, side, col_blocks, side).transpose(0, 2, 1, 3)
    return shaped.reshape(row_blocks * col_blocks, side, side)


def per_device(
    raw_pixels,
    flat_field,
    bias_rows,
    psf_taps,
    term_weights,
    warp_shift,
    warp_scale,
    owner_of,
    patch_slot,
    weight_index,
    weight_table,
    detect_taps,
):
    pieces = []
    for visit_index in range(raw_pixels.shape[0]):
        warped = warp_visit(
            raw_pixels[visit_index, 0],
            flat_field[0],
            bias_rows[visit_index, 0],
            psf_taps[visit_index],
            term_weights[visit_index, 0],
            warp_shift[visit_index, 0],
            warp_scale[visit_index, 0],
        )
        pieces.append(cut_blocks(warped, P_SIZE))
    blocks = jnp.concatenate(pieces, 0)
    device_count = lax.axis_size(("sec", "dev"))
    owners = owner_of[:, 0]
    earlier = jnp.tril(owners[:, None] == owners[None, :], -1)
    ranking = jnp.sum(earlier.astype(jnp.int32), axis=1)
    slot_index = owners * CAP + ranking
    table_size = weight_table.shape[0]
    chosen = jnp.sum(
        jnp.where(
            weight_index[:, 0][:, None] == jnp.arange(table_size, dtype=jnp.int32)[None, :],
            weight_table[None, :],
            0.0,
        ),
        axis=1,
    )
    total_slots = device_count * CAP
    send_blocks = jnp.zeros((total_slots, P_SIZE, P_SIZE), jnp.bfloat16).at[slot_index].set(blocks)
    send_weights = jnp.zeros((total_slots,), jnp.float32).at[slot_index].set(chosen)
    send_slots = jnp.zeros((total_slots,), jnp.int32).at[slot_index].set(patch_slot[:, 0])
    arrived, arrived_weights, arrived_slots = (
        lax.all_to_all(send_blocks, ("sec", "dev"), split_axis=0, concat_axis=0, tiled=True),
        lax.all_to_all(
            send_weights.astype(jnp.bfloat16),
            ("sec", "dev"),
            split_axis=0,
            concat_axis=0,
            tiled=True,
        ).astype(send_weights.dtype),
        lax.all_to_all(send_slots, ("sec", "dev"), split_axis=0, concat_axis=0, tiled=True),
    )
    arrived = arrived.reshape(total_slots, P_SIZE * P_SIZE)
    selector = jnp.where(
        arrived_slots[None, :] == jnp.arange(PATCH_DEV, dtype=jnp.int32)[:, None],
        arrived_weights[None, :],
        0.0,
    )
    numerator = jnp.dot(selector, arrived.astype(jnp.float32), precision=lax.Precision.HIGHEST)
    weight_sum = jnp.sum(selector, axis=1)
    blocks_done = numerator / jnp.maximum(weight_sum, 1.0)[:, None]
    coadd_tile = (
        blocks_done.reshape(PATCH_DEV, P_SIZE, P_SIZE)
        .transpose(1, 0, 2)
        .reshape(P_SIZE, PATCH_DEV * P_SIZE)
    )
    half_width = detect_taps.shape[1] // 2
    extended = extended_2(
        coadd_tile.astype(jnp.bfloat16), ((("sec", "dev"), 0),), half_width
    ).astype(coadd_tile.dtype)
    down_band = band_matrix(detect_taps[0], P_SIZE, P_SIZE + 2 * half_width, 0)
    across_band = band_matrix(detect_taps[1], PATCH_DEV * P_SIZE, PATCH_DEV * P_SIZE, half_width)
    along_rows = jnp.dot(down_band, extended, precision=lax.Precision.HIGHEST)
    detection = contract_last_float(along_rows, across_band)
    return (coadd_tile, detection)


def solution(mesh):
    placed = (
        P(None, ("sec", "dev"), None, None),
        P(("sec", "dev"), None, None),
        P(None, ("sec", "dev"), None),
        P(),
        P(None, ("sec", "dev"), None),
        P(None, ("sec", "dev"), None),
        P(None, ("sec", "dev"), None),
        P(("sec", "dev"), None),
        P(("sec", "dev"), None),
        P(("sec", "dev"), None),
        P(),
        P(),
    )
    return jax.shard_map(
        per_device,
        mesh=mesh,
        in_specs=placed,
        out_specs=(P(("sec", "dev"), None), P(("sec", "dev"), None)),
        check_vma=False,
    )
```

profile of v0, /device:TPU:1, one launch (start us, length us, event | category | flops | bytes accessed | tf_op | source)
XLA Modules:
  0.0 292.4 jit_solution(10906015705704471326)
XLA Ops:
  0.6 0.9 convert_reduce_fusion.1
  1.6 0.7 fusion.981
  2.2 0.8 select_reduce_fusion
  3.0 0.7 scatter_custom_fusion.1
  3.7 0.7 all_to_all.20
  4.4 7.1 %all-to-all-start.1 = ((bf16[32,2,1]{1,2,0:T(2,128)(2,1)}), bf16[32,2,1]{1,2,0:T(2,128)(2,1)S(1)}, u32[]{:S(2)}, u32[]{:S(2)}) async-start(bf16[32,2,1]{1,2,0:T(2,128)(2,1)} %all_to_all.20), calls=%async_computation.1 | async-start | bytes 32768 | tf_op jit(solution)/shard_map/all_to_all | solution.py:166
  11.5 0.7 fusion.979
  12.2 0.7 fusion.1281
  12.9 0.7 fusion.1282
  13.7 0.7 fusion.1283
  14.3 0.7 fusion.1277
  15.0 0.7 fusion.1278
  16.4 0.7 fusion.1287
  17.1 0.7 fusion.1288
  17.9 0.7 fusion.1289
  18.5 0.7 fusion.1284
  19.3 0.7 fusion.1285
  20.6 1.7 fusion.1261
  23.0 1.6 copy.92
  24.6 1.2 fusion.85
  26.9 26.3 %fusion.77 = bf16[512,4,128]{0,2,1:T(8,128)(2,1)S(1)} fusion(bf16[512,4,128]{2,0,1:T(8,128)(2,1)S(1)} %copy.124, bf16[512,4,128]{2,0,1:T(8,128)(2,1)S(1)} %copy.123, bf16[512,4,128]{2,0,1:T(8,128)(2,1)S(1)} %copy.122, f32[]{:T(128)} %bitcast.56, f32[]{:T(128)} %bitcast.55, f32[]{:T(128)} %bitcast.54, f32[]{:T(128)} %bitcast.53, f32[]{:T(128)} %bitcast.52, ...), kind=kOutput, calls=%fused_computation.63 | convolution fusion | flops 212451328 | bytes 2097316 | tf_op jit(solution)/shard_map/rbw,ow->rbo/dot_general | solution.py:81
  54.8 26.8 %fusion.56 = bf16[4,512,128]{1,2,0:T(8,128)(2,1)S(1)} fusion(bf16[4,128,512]{2,1,0:T(8,128)(2,1)S(1)} %bitcast.370, bf16[4,128,512]{2,1,0:T(8,128)(2,1)S(1)} %copy.98, bf16[4,128,512]{2,1,0:T(8,128)(2,1)S(1)} %bitcast.368, f32[]{:T(128)} %bitcast.10, f32[]{:T(128)} %bitcast.101, f32[]{:T(128)} %bitcast.100, f32[]{:T(128)} %bitcast.99, f32[]{:T(128)} %bitcast.98, ...), kind=kOutput, calls=%fused_computation.56 | convolution fusion | flops 212713472 | bytes 2097320 | tf_op jit(solution)/shard_map/ow,bwc->boc/dot_general | solution.py:85
  84.1 1.2 add_add_fusion.2
  87.0 1.3 add_add_fusion.3
  90.3 26.5 %fusion.74 = bf16[512,4,128]{0,2,1:T(8,128)(2,1)S(1)} fusion(bf16[512,4,128]{2,0,1:T(8,128)(2,1)S(1)} %copy.131, bf16[512,4,128]{2,0,1:T(8,128)(2,1)S(1)} %copy.130, bf16[512,4,128]{2,0,1:T(8,128)(2,1)S(1)} %copy.129, f32[]{:T(128)} %bitcast.160, f32[]{:T(128)} %bitcast.159, f32[]{:T(128)} %bitcast.158, f32[]{:T(128)} %bitcast.157, f32[]{:T(128)} %bitcast.156, ...), kind=kOutput, calls=%fused_computation.62 | convolution fusion | flops 212451328 | bytes 2097316 | tf_op jit(solution)/shard_map/rbw,ow->rbo/dot_general | solution.py:81
  117.8 27.0 %fusion.59 = bf16[4,512,128]{1,2,0:T(8,128)(2,1)S(1)} fusion(bf16[4,128,512]{2,1,0:T(8,128)(2,1)S(1)} %bitcast.371, bf16[4,128,512]{2,1,0:T(8,128)(2,1)S(1)} %copy.112, bf16[4,128,512]{2,1,0:T(8,128)(2,1)S(1)} %bitcast.369, f32[]{:T(128)} %bitcast.115, f32[]{:T(128)} %bitcast.205, f32[]{:T(128)} %bitcast.204, f32[]{:T(128)} %bitcast.203, f32[]{:T(128)} %bitcast.202, ...), kind=kOutput, calls=%fused_computation.57 | convolution fusion | flops 212713472 | bytes 2097320 | tf_op jit(solution)/shard_map/ow,bwc->boc/dot_general | solution.py:85
  146.3 1.2 add_add_fusion
  147.5 0.6 fusion.65
  149.1 1.3 add_add_fusion.1
  151.1 0.8 scatter_custom_fusion
  151.9 0.7 all_to_all.15
  152.6 5.8 %all-to-all-start = ((s32[32,2,1]{1,2,0:T(1,128)}), s32[32,2,1]{1,2,0:T(1,128)S(1)}, u32[]{:S(2)}, u32[]{:S(2)}) async-start(s32[32,2,1]{1,2,0:T(1,128)} %bitcast.4), calls=%async_computation | async-start | bytes 32768 | tf_op jit(solution)/shard_map/all_to_all | solution.py:173
  158.5 1.9 broadcast_in_dim.1077
  160.4 4.7 %scatter_fusion = bf16[64,128,128]{2,1,0:T(8,128)(2,1)} fusion(bf16[64,128,128]{2,1,0:T(8,128)(2,1)} %broadcast_in_dim.1077, s32[32]{0:T(128)S(1)} %fusion.981, bf16[32,128,128]{2,1,0:T(8,128)(2,1)S(1)} %pad_maximum_fusion), kind=kCustom, calls=%fused_computation.2 | custom fusion | bytes 3145856 | tf_op jit(solution)/shard_map/scatter | solution.py:161
  165.1 5.8 %all-to-all-start.2 = ((bf16[64,128,128]{2,1,0:T(8,128)(2,1)}), bf16[64,128,128]{2,1,0:T(8,128)(2,1)S(1)}, u32[]{:S(2)}, u32[]{:S(2)}) async-start(bf16[64,128,128]{2,1,0:T(8,128)(2,1)} %scatter_fusion), calls=%async_computation.2 | async-start | bytes 4194304 | tf_op jit(solution)/shard_map/all_to_all | solution.py:165
  170.9 0.7 fusion.1273
  171.6 0.7 fusion.1272
  172.4 0.7 fusion.1270
  173.1 0.7 fusion.1271
  174.5 0.7 reduce.7
  175.4 45.5 %all-to-all-done.2 = bf16[64,128,128]{2,1,0:T(8,128)(2,1)S(1)} async-done(((bf16[64,128,128]{2,1,0:T(8,128)(2,1)}), bf16[64,128,128]{2,1,0:T(8,128)(2,1)S(1)}, u32[]{:S(2)}, u32[]{:S(2)}) %all-to-all-start.2) | async-done | bytes 2097184 | tf_op jit(solution)/shard_map/all_to_all | solution.py:165
  220.9 1.8 fusion.80
  222.7 0.7 fusion.1260
  223.5 1.9 collective-permute-start
  225.4 7.2 %collective-permute-start.1 = (bf16[20,512]{1,0:T(8,128)(2,1)S(1)}, bf16[20,512]{1,0:T(8,128)(2,1)S(1)}, u32[]{:S(2)}, u32[]{:S(2)}) collective-permute-start(bf16[20,512]{1,0:T(8,128)(2,1)S(1)} %get-tuple-element.37), channel_id=1, source_target_pairs={{1,0},{2,1},{3,2},{4,3},{5,4},{6,5},{7,6},{8,7},{9,8},{10,9},{11,1... | collective-permute-start | bytes 61448 | tf_op jit(solution)/shard_map/ppermute | solution.py:19
  232.7 0.7 fusion.1274
  233.6 25.8 %fusion.390 = f32[128,512]{1,0:T(8,128)S(1)} fusion(bf16[20,512]{1,0:T(8,128)(2,1)S(1)} %collective-permute-done.1, bf16[128,512]{1,0:T(8,128)(2,1)S(1)} %get-tuple-element.2, bf16[20,512]{1,0:T(8,128)(2,1)S(1)} %collective-permute-done, f32[]{:T(128)} %bitcast.256, f32[]{:T(128)} %bitcast.255, f32[]{:T(128)} %bitcast.254, f32[]{:T(128)} %bitcast.253, ...), kind=kOutput, calls=%fused_computation.357 | convolution fusion | flops 135281664 | bytes 434340 | tf_op jit(solution)/shard_map/dot_general | solution.py:195
  259.4 32.9 %fusion.86 = f32[128,512]{1,0:T(8,128)} fusion(f32[128,512]{1,0:T(8,128)S(1)} %fusion.390, f32[]{:T(128)} %bitcast.297, f32[]{:T(128)} %bitcast.296, f32[]{:T(128)} %bitcast.295, f32[]{:T(128)} %bitcast.294, f32[]{:T(128)} %bitcast.293, f32[]{:T(128)} %bitcast.292, f32[]{:T(128)} %bitcast.291, f32[]{:T(128)} %bitcast.290, f32[]{:T(128)} %bitcast.289, ...), kind=kOutput, calls=%fused_computation.72 | convolution fusion | flops 435159040 | bytes 524452 | tf_op jit(solution)/shard_map/dot_general | solution.py:59
  (87 shorter events, 15.8 us)
Async XLA Ops:
  4.4 148.2 %all-to-all-start.1 = ((bf16[32,2,1]{1,2,0:T(2,128)(2,1)}), bf16[32,2,1]{1,2,0:T(2,128)(2,1)S(1)}, u32[]{:S(2)}, u32[]{:S(2)}) async-start(bf16[32,2,1]{1,2,0:T(2,128)(2,1)} %all_to_all.20), calls=%async_computation.1 | async-start | bytes 32768 | tf_op jit(solution)/shard_map/all_to_all | solution.py:166
  22.3 0.7 copy-start.2
  53.3 0.9 copy-start.5
  82.0 0.9 copy-start.3
  82.0 1.5 copy-start.4
  88.3 1.0 copy-start
  152.6 12.5 %all-to-all-start = ((s32[32,2,1]{1,2,0:T(1,128)}), s32[32,2,1]{1,2,0:T(1,128)S(1)}, u32[]{:S(2)}, u32[]{:S(2)}) async-start(s32[32,2,1]{1,2,0:T(1,128)} %bitcast.4), calls=%async_computation | async-start | bytes 32768 | tf_op jit(solution)/shard_map/all_to_all | solution.py:173
  165.1 5.8 %copy-start.1 = (f32[2,41]{1,0:T(2,128)S(1)}, f32[2,41]{1,0:T(2,128)}, u32[]{:S(2)}) copy-start(f32[2,41]{1,0:T(2,128)} %param.23) | copy-start | bytes 988
  165.1 55.8 %all-to-all-start.2 = ((bf16[64,128,128]{2,1,0:T(8,128)(2,1)}), bf16[64,128,128]{2,1,0:T(8,128)(2,1)S(1)}, u32[]{:S(2)}, u32[]{:S(2)}) async-start(bf16[64,128,128]{2,1,0:T(8,128)(2,1)} %scatter_fusion), calls=%async_computation.2 | async-start | bytes 4194304 | tf_op jit(solution)/shard_map/all_to_all | solution.py:165
  223.5 9.9 %collective-permute-start = (bf16[20,512]{1,0:T(8,128)(2,1)S(1)}, bf16[20,512]{1,0:T(8,128)(2,1)S(1)}, u32[]{:S(2)}, u32[]{:S(2)}) collective-permute-start(bf16[20,512]{1,0:T(8,128)(2,1)S(1)} %get-tuple-element.36), channel_id=1, source_target_pairs={{0,1},{1,2},{2,3},{3,4},{4,5},{5,6},{6,7},{7,8},{8,9},{9,10},{10,1... | collective-permute-start | bytes 61448 | tf_op jit(solution)/shard_map/ppermute | solution.py:16
  225.4 8.2 %collective-permute-start.1 = (bf16[20,512]{1,0:T(8,128)(2,1)S(1)}, bf16[20,512]{1,0:T(8,128)(2,1)S(1)}, u32[]{:S(2)}, u32[]{:S(2)}) collective-permute-start(bf16[20,512]{1,0:T(8,128)(2,1)S(1)} %get-tuple-element.37), channel_id=1, source_target_pairs={{1,0},{2,1},{3,2},{4,3},{5,4},{6,5},{7,6},{8,7},{9,8},{10,9},{11,1... | collective-permute-start | bytes 61448 | tf_op jit(solution)/shard_map/ppermute | solution.py:19
where the time goes:
time: 295 us; the launch traced here: 292 us
  matrix products  169 us (57%)
  waiting for transfers between devices  45.7 us (15%)
  local copies, waits for them, and re-layouts  37.6 us (13%)
  starting transfers between devices  27.9 us (9%)
  other arithmetic  10.4 us (4%)
    dot_general x2, matrix products, warp_visit(): jnp.einsum('ow,bwc->boc', down_band, row_windows(smoothed, P_SIZE), prefe...  53.8 us
    dot_general x2, matrix products, warp_visit(): jnp.einsum('rbw,ow->rbo', exposure_windows, across_band, preferred_elemen...  52.8 us
    all_to_all x1, waiting for transfers between devices, per_device(): lax.all_to_all(send_blocks, ('sec', 'dev'), split_axis=0, concat_axis=0,...  45.5 us
    dot_general x1, matrix products, contract_last_float(): lax.dot_general(left, right, (((1,), (1,)), ((), ())), precision=lax.Prec...  32.9 us
    dot_general x1, matrix products, per_device(): along_rows = jnp.dot(down_band, extended, precision=lax.Precision.HIGHEST)  25.8 us
    slice x17, local copies, waits for them, and re-layouts, band_matrix(): matrix = matrix + jnp.where(offset == tap_index, tap_values[tap_index], 0.0)  12 us
    ppermute x1, starting transfers between devices, extended_2(): lax.ppermute(lax.slice_in_dim(block, 0, width, axis=dim), axis, backward)  7.24 us
    all_to_all x1, starting transfers between devices, per_device(): lax.all_to_all(send_weights.astype(jnp.bfloat16), ('sec', 'dev'), split_a...  7.1 us
  transfers between devices with their start and end apart: 5, of which 2 were waited for; matrix products, arithmetic and copies ran while one was open for 52% of the time, Pallas kernels for 0%

commit v1 on v0

v1 whole, which is shorter than its diff:
```python
import functools
import math

import jax
import jax.numpy as jnp
from jax import lax
from jax.experimental import pallas as pl
from jax.experimental.pallas import tpu as pltpu
from jax.sharding import Mesh
from jax.sharding import PartitionSpec as P

SIDE = 128
CAP = 2
PATCH_DEV = 4
HALO = 32
VMEM_LIMIT = 48 * 1024 * 1024


def tap_row(tap, count, start, width, reverse):
    lane = lax.broadcasted_iota(jnp.int32, (1, width), 1)
    row = jnp.zeros((1, width), jnp.float32)
    for k in range(count):
        at = start + (count - 1 - k if reverse else k)
        row = jnp.where(lane == at, tap(k), row)
    return row


def toeplitz(row, height):
    return pltpu.roll(
        jnp.broadcast_to(row, (height, row.shape[1])), 0, 1, stride=1, stride_axis=0
    )


def store_band(band_ref, tiles):
    blocks = band_ref.shape[0] // SIDE
    for i in range(blocks):
        for j in range(blocks):
            place = (pl.ds(i * SIDE, SIDE), pl.ds(j * SIDE, SIDE))
            if abs(i - j) <= 1:
                first = (j - i + 1) * SIDE
                band_ref[place] = tiles[:, first : first + SIDE]
            else:
                band_ref[place] = jnp.zeros((SIDE, SIDE), band_ref.dtype)


def dot32(left, right):
    return jnp.dot(left, right, preferred_element_type=jnp.float32)


def warp_kernel(
    split,
    owner_ref,
    taps_ref,
    weights_ref,
    shift_ref,
    scale_ref,
    bias_ref,
    raw_ref,
    flat_ref,
    out_ref,
    count_ref,
    band_ref,
    left_ref,
    mid_ref,
):
    nz, pn = split
    visit = pl.program_id(0)
    rows, cols = raw_ref.shape[2], raw_ref.shape[3]
    terms, tap_count = taps_ref.shape[1], taps_ref.shape[3]
    half = tap_count // 2

    @pl.when(visit == 0)
    def _():
        def clear(i, c):
            count_ref[i] = 0
            return c

        lax.fori_loop(0, count_ref.shape[0], clear, 0)

    bias = jnp.broadcast_to(bias_ref[0], (SIDE, rows)).T
    for j in range(cols // SIDE):
        sl = pl.ds(j * SIDE, SIDE)
        left_ref[:, sl] = ((raw_ref[0, 0, :, sl] - bias) * flat_ref[0, :, sl]).astype(jnp.bfloat16)

    matched = None
    for term in range(terms):
        across = tap_row(
            lambda k: taps_ref[visit, term, 1, k], tap_count, SIDE - half, 3 * SIDE, True
        )
        store_band(band_ref, toeplitz(across, SIDE).astype(jnp.bfloat16))
        mid_ref[...] = dot32(left_ref[...], band_ref[...]).astype(jnp.bfloat16)
        down = tap_row(
            lambda k: taps_ref[visit, term, 0, k], tap_count, SIDE - half, 3 * SIDE, False
        )
        store_band(band_ref, toeplitz(down, SIDE).astype(jnp.bfloat16))
        part = weights_ref[visit, term] * dot32(band_ref[...], mid_ref[...])
        matched = part if matched is None else matched + part
    left_ref[...] = matched.astype(jnp.bfloat16)

    def hat(length, axis, shift, scale):
        centre = (length - 1) / 2.0
        shape = (1, length) if axis == 1 else (length, 1)
        out_pos = lax.broadcasted_iota(jnp.int32, shape, axis).astype(jnp.float32)
        source = scale * (out_pos - centre) + centre + shift
        in_pos = lax.broadcasted_iota(jnp.int32, (length, length), 1 - axis).astype(jnp.float32)
        return jnp.maximum(0.0, 1.0 - jnp.abs(in_pos - source)).astype(jnp.bfloat16)

    band_ref[...] = hat(cols, 1, shift_ref[visit, 1], scale_ref[visit, 1])
    mid_ref[...] = dot32(left_ref[...], band_ref[...]).astype(jnp.bfloat16)
    band_ref[...] = hat(rows, 0, shift_ref[visit, 0], scale_ref[visit, 0])
    left_ref[...] = dot32(band_ref[...], mid_ref[...]).astype(jnp.bfloat16)

    row_blocks, col_blocks = rows // SIDE, cols // SIDE
    for i in range(row_blocks):
        for j in range(col_blocks):
            owner = owner_ref[visit * (row_blocks * col_blocks) + i * col_blocks + j]
            rank = count_ref[owner]
            count_ref[owner] = rank + 1
            sec = owner // (nz * pn)
            dev = owner - sec * (nz * pn)
            z = dev // pn
            p = dev - z * pn
            slot = ((sec * pn + p) * nz + z) * CAP + rank
            out_ref[slot] = left_ref[pl.ds(i * SIDE, SIDE), pl.ds(j * SIDE, SIDE)]


def table_kernel(split, me_ref, meta_ref, table_ref, slot_ref, weight_ref, count_ref):
    nz, pn, ns = split
    blocks = meta_ref.shape[0] // (3 * ns * nz * pn)
    my_sec, my_z, my_p = me_ref[0], me_ref[1], me_ref[2]

    def clear(i, c):
        slot_ref[i] = -1
        weight_ref[i] = 0.0
        return c

    lax.fori_loop(0, slot_ref.shape[0], clear, 0)

    def source(g, c):
        sec = g // pn
        base = ((sec * nz + my_z) * pn + (g - sec * pn)) * (3 * blocks)
        for z in range(nz):
            count_ref[z] = 0

        def block(b, cc):
            owner = meta_ref[base + b]
            osec = owner // (nz * pn)
            dev = owner - osec * (nz * pn)
            oz = dev // pn
            op = dev - oz * pn

            @pl.when((osec == my_sec) & (op == my_p))
            def _():
                rank = count_ref[oz]
                count_ref[oz] = rank + 1
                at = (g * nz + oz) * CAP + rank
                slot_ref[at] = meta_ref[base + blocks + b]
                weight_ref[at] = table_ref[meta_ref[base + 2 * blocks + b]]

            return cc

        return lax.fori_loop(0, blocks, block, c)

    lax.fori_loop(0, ns * pn, source, 0)


def reduce_kernel(nz, slot_ref, weight_ref, in_ref, out_ref, acc_ref):
    z = pl.program_id(0)
    acc_ref[...] = jnp.zeros_like(acc_ref)
    for g in range(in_ref.shape[0]):
        for r in range(CAP):
            at = (g * nz + z) * CAP + r
            slot = slot_ref[at]

            @pl.when(slot >= 0)
            def _():
                acc_ref[slot] += weight_ref[at] * in_ref[g, 0, r].astype(jnp.float32)

    out_ref[0] = acc_ref[...].astype(out_ref.dtype)


def coadd_kernel(me_ref, table_ref, owner_ref, slot_ref, index_ref, in_ref, coadd_ref, low_ref, high_ref):
    owners = owner_ref[...]
    slots = slot_ref[...]
    index = index_ref[...]
    weights = jnp.zeros(index.shape, jnp.float32)
    for k in range(table_ref.shape[0]):
        weights = jnp.where(index == k, table_ref[k], weights)
    weights = jnp.where(owners == me_ref[3], weights, 0.0)
    for j in range(PATCH_DEV):
        total = jnp.sum(jnp.where(slots == j, weights, 0.0), keepdims=True)
        numerator = in_ref[0, j].astype(jnp.float32)
        for z in range(1, in_ref.shape[0]):
            numerator = numerator + in_ref[z, j].astype(jnp.float32)
        tile = numerator / jnp.maximum(total, 1.0)
        sl = pl.ds(j * SIDE, SIDE)
        coadd_ref[:, sl] = tile
        high_ref[:, sl] = tile[:HALO].astype(jnp.bfloat16)
        low_ref[:, sl] = tile[SIDE - HALO :].astype(jnp.bfloat16)


def split_dot(left, right):
    lh = left.astype(jnp.bfloat16)
    ll = (left - lh.astype(jnp.float32)).astype(jnp.bfloat16)
    rh = right.astype(jnp.bfloat16)
    rl = (right - rh.astype(jnp.float32)).astype(jnp.bfloat16)
    return dot32(lh, rh) + (dot32(lh, rl) + dot32(ll, rh))


def detect_kernel(taps_ref, coadd_ref, low_ref, high_ref, out_ref, ext_ref, band_ref):
    tap_count = taps_ref.shape[1]
    half = tap_count // 2
    depth = ext_ref.shape[0]
    ext_ref[...] = jnp.zeros_like(ext_ref)
    ext_ref[pl.ds(0, HALO)] = low_ref[...].astype(jnp.float32)
    ext_ref[pl.ds(HALO, SIDE)] = coadd_ref[...]
    ext_ref[pl.ds(HALO + SIDE, HALO)] = high_ref[...].astype(jnp.float32)
    down = tap_row(lambda k: taps_ref[0, k], tap_count, HALO - half, depth, False)
    along = split_dot(toeplitz(down, SIDE), ext_ref[...])
    across = tap_row(lambda k: taps_ref[1, k], tap_count, SIDE - half, 3 * SIDE, True)
    store_band(band_ref, toeplitz(across, SIDE))
    out_ref[...] = split_dot(along, band_ref[...])


def per_device(
    split,
    raw_pixels,
    flat_field,
    bias_rows,
    psf_taps,
    term_weights,
    warp_shift,
    warp_scale,
    owner_of,
    patch_slot,
    weight_index,
    weight_table,
    detect_taps,
):
    nz, pn, ns = split
    devices = nz * pn * ns
    visits, _, rows, cols = raw_pixels.shape
    blocks = owner_of.shape[0]
    smem = pl.BlockSpec(memory_space=pltpu.SMEM)
    vmem = pl.BlockSpec(memory_space=pltpu.VMEM)
    params = pltpu.CompilerParams(vmem_limit_bytes=VMEM_LIMIT)

    owners = owner_of.reshape(blocks)
    meta = jnp.concatenate([owners, patch_slot.reshape(blocks), weight_index.reshape(blocks)])
    meta = lax.all_gather(meta, ("sec", "z", "p"), tiled=True)
    sec, z, p = lax.axis_index("sec"), lax.axis_index("z"), lax.axis_index("p")
    me = jnp.stack([sec, z, p, (sec * nz + z) * pn + p]).astype(jnp.int32)

    slots = devices * CAP
    send = pl.pallas_call(
        functools.partial(warp_kernel, (nz, pn)),
        grid=(visits,),
        out_shape=jax.ShapeDtypeStruct((slots, SIDE, SIDE), jnp.bfloat16),
        in_specs=[
            smem,
            smem,
            smem,
            smem,
            smem,
            pl.BlockSpec((1, 1, rows), lambda v: (v, 0, 0)),
            pl.BlockSpec((1, 1, rows, cols), lambda v: (v, 0, 0, 0)),
            pl.BlockSpec((1, rows, cols), lambda v: (0, 0, 0)),
        ],
        out_specs=pl.BlockSpec((slots, SIDE, SIDE), lambda v: (0, 0, 0)),
        scratch_shapes=[
            pltpu.SMEM((devices,), jnp.int32),
            pltpu.VMEM((rows, rows), jnp.bfloat16),
            pltpu.VMEM((rows, cols), jnp.bfloat16),
            pltpu.VMEM((rows, cols), jnp.bfloat16),
        ],
        compiler_params=params,
        name="warp",
    )(
        owners,
        psf_taps,
        term_weights.reshape(visits, -1),
        warp_shift.reshape(visits, 2),
        warp_scale.reshape(visits, 2),
        bias_rows,
        raw_pixels,
        flat_field,
    )
    arrived = lax.all_to_all(send, ("sec", "p"), split_axis=0, concat_axis=0, tiled=True)

    slot_table, weight_of = pl.pallas_call(
        functools.partial(table_kernel, split),
        out_shape=(
            jax.ShapeDtypeStruct((slots,), jnp.int32),
            jax.ShapeDtypeStruct((slots,), jnp.float32),
        ),
        in_specs=[smem, smem, smem],
        out_specs=(smem, smem),
        scratch_shapes=[pltpu.SMEM((nz,), jnp.int32)],
        name="tables",
    )(me, meta, weight_table)

    group = ns * pn
    partial_sums = pl.pallas_call(
        functools.partial(reduce_kernel, nz),
        grid=(nz,),
        out_shape=jax.ShapeDtypeStruct((nz, PATCH_DEV, SIDE, SIDE), jnp.bfloat16),
        in_specs=[
            smem,
            smem,
            pl.BlockSpec((group, 1, CAP, SIDE, SIDE), lambda v: (0, v, 0, 0, 0)),
        ],
        out_specs=pl.BlockSpec((1, PATCH_DEV, SIDE, SIDE), lambda v: (v, 0, 0, 0)),
        scratch_shapes=[pltpu.VMEM((PATCH_DEV, SIDE, SIDE), jnp.float32)],
        compiler_params=params,
        name="plane_sums",
    )(slot_table, weight_of, arrived.reshape(group, nz, CAP, SIDE, SIDE))
    gathered = lax.all_to_all(partial_sums, "z", split_axis=0, concat_axis=0, tiled=True)

    per_field = meta.reshape(devices, 3, blocks)
    width = PATCH_DEV * SIDE
    coadd, low_rows, high_rows = pl.pallas_call(
        coadd_kernel,
        out_shape=(
            jax.ShapeDtypeStruct((SIDE, width), jnp.float32),
            jax.ShapeDtypeStruct((HALO, width), jnp.bfloat16),
            jax.ShapeDtypeStruct((HALO, width), jnp.bfloat16),
        ),
        in_specs=[smem, smem, vmem, vmem, vmem, vmem],
        out_specs=(vmem, vmem, vmem),
        compiler_params=params,
        name="coadd",
    )(me, weight_table, per_field[:, 0], per_field[:, 1], per_field[:, 2], gathered)

    forward = [(i, i + 1) for i in range(devices - 1)]
    backward = [(i + 1, i) for i in range(devices - 1)]
    low = lax.ppermute(low_rows, ("sec", "z", "p"), forward)
    high = lax.ppermute(high_rows, ("sec", "z", "p"), backward)

    detection = pl.pallas_call(
        detect_kernel,
        out_shape=jax.ShapeDtypeStruct((SIDE, width), jnp.float32),
        in_specs=[smem, vmem, vmem, vmem],
        out_specs=vmem,
        scratch_shapes=[
            pltpu.VMEM((2 * SIDE, width), jnp.float32),
            pltpu.VMEM((width, width), jnp.float32),
        ],
        compiler_params=params,
        name="detection",
    )(detect_taps, coadd, low, high)
    return coadd, detection


def solution(mesh):
    ns, nd = mesh.shape["sec"], mesh.shape["dev"]
    nz = math.gcd(nd, 4)
    pn = nd // nz
    cut = Mesh(mesh.devices.reshape(ns, nz, pn), ("sec", "z", "p"))
    every = ("sec", "z", "p")
    placed = (
        P(None, every, None, None),
        P(every, None, None),
        P(None, every, None),
        P(),
        P(None, every, None),
        P(None, every, None),
        P(None, every, None),
        P(every, None),
        P(every, None),
        P(every, None),
        P(),
        P(),
    )
    return jax.shard_map(
        functools.partial(per_device, (nz, pn, ns)),
        mesh=cut,
        in_specs=placed,
        out_specs=(P(every, None), P(every, None)),
        check_vma=False,
    )
```

time: 295 us -> 125 us (0.42)
  matrix products: 169 us -> 0 us
  blocking collectives: 0 us -> 58.8 us
  waiting for transfers between devices: 45.7 us -> 14.8 us
  local copies, waits for them, and re-layouts: 37.6 us -> 10.6 us
  Pallas kernels: 0 us -> 20.5 us
  starting transfers between devices: 27.9 us -> 18 us
  other arithmetic: 10.4 us -> 0.86 us
    dot_general x11 -> x0, matrix products: 169 us -> none  [the longest x2 53.8 us: warp_visit(): jnp.einsum('ow,bwc->boc', down_band, row_windows(smoothed, P_SIZE), prefe...]
    unnamed x0 -> x1, blocking collectives: none -> 58.8 us
    all_to_all x3 -> x2, waiting for transfers between devices: 45.5 us -> 13.8 us  [the longest x1 13.8 us: per_device(): lax.all_to_all(partial_sums, 'z', split_axis=0, concat_axis=0, tiled=True)]
    pallas_call x0 -> x5, Pallas kernels: none -> 20.5 us  [the longest x1 9.89 us: per_device(): pl.pallas_call(functools.partial(table_kernel, split), out_shape=(jax.Sha...]
    slice x39 -> x1, local copies, waits for them, and re-layouts: 18 us -> 0.04 us  [per_device(): per_field[:, 2]]
    all_to_all x3 -> x2, starting transfers between devices: 18.7 us -> 8.82 us  [the longest x1 5.36 us: per_device(): lax.all_to_all(send, ('sec', 'p'), split_axis=0, concat_axis=0, tiled=True)]
    scatter x3 -> x0, local copies, waits for them, and re-layouts: 6.16 us -> none  [the longest x1 4.69 us: per_device(): jnp.zeros((total_slots, P_SIZE, P_SIZE), jnp.bfloat16).at[slot_index]]
    add x6 -> x0, other arithmetic: 5.02 us -> none  [the longest x4 4.95 us: blocked_interpolation(): source = scale_value * (out_pos - centre) + centre + shift_value]
  transfers between devices with their start and end apart: 5 -> 4, of which waited for: 2 -> 2; matrix products, arithmetic and copies ran while one was open for 52% -> 1% of each run, Pallas kernels for 0% -> 8%
where the time goes in v1:
time: 125 us; the launch traced here: 124 us
  blocking collectives  58.8 us (47%)
  Pallas kernels  20.5 us (16%)
  starting transfers between devices  18 us (14%)
  waiting for transfers between devices  14.8 us (12%)
  local copies, waits for them, and re-layouts  10.6 us (8%)
    unnamed x1, blocking collectives  58.8 us
    all_to_all x1, waiting for transfers between devices, per_device(): lax.all_to_all(partial_sums, 'z', split_axis=0, concat_axis=0, tiled=True)  13.8 us
    pallas_call x1, Pallas kernels, per_device(): pl.pallas_call(functools.partial(table_kernel, split), out_shape=(jax.Sha...  9.89 us
    unnamed x37, local copies, waits for them, and re-layouts  9.78 us
    ppermute x1, starting transfers between devices, per_device(): high = lax.ppermute(high_rows, ('sec', 'z', 'p'), backward)  6.27 us
    all_to_all x1, starting transfers between devices, per_device(): lax.all_to_all(send, ('sec', 'p'), split_axis=0, concat_axis=0, tiled=True)  5.36 us
    pallas_call x1, Pallas kernels, per_device(): pl.pallas_call(functools.partial(warp_kernel, (nz, pn)), grid=(visits,),...  4.65 us
    all_to_all x1, starting transfers between devices, per_device(): lax.all_to_all(partial_sums, 'z', split_axis=0, concat_axis=0, tiled=True)  3.47 us
  transfers between devices with their start and end apart: 4, of which 2 were waited for; matrix products, arithmetic and copies ran while one was open for 1% of the time, Pallas kernels for 8%

profile of v1, /device:TPU:1, one launch (start us, length us, event | category | flops | bytes accessed | tf_op | source)
XLA Modules:
  0.0 124.4 jit_solution(13342421437008174176)
XLA Ops:
  0.6 0.7 copy.18.weights_ref
  1.4 0.0 copy-start.1
  1.4 1.6 %copy-done.1 = f32[2,1,512,512]{3,2,1,0:T(8,128)S(1)} copy-done((f32[2,1,512,512]{3,2,1,0:T(8,128)S(1)}, f32[2,1,512,512]{3,2,1,0:T(8,128)}, u32[]{:S(2)}) %copy-start.1) | copy-done | bytes 2097176
  3.0 0.0 copy-start.2
  3.0 1.2 copy-done.2
  4.2 0.0 copy-start.5
  4.2 0.7 copy-done.5
  4.9 0.0 copy-start.6
  4.9 0.7 copy-done.6
  5.6 0.0 copy-start.7
  5.6 0.7 copy-done.7
  6.2 0.0 copy-start.10
  6.2 0.7 copy-done.10
  6.9 0.0 copy-start.11
  6.9 0.7 copy-done.11
  7.6 4.6 %warp.1 = bf16[64,128,128]{2,1,0:T(8,128)(2,1)S(1)} custom-call(s32[32]{0:T(128)S(1)} %bitcast.24, f32[2,1,2,41]{3,2,1,0:T(2,128)S(1)} %copy-done.6, f32[2,1]{1,0:T(2,128)S(1)} %copy.18.weights_ref, f32[2,2]{1,0:T(2,128)S(1)} %bitcast.26, f32[2,2]{1,0:T(2,128)S(1)} %bitcast.27, f32[2,1,512]{2,1,0:T(1,128)S(1)} %copy-done.5, ...), custom_call_target="tpu_custom_call" | custom-call | tf_op jit(solution)/shard_map/warp/pallas_call | solution.py:255
  12.2 0.0 copy-start
  12.2 1.3 %copy-done = bf16[64,128,128]{2,1,0:T(8,128)(2,1)} copy-done((bf16[64,128,128]{2,1,0:T(8,128)(2,1)}, bf16[64,128,128]{2,1,0:T(8,128)(2,1)S(1)}, u32[]{:S(2)}) %copy-start) | copy-done | bytes 2097176
  13.6 0.0 copy-start.16
  13.6 0.0 copy-start.17
  13.6 5.4 %all-to-all-start = ((bf16[64,128,128]{2,1,0:T(8,128)(2,1)}), bf16[64,128,128]{2,1,0:T(8,128)(2,1)S(1)}, u32[]{:S(2)}, u32[]{:S(2)}) async-start(bf16[64,128,128]{2,1,0:T(8,128)(2,1)} %copy-done), calls=%async_computation | async-start | bytes 4194304 | tf_op jit(solution)/shard_map/all_to_all | solution.py:288
  18.9 0.0 copy-start.9
  18.9 0.0 copy-done.8
  18.9 0.0 copy-done.16
  19.0 0.0 copy-done.17
  19.0 0.2 add_dynamic-update-slice_fusion
  19.2 58.8 %all-reduce.meta_ref = s32[3072]{0:T(1024)} all-reduce(s32[3072]{0:T(1024)S(1)} %add_dynamic-update-slice_fusion), channel_id=1, replica_groups=mesh['sec'=2,'z'=4,'p'=4] {'sec','z','p'}, use_global_device_ids=true, to_apply=%add | all-reduce | flops 3072 | bytes 24576
  78.0 0.7 pad_add_fusion.me_ref
  78.6 9.9 %tables.1 = (s32[64]{0:T(128)}, f32[64]{0:T(128)}) custom-call(s32[4]{0:T(128)} %pad_add_fusion.me_ref, s32[3072]{0:T(1024)} %all-reduce.meta_ref, f32[16]{0:T(128)} %table_ref.3), custom_call_target="tpu_custom_call" | custom-call | tf_op jit(solution)/shard_map/tables/pallas_call | solution.py:290
  88.5 0.0 all-to-all-done
  88.5 0.0 copy-start.13
  88.6 0.6 copy-done.13
  89.2 0.6 copy-done.14
  89.8 2.7 %plane_sums.1 = bf16[4,4,128,128]{3,2,1,0:T(8,128)(2,1)} custom-call(s32[64]{0:T(128)S(1)} %copy-done.13, f32[64]{0:T(128)S(1)} %copy-done.14, bf16[8,4,2,128,128]{4,3,2,1,0:T(8,128)(2,1)S(1)} %bitcast.20), custom_call_target="tpu_custom_call" | custom-call | tf_op jit(solution)/shard_map/plane_sums/pallas_call | solution.py:303
  92.5 3.5 %all-to-all-start.1 = ((bf16[4,4,128,128]{3,2,1,0:T(8,128)(2,1)}), bf16[4,4,128,128]{3,2,1,0:T(8,128)(2,1)S(1)}, u32[]{:S(2)}, u32[]{:S(2)}) async-start(bf16[4,4,128,128]{3,2,1,0:T(8,128)(2,1)} %plane_sums.1), calls=%async_computation.1 | async-start | bytes 1048576 | tf_op jit(solution)/shard_map/all_to_all | solution.py:317
  96.0 0.0 copy-done.15
  96.0 0.1 reshape.31
  96.1 13.8 %all-to-all-done.1.in_ref = bf16[4,4,128,128]{3,2,1,0:T(8,128)(2,1)S(1)} async-done(((bf16[4,4,128,128]{3,2,1,0:T(8,128)(2,1)}), bf16[4,4,128,128]{3,2,1,0:T(8,128)(2,1)S(1)}, u32[]{:S(2)}, u32[]{:S(2)}) %all-to-all-start.1) | async-done | bytes 524320 | tf_op jit(solution)/shard_map/all_to_all | solution.py:317
  109.9 0.0 copy-done.9
  109.9 0.0 copy-done.4
  109.9 1.4 %coadd.1 = (f32[128,512]{1,0:T(8,128)}, bf16[32,512]{1,0:T(8,128)(2,1)S(1)}, bf16[32,512]{1,0:T(8,128)(2,1)S(1)}) custom-call(s32[4]{0:T(128)S(1)} %copy-done.4, f32[16]{0:T(128)S(1)} %copy-done.9, s32[32,32]{1,0:T(8,128)S(1)} %bitcast.23, s32[32,32]{1,0:T(8,128)S(1)} %bitcast.22, s32[32,32]{1,0:T(8,128)S(1)} %bitcast.21, ...), custom_call_target="tpu_custom_call" | custom-call | tf_op jit(solution)/shard_map/coadd/pallas_call | solution.py:321
  111.4 2.9 %collective-permute-start = (bf16[32,512]{1,0:T(8,128)(2,1)S(1)}, bf16[32,512]{1,0:T(8,128)(2,1)S(1)}, u32[]{:S(2)}, u32[]{:S(2)}) collective-permute-start(bf16[32,512]{1,0:T(8,128)(2,1)S(1)} %get-tuple-element.10), channel_id=1, source_target_pairs={{0,1},{1,2},{2,3},{3,4},{4,5},{5,6},{6,7},{7,8},{8,9},{9,10},{10,1... | collective-permute-start | bytes 98312 | tf_op jit(solution)/shard_map/ppermute | solution.py:336
  114.2 6.3 %collective-permute-start.1 = (bf16[32,512]{1,0:T(8,128)(2,1)S(1)}, bf16[32,512]{1,0:T(8,128)(2,1)S(1)}, u32[]{:S(2)}, u32[]{:S(2)}) collective-permute-start(bf16[32,512]{1,0:T(8,128)(2,1)S(1)} %get-tuple-element.11), channel_id=1, source_target_pairs={{1,0},{2,1},{3,2},{4,3},{5,4},{6,5},{7,6},{8,7},{9,8},{10,9},{11,1... | collective-permute-start | bytes 98312 | tf_op jit(solution)/shard_map/ppermute | solution.py:337
  120.5 0.0 collective-permute-done.low_ref
  120.5 1.0 collective-permute-done.1.high_ref
  121.5 0.0 copy-done.12
  121.5 0.9 copy-done.3
  122.5 1.9 %detection.1 = f32[128,512]{1,0:T(8,128)} custom-call(f32[2,41]{1,0:T(2,128)S(1)} %copy-done.12, f32[128,512]{1,0:T(8,128)S(1)} %copy-done.3, bf16[32,512]{1,0:T(8,128)(2,1)S(1)} %collective-permute-done.low_ref, bf16[32,512]{1,0:T(8,128)(2,1)S(1)} %collective-permute-done.1.high_ref), custom_call_target="tpu_custom_call" | custom-call | tf_op jit(solution)/shard_map/detection/pallas_call | solution.py:339
  (8 shorter events, 0.0 us)
Async XLA Ops:
  1.4 1.6 %copy-start.1 = (f32[2,1,512,512]{3,2,1,0:T(8,128)S(1)}, f32[2,1,512,512]{3,2,1,0:T(8,128)}, u32[]{:S(2)}) copy-start(f32[2,1,512,512]{3,2,1,0:T(8,128)} %raw_ref.1) | copy-start | bytes 6291460
  3.0 1.2 copy-start.2
  4.2 0.7 copy-start.5
  4.9 0.7 copy-start.6
  5.6 0.7 copy-start.7
  6.2 0.7 copy-start.10
  6.9 0.7 copy-start.11
  12.2 1.3 %copy-start = (bf16[64,128,128]{2,1,0:T(8,128)(2,1)}, bf16[64,128,128]{2,1,0:T(8,128)(2,1)S(1)}, u32[]{:S(2)}) copy-start(bf16[64,128,128]{2,1,0:T(8,128)(2,1)S(1)} %warp.1) | copy-start | bytes 6291460
  13.6 5.4 %copy-start.8 = (s32[32,1]{0,1:T(1,128)S(1)}, s32[32,1]{0,1:T(1,128)}, u32[]{:S(2)}) copy-start(s32[32,1]{0,1:T(1,128)} %param.19) | copy-start | bytes 388
  13.6 5.4 %copy-start.16 = (s32[32,1]{0,1:T(1,128)S(1)}, s32[32,1]{0,1:T(1,128)}, u32[]{:S(2)}) copy-start(s32[32,1]{0,1:T(1,128)} %param.21) | copy-start | bytes 388
  13.6 5.4 %copy-start.17 = (s32[32,1]{0,1:T(1,128)S(1)}, s32[32,1]{0,1:T(1,128)}, u32[]{:S(2)}) copy-start(s32[32,1]{0,1:T(1,128)} %param.20) | copy-start | bytes 388
  13.6 75.0 %all-to-all-start = ((bf16[64,128,128]{2,1,0:T(8,128)(2,1)}), bf16[64,128,128]{2,1,0:T(8,128)(2,1)S(1)}, u32[]{:S(2)}, u32[]{:S(2)}) async-start(bf16[64,128,128]{2,1,0:T(8,128)(2,1)} %copy-done), calls=%async_computation | async-start | bytes 4194304 | tf_op jit(solution)/shard_map/all_to_all | solution.py:288
  18.9 91.0 %copy-start.9 = (f32[16]{0:T(128)S(1)}, f32[16]{0:T(128)}, u32[]{:S(2)}) copy-start(f32[16]{0:T(128)} %table_ref.3) | copy-start | bytes 196
  78.0 18.0 %copy-start.15 = (s32[3072]{0:T(1024)S(1)}, s32[3072]{0:T(1024)}, u32[]{:S(2)}) copy-start(s32[3072]{0:T(1024)} %all-reduce.meta_ref) | copy-start | bytes 36868
  78.6 31.3 %copy-start.4 = (s32[4]{0:T(128)S(1)}, s32[4]{0:T(128)}, u32[]{:S(2)}) copy-start(s32[4]{0:T(128)} %pad_add_fusion.me_ref) | copy-start | bytes 52
  88.5 0.7 copy-start.13
  89.2 0.6 copy-start.14
  89.8 31.7 %copy-start.12 = (f32[2,41]{1,0:T(2,128)S(1)}, f32[2,41]{1,0:T(2,128)}, u32[]{:S(2)}) copy-start(f32[2,41]{1,0:T(2,128)} %taps_ref.3) | copy-start | bytes 988
  92.5 17.4 %all-to-all-start.1 = ((bf16[4,4,128,128]{3,2,1,0:T(8,128)(2,1)}), bf16[4,4,128,128]{3,2,1,0:T(8,128)(2,1)S(1)}, u32[]{:S(2)}, u32[]{:S(2)}) async-start(bf16[4,4,128,128]{3,2,1,0:T(8,128)(2,1)} %plane_sums.1), calls=%async_computation.1 | async-start | bytes 1048576 | tf_op jit(solution)/shard_map/all_to_all | solution.py:317
  111.4 9.2 %collective-permute-start = (bf16[32,512]{1,0:T(8,128)(2,1)S(1)}, bf16[32,512]{1,0:T(8,128)(2,1)S(1)}, u32[]{:S(2)}, u32[]{:S(2)}) collective-permute-start(bf16[32,512]{1,0:T(8,128)(2,1)S(1)} %get-tuple-element.10), channel_id=1, source_target_pairs={{0,1},{1,2},{2,3},{3,4},{4,5},{5,6},{6,7},{7,8},{8,9},{9,10},{10,1... | collective-permute-start | bytes 98312 | tf_op jit(solution)/shard_map/ppermute | solution.py:336
  114.2 7.3 %collective-permute-start.1 = (bf16[32,512]{1,0:T(8,128)(2,1)S(1)}, bf16[32,512]{1,0:T(8,128)(2,1)S(1)}, u32[]{:S(2)}, u32[]{:S(2)}) collective-permute-start(bf16[32,512]{1,0:T(8,128)(2,1)S(1)} %get-tuple-element.11), channel_id=1, source_target_pairs={{1,0},{2,1},{3,2},{4,3},{5,4},{6,5},{7,6},{8,7},{9,8},{10,9},{11,1... | collective-permute-start | bytes 98312 | tf_op jit(solution)/shard_map/ppermute | solution.py:337
  121.5 1.0 copy-start.3

commit v2 on v1

v2 whole, which is shorter than its diff:
```python
import functools
import math

import jax
import jax.numpy as jnp
from jax import lax
from jax.experimental import pallas as pl
from jax.experimental.pallas import tpu as pltpu
from jax.sharding import Mesh
from jax.sharding import PartitionSpec as P

SIDE = 128
CAP = 2
PATCH_DEV = 4
HALO = 32
FIELDS = 4
VMEM_LIMIT = 48 * 1024 * 1024


def tap_row(tap, count, start, width, reverse):
    lane = lax.broadcasted_iota(jnp.int32, (1, width), 1)
    row = jnp.zeros((1, width), jnp.float32)
    for k in range(count):
        at = start + (count - 1 - k if reverse else k)
        row = jnp.where(lane == at % width, tap(k), row)
    return row


def toeplitz(row, height):
    return pltpu.roll(
        jnp.broadcast_to(row, (height, row.shape[1])), 0, 1, stride=1, stride_axis=0
    )


def store_band(band_ref, tiles):
    blocks = band_ref.shape[0] // SIDE
    for i in range(blocks):
        for j in range(blocks):
            place = (pl.ds(i * SIDE, SIDE), pl.ds(j * SIDE, SIDE))
            if abs(i - j) <= 1:
                first = (j - i + 1) * SIDE
                band_ref[place] = tiles[:, first : first + SIDE]
            else:
                band_ref[place] = jnp.zeros((SIDE, SIDE), band_ref.dtype)


def dot32(left, right):
    return jnp.dot(left, right, preferred_element_type=jnp.float32)


def two_parts(value):
    high = value.astype(jnp.bfloat16)
    return high, (value - high.astype(jnp.float32)).astype(jnp.bfloat16)


def three_parts(value):
    high = value.astype(jnp.bfloat16)
    rest = value - high.astype(jnp.float32)
    mid = rest.astype(jnp.bfloat16)
    return high, mid, (rest - mid.astype(jnp.float32)).astype(jnp.bfloat16)


def warp_kernel(
    split,
    owner_hbm,
    patch_hbm,
    index_hbm,
    table_hbm,
    taps_hbm,
    weights_hbm,
    shift_hbm,
    scale_hbm,
    bias_hbm,
    raw_hbm,
    flat_hbm,
    out_ref,
    owner_ref,
    patch_ref,
    index_ref,
    table_ref,
    taps_ref,
    weights_ref,
    shift_ref,
    scale_ref,
    bias_ref,
    raw_ref,
    flat_ref,
    count_ref,
    band_ref,
    left_ref,
    mid_ref,
    slot_rows,
    weight_rows,
    small_sem,
    flat_sem,
    raw_sem,
):
    nz, pn = split
    visits, _, rows, cols = raw_ref.shape
    terms, tap_count = taps_ref.shape[1], taps_ref.shape[3]
    half = tap_count // 2
    per_dest = nz * CAP
    data_rows = per_dest * SIDE

    small = [
        pltpu.make_async_copy(src, dst, small_sem.at[i])
        for i, (src, dst) in enumerate(
            (
                (taps_hbm, taps_ref),
                (bias_hbm, bias_ref),
                (owner_hbm, owner_ref),
                (patch_hbm, patch_ref),
                (index_hbm, index_ref),
                (table_hbm, table_ref),
                (weights_hbm, weights_ref),
                (shift_hbm, shift_ref),
                (scale_hbm, scale_ref),
            )
        )
    ]
    for copy in small:
        copy.start()
    flat_copy = pltpu.make_async_copy(flat_hbm, flat_ref, flat_sem)
    raw_copies = [
        pltpu.make_async_copy(raw_hbm.at[v], raw_ref.at[v], raw_sem.at[v]) for v in range(visits)
    ]
    raw_copies[0].start()
    flat_copy.start()
    for copy in raw_copies[1:]:
        copy.start()

    out_ref[...] = jnp.zeros_like(out_ref)
    slot_rows[...] = jnp.full(slot_rows.shape, -1.0, jnp.float32)
    weight_rows[...] = jnp.zeros_like(weight_rows)

    def clear(i, c):
        count_ref[i] = 0
        return c

    lax.fori_loop(0, count_ref.shape[0], clear, 0)
    for copy in small:
        copy.wait()

    def hat(length, axis, shift, scale):
        centre = (length - 1) / 2.0
        shape = (1, length) if axis == 1 else (length, 1)
        out_pos = lax.broadcasted_iota(jnp.int32, shape, axis).astype(jnp.float32)
        source = scale * (out_pos - centre) + centre + shift
        in_pos = lax.broadcasted_iota(jnp.int32, (length, length), 1 - axis).astype(jnp.float32)
        return jnp.maximum(0.0, 1.0 - jnp.abs(in_pos - source)).astype(jnp.bfloat16)

    row_blocks, col_blocks = rows // SIDE, cols // SIDE
    for visit in range(visits):
        bias = jnp.broadcast_to(bias_ref[visit], (SIDE, rows)).T
        raw_copies[visit].wait()
        if visit == 0:
            flat_copy.wait()
        for j in range(cols // SIDE):
            sl = pl.ds(j * SIDE, SIDE)
            left_ref[:, sl] = ((raw_ref[visit, 0, :, sl] - bias) * flat_ref[0, :, sl]).astype(
                jnp.bfloat16
            )

        matched = None
        for term in range(terms):
            across = tap_row(
                lambda k: taps_ref[visit, term, 1, k], tap_count, SIDE - half, 3 * SIDE, True
            )
            store_band(band_ref, toeplitz(across, SIDE).astype(jnp.bfloat16))
            mid_ref[...] = dot32(left_ref[...], band_ref[...]).astype(jnp.bfloat16)
            down = tap_row(
                lambda k: taps_ref[visit, term, 0, k], tap_count, SIDE - half, 3 * SIDE, False
            )
            store_band(band_ref, toeplitz(down, SIDE).astype(jnp.bfloat16))
            part = weights_ref[0, term, visit] * dot32(band_ref[...], mid_ref[...])
            matched = part if matched is None else matched + part
        left_ref[...] = matched.astype(jnp.bfloat16)

        band_ref[...] = hat(cols, 1, shift_ref[visit, 0, 1], scale_ref[visit, 0, 1])
        mid_ref[...] = dot32(left_ref[...], band_ref[...]).astype(jnp.bfloat16)
        band_ref[...] = hat(rows, 0, shift_ref[visit, 0, 0], scale_ref[visit, 0, 0])
        left_ref[...] = dot32(band_ref[...], mid_ref[...]).astype(jnp.bfloat16)

        for i in range(row_blocks):
            for j in range(col_blocks):
                block = visit * (row_blocks * col_blocks) + i * col_blocks + j
                owner = owner_ref[block]
                rank = count_ref[owner]
                count_ref[owner] = rank + 1
                sec = owner // (nz * pn)
                dev = owner - sec * (nz * pn)
                z = dev // pn
                dest = sec * pn + dev - z * pn
                at = z * CAP + rank
                out_ref[dest, pl.ds(pl.multiple_of(at * SIDE, SIDE), SIDE), :] = left_ref[
                    pl.ds(i * SIDE, SIDE), pl.ds(j * SIDE, SIDE)
                ]
                line = pl.ds(dest * per_dest + at, 1)
                slot_rows[line, :] = jnp.full((1, SIDE), patch_ref[block].astype(jnp.float32))
                weight_rows[line, :] = jnp.full((1, SIDE), table_ref[index_ref[block]])

    for dest in range(out_ref.shape[0]):
        part = pl.ds(dest * per_dest, per_dest)
        fields = jnp.concatenate(
            [slot_rows[part, :]]
            + [w.astype(jnp.float32) for w in three_parts(weight_rows[part, :])],
            axis=0,
        )
        out_ref[dest, pl.ds(data_rows, fields.shape[0]), :] = fields.astype(jnp.bfloat16)


def sum_kernel(nz, in_ref, out_ref, weight_ref):
    sources = in_ref.shape[0]
    per_dest = nz * CAP
    data_rows = per_dest * SIDE
    for g in range(sources):
        fields = in_ref[g, pl.ds(data_rows, FIELDS * per_dest), :].astype(jnp.float32)
        slot = fields[:per_dest]
        weight = (
            fields[per_dest : 2 * per_dest]
            + fields[2 * per_dest : 3 * per_dest]
            + fields[3 * per_dest :]
        )
        for j in range(PATCH_DEV):
            weight_ref[g, j] = jnp.where(slot == float(j), weight, 0.0)
    step = 32
    for z in range(nz):
        for c in range(SIDE // step):
            sums = [jnp.zeros((step, SIDE), jnp.float32) for _ in range(PATCH_DEV)]
            for g in range(sources):
                for r in range(CAP):
                    at = z * CAP + r
                    value = in_ref[g, pl.ds(at * SIDE + c * step, step), :].astype(jnp.float32)
                    for j in range(PATCH_DEV):
                        sums[j] = sums[j] + weight_ref[g, j, pl.ds(at, 1), :] * value
            for j in range(PATCH_DEV):
                out_ref[z, pl.ds(j * SIDE + c * step, step), :] = sums[j].astype(jnp.bfloat16)
        totals = []
        for j in range(PATCH_DEV):
            total = jnp.zeros((1, SIDE), jnp.float32)
            for g in range(sources):
                for r in range(CAP):
                    total = total + weight_ref[g, j, pl.ds(z * CAP + r, 1), :]
            totals.append(total)
        parts = three_parts(jnp.concatenate(totals, axis=0))
        extra = jnp.concatenate(
            [q.astype(jnp.float32) for q in parts] + [jnp.zeros((PATCH_DEV, SIDE), jnp.float32)],
            axis=0,
        )
        out_ref[z, pl.ds(PATCH_DEV * SIDE, FIELDS * PATCH_DEV), :] = extra.astype(jnp.bfloat16)


def coadd_kernel(in_ref, coadd_ref, main_ref, rest_ref, low_ref, high_ref):
    sources = in_ref.shape[0]
    total = jnp.zeros((PATCH_DEV, SIDE), jnp.float32)
    for z in range(sources):
        extra = in_ref[z, pl.ds(PATCH_DEV * SIDE, FIELDS * PATCH_DEV), :].astype(jnp.float32)
        total = total + (
            extra[:PATCH_DEV] + extra[PATCH_DEV : 2 * PATCH_DEV] + extra[2 * PATCH_DEV : 3 * PATCH_DEV]
        )
    total = jnp.maximum(total, 1.0)
    for j in range(PATCH_DEV):
        numerator = in_ref[0, pl.ds(j * SIDE, SIDE), :].astype(jnp.float32)
        for z in range(1, sources):
            numerator = numerator + in_ref[z, pl.ds(j * SIDE, SIDE), :].astype(jnp.float32)
        tile = numerator / total[j : j + 1]
        sl = pl.ds(j * SIDE, SIDE)
        coadd_ref[:, sl] = tile
        main, rest = two_parts(tile)
        main_ref[:, sl] = main
        rest_ref[:, sl] = rest
        high_ref[:, sl] = main[:HALO]
        low_ref[:, sl] = main[SIDE - HALO :]


def prepare_kernel(taps_ref, across_ref, centre_ref, edge_ref, band_ref):
    tap_count = taps_ref.shape[1]
    half = tap_count // 2
    across = tap_row(lambda k: taps_ref[1, k], tap_count, SIDE - half, 3 * SIDE, True)
    store_band(band_ref, toeplitz(across, SIDE))
    across_ref[0], across_ref[1] = two_parts(band_ref[...])
    down = tap_row(lambda k: taps_ref[0, k], tap_count, SIDE - half, 3 * SIDE, False)
    centre_ref[0], centre_ref[1] = two_parts(toeplitz(down, SIDE)[:, SIDE : 2 * SIDE])
    lane = lax.broadcasted_iota(jnp.int32, (2 * HALO, SIDE), 1)
    row = lax.broadcasted_iota(jnp.int32, (2 * HALO, SIDE), 0)
    before = tap_row(lambda k: taps_ref[0, k], tap_count, HALO - half, SIDE, False)
    after = tap_row(lambda k: taps_ref[0, k], tap_count, SIDE - HALO - half, SIDE, False)
    edge = jnp.where(
        (row < HALO) & (lane < HALO),
        toeplitz(before, 2 * HALO),
        jnp.where(
            (row >= HALO) & (lane >= HALO) & (lane < 2 * HALO), toeplitz(after, 2 * HALO), 0.0
        ),
    )
    edge_ref[0], edge_ref[1] = two_parts(edge[:, : 2 * HALO])


def dot_parts(left, across_ref):
    main, rest = two_parts(left)
    return dot32(main, across_ref[0]) + (dot32(main, across_ref[1]) + dot32(rest, across_ref[0]))


def centre_kernel(main_ref, rest_ref, across_ref, centre_ref, out_ref):
    main = main_ref[...]
    along = dot32(centre_ref[0], main) + (
        dot32(centre_ref[0], rest_ref[...]) + dot32(centre_ref[1], main)
    )
    out_ref[...] = dot_parts(along, across_ref)


def edge_kernel(inner_ref, low_ref, high_ref, across_ref, edge_ref, out_ref):
    halo = jnp.concatenate([low_ref[...], high_ref[...]], axis=0)
    along = dot32(edge_ref[0], halo) + dot32(edge_ref[1], halo)
    extra = dot_parts(along, across_ref)
    out_ref[pl.ds(0, HALO)] = inner_ref[pl.ds(0, HALO)] + extra[:HALO]
    out_ref[pl.ds(HALO, SIDE - 2 * HALO)] = inner_ref[pl.ds(HALO, SIDE - 2 * HALO)]
    out_ref[pl.ds(SIDE - HALO, HALO)] = inner_ref[pl.ds(SIDE - HALO, HALO)] + extra[HALO:]


def per_device(
    split,
    raw_pixels,
    flat_field,
    bias_rows,
    psf_taps,
    term_weights,
    warp_shift,
    warp_scale,
    owner_of,
    patch_slot,
    weight_index,
    weight_table,
    detect_taps,
):
    nz, pn, ns = split
    devices = nz * pn * ns
    group = ns * pn
    visits, _, rows, cols = raw_pixels.shape
    blocks = owner_of.shape[0]
    per_dest = nz * CAP
    width = PATCH_DEV * SIDE
    smem = pl.BlockSpec(memory_space=pltpu.SMEM)
    vmem = pl.BlockSpec(memory_space=pltpu.VMEM)
    hbm = pl.BlockSpec(memory_space=pltpu.HBM)
    params = pltpu.CompilerParams(vmem_limit_bytes=VMEM_LIMIT)

    def shaped(shape, dtype):
        return jax.ShapeDtypeStruct(shape, dtype)

    weights = term_weights.transpose(1, 2, 0)
    send = pl.pallas_call(
        functools.partial(warp_kernel, (nz, pn)),
        out_shape=shaped((group, per_dest * SIDE + FIELDS * per_dest, SIDE), jnp.bfloat16),
        in_specs=[hbm] * 11,
        out_specs=vmem,
        scratch_shapes=[
            pltpu.SMEM((blocks,), jnp.int32),
            pltpu.SMEM((blocks,), jnp.int32),
            pltpu.SMEM((blocks,), jnp.int32),
            pltpu.SMEM(weight_table.shape, jnp.float32),
            pltpu.SMEM(psf_taps.shape, jnp.float32),
            pltpu.SMEM(weights.shape, jnp.float32),
            pltpu.SMEM(warp_shift.shape, jnp.float32),
            pltpu.SMEM(warp_scale.shape, jnp.float32),
            pltpu.VMEM(bias_rows.shape, jnp.float32),
            pltpu.VMEM(raw_pixels.shape, jnp.float32),
            pltpu.VMEM(flat_field.shape, jnp.float32),
            pltpu.SMEM((devices,), jnp.int32),
            pltpu.VMEM((rows, cols), jnp.bfloat16),
            pltpu.VMEM((rows, cols), jnp.bfloat16),
            pltpu.VMEM((rows, cols), jnp.bfloat16),
            pltpu.VMEM((group * per_dest, SIDE), jnp.float32),
            pltpu.VMEM((group * per_dest, SIDE), jnp.float32),
            pltpu.SemaphoreType.DMA((9,)),
            pltpu.SemaphoreType.DMA,
            pltpu.SemaphoreType.DMA((visits,)),
        ],
        compiler_params=pltpu.CompilerParams(vmem_limit_bytes=60 * 1024 * 1024),
        name="warp",
    )(
        owner_of.reshape(blocks),
        patch_slot.reshape(blocks),
        weight_index.reshape(blocks),
        weight_table,
        psf_taps,
        weights,
        warp_shift,
        warp_scale,
        bias_rows,
        raw_pixels,
        flat_field,
    )
    arrived = lax.all_to_all(send, ("sec", "p"), split_axis=0, concat_axis=0, tiled=True)

    across, centre, edge = pl.pallas_call(
        prepare_kernel,
        out_shape=(
            shaped((2, width, width), jnp.bfloat16),
            shaped((2, SIDE, SIDE), jnp.bfloat16),
            shaped((2, 2 * HALO, 2 * HALO), jnp.bfloat16),
        ),
        in_specs=[smem],
        out_specs=(vmem, vmem, vmem),
        scratch_shapes=[pltpu.VMEM((width, width), jnp.float32)],
        compiler_params=params,
        name="matrices",
    )(detect_taps)

    plane_sums = pl.pallas_call(
        functools.partial(sum_kernel, nz),
        out_shape=shaped((nz, PATCH_DEV * SIDE + FIELDS * PATCH_DEV, SIDE), jnp.bfloat16),
        in_specs=[vmem],
        out_specs=vmem,
        scratch_shapes=[pltpu.VMEM((group, PATCH_DEV, per_dest, SIDE), jnp.float32)],
        compiler_params=params,
        name="plane_sums",
    )(arrived)
    gathered = lax.all_to_all(plane_sums, "z", split_axis=0, concat_axis=0, tiled=True)

    coadd, main, rest, low_rows, high_rows = pl.pallas_call(
        coadd_kernel,
        out_shape=(
            shaped((SIDE, width), jnp.float32),
            shaped((SIDE, width), jnp.bfloat16),
            shaped((SIDE, width), jnp.bfloat16),
            shaped((HALO, width), jnp.bfloat16),
            shaped((HALO, width), jnp.bfloat16),
        ),
        in_specs=[vmem],
        out_specs=(vmem,) * 5,
        compiler_params=params,
        name="coadd",
    )(gathered)

    every = ("sec", "z", "p")
    low = lax.ppermute(low_rows, every, [(i, i + 1) for i in range(devices - 1)])
    high = lax.ppermute(high_rows, every, [(i + 1, i) for i in range(devices - 1)])

    inner = pl.pallas_call(
        centre_kernel,
        out_shape=shaped((SIDE, width), jnp.float32),
        in_specs=[vmem] * 4,
        out_specs=vmem,
        compiler_params=params,
        cost_estimate=pl.CostEstimate(
            flops=6 * SIDE * width * (SIDE + width), bytes_accessed=2 << 20, transcendentals=0
        ),
        name="detect_centre",
    )(main, rest, across, centre)
    detection = pl.pallas_call(
        edge_kernel,
        out_shape=shaped((SIDE, width), jnp.float32),
        in_specs=[vmem] * 5,
        out_specs=vmem,
        compiler_params=params,
        name="detect_edges",
    )(inner, low, high, across, edge)
    return coadd, detection


def solution(mesh):
    ns, nd = mesh.shape["sec"], mesh.shape["dev"]
    nz = math.gcd(nd, 4)
    pn = nd // nz
    cut = Mesh(mesh.devices.reshape(ns, nz, pn), ("sec", "z", "p"))
    every = ("sec", "z", "p")
    placed = (
        P(None, every, None, None),
        P(every, None, None),
        P(None, every, None),
        P(),
        P(None, every, None),
        P(None, every, None),
        P(None, every, None),
        P(every, None),
        P(every, None),
        P(every, None),
        P(),
        P(),
    )
    return jax.shard_map(
        functools.partial(per_device, (nz, pn, ns)),
        mesh=cut,
        in_specs=placed,
        out_specs=(P(every, None), P(every, None)),
        check_vma=False,
    )
```

time: 125 us -> 72.2 us (0.58)
  waiting for transfers between devices: 14.8 us -> 0.01 us
  local copies, waits for them, and re-layouts: 10.6 us -> 0.01 us
  Pallas kernels: 20.5 us -> 11.3 us
  starting transfers between devices: 18 us -> 9.15 us
  blocking collectives: 58.8 us -> 50.8 us
    unnamed x1 -> x0, blocking collectives: 58.8 us -> none
    all_to_all x0 -> x2, blocking collectives: none -> 50.8 us  [the longest x1 32 us: per_device(): lax.all_to_all(send, ('sec', 'p'), split_axis=0, concat_axis=0, tiled=True)]
    all_to_all x2 -> x0, waiting for transfers between devices: 13.8 us -> none  [the longest x1 13.8 us: per_device(): lax.all_to_all(partial_sums, 'z', split_axis=0, concat_axis=0, tiled=True)]
    unnamed x37 -> x2, local copies, waits for them, and re-layouts: 9.78 us -> 0.01 us
    pallas_call x5 -> x6, Pallas kernels: 20.5 us -> 11.3 us  [the longest x1 6.69 us: per_device(): pl.pallas_call(functools.partial(warp_kernel, (nz, pn)), out_shape=shaped...]
    all_to_all x2 -> x0, starting transfers between devices: 8.82 us -> none  [the longest x1 5.36 us: per_device(): lax.all_to_all(send, ('sec', 'p'), split_axis=0, concat_axis=0, tiled=True)]
  transfers between devices with their start and end apart: 4 -> 2, of which waited for: 2 -> 0; matrix products, arithmetic and copies ran while one was open for 1% -> 0% of each run, Pallas kernels for 8% -> 2%
where the time goes in v2:
time: 72.2 us; the launch traced here: 72 us
  blocking collectives  50.8 us (70%)
  Pallas kernels  11.3 us (16%)
  starting transfers between devices  9.15 us (13%)
    all_to_all x1, blocking collectives, per_device(): lax.all_to_all(send, ('sec', 'p'), split_axis=0, concat_axis=0, tiled=True)  32 us
    all_to_all x1, blocking collectives, per_device(): lax.all_to_all(plane_sums, 'z', split_axis=0, concat_axis=0, tiled=True)  18.8 us
    ppermute x1, starting transfers between devices, per_device(): lax.ppermute(high_rows, every, [(i + 1, i) for i in range(devices - 1)])  6.93 us
    pallas_call x1, Pallas kernels, per_device(): pl.pallas_call(functools.partial(warp_kernel, (nz, pn)), out_shape=shaped...  6.69 us
    ppermute x1, starting transfers between devices, per_device(): lax.ppermute(low_rows, every, [(i, i + 1) for i in range(devices - 1)])  2.22 us
  transfers between devices with their start and end apart: 2, of which 0 were waited for; matrix products, arithmetic and copies ran while one was open for 0% of the time, Pallas kernels for 2%

profile of v2, /device:TPU:1, one launch (start us, length us, event | category | flops | bytes accessed | tf_op | source)
XLA Modules:
  0.0 72.0 jit_solution(10507431814858416083)
XLA Ops:
  0.6 6.7 %warp.1 = bf16[8,1056,128]{2,1,0:T(8,128)(2,1)} custom-call(s32[32]{0:T(128)} %bitcast.4, s32[32]{0:T(128)} %bitcast.5, s32[32]{0:T(128)} %bitcast.6, f32[16]{0:T(128)} %table_hbm.1, f32[2,1,2,41]{3,2,1,0:T(2,128)} %taps_hbm.1, f32[1,1,2]{2,1,0:T(1,128)} %bitcast.7, f32[2,1,2]{2,1,0:T(1,128)} %shift_hbm.1, f32[2,1,2]{2,1,0:T(1,128)} %scale_hbm.1, ...), custom_call_target="tpu_custom_call" | custom-call | tf_op jit(solution)/shard_map/warp/pallas_call | solution.py:351
  7.3 32.0 %all_to_all.10.in_ref = bf16[8,1056,128]{2,1,0:T(8,128)(2,1)S(1)} all-to-all(bf16[8,1056,128]{2,1,0:T(8,128)(2,1)} %warp.1), channel_id=1, replica_groups=mesh['sec'=2,'z'=4,'p'=4] {'sec','p'}, dimensions={0} | all-to-all | bytes 4325376 | tf_op jit(solution)/shard_map/all_to_all | solution.py:393
  39.4 0.0 copy-start
  39.4 1.3 %plane_sums.1 = bf16[4,528,128]{2,1,0:T(8,128)(2,1)S(1)} custom-call(bf16[8,1056,128]{2,1,0:T(8,128)(2,1)S(1)} %all_to_all.10.in_ref), custom_call_target="tpu_custom_call" | custom-call | tf_op jit(solution)/shard_map/plane_sums/pallas_call | solution.py:409
  40.7 18.8 %all_to_all.11.in_ref = bf16[4,528,128]{2,1,0:T(8,128)(2,1)S(1)} all-to-all(bf16[4,528,128]{2,1,0:T(8,128)(2,1)S(1)} %plane_sums.1), channel_id=1, replica_groups=mesh['sec'=2,'z'=4,'p'=4] {'z'}, dimensions={0} | all-to-all | bytes 1081344 | tf_op jit(solution)/shard_map/all_to_all | solution.py:418
  59.5 0.8 %coadd.1 = (f32[128,512]{1,0:T(8,128)}, bf16[128,512]{1,0:T(8,128)(2,1)S(1)}, bf16[128,512]{1,0:T(8,128)(2,1)S(1)}, bf16[32,512]{1,0:T(8,128)(2,1)S(1)}, bf16[32,512]{1,0:T(8,128)(2,1)S(1)}) custom-call(bf16[4,528,128]{2,1,0:T(8,128)(2,1)S(1)} %all_to_all.11.in_ref), custom_call_target="tpu_custom_call" | custom-call | tf_op jit(solution)/shard_map/coadd/pallas_call | solution.py:420
  60.2 2.2 %collective-permute-start = (bf16[32,512]{1,0:T(8,128)(2,1)S(1)}, bf16[32,512]{1,0:T(8,128)(2,1)S(1)}, u32[]{:S(2)}, u32[]{:S(2)}) collective-permute-start(bf16[32,512]{1,0:T(8,128)(2,1)S(1)} %get-tuple-element.15), channel_id=1, source_target_pairs={{0,1},{1,2},{2,3},{3,4},{4,5},{5,6},{6,7},{7,8},{8,9},{9,10},{10,1... | collective-permute-start | bytes 98312 | tf_op jit(solution)/shard_map/ppermute | solution.py:436
  62.5 6.9 %collective-permute-start.1 = (bf16[32,512]{1,0:T(8,128)(2,1)S(1)}, bf16[32,512]{1,0:T(8,128)(2,1)S(1)}, u32[]{:S(2)}, u32[]{:S(2)}) collective-permute-start(bf16[32,512]{1,0:T(8,128)(2,1)S(1)} %get-tuple-element.16), channel_id=1, source_target_pairs={{1,0},{2,1},{3,2},{4,3},{5,4},{6,5},{7,6},{8,7},{9,8},{10,9},{11,1... | collective-permute-start | bytes 98312 | tf_op jit(solution)/shard_map/ppermute | solution.py:437
  69.4 0.0 copy-done
  69.4 0.7 %matrices.1 = (bf16[2,512,512]{2,1,0:T(8,128)(2,1)S(1)}, bf16[2,128,128]{2,1,0:T(8,128)(2,1)S(1)}, bf16[2,64,64]{2,1,0:T(8,128)(2,1)S(1)}) custom-call(f32[2,41]{1,0:T(2,128)S(1)} %copy-done), custom_call_target="tpu_custom_call" | custom-call | tf_op jit(solution)/shard_map/matrices/pallas_call | solution.py:395
  70.1 0.6 detect_centre.1.inner_ref
  70.7 0.0 collective-permute-done.low_ref
  70.7 0.0 collective-permute-done.1.high_ref
  70.7 1.2 %detect_edges.1 = f32[128,512]{1,0:T(8,128)} custom-call(f32[128,512]{1,0:T(8,128)S(1)} %detect_centre.1.inner_ref, bf16[32,512]{1,0:T(8,128)(2,1)S(1)} %collective-permute-done.low_ref, bf16[32,512]{1,0:T(8,128)(2,1)S(1)} %collective-permute-done.1.high_ref, bf16[2,512,512]{2,1,0:T(8,128)(2,1)S(1)} %get-tuple-element.13.across_ref, ...), custom_call_target="tpu_custom_call" | custom-call | tf_op jit(solution)/shard_map/detect_edges/pallas_call | solution.py:450
Async XLA Ops:
  39.4 30.0 %copy-start = (f32[2,41]{1,0:T(2,128)S(1)}, f32[2,41]{1,0:T(2,128)}, u32[]{:S(2)}) copy-start(f32[2,41]{1,0:T(2,128)} %taps_ref.1) | copy-start | bytes 988
  60.2 10.5 %collective-permute-start = (bf16[32,512]{1,0:T(8,128)(2,1)S(1)}, bf16[32,512]{1,0:T(8,128)(2,1)S(1)}, u32[]{:S(2)}, u32[]{:S(2)}) collective-permute-start(bf16[32,512]{1,0:T(8,128)(2,1)S(1)} %get-tuple-element.15), channel_id=1, source_target_pairs={{0,1},{1,2},{2,3},{3,4},{4,5},{5,6},{6,7},{7,8},{8,9},{9,10},{10,1... | collective-permute-start | bytes 98312 | tf_op jit(solution)/shard_map/ppermute | solution.py:436
  62.5 8.3 %collective-permute-start.1 = (bf16[32,512]{1,0:T(8,128)(2,1)S(1)}, bf16[32,512]{1,0:T(8,128)(2,1)S(1)}, u32[]{:S(2)}, u32[]{:S(2)}) collective-permute-start(bf16[32,512]{1,0:T(8,128)(2,1)S(1)} %get-tuple-element.16), channel_id=1, source_target_pairs={{1,0},{2,1},{3,2},{4,3},{5,4},{6,5},{7,6},{8,7},{9,8},{10,9},{11,1... | collective-permute-start | bytes 98312 | tf_op jit(solution)/shard_map/ppermute | solution.py:437

commit v3 on v2

--- a/solution.py
+++ b/solution.py
@@ -73,7 +73,34 @@
     bias_hbm,
     raw_hbm,
     flat_hbm,
-    out_ref,
+    *rest,
+):
+    nz, pn, ns = split
+    outs, rest = rest[: ns * pn], rest[ns * pn :]
+    warp_body(
+        split,
+        (
+            owner_hbm,
+            patch_hbm,
+            index_hbm,
+            table_hbm,
+            taps_hbm,
+            weights_hbm,
+            shift_hbm,
+            scale_hbm,
+            bias_hbm,
+            raw_hbm,
+            flat_hbm,
+        ),
+        outs,
+        *rest,
+    )
+
+
+def warp_body(
+    split,
+    inputs,
+    outs,
     owner_ref,
     patch_ref,
     index_ref,
@@ -94,8 +121,24 @@
     small_sem,
     flat_sem,
     raw_sem,
+    out_ref,
+    out_sem,
 ):
-    nz, pn = split
+    (
+        owner_hbm,
+        patch_hbm,
+        index_hbm,
+        table_hbm,
+        taps_hbm,
+        weights_hbm,
+        shift_hbm,
+        scale_hbm,
+        bias_hbm,
+        raw_hbm,
+        flat_hbm,
+    ) = inputs
+    nz, pn, ns = split
+    mine = lax.axis_index("sec") * pn + lax.axis_index("p")
     visits, _, rows, cols = raw_ref.shape
     terms, tap_count = taps_ref.shape[1], taps_ref.shape[3]
     half = tap_count // 2
@@ -190,14 +233,17 @@
                 sec = owner // (nz * pn)
                 dev = owner - sec * (nz * pn)
                 z = dev // pn
-                dest = sec * pn + dev - z * pn
-                at = z * CAP + rank
+                dest = (sec * pn + dev - z * pn) ^ mine
+                at = (z ^ lax.axis_index("z")) * CAP + rank
                 out_ref[dest, pl.ds(pl.multiple_of(at * SIDE, SIDE), SIDE), :] = left_ref[
                     pl.ds(i * SIDE, SIDE), pl.ds(j * SIDE, SIDE)
                 ]
                 line = pl.ds(dest * per_dest + at, 1)
                 slot_rows[line, :] = jnp.full((1, SIDE), patch_ref[block].astype(jnp.float32))
                 weight_rows[line, :] = jnp.full((1, SIDE), table_ref[index_ref[block]])
+
+    def out_copy(dest):
+        return pltpu.make_async_copy(out_ref.at[dest], outs[dest], out_sem.at[dest])
 
     for dest in range(out_ref.shape[0]):
         part = pl.ds(dest * per_dest, per_dest)
@@ -207,14 +253,17 @@
             axis=0,
         )
         out_ref[dest, pl.ds(data_rows, fields.shape[0]), :] = fields.astype(jnp.bfloat16)
-
-
-def sum_kernel(nz, in_ref, out_ref, weight_ref):
-    sources = in_ref.shape[0]
+        out_copy(dest).start()
+    for dest in range(out_ref.shape[0]):
+        out_copy(dest).wait()
+
+
+def sum_kernel(nz, sources, *refs):
+    ins, outs, weight_ref = refs[:sources], refs[sources:-1], refs[-1]
     per_dest = nz * CAP
     data_rows = per_dest * SIDE
     for g in range(sources):
-        fields = in_ref[g, pl.ds(data_rows, FIELDS * per_dest), :].astype(jnp.float32)
+        fields = ins[g][pl.ds(data_rows, FIELDS * per_dest), :].astype(jnp.float32)
         slot = fields[:per_dest]
         weight = (
             fields[per_dest : 2 * per_dest]
@@ -230,11 +279,11 @@
             for g in range(sources):
                 for r in range(CAP):
                     at = z * CAP + r
-                    value = in_ref[g, pl.ds(at * SIDE + c * step, step), :].astype(jnp.float32)
+                    value = ins[g][pl.ds(at * SIDE + c * step, step), :].astype(jnp.float32)
                     for j in range(PATCH_DEV):
                         sums[j] = sums[j] + weight_ref[g, j, pl.ds(at, 1), :] * value
             for j in range(PATCH_DEV):
-                out_ref[z, pl.ds(j * SIDE + c * step, step), :] = sums[j].astype(jnp.bfloat16)
+                outs[z][pl.ds(j * SIDE + c * step, step), :] = sums[j].astype(jnp.bfloat16)
         totals = []
         for j in range(PATCH_DEV):
             total = jnp.zeros((1, SIDE), jnp.float32)
@@ -247,22 +296,22 @@
             [q.astype(jnp.float32) for q in parts] + [jnp.zeros((PATCH_DEV, SIDE), jnp.float32)],
             axis=0,
         )
-        out_ref[z, pl.ds(PATCH_DEV * SIDE, FIELDS * PATCH_DEV), :] = extra.astype(jnp.bfloat16)
-
-
-def coadd_kernel(in_ref, coadd_ref, main_ref, rest_ref, low_ref, high_ref):
-    sources = in_ref.shape[0]
+        outs[z][pl.ds(PATCH_DEV * SIDE, FIELDS * PATCH_DEV), :] = extra.astype(jnp.bfloat16)
+
+
+def coadd_kernel(sources, *refs):
+    ins, (coadd_ref, main_ref, rest_ref, low_ref, high_ref) = refs[:sources], refs[sources:]
     total = jnp.zeros((PATCH_DEV, SIDE), jnp.float32)
     for z in range(sources):
-        extra = in_ref[z, pl.ds(PATCH_DEV * SIDE, FIELDS * PATCH_DEV), :].astype(jnp.float32)
+        extra = ins[z][pl.ds(PATCH_DEV * SIDE, FIELDS * PATCH_DEV), :].astype(jnp.float32)
         total = total + (
             extra[:PATCH_DEV] + extra[PATCH_DEV : 2 * PATCH_DEV] + extra[2 * PATCH_DEV : 3 * PATCH_DEV]
         )
     total = jnp.maximum(total, 1.0)
     for j in range(PATCH_DEV):
-        numerator = in_ref[0, pl.ds(j * SIDE, SIDE), :].astype(jnp.float32)
+        numerator = ins[0][pl.ds(j * SIDE, SIDE), :].astype(jnp.float32)
         for z in range(1, sources):
-            numerator = numerator + in_ref[z, pl.ds(j * SIDE, SIDE), :].astype(jnp.float32)
+            numerator = numerator + ins[z][pl.ds(j * SIDE, SIDE), :].astype(jnp.float32)
         tile = numerator / total[j : j + 1]
         sl = pl.ds(j * SIDE, SIDE)
         coadd_ref[:, sl] = tile
@@ -338,6 +387,7 @@
     visits, _, rows, cols = raw_pixels.shape
     blocks = owner_of.shape[0]
     per_dest = nz * CAP
+    payload = per_dest * (SIDE + FIELDS)
     width = PATCH_DEV * SIDE
     smem = pl.BlockSpec(memory_space=pltpu.SMEM)
     vmem = pl.BlockSpec(memory_space=pltpu.VMEM)
@@ -349,10 +399,10 @@
 
     weights = term_weights.transpose(1, 2, 0)
     send = pl.pallas_call(
-        functools.partial(warp_kernel, (nz, pn)),
-        out_shape=shaped((group, per_dest * SIDE + FIELDS * per_dest, SIDE), jnp.bfloat16),
+        functools.partial(warp_kernel, split),
+        out_shape=[shaped((payload, SIDE), jnp.bfloat16)] * group,
         in_specs=[hbm] * 11,
-        out_specs=vmem,
+        out_specs=[hbm] * group,
         scratch_shapes=[
             pltpu.SMEM((blocks,), jnp.int32),
             pltpu.SMEM((blocks,), jnp.int32),
@@ -374,6 +424,8 @@
             pltpu.SemaphoreType.DMA((9,)),
             pltpu.SemaphoreType.DMA,
             pltpu.SemaphoreType.DMA((visits,)),
+            pltpu.VMEM((group, payload, SIDE), jnp.bfloat16),
+            pltpu.SemaphoreType.DMA((group,)),
         ],
         compiler_params=pltpu.CompilerParams(vmem_limit_bytes=60 * 1024 * 1024),
         name="warp",
@@ -390,7 +442,11 @@
         raw_pixels,
         flat_field,
     )
-    arrived = lax.all_to_all(send, ("sec", "p"), split_axis=0, concat_axis=0, tiled=True)
+    far_first = sorted(range(1, group), key=lambda k: (k == pn, -bin(k % pn).count("1")))
+    arrived = [send[0]] + [
+        lax.ppermute(send[k], ("sec", "p"), [(g, g ^ k) for g in range(group)])
+        for k in far_first
+    ]
 
     across, centre, edge = pl.pallas_call(
         prepare_kernel,
@@ -407,18 +463,20 @@
     )(detect_taps)
 
     plane_sums = pl.pallas_call(
-        functools.partial(sum_kernel, nz),
-        out_shape=shaped((nz, PATCH_DEV * SIDE + FIELDS * PATCH_DEV, SIDE), jnp.bfloat16),
-        in_specs=[vmem],
-        out_specs=vmem,
+        functools.partial(sum_kernel, nz, group),
+        out_shape=[shaped((PATCH_DEV * (SIDE + FIELDS), SIDE), jnp.bfloat16)] * nz,
+        in_specs=[vmem] * group,
+        out_specs=[vmem] * nz,
         scratch_shapes=[pltpu.VMEM((group, PATCH_DEV, per_dest, SIDE), jnp.float32)],
         compiler_params=params,
         name="plane_sums",
-    )(arrived)
-    gathered = lax.all_to_all(plane_sums, "z", split_axis=0, concat_axis=0, tiled=True)
+    )(*arrived)
+    gathered = [plane_sums[0]] + [
+        lax.ppermute(plane_sums[d], "z", [(z, z ^ d) for z in range(nz)]) for d in range(1, nz)
+    ]
 
     coadd, main, rest, low_rows, high_rows = pl.pallas_call(
-        coadd_kernel,
+        functools.partial(coadd_kernel, nz),
         out_shape=(
             shaped((SIDE, width), jnp.float32),
             shaped((SIDE, width), jnp.bfloat16),
@@ -426,11 +484,11 @@
             shaped((HALO, width), jnp.bfloat16),
             shaped((HALO, width), jnp.bfloat16),
         ),
-        in_specs=[vmem],
+        in_specs=[vmem] * nz,
         out_specs=(vmem,) * 5,
         compiler_params=params,
         name="coadd",
-    )(gathered)
+    )(*gathered)
 
     every = ("sec", "z", "p")
     low = lax.ppermute(low_rows, every, [(i, i + 1) for i in range(devices - 1)])

time: 72.2 us -> 65.2 us (0.903)
  the two profiles are of different devices: /device:TPU:1 before, /device:TPU:14 now
where the time goes in v3:
time: 65.2 us; the launch traced here: 65 us
  waiting for transfers between devices  35.8 us (55%)
  starting transfers between devices  16.2 us (25%)
  Pallas kernels  11.4 us (17%)
  local copies, waits for them, and re-layouts  0.96 us (1%)
  between operations  0.71 us (1%)
    ppermute x7, waiting for transfers between devices, per_device(): lax.ppermute(send[k], ('sec', 'p'), [(g, g ^ k) for g in range(group)])  19.9 us
    ppermute x3, waiting for transfers between devices, per_device(): lax.ppermute(plane_sums[d], 'z', [(z, z ^ d) for z in range(nz)])  12 us
    pallas_call x1, Pallas kernels, per_device(): pl.pallas_call(functools.partial(warp_kernel, split), out_shape=[shaped((...  6.79 us
    ppermute x7, starting transfers between devices, per_device(): lax.ppermute(send[k], ('sec', 'p'), [(g, g ^ k) for g in range(group)])  6.79 us
    ppermute x1, waiting for transfers between devices, per_device(): lax.ppermute(high_rows, every, [(i + 1, i) for i in range(devices - 1)])  3.84 us
    ppermute x3, starting transfers between devices, per_device(): lax.ppermute(plane_sums[d], 'z', [(z, z ^ d) for z in range(nz)])  3.55 us
    ppermute x1, starting transfers between devices, per_device(): lax.ppermute(low_rows, every, [(i, i + 1) for i in range(devices - 1)])  3.4 us
    ppermute x1, starting transfers between devices, per_device(): lax.ppermute(high_rows, every, [(i + 1, i) for i in range(devices - 1)])  2.43 us
  transfers between devices with their start and end apart: 12, of which 9 were waited for; matrix products, arithmetic and copies ran while one was open for 0% of the time, Pallas kernels for 2%

profile of v3, /device:TPU:14, one launch (start us, length us, event | category | flops | bytes accessed | tf_op | source)
XLA Modules:
  0.0 65.0 jit_solution(5923154623203391899)
XLA Ops:
  0.6 6.8 %warp.1 = (bf16[1056,128]{1,0:T(8,128)(2,1)}, bf16[1056,128]{1,0:T(8,128)(2,1)}, bf16[1056,128]{1,0:T(8,128)(2,1)}, bf16[1056,128]{1,0:T(8,128)(2,1)}, bf16[1056...) custom-call(s32[32]{0:T(128)} %bitcast.4, s32[32]{0:T(128)} %bitcast.5, ...), custom_call_target="tpu_custom_call" | custom-call | tf_op jit(solution)/shard_map/warp/pallas_call | solution.py:401
  7.4 0.0 copy-start.1
  7.4 0.5 collective-permute-start
  8.0 1.6 %collective-permute-start.1 = (bf16[1056,128]{1,0:T(8,128)(2,1)}, bf16[1056,128]{1,0:T(8,128)(2,1)S(1)}, u32[]{:S(2)}, u32[]{:S(2)}) collective-permute-start(bf16[1056,128]{1,0:T(8,128)(2,1)} %get-tuple-element.24), channel_id=1, source_target_pairs={{0,19},{1,18},{2,17},{3,16},{16,3},{17,2},{18,1},{19,0},{4,23},{5,... | collective-permute-start | bytes 811016 | tf_op jit(solution)/shard_map/ppermute | solution.py:447
  9.6 0.5 collective-permute-start.2
  10.1 0.9 %collective-permute-start.3 = (bf16[1056,128]{1,0:T(8,128)(2,1)}, bf16[1056,128]{1,0:T(8,128)(2,1)S(1)}, u32[]{:S(2)}, u32[]{:S(2)}) collective-permute-start(bf16[1056,128]{1,0:T(8,128)(2,1)} %get-tuple-element.26), channel_id=1, source_target_pairs={{0,2},{1,3},{2,0},{3,1},{16,18},{17,19},{18,16},{19,17},{4,6},{5,7... | collective-permute-start | bytes 811016 | tf_op jit(solution)/shard_map/ppermute | solution.py:447
  11.0 1.2 %collective-permute-start.4 = (bf16[1056,128]{1,0:T(8,128)(2,1)}, bf16[1056,128]{1,0:T(8,128)(2,1)S(1)}, u32[]{:S(2)}, u32[]{:S(2)}) collective-permute-start(bf16[1056,128]{1,0:T(8,128)(2,1)} %get-tuple-element.27), channel_id=1, source_target_pairs={{0,17},{1,16},{2,19},{3,18},{16,1},{17,0},{18,3},{19,2},{4,21},{5,... | collective-permute-start | bytes 811016 | tf_op jit(solution)/shard_map/ppermute | solution.py:447
  12.2 5.9 %collective-permute-done.refs_1_ = bf16[1056,128]{1,0:T(8,128)(2,1)S(1)} collective-permute-done((bf16[1056,128]{1,0:T(8,128)(2,1)}, bf16[1056,128]{1,0:T(8,128)(2,1)S(1)}, u32[]{:S(2)}, u32[]{:S(2)}) %collective-permute-start) | collective-permute-done | bytes 270368 | tf_op jit(solution)/shard_map/ppermute | solution.py:447
  18.1 0.0 collective-permute-start.5
  18.1 3.5 %collective-permute-done.1.refs_2_ = bf16[1056,128]{1,0:T(8,128)(2,1)S(1)} collective-permute-done((bf16[1056,128]{1,0:T(8,128)(2,1)}, bf16[1056,128]{1,0:T(8,128)(2,1)S(1)}, u32[]{:S(2)}, u32[]{:S(2)}) %collective-permute-start.1) | collective-permute-done | bytes 270368 | tf_op jit(solution)/shard_map/ppermute | solution.py:447
  21.6 2.1 %collective-permute-start.6 = (bf16[1056,128]{1,0:T(8,128)(2,1)}, bf16[1056,128]{1,0:T(8,128)(2,1)S(1)}, u32[]{:S(2)}, u32[]{:S(2)}) collective-permute-start(bf16[1056,128]{1,0:T(8,128)(2,1)} %get-tuple-element.29), channel_id=1, source_target_pairs={{0,16},{1,17},{2,18},{3,19},{16,0},{17,1},{18,2},{19,3},{4,20},{5,... | collective-permute-start | bytes 811016 | tf_op jit(solution)/shard_map/ppermute | solution.py:447
  23.6 5.0 %collective-permute-done.2.refs_3_ = bf16[1056,128]{1,0:T(8,128)(2,1)S(1)} collective-permute-done((bf16[1056,128]{1,0:T(8,128)(2,1)}, bf16[1056,128]{1,0:T(8,128)(2,1)S(1)}, u32[]{:S(2)}, u32[]{:S(2)}) %collective-permute-start.2) | collective-permute-done | bytes 270368 | tf_op jit(solution)/shard_map/ppermute | solution.py:447
  28.7 0.0 collective-permute-done.3.refs_4_
  28.7 3.5 %collective-permute-done.4.refs_5_ = bf16[1056,128]{1,0:T(8,128)(2,1)S(1)} collective-permute-done((bf16[1056,128]{1,0:T(8,128)(2,1)}, bf16[1056,128]{1,0:T(8,128)(2,1)S(1)}, u32[]{:S(2)}, u32[]{:S(2)}) %collective-permute-start.4) | collective-permute-done | bytes 270368 | tf_op jit(solution)/shard_map/ppermute | solution.py:447
  32.1 2.0 %collective-permute-done.5.refs_6_ = bf16[1056,128]{1,0:T(8,128)(2,1)S(1)} collective-permute-done((bf16[1056,128]{1,0:T(8,128)(2,1)}, bf16[1056,128]{1,0:T(8,128)(2,1)S(1)}, u32[]{:S(2)}, u32[]{:S(2)}) %collective-permute-start.5) | collective-permute-done | bytes 270368 | tf_op jit(solution)/shard_map/ppermute | solution.py:447
  34.2 0.0 collective-permute-done.6.refs_7_
  34.2 0.0 copy-start
  34.2 1.0 %copy-done = bf16[1056,128]{1,0:T(8,128)(2,1)S(1)} copy-done((bf16[1056,128]{1,0:T(8,128)(2,1)S(1)}, bf16[1056,128]{1,0:T(8,128)(2,1)}, u32[]{:S(2)}) %copy-start) | copy-done | bytes 270360
  35.1 1.3 %plane_sums.1 = (bf16[528,128]{1,0:T(8,128)(2,1)S(1)}, bf16[528,128]{1,0:T(8,128)(2,1)S(1)}, bf16[528,128]{1,0:T(8,128)(2,1)S(1)}, bf16[528,128]{1,0:T(8,128)(2,1)S(1)}) custom-call(bf16[1056,128]{1,0:T(8,128)(2,1)S(1)} %copy-done, bf16[1056,128]{1,0:T(8,128)(2,1)S(1)} %collective-permute-done.refs_1_, bf16[1056,128]{1,0:T(8,128)(2,1)S(1)} %collective-permute-done.1.refs_2_, ...), custom_call_target="tpu_custom_call" | custom-call | tf_op jit(solution)/shard_map/plane_sums/pallas_call | solution.py:465
  36.4 0.5 collective-permute-start.7
  37.0 2.6 %collective-permute-start.8 = (bf16[528,128]{1,0:T(8,128)(2,1)S(1)}, bf16[528,128]{1,0:T(8,128)(2,1)S(1)}, u32[]{:S(2)}, u32[]{:S(2)}) collective-permute-start(bf16[528,128]{1,0:T(8,128)(2,1)S(1)} %get-tuple-element.32), channel_id=1, source_target_pairs={{0,8},{4,12},{8,0},{12,4},{1,9},{5,13},{9,1},{13,5},{2,10},{6,14},... | collective-permute-start | bytes 405512 | tf_op jit(solution)/shard_map/ppermute | solution.py:475
  39.5 0.4 collective-permute-start.9
  40.0 2.6 %collective-permute-done.7.refs_1_ = bf16[528,128]{1,0:T(8,128)(2,1)S(1)} collective-permute-done((bf16[528,128]{1,0:T(8,128)(2,1)S(1)}, bf16[528,128]{1,0:T(8,128)(2,1)S(1)}, u32[]{:S(2)}, u32[]{:S(2)}) %collective-permute-start.7) | collective-permute-done | bytes 135200 | tf_op jit(solution)/shard_map/ppermute | solution.py:475
  42.6 6.7 %collective-permute-done.8.refs_2_ = bf16[528,128]{1,0:T(8,128)(2,1)S(1)} collective-permute-done((bf16[528,128]{1,0:T(8,128)(2,1)S(1)}, bf16[528,128]{1,0:T(8,128)(2,1)S(1)}, u32[]{:S(2)}, u32[]{:S(2)}) %collective-permute-start.8) | collective-permute-done | bytes 135200 | tf_op jit(solution)/shard_map/ppermute | solution.py:475
  49.3 2.7 %collective-permute-done.9.refs_3_ = bf16[528,128]{1,0:T(8,128)(2,1)S(1)} collective-permute-done((bf16[528,128]{1,0:T(8,128)(2,1)S(1)}, bf16[528,128]{1,0:T(8,128)(2,1)S(1)}, u32[]{:S(2)}, u32[]{:S(2)}) %collective-permute-start.9) | collective-permute-done | bytes 135200 | tf_op jit(solution)/shard_map/ppermute | solution.py:475
  52.0 0.8 %coadd.1 = (f32[128,512]{1,0:T(8,128)}, bf16[128,512]{1,0:T(8,128)(2,1)S(1)}, bf16[128,512]{1,0:T(8,128)(2,1)S(1)}, bf16[32,512]{1,0:T(8,128)(2,1)S(1)}, bf16[32,512]{1,0:T(8,128)(2,1)S(1)}) custom-call(bf16[528,128]{1,0:T(8,128)(2,1)S(1)} %get-tuple-element.30.refs_0_, bf16[528,128]{1,0:T(8,128)(2,1)S(1)} %collective-permute-done.7.refs_1_, ...), custom_call_target="tpu_custom_call" | custom-call | tf_op jit(solution)/shard_map/coadd/pallas_call | solution.py:478
  52.8 3.4 %collective-permute-start.10 = (bf16[32,512]{1,0:T(8,128)(2,1)S(1)}, bf16[32,512]{1,0:T(8,128)(2,1)S(1)}, u32[]{:S(2)}, u32[]{:S(2)}) collective-permute-start(bf16[32,512]{1,0:T(8,128)(2,1)S(1)} %get-tuple-element.39), channel_id=1, source_target_pairs={{0,1},{1,2},{2,3},{3,4},{4,5},{5,6},{6,7},{7,8},{8,9},{9,10},{10,1... | collective-permute-start | bytes 98312 | tf_op jit(solution)/shard_map/ppermute | solution.py:494
  56.2 2.4 %collective-permute-start.11 = (bf16[32,512]{1,0:T(8,128)(2,1)S(1)}, bf16[32,512]{1,0:T(8,128)(2,1)S(1)}, u32[]{:S(2)}, u32[]{:S(2)}) collective-permute-start(bf16[32,512]{1,0:T(8,128)(2,1)S(1)} %get-tuple-element.40), channel_id=1, source_target_pairs={{1,0},{2,1},{3,2},{4,3},{5,4},{6,5},{7,6},{8,7},{9,8},{10,9},{11,1... | collective-permute-start | bytes 98312 | tf_op jit(solution)/shard_map/ppermute | solution.py:495
  58.7 0.0 copy-done.1
  58.7 0.7 %matrices.1 = (bf16[2,512,512]{2,1,0:T(8,128)(2,1)S(1)}, bf16[2,128,128]{2,1,0:T(8,128)(2,1)S(1)}, bf16[2,64,64]{2,1,0:T(8,128)(2,1)S(1)}) custom-call(f32[2,41]{1,0:T(2,128)S(1)} %copy-done.1), custom_call_target="tpu_custom_call" | custom-call | tf_op jit(solution)/shard_map/matrices/pallas_call | solution.py:451
  59.4 0.6 detect_centre.1.inner_ref
  60.0 0.0 collective-permute-done.10.low_ref
  60.0 3.8 %collective-permute-done.11.high_ref = bf16[32,512]{1,0:T(8,128)(2,1)S(1)} collective-permute-done((bf16[32,512]{1,0:T(8,128)(2,1)S(1)}, bf16[32,512]{1,0:T(8,128)(2,1)S(1)}, u32[]{:S(2)}, u32[]{:S(2)}) %collective-permute-start.11) | collective-permute-done | bytes 32800 | tf_op jit(solution)/shard_map/ppermute | solution.py:495
  63.8 1.2 %detect_edges.1 = f32[128,512]{1,0:T(8,128)} custom-call(f32[128,512]{1,0:T(8,128)S(1)} %detect_centre.1.inner_ref, bf16[32,512]{1,0:T(8,128)(2,1)S(1)} %collective-permute-done.10.low_ref, bf16[32,512]{1,0:T(8,128)(2,1)S(1)} %collective-permute-done.11.high_ref, bf16[2,512,512]{2,1,0:T(8,128)(2,1)S(1)} %get-tuple-element.37.across_ref, ...), custom_call_target="tpu_custom_call" | custom-call | tf_op jit(solution)/shard_map/detect_edges/pallas_call | solution.py:508
Async XLA Ops:
  7.4 51.2 %copy-start.1 = (f32[2,41]{1,0:T(2,128)S(1)}, f32[2,41]{1,0:T(2,128)}, u32[]{:S(2)}) copy-start(f32[2,41]{1,0:T(2,128)} %taps_ref.1) | copy-start | bytes 988
  7.4 10.6 %collective-permute-start = (bf16[1056,128]{1,0:T(8,128)(2,1)}, bf16[1056,128]{1,0:T(8,128)(2,1)S(1)}, u32[]{:S(2)}, u32[]{:S(2)}) collective-permute-start(bf16[1056,128]{1,0:T(8,128)(2,1)} %get-tuple-element.23), channel_id=1, source_target_pairs={{0,3},{1,2},{2,1},{3,0},{16,19},{17,18},{18,17},{19,16},{4,7},{5,6... | collective-permute-start | bytes 811016 | tf_op jit(solution)/shard_map/ppermute | solution.py:447
  8.0 13.6 %collective-permute-start.1 = (bf16[1056,128]{1,0:T(8,128)(2,1)}, bf16[1056,128]{1,0:T(8,128)(2,1)S(1)}, u32[]{:S(2)}, u32[]{:S(2)}) collective-permute-start(bf16[1056,128]{1,0:T(8,128)(2,1)} %get-tuple-element.24), channel_id=1, source_target_pairs={{0,19},{1,18},{2,17},{3,16},{16,3},{17,2},{18,1},{19,0},{4,23},{5,... | collective-permute-start | bytes 811016 | tf_op jit(solution)/shard_map/ppermute | solution.py:447
  9.6 19.1 %collective-permute-start.2 = (bf16[1056,128]{1,0:T(8,128)(2,1)}, bf16[1056,128]{1,0:T(8,128)(2,1)S(1)}, u32[]{:S(2)}, u32[]{:S(2)}) collective-permute-start(bf16[1056,128]{1,0:T(8,128)(2,1)} %get-tuple-element.25), channel_id=1, source_target_pairs={{0,1},{1,0},{2,3},{3,2},{16,17},{17,16},{18,19},{19,18},{4,5},{5,4... | collective-permute-start | bytes 811016 | tf_op jit(solution)/shard_map/ppermute | solution.py:447
  10.1 18.5 %collective-permute-start.3 = (bf16[1056,128]{1,0:T(8,128)(2,1)}, bf16[1056,128]{1,0:T(8,128)(2,1)S(1)}, u32[]{:S(2)}, u32[]{:S(2)}) collective-permute-start(bf16[1056,128]{1,0:T(8,128)(2,1)} %get-tuple-element.26), channel_id=1, source_target_pairs={{0,2},{1,3},{2,0},{3,1},{16,18},{17,19},{18,16},{19,17},{4,6},{5,7... | collective-permute-start | bytes 811016 | tf_op jit(solution)/shard_map/ppermute | solution.py:447
  11.0 21.1 %collective-permute-start.4 = (bf16[1056,128]{1,0:T(8,128)(2,1)}, bf16[1056,128]{1,0:T(8,128)(2,1)S(1)}, u32[]{:S(2)}, u32[]{:S(2)}) collective-permute-start(bf16[1056,128]{1,0:T(8,128)(2,1)} %get-tuple-element.27), channel_id=1, source_target_pairs={{0,17},{1,16},{2,19},{3,18},{16,1},{17,0},{18,3},{19,2},{4,21},{5,... | collective-permute-start | bytes 811016 | tf_op jit(solution)/shard_map/ppermute | solution.py:447
  18.1 16.1 %collective-permute-start.5 = (bf16[1056,128]{1,0:T(8,128)(2,1)}, bf16[1056,128]{1,0:T(8,128)(2,1)S(1)}, u32[]{:S(2)}, u32[]{:S(2)}) collective-permute-start(bf16[1056,128]{1,0:T(8,128)(2,1)} %get-tuple-element.28), channel_id=1, source_target_pairs={{0,18},{1,19},{2,16},{3,17},{16,2},{17,3},{18,0},{19,1},{4,22},{5,... | collective-permute-start | bytes 811016 | tf_op jit(solution)/shard_map/ppermute | solution.py:447
  21.6 12.6 %collective-permute-start.6 = (bf16[1056,128]{1,0:T(8,128)(2,1)}, bf16[1056,128]{1,0:T(8,128)(2,1)S(1)}, u32[]{:S(2)}, u32[]{:S(2)}) collective-permute-start(bf16[1056,128]{1,0:T(8,128)(2,1)} %get-tuple-element.29), channel_id=1, source_target_pairs={{0,16},{1,17},{2,18},{3,19},{16,0},{17,1},{18,2},{19,3},{4,20},{5,... | collective-permute-start | bytes 811016 | tf_op jit(solution)/shard_map/ppermute | solution.py:447
  34.2 1.0 %copy-start = (bf16[1056,128]{1,0:T(8,128)(2,1)S(1)}, bf16[1056,128]{1,0:T(8,128)(2,1)}, u32[]{:S(2)}) copy-start(bf16[1056,128]{1,0:T(8,128)(2,1)} %get-tuple-element.22.refs_0_) | copy-start | bytes 811012
  36.4 6.2 %collective-permute-start.7 = (bf16[528,128]{1,0:T(8,128)(2,1)S(1)}, bf16[528,128]{1,0:T(8,128)(2,1)S(1)}, u32[]{:S(2)}, u32[]{:S(2)}) collective-permute-start(bf16[528,128]{1,0:T(8,128)(2,1)S(1)} %get-tuple-element.31), channel_id=1, source_target_pairs={{0,4},{4,0},{8,12},{12,8},{1,5},{5,1},{9,13},{13,9},{2,6},{6,2},{1... | collective-permute-start | bytes 405512 | tf_op jit(solution)/shard_map/ppermute | solution.py:475
  37.0 12.3 %collective-permute-start.8 = (bf16[528,128]{1,0:T(8,128)(2,1)S(1)}, bf16[528,128]{1,0:T(8,128)(2,1)S(1)}, u32[]{:S(2)}, u32[]{:S(2)}) collective-permute-start(bf16[528,128]{1,0:T(8,128)(2,1)S(1)} %get-tuple-element.32), channel_id=1, source_target_pairs={{0,8},{4,12},{8,0},{12,4},{1,9},{5,13},{9,1},{13,5},{2,10},{6,14},... | collective-permute-start | bytes 405512 | tf_op jit(solution)/shard_map/ppermute | solution.py:475
  39.5 12.5 %collective-permute-start.9 = (bf16[528,128]{1,0:T(8,128)(2,1)S(1)}, bf16[528,128]{1,0:T(8,128)(2,1)S(1)}, u32[]{:S(2)}, u32[]{:S(2)}) collective-permute-start(bf16[528,128]{1,0:T(8,128)(2,1)S(1)} %get-tuple-element.33), channel_id=1, source_target_pairs={{0,12},{4,8},{8,4},{12,0},{1,13},{5,9},{9,5},{13,1},{2,14},{6,10},... | collective-permute-start | bytes 405512 | tf_op jit(solution)/shard_map/ppermute | solution.py:475
  52.8 7.2 %collective-permute-start.10 = (bf16[32,512]{1,0:T(8,128)(2,1)S(1)}, bf16[32,512]{1,0:T(8,128)(2,1)S(1)}, u32[]{:S(2)}, u32[]{:S(2)}) collective-permute-start(bf16[32,512]{1,0:T(8,128)(2,1)S(1)} %get-tuple-element.39), channel_id=1, source_target_pairs={{0,1},{1,2},{2,3},{3,4},{4,5},{5,6},{6,7},{7,8},{8,9},{9,10},{10,1... | collective-permute-start | bytes 98312 | tf_op jit(solution)/shard_map/ppermute | solution.py:494
  56.2 7.6 %collective-permute-start.11 = (bf16[32,512]{1,0:T(8,128)(2,1)S(1)}, bf16[32,512]{1,0:T(8,128)(2,1)S(1)}, u32[]{:S(2)}, u32[]{:S(2)}) collective-permute-start(bf16[32,512]{1,0:T(8,128)(2,1)S(1)} %get-tuple-element.40), channel_id=1, source_target_pairs={{1,0},{2,1},{3,2},{4,3},{5,4},{6,5},{7,6},{8,7},{9,8},{10,9},{11,1... | collective-permute-start | bytes 98312 | tf_op jit(solution)/shard_map/ppermute | solution.py:495

commit v4 on v3

--- a/solution.py
+++ b/solution.py
@@ -14,6 +14,7 @@
 PATCH_DEV = 4
 HALO = 32
 FIELDS = 4
+ORDER = {2: 0, 3: 1, 7: 2, 1: 3, 5: 4, 6: 5}
 VMEM_LIMIT = 48 * 1024 * 1024
 
 
@@ -322,7 +323,9 @@
         low_ref[:, sl] = main[SIDE - HALO :]
 
 
-def prepare_kernel(taps_ref, across_ref, centre_ref, edge_ref, band_ref):
+def prepare_kernel(taps_ref, own_hbm, across_ref, centre_ref, edge_ref, own_ref, band_ref, own_sem):
+    own_copy = pltpu.make_async_copy(own_hbm, own_ref, own_sem)
+    own_copy.start()
     tap_count = taps_ref.shape[1]
     half = tap_count // 2
     across = tap_row(lambda k: taps_ref[1, k], tap_count, SIDE - half, 3 * SIDE, True)
@@ -342,6 +345,7 @@
         ),
     )
     edge_ref[0], edge_ref[1] = two_parts(edge[:, : 2 * HALO])
+    own_copy.wait()
 
 
 def dot_parts(left, across_ref):
@@ -442,25 +446,26 @@
         raw_pixels,
         flat_field,
     )
-    far_first = sorted(range(1, group), key=lambda k: (k == pn, -bin(k % pn).count("1")))
-    arrived = [send[0]] + [
-        lax.ppermute(send[k], ("sec", "p"), [(g, g ^ k) for g in range(group)])
-        for k in far_first
+    peers = [pn] + sorted((k for k in range(1, group) if k != pn), key=lambda k: ORDER.get(k, k))
+    arrived = [
+        lax.ppermute(send[k], ("sec", "p"), [(g, g ^ k) for g in range(group)]) for k in peers
     ]
 
-    across, centre, edge = pl.pallas_call(
+    across, centre, edge, own = pl.pallas_call(
         prepare_kernel,
         out_shape=(
             shaped((2, width, width), jnp.bfloat16),
             shaped((2, SIDE, SIDE), jnp.bfloat16),
             shaped((2, 2 * HALO, 2 * HALO), jnp.bfloat16),
+            shaped((payload, SIDE), jnp.bfloat16),
         ),
-        in_specs=[smem],
-        out_specs=(vmem, vmem, vmem),
-        scratch_shapes=[pltpu.VMEM((width, width), jnp.float32)],
+        in_specs=[smem, hbm],
+        out_specs=(vmem,) * 4,
+        scratch_shapes=[pltpu.VMEM((width, width), jnp.float32), pltpu.SemaphoreType.DMA],
         compiler_params=params,
+        cost_estimate=pl.CostEstimate(flops=0, bytes_accessed=8 << 20, transcendentals=0),
         name="matrices",
-    )(detect_taps)
+    )(detect_taps, send[0])
 
     plane_sums = pl.pallas_call(
         functools.partial(sum_kernel, nz, group),
@@ -470,9 +475,10 @@
         scratch_shapes=[pltpu.VMEM((group, PATCH_DEV, per_dest, SIDE), jnp.float32)],
         compiler_params=params,
         name="plane_sums",
-    )(*arrived)
+    )(own, *arrived)
     gathered = [plane_sums[0]] + [
-        lax.ppermute(plane_sums[d], "z", [(z, z ^ d) for z in range(nz)]) for d in range(1, nz)
+        lax.ppermute(plane_sums[d], "z", [(z, z ^ d) for z in range(nz)])
+        for d in sorted(range(1, nz), key=lambda d: d == 1)
     ]
 
     coadd, main, rest, low_rows, high_rows = pl.pallas_call(

time: 65.2 us -> 66.9 us (1.026)
  waiting for transfers between devices: 35.8 us -> 37.7 us
    ppermute x7, waiting for transfers between devices: 19.9 us -> 22.8 us  [per_device(): lax.ppermute(send[k], ('sec', 'p'), [(g, g ^ k) for g in range(group)])]
    ppermute x3, waiting for transfers between devices: 12 us -> 9.79 us  [per_device(): lax.ppermute(plane_sums[d], 'z', [(z, z ^ d) for z in range(nz)])]
    ppermute x7, starting transfers between devices: 6.79 us -> 5.04 us  [per_device(): lax.ppermute(send[k], ('sec', 'p'), [(g, g ^ k) for g in range(group)])]
    ppermute x1, waiting for transfers between devices: 3.84 us -> 5.09 us  [per_device(): lax.ppermute(high_rows, every, [(i + 1, i) for i in range(devices - 1)])]
    ppermute x1, starting transfers between devices: 3.4 us -> 4.53 us  [per_device(): lax.ppermute(low_rows, every, [(i, i + 1) for i in range(devices - 1)])]
    ppermute x3, starting transfers between devices: 3.55 us -> 4.45 us  [per_device(): lax.ppermute(plane_sums[d], 'z', [(z, z ^ d) for z in range(nz)])]
  transfers between devices with their start and end apart: 12 -> 12, of which waited for: 9 -> 7; matrix products, arithmetic and copies ran while one was open for 0% -> 0% of each run, Pallas kernels for 2% -> 2%
where the time goes in v4:
time: 66.9 us; the launch traced here: 66.7 us
  waiting for transfers between devices  37.7 us (56%)
  starting transfers between devices  15.9 us (24%)
  Pallas kernels  11.4 us (17%)
  local copies, waits for them, and re-layouts  0.96 us (1%)
  between operations  0.73 us (1%)
    ppermute x7, waiting for transfers between devices, per_device(): lax.ppermute(send[k], ('sec', 'p'), [(g, g ^ k) for g in range(group)])  22.8 us
    ppermute x3, waiting for transfers between devices, per_device(): lax.ppermute(plane_sums[d], 'z', [(z, z ^ d) for z in range(nz)])  9.79 us
    pallas_call x1, Pallas kernels, per_device(): pl.pallas_call(functools.partial(warp_kernel, split), out_shape=[shaped((...  6.79 us
    ppermute x1, waiting for transfers between devices, per_device(): lax.ppermute(high_rows, every, [(i + 1, i) for i in range(devices - 1)])  5.09 us
    ppermute x7, starting transfers between devices, per_device(): lax.ppermute(send[k], ('sec', 'p'), [(g, g ^ k) for g in range(group)])  5.04 us
    ppermute x1, starting transfers between devices, per_device(): lax.ppermute(low_rows, every, [(i, i + 1) for i in range(devices - 1)])  4.53 us
    ppermute x3, starting transfers between devices, per_device(): lax.ppermute(plane_sums[d], 'z', [(z, z ^ d) for z in range(nz)])  4.45 us
    ppermute x1, starting transfers between devices, per_device(): lax.ppermute(high_rows, every, [(i + 1, i) for i in range(devices - 1)])  1.92 us
  transfers between devices with their start and end apart: 12, of which 7 were waited for; matrix products, arithmetic and copies ran while one was open for 0% of the time, Pallas kernels for 2%

profile of v4, /device:TPU:14, one launch (start us, length us, event | category | flops | bytes accessed | tf_op | source)
XLA Modules:
  0.0 66.7 jit_solution(2842133901083784338)
XLA Ops:
  0.6 0.0 copy-start.1
  0.6 6.8 %warp.1 = (bf16[1056,128]{1,0:T(8,128)(2,1)}, bf16[1056,128]{1,0:T(8,128)(2,1)}, bf16[1056,128]{1,0:T(8,128)(2,1)}, bf16[1056,128]{1,0:T(8,128)(2,1)}, bf16[1056...) custom-call(s32[32]{0:T(128)} %bitcast.4, s32[32]{0:T(128)} %bitcast.5, ...), custom_call_target="tpu_custom_call" | custom-call | tf_op jit(solution)/shard_map/warp/pallas_call | solution.py:405
  7.4 0.1 collective-permute-start
  7.5 0.6 collective-permute-start.1
  8.1 1.5 %collective-permute-start.2 = (bf16[1056,128]{1,0:T(8,128)(2,1)}, bf16[1056,128]{1,0:T(8,128)(2,1)S(1)}, u32[]{:S(2)}, u32[]{:S(2)}) collective-permute-start(bf16[1056,128]{1,0:T(8,128)(2,1)} %get-tuple-element.27), channel_id=1, source_target_pairs={{0,3},{1,2},{2,1},{3,0},{16,19},{17,18},{18,17},{19,16},{4,7},{5,6... | collective-permute-start | bytes 811016 | tf_op jit(solution)/shard_map/ppermute | solution.py:451
  9.6 0.9 %collective-permute-start.3 = (bf16[1056,128]{1,0:T(8,128)(2,1)}, bf16[1056,128]{1,0:T(8,128)(2,1)S(1)}, u32[]{:S(2)}, u32[]{:S(2)}) collective-permute-start(bf16[1056,128]{1,0:T(8,128)(2,1)} %get-tuple-element.28), channel_id=1, source_target_pairs={{0,19},{1,18},{2,17},{3,16},{16,3},{17,2},{18,1},{19,0},{4,23},{5,... | collective-permute-start | bytes 811016 | tf_op jit(solution)/shard_map/ppermute | solution.py:451
  10.5 0.6 collective-permute-start.4
  11.1 0.0 collective-permute-done.refs_1_
  11.1 1.4 %collective-permute-start.5 = (bf16[1056,128]{1,0:T(8,128)(2,1)}, bf16[1056,128]{1,0:T(8,128)(2,1)S(1)}, u32[]{:S(2)}, u32[]{:S(2)}) collective-permute-start(bf16[1056,128]{1,0:T(8,128)(2,1)} %get-tuple-element.30), channel_id=1, source_target_pairs={{0,17},{1,16},{2,19},{3,18},{16,1},{17,0},{18,3},{19,2},{4,21},{5,... | collective-permute-start | bytes 811016 | tf_op jit(solution)/shard_map/ppermute | solution.py:451
  12.5 15.7 %collective-permute-done.1.refs_2_ = bf16[1056,128]{1,0:T(8,128)(2,1)S(1)} collective-permute-done((bf16[1056,128]{1,0:T(8,128)(2,1)}, bf16[1056,128]{1,0:T(8,128)(2,1)S(1)}, u32[]{:S(2)}, u32[]{:S(2)}) %collective-permute-start.1) | collective-permute-done | bytes 270368 | tf_op jit(solution)/shard_map/ppermute | solution.py:451
  28.2 0.0 collective-permute-start.6
  28.2 0.0 copy-done.1
  28.2 0.0 copy-start
  28.2 0.9 %copy-done = bf16[1056,128]{1,0:T(8,128)(2,1)S(1)} copy-done((bf16[1056,128]{1,0:T(8,128)(2,1)S(1)}, bf16[1056,128]{1,0:T(8,128)(2,1)}, u32[]{:S(2)}) %copy-start) | copy-done | bytes 270360
  29.2 0.8 %matrices.1 = (bf16[2,512,512]{2,1,0:T(8,128)(2,1)S(1)}, bf16[2,128,128]{2,1,0:T(8,128)(2,1)S(1)}, bf16[2,64,64]{2,1,0:T(8,128)(2,1)S(1)}, bf16[1056,128]{1,0:T(8,128)(2,1)S(1)}) custom-call(f32[2,41]{1,0:T(2,128)S(1)} %copy-done.1, bf16[1056,128]{1,0:T(8,128)(2,1)S(1)} %copy-done), custom_call_target="tpu_custom_call" | custom-call | bytes 8388608 | tf_op jit(solution)/shard_map/matrices/pallas_call | solution.py:454
  29.9 0.0 collective-permute-done.2.refs_3_
  30.0 0.0 collective-permute-done.3.refs_4_
  30.0 0.3 collective-permute-done.4.refs_5_
  30.2 4.2 %collective-permute-done.5.refs_6_ = bf16[1056,128]{1,0:T(8,128)(2,1)S(1)} collective-permute-done((bf16[1056,128]{1,0:T(8,128)(2,1)}, bf16[1056,128]{1,0:T(8,128)(2,1)S(1)}, u32[]{:S(2)}, u32[]{:S(2)}) %collective-permute-start.5) | collective-permute-done | bytes 270368 | tf_op jit(solution)/shard_map/ppermute | solution.py:451
  34.4 2.6 %collective-permute-done.6.refs_7_ = bf16[1056,128]{1,0:T(8,128)(2,1)S(1)} collective-permute-done((bf16[1056,128]{1,0:T(8,128)(2,1)}, bf16[1056,128]{1,0:T(8,128)(2,1)S(1)}, u32[]{:S(2)}, u32[]{:S(2)}) %collective-permute-start.6) | collective-permute-done | bytes 270368 | tf_op jit(solution)/shard_map/ppermute | solution.py:451
  37.0 1.3 %plane_sums.1 = (bf16[528,128]{1,0:T(8,128)(2,1)S(1)}, bf16[528,128]{1,0:T(8,128)(2,1)S(1)}, bf16[528,128]{1,0:T(8,128)(2,1)S(1)}, bf16[528,128]{1,0:T(8,128)(2,1)S(1)}) custom-call(bf16[1056,128]{1,0:T(8,128)(2,1)S(1)} %get-tuple-element.24.refs_0_, bf16[1056,128]{1,0:T(8,128)(2,1)S(1)} %collective-permute-done.refs_1_, ...), custom_call_target="tpu_custom_call" | custom-call | tf_op jit(solution)/shard_map/plane_sums/pallas_call | solution.py:470
  38.3 2.7 %collective-permute-start.7 = (bf16[528,128]{1,0:T(8,128)(2,1)S(1)}, bf16[528,128]{1,0:T(8,128)(2,1)S(1)}, u32[]{:S(2)}, u32[]{:S(2)}) collective-permute-start(bf16[528,128]{1,0:T(8,128)(2,1)S(1)} %get-tuple-element.33), channel_id=1, source_target_pairs={{0,8},{4,12},{8,0},{12,4},{1,9},{5,13},{9,1},{13,5},{2,10},{6,14},... | collective-permute-start | bytes 405512 | tf_op jit(solution)/shard_map/ppermute | solution.py:480
  41.0 0.0 collective-permute-start.8
  41.0 1.8 %collective-permute-start.9 = (bf16[528,128]{1,0:T(8,128)(2,1)S(1)}, bf16[528,128]{1,0:T(8,128)(2,1)S(1)}, u32[]{:S(2)}, u32[]{:S(2)}) collective-permute-start(bf16[528,128]{1,0:T(8,128)(2,1)S(1)} %get-tuple-element.35), channel_id=1, source_target_pairs={{0,4},{4,0},{8,12},{12,8},{1,5},{5,1},{9,13},{13,9},{2,6},{6,2},{1... | collective-permute-start | bytes 405512 | tf_op jit(solution)/shard_map/ppermute | solution.py:480
  42.8 7.0 %collective-permute-done.7.refs_1_ = bf16[528,128]{1,0:T(8,128)(2,1)S(1)} collective-permute-done((bf16[528,128]{1,0:T(8,128)(2,1)S(1)}, bf16[528,128]{1,0:T(8,128)(2,1)S(1)}, u32[]{:S(2)}, u32[]{:S(2)}) %collective-permute-start.7) | collective-permute-done | bytes 135200 | tf_op jit(solution)/shard_map/ppermute | solution.py:480
  49.8 2.8 %collective-permute-done.8.refs_2_ = bf16[528,128]{1,0:T(8,128)(2,1)S(1)} collective-permute-done((bf16[528,128]{1,0:T(8,128)(2,1)S(1)}, bf16[528,128]{1,0:T(8,128)(2,1)S(1)}, u32[]{:S(2)}, u32[]{:S(2)}) %collective-permute-start.8) | collective-permute-done | bytes 135200 | tf_op jit(solution)/shard_map/ppermute | solution.py:480
  52.6 0.0 collective-permute-done.9.refs_3_
  52.6 0.8 %coadd.1 = (f32[128,512]{1,0:T(8,128)}, bf16[128,512]{1,0:T(8,128)(2,1)S(1)}, bf16[128,512]{1,0:T(8,128)(2,1)S(1)}, bf16[32,512]{1,0:T(8,128)(2,1)S(1)}, bf16[32,512]{1,0:T(8,128)(2,1)S(1)}) custom-call(bf16[528,128]{1,0:T(8,128)(2,1)S(1)} %get-tuple-element.32.refs_0_, bf16[528,128]{1,0:T(8,128)(2,1)S(1)} %collective-permute-done.7.refs_1_, ...), custom_call_target="tpu_custom_call" | custom-call | tf_op jit(solution)/shard_map/coadd/pallas_call | solution.py:484
  53.4 4.5 %collective-permute-start.10 = (bf16[32,512]{1,0:T(8,128)(2,1)S(1)}, bf16[32,512]{1,0:T(8,128)(2,1)S(1)}, u32[]{:S(2)}, u32[]{:S(2)}) collective-permute-start(bf16[32,512]{1,0:T(8,128)(2,1)S(1)} %get-tuple-element.41), channel_id=1, source_target_pairs={{0,1},{1,2},{2,3},{3,4},{4,5},{5,6},{6,7},{7,8},{8,9},{9,10},{10,1... | collective-permute-start | bytes 98312 | tf_op jit(solution)/shard_map/ppermute | solution.py:500
  57.9 1.9 %collective-permute-start.11 = (bf16[32,512]{1,0:T(8,128)(2,1)S(1)}, bf16[32,512]{1,0:T(8,128)(2,1)S(1)}, u32[]{:S(2)}, u32[]{:S(2)}) collective-permute-start(bf16[32,512]{1,0:T(8,128)(2,1)S(1)} %get-tuple-element.42), channel_id=1, source_target_pairs={{1,0},{2,1},{3,2},{4,3},{5,4},{6,5},{7,6},{8,7},{9,8},{10,9},{11,1... | collective-permute-start | bytes 98312 | tf_op jit(solution)/shard_map/ppermute | solution.py:501
  59.8 0.6 detect_centre.1.inner_ref
  60.4 0.0 collective-permute-done.10.low_ref
  60.4 5.1 %collective-permute-done.11.high_ref = bf16[32,512]{1,0:T(8,128)(2,1)S(1)} collective-permute-done((bf16[32,512]{1,0:T(8,128)(2,1)S(1)}, bf16[32,512]{1,0:T(8,128)(2,1)S(1)}, u32[]{:S(2)}, u32[]{:S(2)}) %collective-permute-start.11) | collective-permute-done | bytes 32800 | tf_op jit(solution)/shard_map/ppermute | solution.py:501
  65.5 1.2 %detect_edges.1 = f32[128,512]{1,0:T(8,128)} custom-call(f32[128,512]{1,0:T(8,128)S(1)} %detect_centre.1.inner_ref, bf16[32,512]{1,0:T(8,128)(2,1)S(1)} %collective-permute-done.10.low_ref, bf16[32,512]{1,0:T(8,128)(2,1)S(1)} %collective-permute-done.11.high_ref, bf16[2,512,512]{2,1,0:T(8,128)(2,1)S(1)} %get-tuple-element.39.across_ref, ...), custom_call_target="tpu_custom_call" | custom-call | tf_op jit(solution)/shard_map/detect_edges/pallas_call | solution.py:514
Async XLA Ops:
  0.6 27.6 %copy-start.1 = (f32[2,41]{1,0:T(2,128)S(1)}, f32[2,41]{1,0:T(2,128)}, u32[]{:S(2)}) copy-start(f32[2,41]{1,0:T(2,128)} %taps_ref.1) | copy-start | bytes 988
  7.4 3.7 %collective-permute-start = (bf16[1056,128]{1,0:T(8,128)(2,1)}, bf16[1056,128]{1,0:T(8,128)(2,1)S(1)}, u32[]{:S(2)}, u32[]{:S(2)}) collective-permute-start(bf16[1056,128]{1,0:T(8,128)(2,1)} %get-tuple-element.25), channel_id=1, source_target_pairs={{0,16},{1,17},{2,18},{3,19},{16,0},{17,1},{18,2},{19,3},{4,20},{5,... | collective-permute-start | bytes 811016 | tf_op jit(solution)/shard_map/ppermute | solution.py:451
  7.5 20.7 %collective-permute-start.1 = (bf16[1056,128]{1,0:T(8,128)(2,1)}, bf16[1056,128]{1,0:T(8,128)(2,1)S(1)}, u32[]{:S(2)}, u32[]{:S(2)}) collective-permute-start(bf16[1056,128]{1,0:T(8,128)(2,1)} %get-tuple-element.26), channel_id=1, source_target_pairs={{0,2},{1,3},{2,0},{3,1},{16,18},{17,19},{18,16},{19,17},{4,6},{5,7... | collective-permute-start | bytes 811016 | tf_op jit(solution)/shard_map/ppermute | solution.py:451
  8.1 21.9 %collective-permute-start.2 = (bf16[1056,128]{1,0:T(8,128)(2,1)}, bf16[1056,128]{1,0:T(8,128)(2,1)S(1)}, u32[]{:S(2)}, u32[]{:S(2)}) collective-permute-start(bf16[1056,128]{1,0:T(8,128)(2,1)} %get-tuple-element.27), channel_id=1, source_target_pairs={{0,3},{1,2},{2,1},{3,0},{16,19},{17,18},{18,17},{19,16},{4,7},{5,6... | collective-permute-start | bytes 811016 | tf_op jit(solution)/shard_map/ppermute | solution.py:451
  9.6 20.4 %collective-permute-start.3 = (bf16[1056,128]{1,0:T(8,128)(2,1)}, bf16[1056,128]{1,0:T(8,128)(2,1)S(1)}, u32[]{:S(2)}, u32[]{:S(2)}) collective-permute-start(bf16[1056,128]{1,0:T(8,128)(2,1)} %get-tuple-element.28), channel_id=1, source_target_pairs={{0,19},{1,18},{2,17},{3,16},{16,3},{17,2},{18,1},{19,0},{4,23},{5,... | collective-permute-start | bytes 811016 | tf_op jit(solution)/shard_map/ppermute | solution.py:451
  10.5 19.7 %collective-permute-start.4 = (bf16[1056,128]{1,0:T(8,128)(2,1)}, bf16[1056,128]{1,0:T(8,128)(2,1)S(1)}, u32[]{:S(2)}, u32[]{:S(2)}) collective-permute-start(bf16[1056,128]{1,0:T(8,128)(2,1)} %get-tuple-element.29), channel_id=1, source_target_pairs={{0,1},{1,0},{2,3},{3,2},{16,17},{17,16},{18,19},{19,18},{4,5},{5,4... | collective-permute-start | bytes 811016 | tf_op jit(solution)/shard_map/ppermute | solution.py:451
  11.1 23.3 %collective-permute-start.5 = (bf16[1056,128]{1,0:T(8,128)(2,1)}, bf16[1056,128]{1,0:T(8,128)(2,1)S(1)}, u32[]{:S(2)}, u32[]{:S(2)}) collective-permute-start(bf16[1056,128]{1,0:T(8,128)(2,1)} %get-tuple-element.30), channel_id=1, source_target_pairs={{0,17},{1,16},{2,19},{3,18},{16,1},{17,0},{18,3},{19,2},{4,21},{5,... | collective-permute-start | bytes 811016 | tf_op jit(solution)/shard_map/ppermute | solution.py:451
  28.2 8.8 %collective-permute-start.6 = (bf16[1056,128]{1,0:T(8,128)(2,1)}, bf16[1056,128]{1,0:T(8,128)(2,1)S(1)}, u32[]{:S(2)}, u32[]{:S(2)}) collective-permute-start(bf16[1056,128]{1,0:T(8,128)(2,1)} %get-tuple-element.31), channel_id=1, source_target_pairs={{0,18},{1,19},{2,16},{3,17},{16,2},{17,3},{18,0},{19,1},{4,22},{5,... | collective-permute-start | bytes 811016 | tf_op jit(solution)/shard_map/ppermute | solution.py:451
  28.2 1.0 %copy-start = (bf16[1056,128]{1,0:T(8,128)(2,1)S(1)}, bf16[1056,128]{1,0:T(8,128)(2,1)}, u32[]{:S(2)}) copy-start(bf16[1056,128]{1,0:T(8,128)(2,1)} %get-tuple-element.23.own_hbm) | copy-start | bytes 811012
  38.3 11.4 %collective-permute-start.7 = (bf16[528,128]{1,0:T(8,128)(2,1)S(1)}, bf16[528,128]{1,0:T(8,128)(2,1)S(1)}, u32[]{:S(2)}, u32[]{:S(2)}) collective-permute-start(bf16[528,128]{1,0:T(8,128)(2,1)S(1)} %get-tuple-element.33), channel_id=1, source_target_pairs={{0,8},{4,12},{8,0},{12,4},{1,9},{5,13},{9,1},{13,5},{2,10},{6,14},... | collective-permute-start | bytes 405512 | tf_op jit(solution)/shard_map/ppermute | solution.py:480
  41.0 11.6 %collective-permute-start.8 = (bf16[528,128]{1,0:T(8,128)(2,1)S(1)}, bf16[528,128]{1,0:T(8,128)(2,1)S(1)}, u32[]{:S(2)}, u32[]{:S(2)}) collective-permute-start(bf16[528,128]{1,0:T(8,128)(2,1)S(1)} %get-tuple-element.34), channel_id=1, source_target_pairs={{0,12},{4,8},{8,4},{12,0},{1,13},{5,9},{9,5},{13,1},{2,14},{6,10},... | collective-permute-start | bytes 405512 | tf_op jit(solution)/shard_map/ppermute | solution.py:480
  41.0 11.6 %collective-permute-start.9 = (bf16[528,128]{1,0:T(8,128)(2,1)S(1)}, bf16[528,128]{1,0:T(8,128)(2,1)S(1)}, u32[]{:S(2)}, u32[]{:S(2)}) collective-permute-start(bf16[528,128]{1,0:T(8,128)(2,1)S(1)} %get-tuple-element.35), channel_id=1, source_target_pairs={{0,4},{4,0},{8,12},{12,8},{1,5},{5,1},{9,13},{13,9},{2,6},{6,2},{1... | collective-permute-start | bytes 405512 | tf_op jit(solution)/shard_map/ppermute | solution.py:480
  53.4 7.0 %collective-permute-start.10 = (bf16[32,512]{1,0:T(8,128)(2,1)S(1)}, bf16[32,512]{1,0:T(8,128)(2,1)S(1)}, u32[]{:S(2)}, u32[]{:S(2)}) collective-permute-start(bf16[32,512]{1,0:T(8,128)(2,1)S(1)} %get-tuple-element.41), channel_id=1, source_target_pairs={{0,1},{1,2},{2,3},{3,4},{4,5},{5,6},{6,7},{7,8},{8,9},{9,10},{10,1... | collective-permute-start | bytes 98312 | tf_op jit(solution)/shard_map/ppermute | solution.py:500
  57.9 7.6 %collective-permute-start.11 = (bf16[32,512]{1,0:T(8,128)(2,1)S(1)}, bf16[32,512]{1,0:T(8,128)(2,1)S(1)}, u32[]{:S(2)}, u32[]{:S(2)}) collective-permute-start(bf16[32,512]{1,0:T(8,128)(2,1)S(1)} %get-tuple-element.42), channel_id=1, source_target_pairs={{1,0},{2,1},{3,2},{4,3},{5,4},{6,5},{7,6},{8,7},{9,8},{10,9},{11,1... | collective-permute-start | bytes 98312 | tf_op jit(solution)/shard_map/ppermute | solution.py:501

commit v5 on v4

--- a/solution.py
+++ b/solution.py
@@ -14,7 +14,7 @@
 PATCH_DEV = 4
 HALO = 32
 FIELDS = 4
-ORDER = {2: 0, 3: 1, 7: 2, 1: 3, 5: 4, 6: 5}
+ORDER = {1: 0, 3: 1, 7: 2, 2: 3, 6: 4, 5: 5}
 VMEM_LIMIT = 48 * 1024 * 1024
 
 
@@ -193,38 +193,67 @@
         in_pos = lax.broadcasted_iota(jnp.int32, (length, length), 1 - axis).astype(jnp.float32)
         return jnp.maximum(0.0, 1.0 - jnp.abs(in_pos - source)).astype(jnp.bfloat16)
 
+    for visit in range(visits):
+        for term in range(terms):
+            for axis, reverse in ((1, True), (0, False)):
+                row = tap_row(
+                    lambda k: taps_ref[visit, term, axis, k],
+                    tap_count,
+                    SIDE - half,
+                    3 * SIDE,
+                    reverse,
+                )
+                store_band(
+                    band_ref.at[visit, 2 * term + 1 - axis], toeplitz(row, SIDE).astype(jnp.bfloat16)
+                )
+        band_ref[visit, 2 * terms] = hat(cols, 1, shift_ref[visit, 0, 1], scale_ref[visit, 0, 1])
+        band_ref[visit, 2 * terms + 1] = hat(
+            rows, 0, shift_ref[visit, 0, 0], scale_ref[visit, 0, 0]
+        )
+
+    def windows(length):
+        wide = 2 * SIDE
+        for at in range(0, length, wide):
+            low, high = max(0, at - SIDE), min(length, at + wide + SIDE)
+            yield pl.ds(at, min(wide, length - at)), pl.ds(low, high - low)
+
+    def times_band(out, source, band):
+        for o, k in windows(cols):
+            out[:, o] = dot32(source[:, k], band[k, o]).astype(jnp.bfloat16)
+
+    def band_times(out, band, source):
+        for o, k in windows(rows):
+            out[o, :] = dot32(band[o, k], source[k, :]).astype(jnp.bfloat16)
+
     row_blocks, col_blocks = rows // SIDE, cols // SIDE
     for visit in range(visits):
+        left, mid = left_ref.at[visit], mid_ref.at[visit]
         bias = jnp.broadcast_to(bias_ref[visit], (SIDE, rows)).T
         raw_copies[visit].wait()
         if visit == 0:
             flat_copy.wait()
         for j in range(cols // SIDE):
             sl = pl.ds(j * SIDE, SIDE)
-            left_ref[:, sl] = ((raw_ref[visit, 0, :, sl] - bias) * flat_ref[0, :, sl]).astype(
+            left[:, sl] = ((raw_ref[visit, 0, :, sl] - bias) * flat_ref[0, :, sl]).astype(
                 jnp.bfloat16
             )
 
-        matched = None
-        for term in range(terms):
-            across = tap_row(
-                lambda k: taps_ref[visit, term, 1, k], tap_count, SIDE - half, 3 * SIDE, True
-            )
-            store_band(band_ref, toeplitz(across, SIDE).astype(jnp.bfloat16))
-            mid_ref[...] = dot32(left_ref[...], band_ref[...]).astype(jnp.bfloat16)
-            down = tap_row(
-                lambda k: taps_ref[visit, term, 0, k], tap_count, SIDE - half, 3 * SIDE, False
-            )
-            store_band(band_ref, toeplitz(down, SIDE).astype(jnp.bfloat16))
-            part = weights_ref[0, term, visit] * dot32(band_ref[...], mid_ref[...])
-            matched = part if matched is None else matched + part
-        left_ref[...] = matched.astype(jnp.bfloat16)
-
-        band_ref[...] = hat(cols, 1, shift_ref[visit, 0, 1], scale_ref[visit, 0, 1])
-        mid_ref[...] = dot32(left_ref[...], band_ref[...]).astype(jnp.bfloat16)
-        band_ref[...] = hat(rows, 0, shift_ref[visit, 0, 0], scale_ref[visit, 0, 0])
-        left_ref[...] = dot32(band_ref[...], mid_ref[...]).astype(jnp.bfloat16)
-
+        if terms == 1:
+            times_band(mid, left, band_ref.at[visit, 0])
+            for o, k in windows(rows):
+                part = dot32(band_ref[visit, 1, o, k], mid[k, :])
+                left[o, :] = (weights_ref[0, 0, visit] * part).astype(jnp.bfloat16)
+        else:
+            matched = None
+            for term in range(terms):
+                times_band(mid, left, band_ref.at[visit, 2 * term])
+                part = weights_ref[0, term, visit] * dot32(band_ref[visit, 2 * term + 1], mid[...])
+                matched = part if matched is None else matched + part
+            left[...] = matched.astype(jnp.bfloat16)
+        times_band(mid, left, band_ref.at[visit, 2 * terms])
+        band_times(left, band_ref.at[visit, 2 * terms + 1], mid)
+
+    for visit in range(visits):
         for i in range(row_blocks):
             for j in range(col_blocks):
                 block = visit * (row_blocks * col_blocks) + i * col_blocks + j
@@ -237,7 +266,7 @@
                 dest = (sec * pn + dev - z * pn) ^ mine
                 at = (z ^ lax.axis_index("z")) * CAP + rank
                 out_ref[dest, pl.ds(pl.multiple_of(at * SIDE, SIDE), SIDE), :] = left_ref[
-                    pl.ds(i * SIDE, SIDE), pl.ds(j * SIDE, SIDE)
+                    visit, pl.ds(i * SIDE, SIDE), pl.ds(j * SIDE, SIDE)
                 ]
                 line = pl.ds(dest * per_dest + at, 1)
                 slot_rows[line, :] = jnp.full((1, SIDE), patch_ref[block].astype(jnp.float32))
@@ -301,7 +330,8 @@
 
 
 def coadd_kernel(sources, *refs):
-    ins, (coadd_ref, main_ref, rest_ref, low_ref, high_ref) = refs[:sources], refs[sources:]
+    ins, (coadd_ref, main_ref, rest_ref, first_ref, second_ref) = refs[:sources], refs[sources:]
+    odd = lax.axis_index("p") % 2
     total = jnp.zeros((PATCH_DEV, SIDE), jnp.float32)
     for z in range(sources):
         extra = ins[z][pl.ds(PATCH_DEV * SIDE, FIELDS * PATCH_DEV), :].astype(jnp.float32)
@@ -319,8 +349,16 @@
         main, rest = two_parts(tile)
         main_ref[:, sl] = main
         rest_ref[:, sl] = rest
-        high_ref[:, sl] = main[:HALO]
-        low_ref[:, sl] = main[SIDE - HALO :]
+
+    @pl.when(odd == 0)
+    def _():
+        first_ref[...] = main_ref[pl.ds(SIDE - HALO, HALO)]
+        second_ref[...] = main_ref[pl.ds(0, HALO)]
+
+    @pl.when(odd == 1)
+    def _():
+        first_ref[...] = main_ref[pl.ds(0, HALO)]
+        second_ref[...] = main_ref[pl.ds(SIDE - HALO, HALO)]
 
 
 def prepare_kernel(taps_ref, own_hbm, across_ref, centre_ref, edge_ref, own_ref, band_ref, own_sem):
@@ -350,7 +388,8 @@
 
 def dot_parts(left, across_ref):
     main, rest = two_parts(left)
-    return dot32(main, across_ref[0]) + (dot32(main, across_ref[1]) + dot32(rest, across_ref[0]))
+    both = dot32(jnp.concatenate([main, rest], axis=0), across_ref[0])
+    return both[: left.shape[0]] + (dot32(main, across_ref[1]) + both[left.shape[0] :])
 
 
 def centre_kernel(main_ref, rest_ref, across_ref, centre_ref, out_ref):
@@ -361,8 +400,11 @@
     out_ref[...] = dot_parts(along, across_ref)
 
 
-def edge_kernel(inner_ref, low_ref, high_ref, across_ref, edge_ref, out_ref):
-    halo = jnp.concatenate([low_ref[...], high_ref[...]], axis=0)
+def edge_kernel(inner_ref, first_ref, second_ref, across_ref, edge_ref, out_ref, halo_ref):
+    odd = lax.axis_index("p") % 2
+    halo_ref[pl.ds(pl.multiple_of((1 - odd) * HALO, HALO), HALO)] = first_ref[...]
+    halo_ref[pl.ds(pl.multiple_of(odd * HALO, HALO), HALO)] = second_ref[...]
+    halo = halo_ref[...]
     along = dot32(edge_ref[0], halo) + dot32(edge_ref[1], halo)
     extra = dot_parts(along, across_ref)
     out_ref[pl.ds(0, HALO)] = inner_ref[pl.ds(0, HALO)] + extra[:HALO]
@@ -390,6 +432,7 @@
     group = ns * pn
     visits, _, rows, cols = raw_pixels.shape
     blocks = owner_of.shape[0]
+    terms = psf_taps.shape[1]
     per_dest = nz * CAP
     payload = per_dest * (SIDE + FIELDS)
     width = PATCH_DEV * SIDE
@@ -420,9 +463,9 @@
             pltpu.VMEM(raw_pixels.shape, jnp.float32),
             pltpu.VMEM(flat_field.shape, jnp.float32),
             pltpu.SMEM((devices,), jnp.int32),
-            pltpu.VMEM((rows, cols), jnp.bfloat16),
-            pltpu.VMEM((rows, cols), jnp.bfloat16),
-            pltpu.VMEM((rows, cols), jnp.bfloat16),
+            pltpu.VMEM((visits, 2 * terms + 2, rows, cols), jnp.bfloat16),
+            pltpu.VMEM((visits, rows, cols), jnp.bfloat16),
+            pltpu.VMEM((visits, rows, cols), jnp.bfloat16),
             pltpu.VMEM((group * per_dest, SIDE), jnp.float32),
             pltpu.VMEM((group * per_dest, SIDE), jnp.float32),
             pltpu.SemaphoreType.DMA((9,)),
@@ -481,7 +524,7 @@
         for d in sorted(range(1, nz), key=lambda d: d == 1)
     ]
 
-    coadd, main, rest, low_rows, high_rows = pl.pallas_call(
+    coadd, main, rest, first_rows, second_rows = pl.pallas_call(
         functools.partial(coadd_kernel, nz),
         out_shape=(
             shaped((SIDE, width), jnp.float32),
@@ -497,8 +540,12 @@
     )(*gathered)
 
     every = ("sec", "z", "p")
-    low = lax.ppermute(low_rows, every, [(i, i + 1) for i in range(devices - 1)])
-    high = lax.ppermute(high_rows, every, [(i + 1, i) for i in range(devices - 1)])
+
+    def swap(rows, start):
+        pairs = [(i, i + 1) for i in range(start, devices - 1, 2)]
+        return lax.ppermute(rows, every, pairs + [(j, i) for i, j in pairs])
+
+    first, second = swap(first_rows, 0), swap(second_rows, 1)
 
     inner = pl.pallas_call(
         centre_kernel,
@@ -516,9 +563,10 @@
         out_shape=shaped((SIDE, width), jnp.float32),
         in_specs=[vmem] * 5,
         out_specs=vmem,
+        scratch_shapes=[pltpu.VMEM((2 * HALO, width), jnp.bfloat16)],
         compiler_params=params,
         name="detect_edges",
-    )(inner, low, high, across, edge)
+    )(inner, first, second, across, edge)
     return coadd, detection
 
 

time: 66.9 us -> 65.5 us (0.979)
  the two profiles are of different devices: /device:TPU:14 before, /device:TPU:1 now
where the time goes in v5:
time: 65.5 us; the launch traced here: 65.4 us
  waiting for transfers between devices  29.3 us (45%)
  starting transfers between devices  23 us (35%)
  Pallas kernels  11.4 us (17%)
  local copies, waits for them, and re-layouts  0.96 us (1%)
  between operations  0.7 us (1%)
    ppermute x7, waiting for transfers between devices, per_device(): lax.ppermute(send[k], ('sec', 'p'), [(g, g ^ k) for g in range(group)])  20.1 us
    ppermute x2, starting transfers between devices, swap(): return lax.ppermute(rows, every, pairs + [(j, i) for i, j in pairs])  9.69 us
    ppermute x7, starting transfers between devices, per_device(): lax.ppermute(send[k], ('sec', 'p'), [(g, g ^ k) for g in range(group)])  9.64 us
    ppermute x3, waiting for transfers between devices, per_device(): lax.ppermute(plane_sums[d], 'z', [(z, z ^ d) for z in range(nz)])  8.19 us
    pallas_call x1, Pallas kernels, per_device(): pl.pallas_call(functools.partial(warp_kernel, split), out_shape=[shaped((...  6.84 us
    ppermute x3, starting transfers between devices, per_device(): lax.ppermute(plane_sums[d], 'z', [(z, z ^ d) for z in range(nz)])  3.66 us
  transfers between devices with their start and end apart: 12, of which 8 were waited for; matrix products, arithmetic and copies ran while one was open for 0% of the time, Pallas kernels for 2%

profile of v5, /device:TPU:1, one launch (start us, length us, event | category | flops | bytes accessed | tf_op | source)
XLA Modules:
  0.0 65.4 jit_solution(5407727420182765805)
XLA Ops:
  0.6 0.0 copy-start.1
  0.6 6.8 %warp.1 = (bf16[1056,128]{1,0:T(8,128)(2,1)}, bf16[1056,128]{1,0:T(8,128)(2,1)}, bf16[1056,128]{1,0:T(8,128)(2,1)}, bf16[1056,128]{1,0:T(8,128)(2,1)}, bf16[1056...) custom-call(s32[32]{0:T(128)} %bitcast.4, s32[32]{0:T(128)} %bitcast.5, ...), custom_call_target="tpu_custom_call" | custom-call | tf_op jit(solution)/shard_map/warp/pallas_call | solution.py:448
  7.5 0.1 collective-permute-start
  7.6 2.7 %collective-permute-start.1 = (bf16[1056,128]{1,0:T(8,128)(2,1)}, bf16[1056,128]{1,0:T(8,128)(2,1)S(1)}, u32[]{:S(2)}, u32[]{:S(2)}) collective-permute-start(bf16[1056,128]{1,0:T(8,128)(2,1)} %get-tuple-element.26), channel_id=1, source_target_pairs={{0,1},{1,0},{2,3},{3,2},{16,17},{17,16},{18,19},{19,18},{4,5},{5,4... | collective-permute-start | bytes 811016 | tf_op jit(solution)/shard_map/ppermute | solution.py:494
  10.3 1.2 %collective-permute-start.2 = (bf16[1056,128]{1,0:T(8,128)(2,1)}, bf16[1056,128]{1,0:T(8,128)(2,1)S(1)}, u32[]{:S(2)}, u32[]{:S(2)}) collective-permute-start(bf16[1056,128]{1,0:T(8,128)(2,1)} %get-tuple-element.27), channel_id=1, source_target_pairs={{0,3},{1,2},{2,1},{3,0},{16,19},{17,18},{18,17},{19,16},{4,7},{5,6... | collective-permute-start | bytes 811016 | tf_op jit(solution)/shard_map/ppermute | solution.py:494
  11.5 1.6 %collective-permute-start.3 = (bf16[1056,128]{1,0:T(8,128)(2,1)}, bf16[1056,128]{1,0:T(8,128)(2,1)S(1)}, u32[]{:S(2)}, u32[]{:S(2)}) collective-permute-start(bf16[1056,128]{1,0:T(8,128)(2,1)} %get-tuple-element.28), channel_id=1, source_target_pairs={{0,19},{1,18},{2,17},{3,16},{16,3},{17,2},{18,1},{19,0},{4,23},{5,... | collective-permute-start | bytes 811016 | tf_op jit(solution)/shard_map/ppermute | solution.py:494
  13.2 1.2 %collective-permute-start.4 = (bf16[1056,128]{1,0:T(8,128)(2,1)}, bf16[1056,128]{1,0:T(8,128)(2,1)S(1)}, u32[]{:S(2)}, u32[]{:S(2)}) collective-permute-start(bf16[1056,128]{1,0:T(8,128)(2,1)} %get-tuple-element.29), channel_id=1, source_target_pairs={{0,2},{1,3},{2,0},{3,1},{16,18},{17,19},{18,16},{19,17},{4,6},{5,7... | collective-permute-start | bytes 811016 | tf_op jit(solution)/shard_map/ppermute | solution.py:494
  14.4 0.0 collective-permute-done.refs_1_
  14.4 0.3 collective-permute-start.5
  14.7 2.6 %collective-permute-done.1.refs_2_ = bf16[1056,128]{1,0:T(8,128)(2,1)S(1)} collective-permute-done((bf16[1056,128]{1,0:T(8,128)(2,1)}, bf16[1056,128]{1,0:T(8,128)(2,1)S(1)}, u32[]{:S(2)}, u32[]{:S(2)}) %collective-permute-start.1) | collective-permute-done | bytes 270368 | tf_op jit(solution)/shard_map/ppermute | solution.py:494
  17.2 2.5 %collective-permute-start.6 = (bf16[1056,128]{1,0:T(8,128)(2,1)}, bf16[1056,128]{1,0:T(8,128)(2,1)S(1)}, u32[]{:S(2)}, u32[]{:S(2)}) collective-permute-start(bf16[1056,128]{1,0:T(8,128)(2,1)} %get-tuple-element.31), channel_id=1, source_target_pairs={{0,17},{1,16},{2,19},{3,18},{16,1},{17,0},{18,3},{19,2},{4,21},{5,... | collective-permute-start | bytes 811016 | tf_op jit(solution)/shard_map/ppermute | solution.py:494
  19.7 0.0 copy-done.1
  19.7 0.0 copy-start
  19.7 1.0 %copy-done = bf16[1056,128]{1,0:T(8,128)(2,1)S(1)} copy-done((bf16[1056,128]{1,0:T(8,128)(2,1)S(1)}, bf16[1056,128]{1,0:T(8,128)(2,1)}, u32[]{:S(2)}) %copy-start) | copy-done | bytes 270360
  20.7 0.8 %matrices.1 = (bf16[2,512,512]{2,1,0:T(8,128)(2,1)S(1)}, bf16[2,128,128]{2,1,0:T(8,128)(2,1)S(1)}, bf16[2,64,64]{2,1,0:T(8,128)(2,1)S(1)}, bf16[1056,128]{1,0:T(8,128)(2,1)S(1)}) custom-call(f32[2,41]{1,0:T(2,128)S(1)} %copy-done.1, bf16[1056,128]{1,0:T(8,128)(2,1)S(1)} %copy-done), custom_call_target="tpu_custom_call" | custom-call | bytes 8388608 | tf_op jit(solution)/shard_map/matrices/pallas_call | solution.py:497
  21.4 2.7 %collective-permute-done.2.refs_3_ = bf16[1056,128]{1,0:T(8,128)(2,1)S(1)} collective-permute-done((bf16[1056,128]{1,0:T(8,128)(2,1)}, bf16[1056,128]{1,0:T(8,128)(2,1)S(1)}, u32[]{:S(2)}, u32[]{:S(2)}) %collective-permute-start.2) | collective-permute-done | bytes 270368 | tf_op jit(solution)/shard_map/ppermute | solution.py:494
  24.1 6.4 %collective-permute-done.3.refs_4_ = bf16[1056,128]{1,0:T(8,128)(2,1)S(1)} collective-permute-done((bf16[1056,128]{1,0:T(8,128)(2,1)}, bf16[1056,128]{1,0:T(8,128)(2,1)S(1)}, u32[]{:S(2)}, u32[]{:S(2)}) %collective-permute-start.3) | collective-permute-done | bytes 270368 | tf_op jit(solution)/shard_map/ppermute | solution.py:494
  30.5 2.7 %collective-permute-done.4.refs_5_ = bf16[1056,128]{1,0:T(8,128)(2,1)S(1)} collective-permute-done((bf16[1056,128]{1,0:T(8,128)(2,1)}, bf16[1056,128]{1,0:T(8,128)(2,1)S(1)}, u32[]{:S(2)}, u32[]{:S(2)}) %collective-permute-start.4) | collective-permute-done | bytes 270368 | tf_op jit(solution)/shard_map/ppermute | solution.py:494
  33.2 5.8 %collective-permute-done.5.refs_6_ = bf16[1056,128]{1,0:T(8,128)(2,1)S(1)} collective-permute-done((bf16[1056,128]{1,0:T(8,128)(2,1)}, bf16[1056,128]{1,0:T(8,128)(2,1)S(1)}, u32[]{:S(2)}, u32[]{:S(2)}) %collective-permute-start.5) | collective-permute-done | bytes 270368 | tf_op jit(solution)/shard_map/ppermute | solution.py:494
  39.0 0.0 collective-permute-done.6.refs_7_
  39.0 1.3 %plane_sums.1 = (bf16[528,128]{1,0:T(8,128)(2,1)S(1)}, bf16[528,128]{1,0:T(8,128)(2,1)S(1)}, bf16[528,128]{1,0:T(8,128)(2,1)S(1)}, bf16[528,128]{1,0:T(8,128)(2,1)S(1)}) custom-call(bf16[1056,128]{1,0:T(8,128)(2,1)S(1)} %get-tuple-element.24.refs_0_, bf16[1056,128]{1,0:T(8,128)(2,1)S(1)} %collective-permute-done.refs_1_, ...), custom_call_target="tpu_custom_call" | custom-call | tf_op jit(solution)/shard_map/plane_sums/pallas_call | solution.py:513
  40.3 2.4 %collective-permute-start.7 = (bf16[528,128]{1,0:T(8,128)(2,1)S(1)}, bf16[528,128]{1,0:T(8,128)(2,1)S(1)}, u32[]{:S(2)}, u32[]{:S(2)}) collective-permute-start(bf16[528,128]{1,0:T(8,128)(2,1)S(1)} %get-tuple-element.33), channel_id=1, source_target_pairs={{0,8},{4,12},{8,0},{12,4},{1,9},{5,13},{9,1},{13,5},{2,10},{6,14},... | collective-permute-start | bytes 405512 | tf_op jit(solution)/shard_map/ppermute | solution.py:523
  42.7 1.1 %collective-permute-start.8 = (bf16[528,128]{1,0:T(8,128)(2,1)S(1)}, bf16[528,128]{1,0:T(8,128)(2,1)S(1)}, u32[]{:S(2)}, u32[]{:S(2)}) collective-permute-start(bf16[528,128]{1,0:T(8,128)(2,1)S(1)} %get-tuple-element.34), channel_id=1, source_target_pairs={{0,12},{4,8},{8,4},{12,0},{1,13},{5,9},{9,5},{13,1},{2,14},{6,10},... | collective-permute-start | bytes 405512 | tf_op jit(solution)/shard_map/ppermute | solution.py:523
  43.7 0.2 collective-permute-start.9
  43.9 7.9 %collective-permute-done.7.refs_1_ = bf16[528,128]{1,0:T(8,128)(2,1)S(1)} collective-permute-done((bf16[528,128]{1,0:T(8,128)(2,1)S(1)}, bf16[528,128]{1,0:T(8,128)(2,1)S(1)}, u32[]{:S(2)}, u32[]{:S(2)}) %collective-permute-start.7) | collective-permute-done | bytes 135200 | tf_op jit(solution)/shard_map/ppermute | solution.py:523
  51.9 0.0 collective-permute-done.8.refs_2_
  51.9 0.3 collective-permute-done.9.refs_3_
  52.1 0.8 %coadd.1 = (f32[128,512]{1,0:T(8,128)}, bf16[128,512]{1,0:T(8,128)(2,1)S(1)}, bf16[128,512]{1,0:T(8,128)(2,1)S(1)}, bf16[32,512]{1,0:T(8,128)(2,1)S(1)}, bf16[32,512]{1,0:T(8,128)(2,1)S(1)}) custom-call(bf16[528,128]{1,0:T(8,128)(2,1)S(1)} %get-tuple-element.32.refs_0_, bf16[528,128]{1,0:T(8,128)(2,1)S(1)} %collective-permute-done.7.refs_1_, ...), custom_call_target="tpu_custom_call" | custom-call | tf_op jit(solution)/shard_map/coadd/pallas_call | solution.py:527
  53.0 0.6 collective-permute-start.10
  53.6 9.1 %collective-permute-start.11 = (bf16[32,512]{1,0:T(8,128)(2,1)S(1)}, bf16[32,512]{1,0:T(8,128)(2,1)S(1)}, u32[]{:S(2)}, u32[]{:S(2)}) collective-permute-start(bf16[32,512]{1,0:T(8,128)(2,1)S(1)} %get-tuple-element.42), channel_id=1, source_target_pairs={{1,2},{3,4},{5,6},{7,8},{9,10},{11,12},{13,14},{15,16},{17,18},{19... | collective-permute-start | bytes 98312 | tf_op jit(solution)/shard_map/ppermute | solution.py:546
  62.7 0.6 detect_centre.1.inner_ref
  63.2 0.0 collective-permute-done.10.first_ref
  63.2 1.0 %collective-permute-done.11.second_ref = bf16[32,512]{1,0:T(8,128)(2,1)S(1)} collective-permute-done((bf16[32,512]{1,0:T(8,128)(2,1)S(1)}, bf16[32,512]{1,0:T(8,128)(2,1)S(1)}, u32[]{:S(2)}, u32[]{:S(2)}) %collective-permute-start.11) | collective-permute-done | bytes 32800 | tf_op jit(solution)/shard_map/ppermute | solution.py:546
  64.2 1.1 %detect_edges.1 = f32[128,512]{1,0:T(8,128)} custom-call(f32[128,512]{1,0:T(8,128)S(1)} %detect_centre.1.inner_ref, bf16[32,512]{1,0:T(8,128)(2,1)S(1)} %collective-permute-done.10.first_ref, bf16[32,512]{1,0:T(8,128)(2,1)S(1)} %collective-permute-done.11.second_ref, bf16[2,512,512]{2,1,0:T(8,128)(2,1)S(1)} %get-tuple-element.39.across_ref, ...), custom_call_target="tpu_custom_call" | custom-call | tf_op jit(solution)/shard_map/detect_edges/pallas_call | solution.py:561
Async XLA Ops:
  0.6 19.1 %copy-start.1 = (f32[2,41]{1,0:T(2,128)S(1)}, f32[2,41]{1,0:T(2,128)}, u32[]{:S(2)}) copy-start(f32[2,41]{1,0:T(2,128)} %taps_ref.1) | copy-start | bytes 988
  7.5 6.9 %collective-permute-start = (bf16[1056,128]{1,0:T(8,128)(2,1)}, bf16[1056,128]{1,0:T(8,128)(2,1)S(1)}, u32[]{:S(2)}, u32[]{:S(2)}) collective-permute-start(bf16[1056,128]{1,0:T(8,128)(2,1)} %get-tuple-element.25), channel_id=1, source_target_pairs={{0,16},{1,17},{2,18},{3,19},{16,0},{17,1},{18,2},{19,3},{4,20},{5,... | collective-permute-start | bytes 811016 | tf_op jit(solution)/shard_map/ppermute | solution.py:494
  7.6 9.6 %collective-permute-start.1 = (bf16[1056,128]{1,0:T(8,128)(2,1)}, bf16[1056,128]{1,0:T(8,128)(2,1)S(1)}, u32[]{:S(2)}, u32[]{:S(2)}) collective-permute-start(bf16[1056,128]{1,0:T(8,128)(2,1)} %get-tuple-element.26), channel_id=1, source_target_pairs={{0,1},{1,0},{2,3},{3,2},{16,17},{17,16},{18,19},{19,18},{4,5},{5,4... | collective-permute-start | bytes 811016 | tf_op jit(solution)/shard_map/ppermute | solution.py:494
  10.3 13.9 %collective-permute-start.2 = (bf16[1056,128]{1,0:T(8,128)(2,1)}, bf16[1056,128]{1,0:T(8,128)(2,1)S(1)}, u32[]{:S(2)}, u32[]{:S(2)}) collective-permute-start(bf16[1056,128]{1,0:T(8,128)(2,1)} %get-tuple-element.27), channel_id=1, source_target_pairs={{0,3},{1,2},{2,1},{3,0},{16,19},{17,18},{18,17},{19,16},{4,7},{5,6... | collective-permute-start | bytes 811016 | tf_op jit(solution)/shard_map/ppermute | solution.py:494
  11.5 19.0 %collective-permute-start.3 = (bf16[1056,128]{1,0:T(8,128)(2,1)}, bf16[1056,128]{1,0:T(8,128)(2,1)S(1)}, u32[]{:S(2)}, u32[]{:S(2)}) collective-permute-start(bf16[1056,128]{1,0:T(8,128)(2,1)} %get-tuple-element.28), channel_id=1, source_target_pairs={{0,19},{1,18},{2,17},{3,16},{16,3},{17,2},{18,1},{19,0},{4,23},{5,... | collective-permute-start | bytes 811016 | tf_op jit(solution)/shard_map/ppermute | solution.py:494
  13.2 20.0 %collective-permute-start.4 = (bf16[1056,128]{1,0:T(8,128)(2,1)}, bf16[1056,128]{1,0:T(8,128)(2,1)S(1)}, u32[]{:S(2)}, u32[]{:S(2)}) collective-permute-start(bf16[1056,128]{1,0:T(8,128)(2,1)} %get-tuple-element.29), channel_id=1, source_target_pairs={{0,2},{1,3},{2,0},{3,1},{16,18},{17,19},{18,16},{19,17},{4,6},{5,7... | collective-permute-start | bytes 811016 | tf_op jit(solution)/shard_map/ppermute | solution.py:494
  14.4 24.6 %collective-permute-start.5 = (bf16[1056,128]{1,0:T(8,128)(2,1)}, bf16[1056,128]{1,0:T(8,128)(2,1)S(1)}, u32[]{:S(2)}, u32[]{:S(2)}) collective-permute-start(bf16[1056,128]{1,0:T(8,128)(2,1)} %get-tuple-element.30), channel_id=1, source_target_pairs={{0,18},{1,19},{2,16},{3,17},{16,2},{17,3},{18,0},{19,1},{4,22},{5,... | collective-permute-start | bytes 811016 | tf_op jit(solution)/shard_map/ppermute | solution.py:494
  17.2 21.7 %collective-permute-start.6 = (bf16[1056,128]{1,0:T(8,128)(2,1)}, bf16[1056,128]{1,0:T(8,128)(2,1)S(1)}, u32[]{:S(2)}, u32[]{:S(2)}) collective-permute-start(bf16[1056,128]{1,0:T(8,128)(2,1)} %get-tuple-element.31), channel_id=1, source_target_pairs={{0,17},{1,16},{2,19},{3,18},{16,1},{17,0},{18,3},{19,2},{4,21},{5,... | collective-permute-start | bytes 811016 | tf_op jit(solution)/shard_map/ppermute | solution.py:494
  19.7 1.0 %copy-start = (bf16[1056,128]{1,0:T(8,128)(2,1)S(1)}, bf16[1056,128]{1,0:T(8,128)(2,1)}, u32[]{:S(2)}) copy-start(bf16[1056,128]{1,0:T(8,128)(2,1)} %get-tuple-element.23.own_hbm) | copy-start | bytes 811012
  40.3 11.6 %collective-permute-start.7 = (bf16[528,128]{1,0:T(8,128)(2,1)S(1)}, bf16[528,128]{1,0:T(8,128)(2,1)S(1)}, u32[]{:S(2)}, u32[]{:S(2)}) collective-permute-start(bf16[528,128]{1,0:T(8,128)(2,1)S(1)} %get-tuple-element.33), channel_id=1, source_target_pairs={{0,8},{4,12},{8,0},{12,4},{1,9},{5,13},{9,1},{13,5},{2,10},{6,14},... | collective-permute-start | bytes 405512 | tf_op jit(solution)/shard_map/ppermute | solution.py:523
  42.7 9.2 %collective-permute-start.8 = (bf16[528,128]{1,0:T(8,128)(2,1)S(1)}, bf16[528,128]{1,0:T(8,128)(2,1)S(1)}, u32[]{:S(2)}, u32[]{:S(2)}) collective-permute-start(bf16[528,128]{1,0:T(8,128)(2,1)S(1)} %get-tuple-element.34), channel_id=1, source_target_pairs={{0,12},{4,8},{8,4},{12,0},{1,13},{5,9},{9,5},{13,1},{2,14},{6,10},... | collective-permute-start | bytes 405512 | tf_op jit(solution)/shard_map/ppermute | solution.py:523
  43.7 8.4 %collective-permute-start.9 = (bf16[528,128]{1,0:T(8,128)(2,1)S(1)}, bf16[528,128]{1,0:T(8,128)(2,1)S(1)}, u32[]{:S(2)}, u32[]{:S(2)}) collective-permute-start(bf16[528,128]{1,0:T(8,128)(2,1)S(1)} %get-tuple-element.35), channel_id=1, source_target_pairs={{0,4},{4,0},{8,12},{12,8},{1,5},{5,1},{9,13},{13,9},{2,6},{6,2},{1... | collective-permute-start | bytes 405512 | tf_op jit(solution)/shard_map/ppermute | solution.py:523
  53.0 10.3 %collective-permute-start.10 = (bf16[32,512]{1,0:T(8,128)(2,1)S(1)}, bf16[32,512]{1,0:T(8,128)(2,1)S(1)}, u32[]{:S(2)}, u32[]{:S(2)}) collective-permute-start(bf16[32,512]{1,0:T(8,128)(2,1)S(1)} %get-tuple-element.41), channel_id=1, source_target_pairs={{0,1},{2,3},{4,5},{6,7},{8,9},{10,11},{12,13},{14,15},{16,17},{18,... | collective-permute-start | bytes 98312 | tf_op jit(solution)/shard_map/ppermute | solution.py:546
  53.6 10.7 %collective-permute-start.11 = (bf16[32,512]{1,0:T(8,128)(2,1)S(1)}, bf16[32,512]{1,0:T(8,128)(2,1)S(1)}, u32[]{:S(2)}, u32[]{:S(2)}) collective-permute-start(bf16[32,512]{1,0:T(8,128)(2,1)S(1)} %get-tuple-element.42), channel_id=1, source_target_pairs={{1,2},{3,4},{5,6},{7,8},{9,10},{11,12},{13,14},{15,16},{17,18},{19... | collective-permute-start | bytes 98312 | tf_op jit(solution)/shard_map/ppermute | solution.py:546

commit v6 on v5

--- a/solution.py
+++ b/solution.py
@@ -14,8 +14,16 @@
 PATCH_DEV = 4
 HALO = 32
 FIELDS = 4
-ORDER = {1: 0, 3: 1, 7: 2, 2: 3, 6: 4, 5: 5}
 VMEM_LIMIT = 48 * 1024 * 1024
+
+
+def turned(q, pn):
+    bits = (pn.bit_length() - 1) // 2
+    return ((q >> bits) | (q << bits)) & (pn - 1) if bits else q
+
+
+def shifted(d, nz):
+    return 0 if d == 0 else d % (nz - 1) + 1
 
 
 def tap_row(tap, count, start, width, reverse):
@@ -139,7 +147,7 @@
         flat_hbm,
     ) = inputs
     nz, pn, ns = split
-    mine = lax.axis_index("sec") * pn + lax.axis_index("p")
+    my_sec, my_p, my_z = lax.axis_index("sec"), lax.axis_index("p"), lax.axis_index("z")
     visits, _, rows, cols = raw_ref.shape
     terms, tap_count = taps_ref.shape[1], taps_ref.shape[3]
     half = tap_count // 2
@@ -263,8 +271,12 @@
                 sec = owner // (nz * pn)
                 dev = owner - sec * (nz * pn)
                 z = dev // pn
-                dest = (sec * pn + dev - z * pn) ^ mine
-                at = (z ^ lax.axis_index("z")) * CAP + rank
+                step = (dev - z * pn) ^ my_p
+                step = jnp.where(my_sec == 0, step, turned(step, pn))
+                dest = (sec ^ my_sec) * pn + step
+                apart = z ^ my_z
+                later = jnp.where(apart > 1, apart - 1, apart * (nz - 1))
+                at = jnp.where(sec == 0, apart, later) * CAP + rank
                 out_ref[dest, pl.ds(pl.multiple_of(at * SIDE, SIDE), SIDE), :] = left_ref[
                     visit, pl.ds(i * SIDE, SIDE), pl.ds(j * SIDE, SIDE)
                 ]
@@ -489,10 +501,24 @@
         raw_pixels,
         flat_field,
     )
-    peers = [pn] + sorted((k for k in range(1, group) if k != pn), key=lambda k: ORDER.get(k, k))
-    arrived = [
-        lax.ppermute(send[k], ("sec", "p"), [(g, g ^ k) for g in range(group)]) for k in peers
-    ]
+    def in_plane(part, k):
+        pairs = []
+        for sec in range(ns):
+            for p in range(pn):
+                q = k % pn if sec == 0 else turned(k % pn, pn)
+                pairs.append((sec * pn + p, (sec ^ (k // pn)) * pn + (p ^ q)))
+        return lax.ppermute(part, ("sec", "p"), pairs)
+
+    def along_z(part, d):
+        pairs = []
+        for i in range(devices):
+            apart = d if i < nz * pn else shifted(d, nz)
+            pairs.append((i, i ^ (apart * pn)))
+        return lax.ppermute(part, every, pairs)
+
+    every = ("sec", "z", "p")
+    peers = sorted(range(1, group), key=lambda k: (k != pn, -bin(k % pn).count("1"), k))
+    arrived = [in_plane(send[k], k) for k in peers]
 
     across, centre, edge, own = pl.pallas_call(
         prepare_kernel,
@@ -519,10 +545,7 @@
         compiler_params=params,
         name="plane_sums",
     )(own, *arrived)
-    gathered = [plane_sums[0]] + [
-        lax.ppermute(plane_sums[d], "z", [(z, z ^ d) for z in range(nz)])
-        for d in sorted(range(1, nz), key=lambda d: d == 1)
-    ]
+    gathered = [plane_sums[0]] + [along_z(plane_sums[d], d) for d in range(1, nz)]
 
     coadd, main, rest, first_rows, second_rows = pl.pallas_call(
         functools.partial(coadd_kernel, nz),
@@ -539,7 +562,6 @@
         name="coadd",
     )(*gathered)
 
-    every = ("sec", "z", "p")
 
     def swap(rows, start):
         pairs = [(i, i + 1) for i in range(start, devices - 1, 2)]

time: 65.5 us -> 62.8 us (0.959); the launches traced: 65.4 us -> 61.8 us
  waiting for transfers between devices: 29.3 us -> 25.5 us
    ppermute x10, waiting for transfers between devices: 28.3 us -> 24.5 us  [the longest x7 16.7 us: in_plane(): return lax.ppermute(part, ('sec', 'p'), pairs)]
where the time goes in v6:
time: 62.8 us; the launch traced here: 61.8 us
  waiting for transfers between devices  25.5 us (41%)
  starting transfers between devices  23.1 us (37%)
  Pallas kernels  11.5 us (18%)
  local copies, waits for them, and re-layouts  0.96 us (2%)
  between operations  0.7 us (1%)
    ppermute x7, waiting for transfers between devices, in_plane(): return lax.ppermute(part, ('sec', 'p'), pairs)  16.7 us
    ppermute x7, starting transfers between devices, in_plane(): return lax.ppermute(part, ('sec', 'p'), pairs)  9.93 us
    ppermute x2, starting transfers between devices, swap(): return lax.ppermute(rows, every, pairs + [(j, i) for i, j in pairs])  9.45 us
    ppermute x3, waiting for transfers between devices, along_z(): return lax.ppermute(part, every, pairs)  7.79 us
    pallas_call x1, Pallas kernels, per_device(): pl.pallas_call(functools.partial(warp_kernel, split), out_shape=[shaped((...  6.94 us
    ppermute x3, starting transfers between devices, along_z(): return lax.ppermute(part, every, pairs)  3.74 us
    pallas_call x1, Pallas kernels, per_device(): pl.pallas_call(functools.partial(sum_kernel, nz, group), out_shape=[shape...  1.29 us
  transfers between devices with their start and end apart: 12, of which 8 were waited for; matrix products, arithmetic and copies ran while one was open for 0% of the time, Pallas kernels for 2%

profile of v6, /device:TPU:1, one launch (start us, length us, event | category | flops | bytes accessed | tf_op | source)
XLA Modules:
  0.0 61.8 jit_solution(1526135343751559544)
XLA Ops:
  0.6 0.0 copy-start.1
  0.6 6.9 %warp.1 = (bf16[1056,128]{1,0:T(8,128)(2,1)}, bf16[1056,128]{1,0:T(8,128)(2,1)}, bf16[1056,128]{1,0:T(8,128)(2,1)}, bf16[1056,128]{1,0:T(8,128)(2,1)}, bf16[1056...) custom-call(s32[32]{0:T(128)} %bitcast.4, s32[32]{0:T(128)} %bitcast.5, ...), custom_call_target="tpu_custom_call" | custom-call | tf_op jit(solution)/shard_map/warp/pallas_call | solution.py:460
  7.6 0.1 collective-permute-start
  7.7 3.6 %collective-permute-start.1 = (bf16[1056,128]{1,0:T(8,128)(2,1)}, bf16[1056,128]{1,0:T(8,128)(2,1)S(1)}, u32[]{:S(2)}, u32[]{:S(2)}) collective-permute-start(bf16[1056,128]{1,0:T(8,128)(2,1)} %get-tuple-element.26), channel_id=1, source_target_pairs={{0,3},{1,2},{2,1},{3,0},{16,19},{17,18},{18,17},{19,16},{4,7},{5,6... | collective-permute-start | bytes 811016 | tf_op jit(solution)/shard_map/ppermute | solution.py:510
  11.3 0.0 collective-permute-start.2
  11.4 1.6 %collective-permute-start.3 = (bf16[1056,128]{1,0:T(8,128)(2,1)}, bf16[1056,128]{1,0:T(8,128)(2,1)S(1)}, u32[]{:S(2)}, u32[]{:S(2)}) collective-permute-start(bf16[1056,128]{1,0:T(8,128)(2,1)} %get-tuple-element.28), channel_id=1, source_target_pairs={{0,1},{1,0},{2,3},{3,2},{16,18},{17,19},{18,16},{19,17},{4,5},{5,4... | collective-permute-start | bytes 811016 | tf_op jit(solution)/shard_map/ppermute | solution.py:510
  13.0 1.2 %collective-permute-start.4 = (bf16[1056,128]{1,0:T(8,128)(2,1)}, bf16[1056,128]{1,0:T(8,128)(2,1)S(1)}, u32[]{:S(2)}, u32[]{:S(2)}) collective-permute-start(bf16[1056,128]{1,0:T(8,128)(2,1)} %get-tuple-element.29), channel_id=1, source_target_pairs={{0,2},{1,3},{2,0},{3,1},{16,17},{17,16},{18,19},{19,18},{4,6},{5,7... | collective-permute-start | bytes 811016 | tf_op jit(solution)/shard_map/ppermute | solution.py:510
  14.2 0.0 collective-permute-done.refs_1_
  14.2 0.8 %collective-permute-start.5 = (bf16[1056,128]{1,0:T(8,128)(2,1)}, bf16[1056,128]{1,0:T(8,128)(2,1)S(1)}, u32[]{:S(2)}, u32[]{:S(2)}) collective-permute-start(bf16[1056,128]{1,0:T(8,128)(2,1)} %get-tuple-element.30), channel_id=1, source_target_pairs={{0,17},{1,16},{2,19},{3,18},{16,2},{17,3},{18,0},{19,1},{4,21},{5,... | collective-permute-start | bytes 811016 | tf_op jit(solution)/shard_map/ppermute | solution.py:510
  15.0 3.3 %collective-permute-done.1.refs_2_ = bf16[1056,128]{1,0:T(8,128)(2,1)S(1)} collective-permute-done((bf16[1056,128]{1,0:T(8,128)(2,1)}, bf16[1056,128]{1,0:T(8,128)(2,1)S(1)}, u32[]{:S(2)}, u32[]{:S(2)}) %collective-permute-start.1) | collective-permute-done | bytes 270368 | tf_op jit(solution)/shard_map/ppermute | solution.py:510
  18.3 2.5 %collective-permute-start.6 = (bf16[1056,128]{1,0:T(8,128)(2,1)}, bf16[1056,128]{1,0:T(8,128)(2,1)S(1)}, u32[]{:S(2)}, u32[]{:S(2)}) collective-permute-start(bf16[1056,128]{1,0:T(8,128)(2,1)} %get-tuple-element.31), channel_id=1, source_target_pairs={{0,18},{1,19},{2,16},{3,17},{16,1},{17,0},{18,3},{19,2},{4,22},{5,... | collective-permute-start | bytes 811016 | tf_op jit(solution)/shard_map/ppermute | solution.py:510
  20.8 0.0 copy-done.1
  20.8 0.0 copy-start
  20.8 1.0 %copy-done = bf16[1056,128]{1,0:T(8,128)(2,1)S(1)} copy-done((bf16[1056,128]{1,0:T(8,128)(2,1)S(1)}, bf16[1056,128]{1,0:T(8,128)(2,1)}, u32[]{:S(2)}) %copy-start) | copy-done | bytes 270360
  21.8 0.8 %matrices.1 = (bf16[2,512,512]{2,1,0:T(8,128)(2,1)S(1)}, bf16[2,128,128]{2,1,0:T(8,128)(2,1)S(1)}, bf16[2,64,64]{2,1,0:T(8,128)(2,1)S(1)}, bf16[1056,128]{1,0:T(8,128)(2,1)S(1)}) custom-call(f32[2,41]{1,0:T(2,128)S(1)} %copy-done.1, bf16[1056,128]{1,0:T(8,128)(2,1)S(1)} %copy-done), custom_call_target="tpu_custom_call" | custom-call | bytes 8388608 | tf_op jit(solution)/shard_map/matrices/pallas_call | solution.py:523
  22.5 1.8 %collective-permute-done.2.refs_3_ = bf16[1056,128]{1,0:T(8,128)(2,1)S(1)} collective-permute-done((bf16[1056,128]{1,0:T(8,128)(2,1)}, bf16[1056,128]{1,0:T(8,128)(2,1)S(1)}, u32[]{:S(2)}, u32[]{:S(2)}) %collective-permute-start.2) | collective-permute-done | bytes 270368 | tf_op jit(solution)/shard_map/ppermute | solution.py:510
  24.4 5.7 %collective-permute-done.3.refs_4_ = bf16[1056,128]{1,0:T(8,128)(2,1)S(1)} collective-permute-done((bf16[1056,128]{1,0:T(8,128)(2,1)}, bf16[1056,128]{1,0:T(8,128)(2,1)S(1)}, u32[]{:S(2)}, u32[]{:S(2)}) %collective-permute-start.3) | collective-permute-done | bytes 270368 | tf_op jit(solution)/shard_map/ppermute | solution.py:510
  30.0 0.0 collective-permute-done.4.refs_5_
  30.0 5.9 %collective-permute-done.5.refs_6_ = bf16[1056,128]{1,0:T(8,128)(2,1)S(1)} collective-permute-done((bf16[1056,128]{1,0:T(8,128)(2,1)}, bf16[1056,128]{1,0:T(8,128)(2,1)S(1)}, u32[]{:S(2)}, u32[]{:S(2)}) %collective-permute-start.5) | collective-permute-done | bytes 270368 | tf_op jit(solution)/shard_map/ppermute | solution.py:510
  36.0 0.0 collective-permute-done.6.refs_7_
  36.0 1.3 %plane_sums.1 = (bf16[528,128]{1,0:T(8,128)(2,1)S(1)}, bf16[528,128]{1,0:T(8,128)(2,1)S(1)}, bf16[528,128]{1,0:T(8,128)(2,1)S(1)}, bf16[528,128]{1,0:T(8,128)(2,1)S(1)}) custom-call(bf16[1056,128]{1,0:T(8,128)(2,1)S(1)} %get-tuple-element.24.refs_0_, bf16[1056,128]{1,0:T(8,128)(2,1)S(1)} %collective-permute-done.refs_1_, ...), custom_call_target="tpu_custom_call" | custom-call | tf_op jit(solution)/shard_map/plane_sums/pallas_call | solution.py:539
  37.3 2.5 %collective-permute-start.7 = (bf16[528,128]{1,0:T(8,128)(2,1)S(1)}, bf16[528,128]{1,0:T(8,128)(2,1)S(1)}, u32[]{:S(2)}, u32[]{:S(2)}) collective-permute-start(bf16[528,128]{1,0:T(8,128)(2,1)S(1)} %get-tuple-element.33), channel_id=1, source_target_pairs={{0,4},{1,5},{2,6},{3,7},{4,0},{5,1},{6,2},{7,3},{8,12},{9,13},{10,... | collective-permute-start | bytes 405512 | tf_op jit(solution)/shard_map/ppermute | solution.py:517
  39.7 1.1 %collective-permute-start.8 = (bf16[528,128]{1,0:T(8,128)(2,1)S(1)}, bf16[528,128]{1,0:T(8,128)(2,1)S(1)}, u32[]{:S(2)}, u32[]{:S(2)}) collective-permute-start(bf16[528,128]{1,0:T(8,128)(2,1)S(1)} %get-tuple-element.34), channel_id=1, source_target_pairs={{0,8},{1,9},{2,10},{3,11},{4,12},{5,13},{6,14},{7,15},{8,0},{9,1},... | collective-permute-start | bytes 405512 | tf_op jit(solution)/shard_map/ppermute | solution.py:517
  40.8 0.2 collective-permute-start.9
  41.0 3.0 %collective-permute-done.7.refs_1_ = bf16[528,128]{1,0:T(8,128)(2,1)S(1)} collective-permute-done((bf16[528,128]{1,0:T(8,128)(2,1)S(1)}, bf16[528,128]{1,0:T(8,128)(2,1)S(1)}, u32[]{:S(2)}, u32[]{:S(2)}) %collective-permute-start.7) | collective-permute-done | bytes 135200 | tf_op jit(solution)/shard_map/ppermute | solution.py:517
  44.0 2.8 %collective-permute-done.8.refs_2_ = bf16[528,128]{1,0:T(8,128)(2,1)S(1)} collective-permute-done((bf16[528,128]{1,0:T(8,128)(2,1)S(1)}, bf16[528,128]{1,0:T(8,128)(2,1)S(1)}, u32[]{:S(2)}, u32[]{:S(2)}) %collective-permute-start.8) | collective-permute-done | bytes 135200 | tf_op jit(solution)/shard_map/ppermute | solution.py:517
  46.9 1.9 %collective-permute-done.9.refs_3_ = bf16[528,128]{1,0:T(8,128)(2,1)S(1)} collective-permute-done((bf16[528,128]{1,0:T(8,128)(2,1)S(1)}, bf16[528,128]{1,0:T(8,128)(2,1)S(1)}, u32[]{:S(2)}, u32[]{:S(2)}) %collective-permute-start.9) | collective-permute-done | bytes 135200 | tf_op jit(solution)/shard_map/ppermute | solution.py:517
  48.8 0.8 %coadd.1 = (f32[128,512]{1,0:T(8,128)}, bf16[128,512]{1,0:T(8,128)(2,1)S(1)}, bf16[128,512]{1,0:T(8,128)(2,1)S(1)}, bf16[32,512]{1,0:T(8,128)(2,1)S(1)}, bf16[32,512]{1,0:T(8,128)(2,1)S(1)}) custom-call(bf16[528,128]{1,0:T(8,128)(2,1)S(1)} %get-tuple-element.32.refs_0_, bf16[528,128]{1,0:T(8,128)(2,1)S(1)} %collective-permute-done.7.refs_1_, ...), custom_call_target="tpu_custom_call" | custom-call | tf_op jit(solution)/shard_map/coadd/pallas_call | solution.py:550
  49.6 1.2 %collective-permute-start.10 = (bf16[32,512]{1,0:T(8,128)(2,1)S(1)}, bf16[32,512]{1,0:T(8,128)(2,1)S(1)}, u32[]{:S(2)}, u32[]{:S(2)}) collective-permute-start(bf16[32,512]{1,0:T(8,128)(2,1)S(1)} %get-tuple-element.41), channel_id=1, source_target_pairs={{0,1},{2,3},{4,5},{6,7},{8,9},{10,11},{12,13},{14,15},{16,17},{18,... | collective-permute-start | bytes 98312 | tf_op jit(solution)/shard_map/ppermute | solution.py:568
  50.9 8.2 %collective-permute-start.11 = (bf16[32,512]{1,0:T(8,128)(2,1)S(1)}, bf16[32,512]{1,0:T(8,128)(2,1)S(1)}, u32[]{:S(2)}, u32[]{:S(2)}) collective-permute-start(bf16[32,512]{1,0:T(8,128)(2,1)S(1)} %get-tuple-element.42), channel_id=1, source_target_pairs={{1,2},{3,4},{5,6},{7,8},{9,10},{11,12},{13,14},{15,16},{17,18},{19... | collective-permute-start | bytes 98312 | tf_op jit(solution)/shard_map/ppermute | solution.py:568
  59.1 0.6 detect_centre.1.inner_ref
  59.6 0.0 collective-permute-done.10.first_ref
  59.7 1.0 %collective-permute-done.11.second_ref = bf16[32,512]{1,0:T(8,128)(2,1)S(1)} collective-permute-done((bf16[32,512]{1,0:T(8,128)(2,1)S(1)}, bf16[32,512]{1,0:T(8,128)(2,1)S(1)}, u32[]{:S(2)}, u32[]{:S(2)}) %collective-permute-start.11) | collective-permute-done | bytes 32800 | tf_op jit(solution)/shard_map/ppermute | solution.py:568
  60.7 1.1 %detect_edges.1 = f32[128,512]{1,0:T(8,128)} custom-call(f32[128,512]{1,0:T(8,128)S(1)} %detect_centre.1.inner_ref, bf16[32,512]{1,0:T(8,128)(2,1)S(1)} %collective-permute-done.10.first_ref, bf16[32,512]{1,0:T(8,128)(2,1)S(1)} %collective-permute-done.11.second_ref, bf16[2,512,512]{2,1,0:T(8,128)(2,1)S(1)} %get-tuple-element.39.across_ref, ...), custom_call_target="tpu_custom_call" | custom-call | tf_op jit(solution)/shard_map/detect_edges/pallas_call | solution.py:583
Async XLA Ops:
  0.6 20.2 %copy-start.1 = (f32[2,41]{1,0:T(2,128)S(1)}, f32[2,41]{1,0:T(2,128)}, u32[]{:S(2)}) copy-start(f32[2,41]{1,0:T(2,128)} %taps_ref.1) | copy-start | bytes 988
  7.6 6.6 %collective-permute-start = (bf16[1056,128]{1,0:T(8,128)(2,1)}, bf16[1056,128]{1,0:T(8,128)(2,1)S(1)}, u32[]{:S(2)}, u32[]{:S(2)}) collective-permute-start(bf16[1056,128]{1,0:T(8,128)(2,1)} %get-tuple-element.25), channel_id=1, source_target_pairs={{0,16},{1,17},{2,18},{3,19},{16,0},{17,1},{18,2},{19,3},{4,20},{5,... | collective-permute-start | bytes 811016 | tf_op jit(solution)/shard_map/ppermute | solution.py:510
  7.7 10.6 %collective-permute-start.1 = (bf16[1056,128]{1,0:T(8,128)(2,1)}, bf16[1056,128]{1,0:T(8,128)(2,1)S(1)}, u32[]{:S(2)}, u32[]{:S(2)}) collective-permute-start(bf16[1056,128]{1,0:T(8,128)(2,1)} %get-tuple-element.26), channel_id=1, source_target_pairs={{0,3},{1,2},{2,1},{3,0},{16,19},{17,18},{18,17},{19,16},{4,7},{5,6... | collective-permute-start | bytes 811016 | tf_op jit(solution)/shard_map/ppermute | solution.py:510
  11.3 13.0 %collective-permute-start.2 = (bf16[1056,128]{1,0:T(8,128)(2,1)}, bf16[1056,128]{1,0:T(8,128)(2,1)S(1)}, u32[]{:S(2)}, u32[]{:S(2)}) collective-permute-start(bf16[1056,128]{1,0:T(8,128)(2,1)} %get-tuple-element.27), channel_id=1, source_target_pairs={{0,19},{1,18},{2,17},{3,16},{16,3},{17,2},{18,1},{19,0},{4,23},{5,... | collective-permute-start | bytes 811016 | tf_op jit(solution)/shard_map/ppermute | solution.py:510
  11.4 18.7 %collective-permute-start.3 = (bf16[1056,128]{1,0:T(8,128)(2,1)}, bf16[1056,128]{1,0:T(8,128)(2,1)S(1)}, u32[]{:S(2)}, u32[]{:S(2)}) collective-permute-start(bf16[1056,128]{1,0:T(8,128)(2,1)} %get-tuple-element.28), channel_id=1, source_target_pairs={{0,1},{1,0},{2,3},{3,2},{16,18},{17,19},{18,16},{19,17},{4,5},{5,4... | collective-permute-start | bytes 811016 | tf_op jit(solution)/shard_map/ppermute | solution.py:510
  13.0 17.0 %collective-permute-start.4 = (bf16[1056,128]{1,0:T(8,128)(2,1)}, bf16[1056,128]{1,0:T(8,128)(2,1)S(1)}, u32[]{:S(2)}, u32[]{:S(2)}) collective-permute-start(bf16[1056,128]{1,0:T(8,128)(2,1)} %get-tuple-element.29), channel_id=1, source_target_pairs={{0,2},{1,3},{2,0},{3,1},{16,17},{17,16},{18,19},{19,18},{4,6},{5,7... | collective-permute-start | bytes 811016 | tf_op jit(solution)/shard_map/ppermute | solution.py:510
  14.2 21.8 %collective-permute-start.5 = (bf16[1056,128]{1,0:T(8,128)(2,1)}, bf16[1056,128]{1,0:T(8,128)(2,1)S(1)}, u32[]{:S(2)}, u32[]{:S(2)}) collective-permute-start(bf16[1056,128]{1,0:T(8,128)(2,1)} %get-tuple-element.30), channel_id=1, source_target_pairs={{0,17},{1,16},{2,19},{3,18},{16,2},{17,3},{18,0},{19,1},{4,21},{5,... | collective-permute-start | bytes 811016 | tf_op jit(solution)/shard_map/ppermute | solution.py:510
  18.3 17.6 %collective-permute-start.6 = (bf16[1056,128]{1,0:T(8,128)(2,1)}, bf16[1056,128]{1,0:T(8,128)(2,1)S(1)}, u32[]{:S(2)}, u32[]{:S(2)}) collective-permute-start(bf16[1056,128]{1,0:T(8,128)(2,1)} %get-tuple-element.31), channel_id=1, source_target_pairs={{0,18},{1,19},{2,16},{3,17},{16,1},{17,0},{18,3},{19,2},{4,22},{5,... | collective-permute-start | bytes 811016 | tf_op jit(solution)/shard_map/ppermute | solution.py:510
  20.8 1.0 %copy-start = (bf16[1056,128]{1,0:T(8,128)(2,1)S(1)}, bf16[1056,128]{1,0:T(8,128)(2,1)}, u32[]{:S(2)}) copy-start(bf16[1056,128]{1,0:T(8,128)(2,1)} %get-tuple-element.23.own_hbm) | copy-start | bytes 811012
  37.3 6.8 %collective-permute-start.7 = (bf16[528,128]{1,0:T(8,128)(2,1)S(1)}, bf16[528,128]{1,0:T(8,128)(2,1)S(1)}, u32[]{:S(2)}, u32[]{:S(2)}) collective-permute-start(bf16[528,128]{1,0:T(8,128)(2,1)S(1)} %get-tuple-element.33), channel_id=1, source_target_pairs={{0,4},{1,5},{2,6},{3,7},{4,0},{5,1},{6,2},{7,3},{8,12},{9,13},{10,... | collective-permute-start | bytes 405512 | tf_op jit(solution)/shard_map/ppermute | solution.py:517
  39.7 7.1 %collective-permute-start.8 = (bf16[528,128]{1,0:T(8,128)(2,1)S(1)}, bf16[528,128]{1,0:T(8,128)(2,1)S(1)}, u32[]{:S(2)}, u32[]{:S(2)}) collective-permute-start(bf16[528,128]{1,0:T(8,128)(2,1)S(1)} %get-tuple-element.34), channel_id=1, source_target_pairs={{0,8},{1,9},{2,10},{3,11},{4,12},{5,13},{6,14},{7,15},{8,0},{9,1},... | collective-permute-start | bytes 405512 | tf_op jit(solution)/shard_map/ppermute | solution.py:517
  40.8 8.0 %collective-permute-start.9 = (bf16[528,128]{1,0:T(8,128)(2,1)S(1)}, bf16[528,128]{1,0:T(8,128)(2,1)S(1)}, u32[]{:S(2)}, u32[]{:S(2)}) collective-permute-start(bf16[528,128]{1,0:T(8,128)(2,1)S(1)} %get-tuple-element.35), channel_id=1, source_target_pairs={{0,12},{1,13},{2,14},{3,15},{4,8},{5,9},{6,10},{7,11},{8,4},{9,5},... | collective-permute-start | bytes 405512 | tf_op jit(solution)/shard_map/ppermute | solution.py:517
  49.6 10.0 %collective-permute-start.10 = (bf16[32,512]{1,0:T(8,128)(2,1)S(1)}, bf16[32,512]{1,0:T(8,128)(2,1)S(1)}, u32[]{:S(2)}, u32[]{:S(2)}) collective-permute-start(bf16[32,512]{1,0:T(8,128)(2,1)S(1)} %get-tuple-element.41), channel_id=1, source_target_pairs={{0,1},{2,3},{4,5},{6,7},{8,9},{10,11},{12,13},{14,15},{16,17},{18,... | collective-permute-start | bytes 98312 | tf_op jit(solution)/shard_map/ppermute | solution.py:568
  50.9 9.8 %collective-permute-start.11 = (bf16[32,512]{1,0:T(8,128)(2,1)S(1)}, bf16[32,512]{1,0:T(8,128)(2,1)S(1)}, u32[]{:S(2)}, u32[]{:S(2)}) collective-permute-start(bf16[32,512]{1,0:T(8,128)(2,1)S(1)} %get-tuple-element.42), channel_id=1, source_target_pairs={{1,2},{3,4},{5,6},{7,8},{9,10},{11,12},{13,14},{15,16},{17,18},{19... | collective-permute-start | bytes 98312 | tf_op jit(solution)/shard_map/ppermute | solution.py:568

commit v7 on v6

--- a/solution.py
+++ b/solution.py
@@ -193,13 +193,23 @@
     for copy in small:
         copy.wait()
 
-    def hat(length, axis, shift, scale):
+    def store_hat(ref, length, axis, shift, scale):
         centre = (length - 1) / 2.0
-        shape = (1, length) if axis == 1 else (length, 1)
-        out_pos = lax.broadcasted_iota(jnp.int32, shape, axis).astype(jnp.float32)
-        source = scale * (out_pos - centre) + centre + shift
-        in_pos = lax.broadcasted_iota(jnp.int32, (length, length), 1 - axis).astype(jnp.float32)
-        return jnp.maximum(0.0, 1.0 - jnp.abs(in_pos - source)).astype(jnp.bfloat16)
+        count = length // SIDE
+        for o in range(count):
+            out_pos = o * SIDE + lax.broadcasted_iota(
+                jnp.int32, (1, SIDE) if axis == 1 else (SIDE, 1), axis
+            )
+            source = scale * (out_pos.astype(jnp.float32) - centre) + centre + shift
+            for i in range(count):
+                at = (i, o) if axis == 1 else (o, i)
+                place = tuple(pl.ds(k * SIDE, SIDE) for k in at)
+                if abs(i - o) <= 1:
+                    in_pos = i * SIDE + lax.broadcasted_iota(jnp.int32, (SIDE, SIDE), 1 - axis)
+                    near = jnp.maximum(0.0, 1.0 - jnp.abs(in_pos.astype(jnp.float32) - source))
+                    ref[place] = near.astype(jnp.bfloat16)
+                else:
+                    ref[place] = jnp.zeros((SIDE, SIDE), jnp.bfloat16)
 
     for visit in range(visits):
         for term in range(terms):
@@ -214,10 +224,14 @@
                 store_band(
                     band_ref.at[visit, 2 * term + 1 - axis], toeplitz(row, SIDE).astype(jnp.bfloat16)
                 )
-        band_ref[visit, 2 * terms] = hat(cols, 1, shift_ref[visit, 0, 1], scale_ref[visit, 0, 1])
-        band_ref[visit, 2 * terms + 1] = hat(
-            rows, 0, shift_ref[visit, 0, 0], scale_ref[visit, 0, 0]
-        )
+        for axis, length in ((1, cols), (0, rows)):
+            store_hat(
+                band_ref.at[visit, 2 * terms + 1 - axis],
+                length,
+                axis,
+                shift_ref[visit, 0, axis],
+                scale_ref[visit, 0, axis],
+            )
 
     def windows(length):
         wide = 2 * SIDE
@@ -300,10 +314,11 @@
         out_copy(dest).wait()
 
 
-def sum_kernel(nz, sources, *refs):
+def sum_kernel(nz, sources, chunks, *refs):
     ins, outs, weight_ref = refs[:sources], refs[sources:-1], refs[-1]
     per_dest = nz * CAP
     data_rows = per_dest * SIDE
+    with_totals = chunks[0] == 0
     for g in range(sources):
         fields = ins[g][pl.ds(data_rows, FIELDS * per_dest), :].astype(jnp.float32)
         slot = fields[:per_dest]
@@ -314,63 +329,88 @@
         )
         for j in range(PATCH_DEV):
             weight_ref[g, j] = jnp.where(slot == float(j), weight, 0.0)
-    step = 32
     for z in range(nz):
-        for c in range(SIDE // step):
-            sums = [jnp.zeros((step, SIDE), jnp.float32) for _ in range(PATCH_DEV)]
+        for place, c in enumerate(chunks):
+            sums = [jnp.zeros((HALO, SIDE), jnp.float32) for _ in range(PATCH_DEV)]
             for g in range(sources):
                 for r in range(CAP):
                     at = z * CAP + r
-                    value = ins[g][pl.ds(at * SIDE + c * step, step), :].astype(jnp.float32)
+                    value = ins[g][pl.ds(at * SIDE + c * HALO, HALO), :].astype(jnp.float32)
                     for j in range(PATCH_DEV):
                         sums[j] = sums[j] + weight_ref[g, j, pl.ds(at, 1), :] * value
             for j in range(PATCH_DEV):
-                outs[z][pl.ds(j * SIDE + c * step, step), :] = sums[j].astype(jnp.bfloat16)
-        totals = []
-        for j in range(PATCH_DEV):
-            total = jnp.zeros((1, SIDE), jnp.float32)
-            for g in range(sources):
-                for r in range(CAP):
-                    total = total + weight_ref[g, j, pl.ds(z * CAP + r, 1), :]
-            totals.append(total)
-        parts = three_parts(jnp.concatenate(totals, axis=0))
-        extra = jnp.concatenate(
-            [q.astype(jnp.float32) for q in parts] + [jnp.zeros((PATCH_DEV, SIDE), jnp.float32)],
-            axis=0,
-        )
-        outs[z][pl.ds(PATCH_DEV * SIDE, FIELDS * PATCH_DEV), :] = extra.astype(jnp.bfloat16)
-
-
-def coadd_kernel(sources, *refs):
-    ins, (coadd_ref, main_ref, rest_ref, first_ref, second_ref) = refs[:sources], refs[sources:]
-    odd = lax.axis_index("p") % 2
+                row = (j * len(chunks) + place) * HALO
+                outs[z][pl.ds(row, HALO), :] = sums[j].astype(jnp.bfloat16)
+        if with_totals:
+            totals = []
+            for j in range(PATCH_DEV):
+                total = jnp.zeros((1, SIDE), jnp.float32)
+                for g in range(sources):
+                    for r in range(CAP):
+                        total = total + weight_ref[g, j, pl.ds(z * CAP + r, 1), :]
+                totals.append(total)
+            parts = [q.astype(jnp.float32) for q in three_parts(jnp.concatenate(totals, axis=0))]
+            parts.append(jnp.zeros((PATCH_DEV, SIDE), jnp.float32))
+            outs[z][pl.ds(PATCH_DEV * len(chunks) * HALO, FIELDS * PATCH_DEV), :] = (
+                jnp.concatenate(parts, axis=0).astype(jnp.bfloat16)
+            )
+
+
+def totals_of(ins, start):
     total = jnp.zeros((PATCH_DEV, SIDE), jnp.float32)
-    for z in range(sources):
-        extra = ins[z][pl.ds(PATCH_DEV * SIDE, FIELDS * PATCH_DEV), :].astype(jnp.float32)
+    for ref in ins:
+        extra = ref[pl.ds(start, FIELDS * PATCH_DEV), :].astype(jnp.float32)
         total = total + (
             extra[:PATCH_DEV] + extra[PATCH_DEV : 2 * PATCH_DEV] + extra[2 * PATCH_DEV : 3 * PATCH_DEV]
         )
-    total = jnp.maximum(total, 1.0)
+    return jnp.maximum(total, 1.0)
+
+
+def average(ins, row, count, total):
+    numerator = ins[0][pl.ds(row, count), :].astype(jnp.float32)
+    for ref in ins[1:]:
+        numerator = numerator + ref[pl.ds(row, count), :].astype(jnp.float32)
+    return numerator / total
+
+
+def edges_kernel(*refs):
+    ins, first_ref, second_ref = refs[:-2], refs[-2], refs[-1]
+    odd = lax.axis_index("p") % 2
+    total = totals_of(ins, 2 * PATCH_DEV * HALO)
     for j in range(PATCH_DEV):
-        numerator = ins[0][pl.ds(j * SIDE, SIDE), :].astype(jnp.float32)
-        for z in range(1, sources):
-            numerator = numerator + ins[z][pl.ds(j * SIDE, SIDE), :].astype(jnp.float32)
-        tile = numerator / total[j : j + 1]
         sl = pl.ds(j * SIDE, SIDE)
-        coadd_ref[:, sl] = tile
-        main, rest = two_parts(tile)
-        main_ref[:, sl] = main
-        rest_ref[:, sl] = rest
-
-    @pl.when(odd == 0)
-    def _():
-        first_ref[...] = main_ref[pl.ds(SIDE - HALO, HALO)]
-        second_ref[...] = main_ref[pl.ds(0, HALO)]
-
-    @pl.when(odd == 1)
-    def _():
-        first_ref[...] = main_ref[pl.ds(0, HALO)]
-        second_ref[...] = main_ref[pl.ds(SIDE - HALO, HALO)]
+        rows = average(ins, 2 * j * HALO, 2 * HALO, total[j : j + 1])
+        top, bottom = rows[:HALO], rows[HALO:]
+        first_ref[:, sl] = jnp.where(odd == 0, bottom, top).astype(jnp.bfloat16)
+        second_ref[:, sl] = jnp.where(odd == 0, top, bottom).astype(jnp.bfloat16)
+
+
+def detect_kernel(nz, *refs):
+    edges, inner = refs[:nz], refs[nz : 2 * nz]
+    first_ref, second_ref, across_ref, centre_ref, edge_ref = refs[2 * nz : 2 * nz + 5]
+    coadd_ref, out_ref, halo_ref = refs[2 * nz + 5 :]
+    odd = lax.axis_index("p") % 2
+    halo_ref[pl.ds(pl.multiple_of((1 - odd) * HALO, HALO), HALO)] = first_ref[...]
+    halo_ref[pl.ds(pl.multiple_of(odd * HALO, HALO), HALO)] = second_ref[...]
+    halo = halo_ref[...]
+    total = totals_of(edges, 2 * PATCH_DEV * HALO)
+    depth = SIDE - 2 * HALO
+    for j in range(PATCH_DEV):
+        sl = pl.ds(j * SIDE, SIDE)
+        weight = total[j : j + 1]
+        coadd_ref[pl.ds(0, HALO), sl] = average(edges, 2 * j * HALO, HALO, weight)
+        coadd_ref[pl.ds(HALO, depth), sl] = average(inner, j * depth, depth, weight)
+        coadd_ref[pl.ds(SIDE - HALO, HALO), sl] = average(edges, (2 * j + 1) * HALO, HALO, weight)
+    main, rest = two_parts(coadd_ref[...])
+    along = dot32(centre_ref[0], main) + (
+        dot32(centre_ref[0], rest) + dot32(centre_ref[1], main)
+    )
+    ends = dot32(edge_ref[0], halo) + dot32(edge_ref[1], halo)
+    along = jnp.concatenate(
+        [along[:HALO] + ends[:HALO], along[HALO : SIDE - HALO], along[SIDE - HALO :] + ends[HALO:]],
+        axis=0,
+    )
+    out_ref[...] = dot_parts(along, across_ref)
 
 
 def prepare_kernel(taps_ref, own_hbm, across_ref, centre_ref, edge_ref, own_ref, band_ref, own_sem):
@@ -402,26 +442,6 @@
     main, rest = two_parts(left)
     both = dot32(jnp.concatenate([main, rest], axis=0), across_ref[0])
     return both[: left.shape[0]] + (dot32(main, across_ref[1]) + both[left.shape[0] :])
-
-
-def centre_kernel(main_ref, rest_ref, across_ref, centre_ref, out_ref):
-    main = main_ref[...]
-    along = dot32(centre_ref[0], main) + (
-        dot32(centre_ref[0], rest_ref[...]) + dot32(centre_ref[1], main)
-    )
-    out_ref[...] = dot_parts(along, across_ref)
-
-
-def edge_kernel(inner_ref, first_ref, second_ref, across_ref, edge_ref, out_ref, halo_ref):
-    odd = lax.axis_index("p") % 2
-    halo_ref[pl.ds(pl.multiple_of((1 - odd) * HALO, HALO), HALO)] = first_ref[...]
-    halo_ref[pl.ds(pl.multiple_of(odd * HALO, HALO), HALO)] = second_ref[...]
-    halo = halo_ref[...]
-    along = dot32(edge_ref[0], halo) + dot32(edge_ref[1], halo)
-    extra = dot_parts(along, across_ref)
-    out_ref[pl.ds(0, HALO)] = inner_ref[pl.ds(0, HALO)] + extra[:HALO]
-    out_ref[pl.ds(HALO, SIDE - 2 * HALO)] = inner_ref[pl.ds(HALO, SIDE - 2 * HALO)]
-    out_ref[pl.ds(SIDE - HALO, HALO)] = inner_ref[pl.ds(SIDE - HALO, HALO)] + extra[HALO:]
 
 
 def per_device(
@@ -536,32 +556,33 @@
         name="matrices",
     )(detect_taps, send[0])
 
-    plane_sums = pl.pallas_call(
-        functools.partial(sum_kernel, nz, group),
-        out_shape=[shaped((PATCH_DEV * (SIDE + FIELDS), SIDE), jnp.bfloat16)] * nz,
-        in_specs=[vmem] * group,
-        out_specs=[vmem] * nz,
-        scratch_shapes=[pltpu.VMEM((group, PATCH_DEV, per_dest, SIDE), jnp.float32)],
+    def plane_sums(chunks, rows, name):
+        return pl.pallas_call(
+            functools.partial(sum_kernel, nz, group, chunks),
+            out_shape=[shaped((rows, SIDE), jnp.bfloat16)] * nz,
+            in_specs=[vmem] * group,
+            out_specs=[vmem] * nz,
+            scratch_shapes=[pltpu.VMEM((group, PATCH_DEV, per_dest, SIDE), jnp.float32)],
+            compiler_params=params,
+            cost_estimate=pl.CostEstimate(flops=0, bytes_accessed=4 << 20, transcendentals=0),
+            name=name,
+        )(own, *arrived)
+
+    last = SIDE // HALO - 1
+    edge_rows = PATCH_DEV * (2 * HALO + FIELDS)
+    edge_sums = plane_sums((0, last), edge_rows, "edge_sums")
+    inner_sums = plane_sums(tuple(range(1, last)), PATCH_DEV * (SIDE - 2 * HALO), "inner_sums")
+    edges = [edge_sums[0]] + [along_z(edge_sums[d], d) for d in range(1, nz)]
+    inner = [inner_sums[0]] + [along_z(inner_sums[d], d) for d in range(1, nz)]
+
+    first_rows, second_rows = pl.pallas_call(
+        edges_kernel,
+        out_shape=[shaped((HALO, width), jnp.bfloat16)] * 2,
+        in_specs=[vmem] * nz,
+        out_specs=[vmem] * 2,
         compiler_params=params,
-        name="plane_sums",
-    )(own, *arrived)
-    gathered = [plane_sums[0]] + [along_z(plane_sums[d], d) for d in range(1, nz)]
-
-    coadd, main, rest, first_rows, second_rows = pl.pallas_call(
-        functools.partial(coadd_kernel, nz),
-        out_shape=(
-            shaped((SIDE, width), jnp.float32),
-            shaped((SIDE, width), jnp.bfloat16),
-            shaped((SIDE, width), jnp.bfloat16),
-            shaped((HALO, width), jnp.bfloat16),
-            shaped((HALO, width), jnp.bfloat16),
-        ),
-        in_specs=[vmem] * nz,
-        out_specs=(vmem,) * 5,
-        compiler_params=params,
-        name="coadd",
-    )(*gathered)
-
+        name="edge_rows",
+    )(*edges)
 
     def swap(rows, start):
         pairs = [(i, i + 1) for i in range(start, devices - 1, 2)]
@@ -569,26 +590,15 @@
 
     first, second = swap(first_rows, 0), swap(second_rows, 1)
 
-    inner = pl.pallas_call(
-        centre_kernel,
-        out_shape=shaped((SIDE, width), jnp.float32),
-        in_specs=[vmem] * 4,
-        out_specs=vmem,
-        compiler_params=params,
-        cost_estimate=pl.CostEstimate(
-            flops=6 * SIDE * width * (SIDE + width), bytes_accessed=2 << 20, transcendentals=0
-        ),
-        name="detect_centre",
-    )(main, rest, across, centre)
-    detection = pl.pallas_call(
-        edge_kernel,
-        out_shape=shaped((SIDE, width), jnp.float32),
-        in_specs=[vmem] * 5,
-        out_specs=vmem,
+    coadd, detection = pl.pallas_call(
+        functools.partial(detect_kernel, nz),
+        out_shape=[shaped((SIDE, width), jnp.float32)] * 2,
+        in_specs=[vmem] * (2 * nz + 5),
+        out_specs=[vmem] * 2,
         scratch_shapes=[pltpu.VMEM((2 * HALO, width), jnp.bfloat16)],
         compiler_params=params,
-        name="detect_edges",
-    )(inner, first, second, across, edge)
+        name="coadd_detect",
+    )(*edges, *inner, first, second, across, centre, edge)
     return coadd, detection
 
 

time: 62.8 us -> 59.2 us (0.943)
  the two profiles are of different devices: /device:TPU:1 before, /device:TPU:16 now
where the time goes in v7:
time: 59.2 us; the launch traced here: 59 us
  waiting for transfers between devices  29.4 us (50%)
  starting transfers between devices  17.8 us (30%)
  Pallas kernels  10 us (17%)
  local copies, waits for them, and re-layouts  0.96 us (2%)
  between operations  0.73 us (1%)
    ppermute x7, waiting for transfers between devices, in_plane(): return lax.ppermute(part, ('sec', 'p'), pairs)  19.5 us
    ppermute x6, starting transfers between devices, along_z(): return lax.ppermute(part, every, pairs)  7.65 us
    pallas_call x1, Pallas kernels, per_device(): pl.pallas_call(functools.partial(warp_kernel, split), out_shape=[shaped((...  6.53 us
    ppermute x7, starting transfers between devices, in_plane(): return lax.ppermute(part, ('sec', 'p'), pairs)  6.1 us
    ppermute x2, waiting for transfers between devices, swap(): return lax.ppermute(rows, every, pairs + [(j, i) for i, j in pairs])  5.03 us
    ppermute x6, waiting for transfers between devices, along_z(): return lax.ppermute(part, every, pairs)  4.89 us
    ppermute x2, starting transfers between devices, swap(): return lax.ppermute(rows, every, pairs + [(j, i) for i, j in pairs])  4.07 us
    pallas_call x1, Pallas kernels, per_device(): pl.pallas_call(functools.partial(detect_kernel, nz), out_shape=[shaped((S...  1.38 us
  transfers between devices with their start and end apart: 15, of which 6 were waited for; matrix products, arithmetic and copies ran while one was open for 0% of the time, Pallas kernels for 2%

profile of v7, /device:TPU:16, one launch (start us, length us, event | category | flops | bytes accessed | tf_op | source)
XLA Modules:
  0.0 59.0 jit_solution(9628735654384034549)
XLA Ops:
  0.6 0.0 copy-start.1
  0.6 6.5 %warp.1 = (bf16[1056,128]{1,0:T(8,128)(2,1)}, bf16[1056,128]{1,0:T(8,128)(2,1)}, bf16[1056,128]{1,0:T(8,128)(2,1)}, bf16[1056,128]{1,0:T(8,128)(2,1)}, bf16[1056...) custom-call(s32[32]{0:T(128)} %bitcast.4, s32[32]{0:T(128)} %bitcast.5, ...), custom_call_target="tpu_custom_call" | custom-call | tf_op jit(solution)/shard_map/warp/pallas_call | solution.py:480
  7.2 0.1 collective-permute-start
  7.3 2.5 %collective-permute-start.1 = (bf16[1056,128]{1,0:T(8,128)(2,1)}, bf16[1056,128]{1,0:T(8,128)(2,1)S(1)}, u32[]{:S(2)}, u32[]{:S(2)}) collective-permute-start(bf16[1056,128]{1,0:T(8,128)(2,1)} %get-tuple-element.27), channel_id=1, source_target_pairs={{0,3},{1,2},{2,1},{3,0},{16,19},{17,18},{18,17},{19,16},{4,7},{5,6... | collective-permute-start | bytes 811016 | tf_op jit(solution)/shard_map/ppermute | solution.py:530
  9.8 0.3 collective-permute-start.2
  10.0 1.5 %collective-permute-start.3 = (bf16[1056,128]{1,0:T(8,128)(2,1)}, bf16[1056,128]{1,0:T(8,128)(2,1)S(1)}, u32[]{:S(2)}, u32[]{:S(2)}) collective-permute-start(bf16[1056,128]{1,0:T(8,128)(2,1)} %get-tuple-element.29), channel_id=1, source_target_pairs={{0,1},{1,0},{2,3},{3,2},{16,18},{17,19},{18,16},{19,17},{4,5},{5,4... | collective-permute-start | bytes 811016 | tf_op jit(solution)/shard_map/ppermute | solution.py:530
  11.5 1.5 %collective-permute-start.4 = (bf16[1056,128]{1,0:T(8,128)(2,1)}, bf16[1056,128]{1,0:T(8,128)(2,1)S(1)}, u32[]{:S(2)}, u32[]{:S(2)}) collective-permute-start(bf16[1056,128]{1,0:T(8,128)(2,1)} %get-tuple-element.30), channel_id=1, source_target_pairs={{0,2},{1,3},{2,0},{3,1},{16,17},{17,16},{18,19},{19,18},{4,6},{5,7... | collective-permute-start | bytes 811016 | tf_op jit(solution)/shard_map/ppermute | solution.py:530
  13.0 0.0 collective-permute-done.refs_1_
  13.0 0.0 collective-permute-start.5
  13.0 4.8 %collective-permute-done.1.refs_2_ = bf16[1056,128]{1,0:T(8,128)(2,1)S(1)} collective-permute-done((bf16[1056,128]{1,0:T(8,128)(2,1)}, bf16[1056,128]{1,0:T(8,128)(2,1)S(1)}, u32[]{:S(2)}, u32[]{:S(2)}) %collective-permute-start.1) | collective-permute-done | bytes 270368 | tf_op jit(solution)/shard_map/ppermute | solution.py:530
  17.8 0.3 collective-permute-start.6
  18.1 0.0 copy-done.1
  18.1 0.0 copy-start
  18.1 1.0 %copy-done = bf16[1056,128]{1,0:T(8,128)(2,1)S(1)} copy-done((bf16[1056,128]{1,0:T(8,128)(2,1)S(1)}, bf16[1056,128]{1,0:T(8,128)(2,1)}, u32[]{:S(2)}) %copy-start) | copy-done | bytes 270360
  19.0 0.8 %matrices.1 = (bf16[2,512,512]{2,1,0:T(8,128)(2,1)S(1)}, bf16[2,128,128]{2,1,0:T(8,128)(2,1)S(1)}, bf16[2,64,64]{2,1,0:T(8,128)(2,1)S(1)}, bf16[1056,128]{1,0:T(8,128)(2,1)S(1)}) custom-call(f32[2,41]{1,0:T(2,128)S(1)} %copy-done.1, bf16[1056,128]{1,0:T(8,128)(2,1)S(1)} %copy-done), custom_call_target="tpu_custom_call" | custom-call | bytes 8388608 | tf_op jit(solution)/shard_map/matrices/pallas_call | solution.py:543
  19.8 2.9 %collective-permute-done.2.refs_3_ = bf16[1056,128]{1,0:T(8,128)(2,1)S(1)} collective-permute-done((bf16[1056,128]{1,0:T(8,128)(2,1)}, bf16[1056,128]{1,0:T(8,128)(2,1)S(1)}, u32[]{:S(2)}, u32[]{:S(2)}) %collective-permute-start.2) | collective-permute-done | bytes 270368 | tf_op jit(solution)/shard_map/ppermute | solution.py:530
  22.7 6.7 %collective-permute-done.3.refs_4_ = bf16[1056,128]{1,0:T(8,128)(2,1)S(1)} collective-permute-done((bf16[1056,128]{1,0:T(8,128)(2,1)}, bf16[1056,128]{1,0:T(8,128)(2,1)S(1)}, u32[]{:S(2)}, u32[]{:S(2)}) %collective-permute-start.3) | collective-permute-done | bytes 270368 | tf_op jit(solution)/shard_map/ppermute | solution.py:530
  29.4 0.0 collective-permute-done.4.refs_5_
  29.4 5.2 %collective-permute-done.5.refs_6_ = bf16[1056,128]{1,0:T(8,128)(2,1)S(1)} collective-permute-done((bf16[1056,128]{1,0:T(8,128)(2,1)}, bf16[1056,128]{1,0:T(8,128)(2,1)S(1)}, u32[]{:S(2)}, u32[]{:S(2)}) %collective-permute-start.5) | collective-permute-done | bytes 270368 | tf_op jit(solution)/shard_map/ppermute | solution.py:530
  34.5 0.0 collective-permute-done.6.refs_7_
  34.6 0.7 %edge_sums.1 = (bf16[272,128]{1,0:T(8,128)(2,1)S(1)}, bf16[272,128]{1,0:T(8,128)(2,1)S(1)}, bf16[272,128]{1,0:T(8,128)(2,1)S(1)}, bf16[272,128]{1,0:T(8,128)(2,1)S(1)}) custom-call(bf16[1056,128]{1,0:T(8,128)(2,1)S(1)} %get-tuple-element.25.refs_0_, bf16[1056,128]{1,0:T(8,128)(2,1)S(1)} %collective-permute-done.refs_1_, ...), custom_call_target="tpu_custom_call" | custom-call | bytes 4194304 | tf_op jit(solution)/shard_map/edge_sums/pallas_call | solution.py:560
  35.2 1.7 %collective-permute-start.7 = (bf16[272,128]{1,0:T(8,128)(2,1)S(1)}, bf16[272,128]{1,0:T(8,128)(2,1)S(1)}, u32[]{:S(2)}, u32[]{:S(2)}) collective-permute-start(bf16[272,128]{1,0:T(8,128)(2,1)S(1)} %get-tuple-element.34), channel_id=1, source_target_pairs={{0,4},{1,5},{2,6},{3,7},{4,0},{5,1},{6,2},{7,3},{8,12},{9,13},{10,... | collective-permute-start | bytes 208904 | tf_op jit(solution)/shard_map/ppermute | solution.py:537
  36.9 0.3 collective-permute-start.8
  37.2 1.6 %collective-permute-start.9 = (bf16[272,128]{1,0:T(8,128)(2,1)S(1)}, bf16[272,128]{1,0:T(8,128)(2,1)S(1)}, u32[]{:S(2)}, u32[]{:S(2)}) collective-permute-start(bf16[272,128]{1,0:T(8,128)(2,1)S(1)} %get-tuple-element.36), channel_id=1, source_target_pairs={{0,12},{1,13},{2,14},{3,15},{4,8},{5,9},{6,10},{7,11},{8,4},{9,5},... | collective-permute-start | bytes 208904 | tf_op jit(solution)/shard_map/ppermute | solution.py:537
  38.8 0.6 %inner_sums.1 = (bf16[256,128]{1,0:T(8,128)(2,1)S(1)}, bf16[256,128]{1,0:T(8,128)(2,1)S(1)}, bf16[256,128]{1,0:T(8,128)(2,1)S(1)}, bf16[256,128]{1,0:T(8,128)(2,1)S(1)}) custom-call(bf16[1056,128]{1,0:T(8,128)(2,1)S(1)} %get-tuple-element.25.refs_0_, bf16[1056,128]{1,0:T(8,128)(2,1)S(1)} %collective-permute-done.refs_1_, ...), custom_call_target="tpu_custom_call" | custom-call | bytes 4194304 | tf_op jit(solution)/shard_map/inner_sums/pallas_call | solution.py:560
  39.4 2.6 %collective-permute-start.10 = (bf16[256,128]{1,0:T(8,128)(2,1)S(1)}, bf16[256,128]{1,0:T(8,128)(2,1)S(1)}, u32[]{:S(2)}, u32[]{:S(2)}) collective-permute-start(bf16[256,128]{1,0:T(8,128)(2,1)S(1)} %get-tuple-element.38), channel_id=1, source_target_pairs={{0,4},{1,5},{2,6},{3,7},{4,0},{5,1},{6,2},{7,3},{8,12},{9,13},{10,... | collective-permute-start | bytes 196616 | tf_op jit(solution)/shard_map/ppermute | solution.py:537
  42.0 0.0 collective-permute-start.11
  42.0 0.0 collective-permute-done.7.refs_1_
  42.0 1.5 %collective-permute-start.12 = (bf16[256,128]{1,0:T(8,128)(2,1)S(1)}, bf16[256,128]{1,0:T(8,128)(2,1)S(1)}, u32[]{:S(2)}, u32[]{:S(2)}) collective-permute-start(bf16[256,128]{1,0:T(8,128)(2,1)S(1)} %get-tuple-element.40), channel_id=1, source_target_pairs={{0,12},{1,13},{2,14},{3,15},{4,8},{5,9},{6,10},{7,11},{8,4},{9,5},... | collective-permute-start | bytes 196616 | tf_op jit(solution)/shard_map/ppermute | solution.py:537
  43.5 0.0 collective-permute-done.8.refs_2_
  43.5 4.9 %collective-permute-done.9.refs_3_ = bf16[272,128]{1,0:T(8,128)(2,1)S(1)} collective-permute-done((bf16[272,128]{1,0:T(8,128)(2,1)S(1)}, bf16[272,128]{1,0:T(8,128)(2,1)S(1)}, u32[]{:S(2)}, u32[]{:S(2)}) %collective-permute-start.9) | collective-permute-done | bytes 69664 | tf_op jit(solution)/shard_map/ppermute | solution.py:537
  48.4 0.1 edge_rows.1
  48.5 1.6 %collective-permute-start.13 = (bf16[32,512]{1,0:T(8,128)(2,1)S(1)}, bf16[32,512]{1,0:T(8,128)(2,1)S(1)}, u32[]{:S(2)}, u32[]{:S(2)}) collective-permute-start(bf16[32,512]{1,0:T(8,128)(2,1)S(1)} %get-tuple-element.41), channel_id=1, source_target_pairs={{0,1},{2,3},{4,5},{6,7},{8,9},{10,11},{12,13},{14,15},{16,17},{18,... | collective-permute-start | bytes 98312 | tf_op jit(solution)/shard_map/ppermute | solution.py:589
  50.0 2.5 %collective-permute-start.14 = (bf16[32,512]{1,0:T(8,128)(2,1)S(1)}, bf16[32,512]{1,0:T(8,128)(2,1)S(1)}, u32[]{:S(2)}, u32[]{:S(2)}) collective-permute-start(bf16[32,512]{1,0:T(8,128)(2,1)S(1)} %get-tuple-element.42), channel_id=1, source_target_pairs={{1,2},{3,4},{5,6},{7,8},{9,10},{11,12},{13,14},{15,16},{17,18},{19... | collective-permute-start | bytes 98312 | tf_op jit(solution)/shard_map/ppermute | solution.py:589
  52.5 0.0 collective-permute-done.10.refs_5_
  52.5 0.0 collective-permute-done.11.refs_6_
  52.6 0.0 collective-permute-done.12.refs_7_
  52.6 0.0 collective-permute-done.13.refs_8_
  52.6 5.0 %collective-permute-done.14.refs_9_ = bf16[32,512]{1,0:T(8,128)(2,1)S(1)} collective-permute-done((bf16[32,512]{1,0:T(8,128)(2,1)S(1)}, bf16[32,512]{1,0:T(8,128)(2,1)S(1)}, u32[]{:S(2)}, u32[]{:S(2)}) %collective-permute-start.14) | collective-permute-done | bytes 32800 | tf_op jit(solution)/shard_map/ppermute | solution.py:589
  57.6 1.4 %coadd_detect.1 = (f32[128,512]{1,0:T(8,128)}, f32[128,512]{1,0:T(8,128)}) custom-call(bf16[272,128]{1,0:T(8,128)(2,1)S(1)} %get-tuple-element.33.refs_0_, bf16[272,128]{1,0:T(8,128)(2,1)S(1)} %collective-permute-done.7.refs_1_, bf16[272,128]{1,0:T(8,128)(2,1)S(1)} %collective-permute-done.8.refs_2_, bf16[272,128]{1,0:T(8,128)(2,1)S(1)} %collective-permute-done.9.refs_3_, ...), custom_call_target="tpu_custom_call" | custom-call | tf_op jit(solution)/shard_map/coadd_detect/pallas_call | solution.py:593
Async XLA Ops:
  0.6 17.5 %copy-start.1 = (f32[2,41]{1,0:T(2,128)S(1)}, f32[2,41]{1,0:T(2,128)}, u32[]{:S(2)}) copy-start(f32[2,41]{1,0:T(2,128)} %taps_ref.1) | copy-start | bytes 988
  7.2 5.8 %collective-permute-start = (bf16[1056,128]{1,0:T(8,128)(2,1)}, bf16[1056,128]{1,0:T(8,128)(2,1)S(1)}, u32[]{:S(2)}, u32[]{:S(2)}) collective-permute-start(bf16[1056,128]{1,0:T(8,128)(2,1)} %get-tuple-element.26), channel_id=1, source_target_pairs={{0,16},{1,17},{2,18},{3,19},{16,0},{17,1},{18,2},{19,3},{4,20},{5,... | collective-permute-start | bytes 811016 | tf_op jit(solution)/shard_map/ppermute | solution.py:530
  7.3 10.6 %collective-permute-start.1 = (bf16[1056,128]{1,0:T(8,128)(2,1)}, bf16[1056,128]{1,0:T(8,128)(2,1)S(1)}, u32[]{:S(2)}, u32[]{:S(2)}) collective-permute-start(bf16[1056,128]{1,0:T(8,128)(2,1)} %get-tuple-element.27), channel_id=1, source_target_pairs={{0,3},{1,2},{2,1},{3,0},{16,19},{17,18},{18,17},{19,16},{4,7},{5,6... | collective-permute-start | bytes 811016 | tf_op jit(solution)/shard_map/ppermute | solution.py:530
  9.8 13.0 %collective-permute-start.2 = (bf16[1056,128]{1,0:T(8,128)(2,1)}, bf16[1056,128]{1,0:T(8,128)(2,1)S(1)}, u32[]{:S(2)}, u32[]{:S(2)}) collective-permute-start(bf16[1056,128]{1,0:T(8,128)(2,1)} %get-tuple-element.28), channel_id=1, source_target_pairs={{0,19},{1,18},{2,17},{3,16},{16,3},{17,2},{18,1},{19,0},{4,23},{5,... | collective-permute-start | bytes 811016 | tf_op jit(solution)/shard_map/ppermute | solution.py:530
  10.0 19.4 %collective-permute-start.3 = (bf16[1056,128]{1,0:T(8,128)(2,1)}, bf16[1056,128]{1,0:T(8,128)(2,1)S(1)}, u32[]{:S(2)}, u32[]{:S(2)}) collective-permute-start(bf16[1056,128]{1,0:T(8,128)(2,1)} %get-tuple-element.29), channel_id=1, source_target_pairs={{0,1},{1,0},{2,3},{3,2},{16,18},{17,19},{18,16},{19,17},{4,5},{5,4... | collective-permute-start | bytes 811016 | tf_op jit(solution)/shard_map/ppermute | solution.py:530
  11.5 17.9 %collective-permute-start.4 = (bf16[1056,128]{1,0:T(8,128)(2,1)}, bf16[1056,128]{1,0:T(8,128)(2,1)S(1)}, u32[]{:S(2)}, u32[]{:S(2)}) collective-permute-start(bf16[1056,128]{1,0:T(8,128)(2,1)} %get-tuple-element.30), channel_id=1, source_target_pairs={{0,2},{1,3},{2,0},{3,1},{16,17},{17,16},{18,19},{19,18},{4,6},{5,7... | collective-permute-start | bytes 811016 | tf_op jit(solution)/shard_map/ppermute | solution.py:530
  13.0 21.5 %collective-permute-start.5 = (bf16[1056,128]{1,0:T(8,128)(2,1)}, bf16[1056,128]{1,0:T(8,128)(2,1)S(1)}, u32[]{:S(2)}, u32[]{:S(2)}) collective-permute-start(bf16[1056,128]{1,0:T(8,128)(2,1)} %get-tuple-element.31), channel_id=1, source_target_pairs={{0,17},{1,16},{2,19},{3,18},{16,2},{17,3},{18,0},{19,1},{4,21},{5,... | collective-permute-start | bytes 811016 | tf_op jit(solution)/shard_map/ppermute | solution.py:530
  17.8 16.7 %collective-permute-start.6 = (bf16[1056,128]{1,0:T(8,128)(2,1)}, bf16[1056,128]{1,0:T(8,128)(2,1)S(1)}, u32[]{:S(2)}, u32[]{:S(2)}) collective-permute-start(bf16[1056,128]{1,0:T(8,128)(2,1)} %get-tuple-element.32), channel_id=1, source_target_pairs={{0,18},{1,19},{2,16},{3,17},{16,1},{17,0},{18,3},{19,2},{4,22},{5,... | collective-permute-start | bytes 811016 | tf_op jit(solution)/shard_map/ppermute | solution.py:530
  18.1 1.0 %copy-start = (bf16[1056,128]{1,0:T(8,128)(2,1)S(1)}, bf16[1056,128]{1,0:T(8,128)(2,1)}, u32[]{:S(2)}) copy-start(bf16[1056,128]{1,0:T(8,128)(2,1)} %get-tuple-element.24.own_hbm) | copy-start | bytes 811012
  35.2 6.7 %collective-permute-start.7 = (bf16[272,128]{1,0:T(8,128)(2,1)S(1)}, bf16[272,128]{1,0:T(8,128)(2,1)S(1)}, u32[]{:S(2)}, u32[]{:S(2)}) collective-permute-start(bf16[272,128]{1,0:T(8,128)(2,1)S(1)} %get-tuple-element.34), channel_id=1, source_target_pairs={{0,4},{1,5},{2,6},{3,7},{4,0},{5,1},{6,2},{7,3},{8,12},{9,13},{10,... | collective-permute-start | bytes 208904 | tf_op jit(solution)/shard_map/ppermute | solution.py:537
  36.9 6.6 %collective-permute-start.8 = (bf16[272,128]{1,0:T(8,128)(2,1)S(1)}, bf16[272,128]{1,0:T(8,128)(2,1)S(1)}, u32[]{:S(2)}, u32[]{:S(2)}) collective-permute-start(bf16[272,128]{1,0:T(8,128)(2,1)S(1)} %get-tuple-element.35), channel_id=1, source_target_pairs={{0,8},{1,9},{2,10},{3,11},{4,12},{5,13},{6,14},{7,15},{8,0},{9,1},... | collective-permute-start | bytes 208904 | tf_op jit(solution)/shard_map/ppermute | solution.py:537
  37.2 11.2 %collective-permute-start.9 = (bf16[272,128]{1,0:T(8,128)(2,1)S(1)}, bf16[272,128]{1,0:T(8,128)(2,1)S(1)}, u32[]{:S(2)}, u32[]{:S(2)}) collective-permute-start(bf16[272,128]{1,0:T(8,128)(2,1)S(1)} %get-tuple-element.36), channel_id=1, source_target_pairs={{0,12},{1,13},{2,14},{3,15},{4,8},{5,9},{6,10},{7,11},{8,4},{9,5},... | collective-permute-start | bytes 208904 | tf_op jit(solution)/shard_map/ppermute | solution.py:537
  39.4 13.1 %collective-permute-start.10 = (bf16[256,128]{1,0:T(8,128)(2,1)S(1)}, bf16[256,128]{1,0:T(8,128)(2,1)S(1)}, u32[]{:S(2)}, u32[]{:S(2)}) collective-permute-start(bf16[256,128]{1,0:T(8,128)(2,1)S(1)} %get-tuple-element.38), channel_id=1, source_target_pairs={{0,4},{1,5},{2,6},{3,7},{4,0},{5,1},{6,2},{7,3},{8,12},{9,13},{10,... | collective-permute-start | bytes 196616 | tf_op jit(solution)/shard_map/ppermute | solution.py:537
  42.0 10.6 %collective-permute-start.11 = (bf16[256,128]{1,0:T(8,128)(2,1)S(1)}, bf16[256,128]{1,0:T(8,128)(2,1)S(1)}, u32[]{:S(2)}, u32[]{:S(2)}) collective-permute-start(bf16[256,128]{1,0:T(8,128)(2,1)S(1)} %get-tuple-element.39), channel_id=1, source_target_pairs={{0,8},{1,9},{2,10},{3,11},{4,12},{5,13},{6,14},{7,15},{8,0},{9,1},... | collective-permute-start | bytes 196616 | tf_op jit(solution)/shard_map/ppermute | solution.py:537
  42.0 10.6 %collective-permute-start.12 = (bf16[256,128]{1,0:T(8,128)(2,1)S(1)}, bf16[256,128]{1,0:T(8,128)(2,1)S(1)}, u32[]{:S(2)}, u32[]{:S(2)}) collective-permute-start(bf16[256,128]{1,0:T(8,128)(2,1)S(1)} %get-tuple-element.40), channel_id=1, source_target_pairs={{0,12},{1,13},{2,14},{3,15},{4,8},{5,9},{6,10},{7,11},{8,4},{9,5},... | collective-permute-start | bytes 196616 | tf_op jit(solution)/shard_map/ppermute | solution.py:537
  48.5 4.1 %collective-permute-start.13 = (bf16[32,512]{1,0:T(8,128)(2,1)S(1)}, bf16[32,512]{1,0:T(8,128)(2,1)S(1)}, u32[]{:S(2)}, u32[]{:S(2)}) collective-permute-start(bf16[32,512]{1,0:T(8,128)(2,1)S(1)} %get-tuple-element.41), channel_id=1, source_target_pairs={{0,1},{2,3},{4,5},{6,7},{8,9},{10,11},{12,13},{14,15},{16,17},{18,... | collective-permute-start | bytes 98312 | tf_op jit(solution)/shard_map/ppermute | solution.py:589
  50.0 7.6 %collective-permute-start.14 = (bf16[32,512]{1,0:T(8,128)(2,1)S(1)}, bf16[32,512]{1,0:T(8,128)(2,1)S(1)}, u32[]{:S(2)}, u32[]{:S(2)}) collective-permute-start(bf16[32,512]{1,0:T(8,128)(2,1)S(1)} %get-tuple-element.42), channel_id=1, source_target_pairs={{1,2},{3,4},{5,6},{7,8},{9,10},{11,12},{13,14},{15,16},{17,18},{19... | collective-permute-start | bytes 98312 | tf_op jit(solution)/shard_map/ppermute | solution.py:589

commit v8 on v7

--- a/solution.py
+++ b/solution.py
@@ -14,6 +14,9 @@
 PATCH_DEV = 4
 HALO = 32
 FIELDS = 4
+TIED = 2
+TAIL = 2
+PART = SIDE // 2
 VMEM_LIMIT = 48 * 1024 * 1024
 
 
@@ -85,7 +88,7 @@
     *rest,
 ):
     nz, pn, ns = split
-    outs, rest = rest[: ns * pn], rest[ns * pn :]
+    outs, rest = rest[: 2 * ns * pn], rest[2 * ns * pn :]
     warp_body(
         split,
         (
@@ -152,7 +155,8 @@
     terms, tap_count = taps_ref.shape[1], taps_ref.shape[3]
     half = tap_count // 2
     per_dest = nz * CAP
-    data_rows = per_dest * SIDE
+    data_rows = per_dest * PART
+    edge_rows = data_rows + FIELDS * per_dest
 
     small = [
         pltpu.make_async_copy(src, dst, small_sem.at[i])
@@ -291,17 +295,23 @@
                 apart = z ^ my_z
                 later = jnp.where(apart > 1, apart - 1, apart * (nz - 1))
                 at = jnp.where(sec == 0, apart, later) * CAP + rank
-                out_ref[dest, pl.ds(pl.multiple_of(at * SIDE, SIDE), SIDE), :] = left_ref[
-                    visit, pl.ds(i * SIDE, SIDE), pl.ds(j * SIDE, SIDE)
-                ]
+                first = pl.multiple_of(at * PART, PART)
+                columns = pl.ds(j * SIDE, SIDE)
+                for target, source, count in (
+                    (first, 0, HALO),
+                    (first + HALO, SIDE - HALO, HALO),
+                    (first + edge_rows, HALO, SIDE - 2 * HALO),
+                ):
+                    out_ref[dest, pl.ds(target, count), :] = left_ref[
+                        visit, pl.ds(i * SIDE + source, count), columns
+                    ]
                 line = pl.ds(dest * per_dest + at, 1)
                 slot_rows[line, :] = jnp.full((1, SIDE), patch_ref[block].astype(jnp.float32))
                 weight_rows[line, :] = jnp.full((1, SIDE), table_ref[index_ref[block]])
 
-    def out_copy(dest):
-        return pltpu.make_async_copy(out_ref.at[dest], outs[dest], out_sem.at[dest])
-
-    for dest in range(out_ref.shape[0]):
+    group = out_ref.shape[0]
+    copies = []
+    for dest in range(group):
         part = pl.ds(dest * per_dest, per_dest)
         fields = jnp.concatenate(
             [slot_rows[part, :]]
@@ -309,18 +319,38 @@
             axis=0,
         )
         out_ref[dest, pl.ds(data_rows, fields.shape[0]), :] = fields.astype(jnp.bfloat16)
-        out_copy(dest).start()
-    for dest in range(out_ref.shape[0]):
-        out_copy(dest).wait()
-
-
-def sum_kernel(nz, sources, chunks, *refs):
+    for i, rows_of in enumerate((pl.ds(0, edge_rows), pl.ds(edge_rows, data_rows))):
+        for dest in range(group):
+            copies.append(
+                pltpu.make_async_copy(
+                    out_ref.at[dest, rows_of], outs[i * group + dest], out_sem.at[i, dest]
+                )
+            )
+            copies[-1].start()
+    for copy in copies:
+        copy.wait()
+
+
+def add_blocks(nz, ins, weight_ref, outs):
+    for z in range(nz):
+        for place in range(PART // HALO):
+            sums = [jnp.zeros((HALO, SIDE), jnp.float32) for _ in range(PATCH_DEV)]
+            for g, ref in enumerate(ins):
+                for r in range(CAP):
+                    at = z * CAP + r
+                    value = ref[pl.ds(at * PART + place * HALO, HALO), :].astype(jnp.float32)
+                    for j in range(PATCH_DEV):
+                        sums[j] = sums[j] + weight_ref[g, j, pl.ds(at, 1), :] * value
+            for j in range(PATCH_DEV):
+                row = j * PART + place * HALO
+                outs[z][pl.ds(row, HALO), :] = sums[j].astype(jnp.bfloat16)
+
+
+def edge_sum_kernel(nz, sources, *refs):
     ins, outs, weight_ref = refs[:sources], refs[sources:-1], refs[-1]
     per_dest = nz * CAP
-    data_rows = per_dest * SIDE
-    with_totals = chunks[0] == 0
     for g in range(sources):
-        fields = ins[g][pl.ds(data_rows, FIELDS * per_dest), :].astype(jnp.float32)
+        fields = ins[g][pl.ds(per_dest * PART, FIELDS * per_dest), :].astype(jnp.float32)
         slot = fields[:per_dest]
         weight = (
             fields[per_dest : 2 * per_dest]
@@ -329,31 +359,24 @@
         )
         for j in range(PATCH_DEV):
             weight_ref[g, j] = jnp.where(slot == float(j), weight, 0.0)
+    add_blocks(nz, ins, weight_ref, outs)
     for z in range(nz):
-        for place, c in enumerate(chunks):
-            sums = [jnp.zeros((HALO, SIDE), jnp.float32) for _ in range(PATCH_DEV)]
+        totals = []
+        for j in range(PATCH_DEV):
+            total = jnp.zeros((1, SIDE), jnp.float32)
             for g in range(sources):
                 for r in range(CAP):
-                    at = z * CAP + r
-                    value = ins[g][pl.ds(at * SIDE + c * HALO, HALO), :].astype(jnp.float32)
-                    for j in range(PATCH_DEV):
-                        sums[j] = sums[j] + weight_ref[g, j, pl.ds(at, 1), :] * value
-            for j in range(PATCH_DEV):
-                row = (j * len(chunks) + place) * HALO
-                outs[z][pl.ds(row, HALO), :] = sums[j].astype(jnp.bfloat16)
-        if with_totals:
-            totals = []
-            for j in range(PATCH_DEV):
-                total = jnp.zeros((1, SIDE), jnp.float32)
-                for g in range(sources):
-                    for r in range(CAP):
-                        total = total + weight_ref[g, j, pl.ds(z * CAP + r, 1), :]
-                totals.append(total)
-            parts = [q.astype(jnp.float32) for q in three_parts(jnp.concatenate(totals, axis=0))]
-            parts.append(jnp.zeros((PATCH_DEV, SIDE), jnp.float32))
-            outs[z][pl.ds(PATCH_DEV * len(chunks) * HALO, FIELDS * PATCH_DEV), :] = (
-                jnp.concatenate(parts, axis=0).astype(jnp.bfloat16)
-            )
+                    total = total + weight_ref[g, j, pl.ds(z * CAP + r, 1), :]
+            totals.append(total)
+        parts = [q.astype(jnp.float32) for q in three_parts(jnp.concatenate(totals, axis=0))]
+        parts.append(jnp.zeros((PATCH_DEV, SIDE), jnp.float32))
+        outs[z][pl.ds(PATCH_DEV * PART, FIELDS * PATCH_DEV), :] = jnp.concatenate(
+            parts, axis=0
+        ).astype(jnp.bfloat16)
+
+
+def inner_sum_kernel(nz, sources, weight_ref, *refs):
+    add_blocks(nz, refs[:sources], weight_ref, refs[sources:])
 
 
 def totals_of(ins, start):
@@ -413,9 +436,14 @@
     out_ref[...] = dot_parts(along, across_ref)
 
 
-def prepare_kernel(taps_ref, own_hbm, across_ref, centre_ref, edge_ref, own_ref, band_ref, own_sem):
-    own_copy = pltpu.make_async_copy(own_hbm, own_ref, own_sem)
-    own_copy.start()
+def prepare_kernel(taps_ref, *refs):
+    owns_hbm, (across_ref, centre_ref, edge_ref), owns = refs[:2], refs[2:5], refs[5:7]
+    band_ref, own_sem = refs[7:]
+    own_copies = [
+        pltpu.make_async_copy(owns_hbm[i], owns[i], own_sem.at[i]) for i in range(len(owns))
+    ]
+    for copy in own_copies:
+        copy.start()
     tap_count = taps_ref.shape[1]
     half = tap_count // 2
     across = tap_row(lambda k: taps_ref[1, k], tap_count, SIDE - half, 3 * SIDE, True)
@@ -435,7 +463,8 @@
         ),
     )
     edge_ref[0], edge_ref[1] = two_parts(edge[:, : 2 * HALO])
-    own_copy.wait()
+    for copy in own_copies:
+        copy.wait()
 
 
 def dot_parts(left, across_ref):
@@ -466,7 +495,8 @@
     blocks = owner_of.shape[0]
     terms = psf_taps.shape[1]
     per_dest = nz * CAP
-    payload = per_dest * (SIDE + FIELDS)
+    inner_rows = per_dest * PART
+    edge_rows = inner_rows + FIELDS * per_dest
     width = PATCH_DEV * SIDE
     smem = pl.BlockSpec(memory_space=pltpu.SMEM)
     vmem = pl.BlockSpec(memory_space=pltpu.VMEM)
@@ -479,9 +509,10 @@
     weights = term_weights.transpose(1, 2, 0)
     send = pl.pallas_call(
         functools.partial(warp_kernel, split),
-        out_shape=[shaped((payload, SIDE), jnp.bfloat16)] * group,
+        out_shape=[shaped((edge_rows, SIDE), jnp.bfloat16)] * group
+        + [shaped((inner_rows, SIDE), jnp.bfloat16)] * group,
         in_specs=[hbm] * 11,
-        out_specs=[hbm] * group,
+        out_specs=[hbm] * (2 * group),
         scratch_shapes=[
             pltpu.SMEM((blocks,), jnp.int32),
             pltpu.SMEM((blocks,), jnp.int32),
@@ -503,8 +534,8 @@
             pltpu.SemaphoreType.DMA((9,)),
             pltpu.SemaphoreType.DMA,
             pltpu.SemaphoreType.DMA((visits,)),
-            pltpu.VMEM((group, payload, SIDE), jnp.bfloat16),
-            pltpu.SemaphoreType.DMA((group,)),
+            pltpu.VMEM((group, edge_rows + inner_rows, SIDE), jnp.bfloat16),
+            pltpu.SemaphoreType.DMA((2, group)),
         ],
         compiler_params=pltpu.CompilerParams(vmem_limit_bytes=60 * 1024 * 1024),
         name="warp",
@@ -538,41 +569,51 @@
 
     every = ("sec", "z", "p")
     peers = sorted(range(1, group), key=lambda k: (k != pn, -bin(k % pn).count("1"), k))
-    arrived = [in_plane(send[k], k) for k in peers]
-
-    across, centre, edge, own = pl.pallas_call(
+    edge_blocks = [in_plane(send[k], k) for k in peers]
+
+    across, centre, edge, own_edge, own_inner = pl.pallas_call(
         prepare_kernel,
         out_shape=(
             shaped((2, width, width), jnp.bfloat16),
             shaped((2, SIDE, SIDE), jnp.bfloat16),
             shaped((2, 2 * HALO, 2 * HALO), jnp.bfloat16),
-            shaped((payload, SIDE), jnp.bfloat16),
+            shaped((edge_rows, SIDE), jnp.bfloat16),
+            shaped((inner_rows, SIDE), jnp.bfloat16),
         ),
-        in_specs=[smem, hbm],
-        out_specs=(vmem,) * 4,
-        scratch_shapes=[pltpu.VMEM((width, width), jnp.float32), pltpu.SemaphoreType.DMA],
+        in_specs=[smem, hbm, hbm],
+        out_specs=(vmem,) * 5,
+        scratch_shapes=[pltpu.VMEM((width, width), jnp.float32), pltpu.SemaphoreType.DMA((2,))],
         compiler_params=params,
         cost_estimate=pl.CostEstimate(flops=0, bytes_accessed=8 << 20, transcendentals=0),
         name="matrices",
-    )(detect_taps, send[0])
-
-    def plane_sums(chunks, rows, name):
-        return pl.pallas_call(
-            functools.partial(sum_kernel, nz, group, chunks),
-            out_shape=[shaped((rows, SIDE), jnp.bfloat16)] * nz,
-            in_specs=[vmem] * group,
-            out_specs=[vmem] * nz,
-            scratch_shapes=[pltpu.VMEM((group, PATCH_DEV, per_dest, SIDE), jnp.float32)],
-            compiler_params=params,
-            cost_estimate=pl.CostEstimate(flops=0, bytes_accessed=4 << 20, transcendentals=0),
-            name=name,
-        )(own, *arrived)
-
-    last = SIDE // HALO - 1
-    edge_rows = PATCH_DEV * (2 * HALO + FIELDS)
-    edge_sums = plane_sums((0, last), edge_rows, "edge_sums")
-    inner_sums = plane_sums(tuple(range(1, last)), PATCH_DEV * (SIDE - 2 * HALO), "inner_sums")
+    )(detect_taps, send[0], send[group])
+
+    busy = pl.CostEstimate(flops=0, bytes_accessed=4 << 20, transcendentals=0)
+    edge_sums = list(pl.pallas_call(
+        functools.partial(edge_sum_kernel, nz, group),
+        out_shape=[shaped((PATCH_DEV * (PART + FIELDS), SIDE), jnp.bfloat16)] * nz
+        + [shaped((group, PATCH_DEV, per_dest, SIDE), jnp.float32)],
+        in_specs=[vmem] * group,
+        out_specs=[vmem] * (nz + 1),
+        compiler_params=params,
+        cost_estimate=busy,
+        name="edge_sums",
+    )(own_edge, *edge_blocks))
     edges = [edge_sums[0]] + [along_z(edge_sums[d], d) for d in range(1, nz)]
+    count = 2
+    held = lax.optimization_barrier((edge_blocks[TIED], *(send[group + k] for k in peers[:-TAIL])))
+    kept = lax.optimization_barrier((*edges[1:3], *(send[group + k] for k in peers[-TAIL:])))
+    edges[1 : 1 + count], kept = kept[:count], kept[count:]
+    inner_blocks = [in_plane(part, k) for part, k in zip((*held[1:], *kept), peers)]
+    inner_sums = pl.pallas_call(
+        functools.partial(inner_sum_kernel, nz, group),
+        out_shape=[shaped((PATCH_DEV * PART, SIDE), jnp.bfloat16)] * nz,
+        in_specs=[vmem] * (group + 1),
+        out_specs=[vmem] * nz,
+        compiler_params=params,
+        cost_estimate=busy,
+        name="inner_sums",
+    )(edge_sums[nz], own_inner, *inner_blocks)
     inner = [inner_sums[0]] + [along_z(inner_sums[d], d) for d in range(1, nz)]
 
     first_rows, second_rows = pl.pallas_call(

time: 59.2 us -> 58.5 us (0.988)
  the two profiles are of different devices: /device:TPU:16 before, /device:TPU:1 now
where the time goes in v8:
time: 58.5 us; the launch traced here: 58.3 us
  starting transfers between devices  31.6 us (54%)
  waiting for transfers between devices  13.6 us (23%)
  Pallas kernels  10.5 us (18%)
  local copies, waits for them, and re-layouts  1.81 us (3%)
  between operations  0.73 us (1%)
    ppermute x14, starting transfers between devices, in_plane(): return lax.ppermute(part, ('sec', 'p'), pairs)  18 us
    ppermute x14, waiting for transfers between devices, in_plane(): return lax.ppermute(part, ('sec', 'p'), pairs)  10 us
    ppermute x2, starting transfers between devices, swap(): return lax.ppermute(rows, every, pairs + [(j, i) for i, j in pairs])  7.29 us
    pallas_call x1, Pallas kernels, per_device(): pl.pallas_call(functools.partial(warp_kernel, split), out_shape=[shaped((...  6.67 us
    ppermute x6, starting transfers between devices, along_z(): return lax.ppermute(part, every, pairs)  6.36 us
    ppermute x2, waiting for transfers between devices, swap(): return lax.ppermute(rows, every, pairs + [(j, i) for i, j in pairs])  1.83 us
    unnamed x6, local copies, waits for them, and re-layouts  1.81 us
    ppermute x6, waiting for transfers between devices, along_z(): return lax.ppermute(part, every, pairs)  1.76 us
  transfers between devices with their start and end apart: 22, of which 9 were waited for; matrix products, arithmetic and copies ran while one was open for 0% of the time, Pallas kernels for 4%

profile of v8, /device:TPU:1, one launch (start us, length us, event | category | flops | bytes accessed | tf_op | source)
XLA Modules:
  0.0 58.3 jit_solution(15586902469802789449)
XLA Ops:
  0.6 6.7 %warp.1 = (bf16[544,128]{1,0:T(8,128)(2,1)}, bf16[544,128]{1,0:T(8,128)(2,1)}, bf16[544,128]{1,0:T(8,128)(2,1)}, bf16[544,128]{1,0:T(8,128)(2,1)}, bf16[544,128]...) custom-call(s32[32]{0:T(128)} %bitcast.4, ...), custom_call_target="tpu_custom_call" | custom-call | tf_op jit(solution)/shard_map/warp/pallas_call | solution.py:510
  7.3 0.1 collective-permute-start
  7.4 3.6 %collective-permute-start.2 = (bf16[544,128]{1,0:T(8,128)(2,1)}, bf16[544,128]{1,0:T(8,128)(2,1)S(1)}, u32[]{:S(2)}, u32[]{:S(2)}) collective-permute-start(bf16[544,128]{1,0:T(8,128)(2,1)} %get-tuple-element.48), channel_id=1, source_target_pairs={{0,19},{1,18},{2,17},{3,16},{16,3},{17,2},{18,1},{19,0},{4,23},{5,... | collective-permute-start | bytes 417800 | tf_op jit(solution)/shard_map/ppermute | solution.py:561
  11.0 0.1 collective-permute-start.1
  11.1 1.4 %collective-permute-start.3 = (bf16[544,128]{1,0:T(8,128)(2,1)}, bf16[544,128]{1,0:T(8,128)(2,1)S(1)}, u32[]{:S(2)}, u32[]{:S(2)}) collective-permute-start(bf16[544,128]{1,0:T(8,128)(2,1)} %get-tuple-element.49), channel_id=1, source_target_pairs={{0,1},{1,0},{2,3},{3,2},{16,18},{17,19},{18,16},{19,17},{4,5},{5,4... | collective-permute-start | bytes 417800 | tf_op jit(solution)/shard_map/ppermute | solution.py:561
  12.5 1.2 %collective-permute-start.4 = (bf16[544,128]{1,0:T(8,128)(2,1)}, bf16[544,128]{1,0:T(8,128)(2,1)S(1)}, u32[]{:S(2)}, u32[]{:S(2)}) collective-permute-start(bf16[544,128]{1,0:T(8,128)(2,1)} %get-tuple-element.50), channel_id=1, source_target_pairs={{0,2},{1,3},{2,0},{3,1},{16,17},{17,16},{18,19},{19,18},{4,6},{5,7... | collective-permute-start | bytes 417800 | tf_op jit(solution)/shard_map/ppermute | solution.py:561
  13.7 0.0 collective-permute-done.refs_1_
  13.7 1.4 %collective-permute-start.5 = (bf16[544,128]{1,0:T(8,128)(2,1)}, bf16[544,128]{1,0:T(8,128)(2,1)S(1)}, u32[]{:S(2)}, u32[]{:S(2)}) collective-permute-start(bf16[544,128]{1,0:T(8,128)(2,1)} %get-tuple-element.51), channel_id=1, source_target_pairs={{0,17},{1,16},{2,19},{3,18},{16,2},{17,3},{18,0},{19,1},{4,21},{5,... | collective-permute-start | bytes 417800 | tf_op jit(solution)/shard_map/ppermute | solution.py:561
  15.1 0.5 collective-permute-done.2.refs_3_
  15.6 1.1 %collective-permute-start.6 = (bf16[544,128]{1,0:T(8,128)(2,1)}, bf16[544,128]{1,0:T(8,128)(2,1)S(1)}, u32[]{:S(2)}, u32[]{:S(2)}) collective-permute-start(bf16[544,128]{1,0:T(8,128)(2,1)} %get-tuple-element.52), channel_id=1, source_target_pairs={{0,18},{1,19},{2,16},{3,17},{16,1},{17,0},{18,3},{19,2},{4,22},{5,... | collective-permute-start | bytes 417800 | tf_op jit(solution)/shard_map/ppermute | solution.py:561
  16.7 1.6 %collective-permute-done.1.refs_2_ = bf16[544,128]{1,0:T(8,128)(2,1)S(1)} collective-permute-done((bf16[544,128]{1,0:T(8,128)(2,1)}, bf16[544,128]{1,0:T(8,128)(2,1)S(1)}, u32[]{:S(2)}, u32[]{:S(2)}) %collective-permute-start.1) | collective-permute-done | bytes 139296 | tf_op jit(solution)/shard_map/ppermute | solution.py:561
  18.3 0.9 %collective-permute-start.10 = (bf16[512,128]{1,0:T(8,128)(2,1)}, bf16[512,128]{1,0:T(8,128)(2,1)S(1)}, u32[]{:S(2)}, u32[]{:S(2)}) collective-permute-start(bf16[512,128]{1,0:T(8,128)(2,1)} %get-tuple-element.68), channel_id=1, source_target_pairs={{0,16},{1,17},{2,18},{3,19},{16,0},{17,1},{18,2},{19,3},{4,20},{5,... | collective-permute-start | bytes 393224 | tf_op jit(solution)/shard_map/ppermute | solution.py:561
  19.2 2.2 %collective-permute-done.3.refs_4_ = bf16[544,128]{1,0:T(8,128)(2,1)S(1)} collective-permute-done((bf16[544,128]{1,0:T(8,128)(2,1)}, bf16[544,128]{1,0:T(8,128)(2,1)S(1)}, u32[]{:S(2)}, u32[]{:S(2)}) %collective-permute-start.3) | collective-permute-done | bytes 139296 | tf_op jit(solution)/shard_map/ppermute | solution.py:561
  21.4 2.3 %collective-permute-start.11 = (bf16[512,128]{1,0:T(8,128)(2,1)}, bf16[512,128]{1,0:T(8,128)(2,1)S(1)}, u32[]{:S(2)}, u32[]{:S(2)}) collective-permute-start(bf16[512,128]{1,0:T(8,128)(2,1)} %get-tuple-element.69), channel_id=1, source_target_pairs={{0,3},{1,2},{2,1},{3,0},{16,19},{17,18},{18,17},{19,16},{4,7},{5,6... | collective-permute-start | bytes 393224 | tf_op jit(solution)/shard_map/ppermute | solution.py:561
  23.7 0.9 %copy-done = bf16[544,128]{1,0:T(8,128)(2,1)S(1)} copy-done((bf16[544,128]{1,0:T(8,128)(2,1)S(1)}, bf16[544,128]{1,0:T(8,128)(2,1)}, u32[]{:S(2)}) %copy-start) | copy-done | bytes 139288
  24.6 0.9 %copy-done.1 = bf16[512,128]{1,0:T(8,128)(2,1)S(1)} copy-done((bf16[512,128]{1,0:T(8,128)(2,1)S(1)}, bf16[512,128]{1,0:T(8,128)(2,1)}, u32[]{:S(2)}) %copy-start.1) | copy-done | bytes 131096
  25.5 1.1 %matrices.1 = (bf16[2,512,512]{2,1,0:T(8,128)(2,1)S(1)}, bf16[2,128,128]{2,1,0:T(8,128)(2,1)S(1)}, bf16[2,64,64]{2,1,0:T(8,128)(2,1)S(1)}, bf16[544,128]{1,0:T(8,128)(2,1)S(1)}, bf16[512,128]{1,0:T(8,128)(2,1)S(1)}) custom-call(f32[2,41]{1,0:T(2,128)S(1)} %copy-done.2, bf16[544,128]{1,0:T(8,128)(2,1)S(1)} %copy-done, bf16[512,128]{1,0:T(8,128)(2,1)S(1)} %copy-done.1), custom_call_target="tpu_custom_call" | custom-call | bytes 8388608 | tf_op jit(solution)/shard_map/matrices/pallas_call | solution.py:574
  26.6 0.0 collective-permute-done.5.refs_6_
  26.6 0.7 %edge_sums.1 = (bf16[272,128]{1,0:T(8,128)(2,1)S(1)}, bf16[272,128]{1,0:T(8,128)(2,1)S(1)}, bf16[272,128]{1,0:T(8,128)(2,1)S(1)}, bf16[272,128]{1,0:T(8,128)(2,1)S(1)}, f32[8,4,8,128]{3,2,1,0:T(8,128)S(1)}) custom-call(bf16[544,128]{1,0:T(8,128)(2,1)S(1)} %get-tuple-element.45.refs_0_, bf16[544,128]{1,0:T(8,128)(2,1)S(1)} %collective-permute-done.refs_1_, ...), custom_call_target="tpu_custom_call" | custom-call | bytes 4194304 | tf_op jit(solution)/shard_map/edge_sums/pallas_call | solution.py:592
  27.3 2.4 %collective-permute-start.7 = (bf16[272,128]{1,0:T(8,128)(2,1)S(1)}, bf16[272,128]{1,0:T(8,128)(2,1)S(1)}, u32[]{:S(2)}, u32[]{:S(2)}) collective-permute-start(bf16[272,128]{1,0:T(8,128)(2,1)S(1)} %get-tuple-element.54), channel_id=1, source_target_pairs={{0,4},{1,5},{2,6},{3,7},{4,0},{5,1},{6,2},{7,3},{8,12},{9,13},{10,... | collective-permute-start | bytes 208904 | tf_op jit(solution)/shard_map/ppermute | solution.py:568
  29.7 1.1 %collective-permute-start.8 = (bf16[272,128]{1,0:T(8,128)(2,1)S(1)}, bf16[272,128]{1,0:T(8,128)(2,1)S(1)}, u32[]{:S(2)}, u32[]{:S(2)}) collective-permute-start(bf16[272,128]{1,0:T(8,128)(2,1)S(1)} %get-tuple-element.55), channel_id=1, source_target_pairs={{0,8},{1,9},{2,10},{3,11},{4,12},{5,13},{6,14},{7,15},{8,0},{9,1},... | collective-permute-start | bytes 208904 | tf_op jit(solution)/shard_map/ppermute | solution.py:568
  30.8 2.3 %collective-permute-start.12 = (bf16[512,128]{1,0:T(8,128)(2,1)}, bf16[512,128]{1,0:T(8,128)(2,1)S(1)}, u32[]{:S(2)}, u32[]{:S(2)}) collective-permute-start(bf16[512,128]{1,0:T(8,128)(2,1)} %get-tuple-element.70), channel_id=1, source_target_pairs={{0,19},{1,18},{2,17},{3,16},{16,3},{17,2},{18,1},{19,0},{4,23},{5,... | collective-permute-start | bytes 393224 | tf_op jit(solution)/shard_map/ppermute | solution.py:561
  33.1 0.0 collective-permute-done.7.refs_1_
  33.1 0.2 collective-permute-start.13
  33.3 1.8 %collective-permute-done.8.refs_2_ = bf16[272,128]{1,0:T(8,128)(2,1)S(1)} collective-permute-done((bf16[272,128]{1,0:T(8,128)(2,1)S(1)}, bf16[272,128]{1,0:T(8,128)(2,1)S(1)}, u32[]{:S(2)}, u32[]{:S(2)}) %collective-permute-start.8) | collective-permute-done | bytes 69664 | tf_op jit(solution)/shard_map/ppermute | solution.py:568
  35.1 0.3 collective-permute-start.14
  35.3 0.0 collective-permute-done.10.refs_1_
  35.3 3.1 %collective-permute-start.15 = (bf16[512,128]{1,0:T(8,128)(2,1)}, bf16[512,128]{1,0:T(8,128)(2,1)S(1)}, u32[]{:S(2)}, u32[]{:S(2)}) collective-permute-start(bf16[512,128]{1,0:T(8,128)(2,1)} %get-tuple-element.73), channel_id=1, source_target_pairs={{0,17},{1,16},{2,19},{3,18},{16,2},{17,3},{18,0},{19,1},{4,21},{5,... | collective-permute-start | bytes 393224 | tf_op jit(solution)/shard_map/ppermute | solution.py:561
  38.4 0.0 collective-permute-done.11.refs_2_
  38.4 0.0 collective-permute-start.16
  38.4 0.2 collective-permute-start.9
  38.6 0.5 collective-permute-done.13.refs_4_
  39.1 1.4 %collective-permute-done.14.refs_5_ = bf16[512,128]{1,0:T(8,128)(2,1)S(1)} collective-permute-done((bf16[512,128]{1,0:T(8,128)(2,1)}, bf16[512,128]{1,0:T(8,128)(2,1)S(1)}, u32[]{:S(2)}, u32[]{:S(2)}) %collective-permute-start.14) | collective-permute-done | bytes 131104 | tf_op jit(solution)/shard_map/ppermute | solution.py:561
  40.5 1.8 %collective-permute-done.15.refs_6_ = bf16[512,128]{1,0:T(8,128)(2,1)S(1)} collective-permute-done((bf16[512,128]{1,0:T(8,128)(2,1)}, bf16[512,128]{1,0:T(8,128)(2,1)S(1)}, u32[]{:S(2)}, u32[]{:S(2)}) %collective-permute-start.15) | collective-permute-done | bytes 131104 | tf_op jit(solution)/shard_map/ppermute | solution.py:561
  42.2 2.1 %collective-permute-done.16.refs_7_ = bf16[512,128]{1,0:T(8,128)(2,1)S(1)} collective-permute-done((bf16[512,128]{1,0:T(8,128)(2,1)}, bf16[512,128]{1,0:T(8,128)(2,1)S(1)}, u32[]{:S(2)}, u32[]{:S(2)}) %collective-permute-start.16) | collective-permute-done | bytes 131104 | tf_op jit(solution)/shard_map/ppermute | solution.py:561
  44.4 0.6 %inner_sums.1 = (bf16[256,128]{1,0:T(8,128)(2,1)S(1)}, bf16[256,128]{1,0:T(8,128)(2,1)S(1)}, bf16[256,128]{1,0:T(8,128)(2,1)S(1)}, bf16[256,128]{1,0:T(8,128)(2,1)S(1)}) custom-call(f32[8,4,8,128]{3,2,1,0:T(8,128)S(1)} %get-tuple-element.61.weight_ref, bf16[512,128]{1,0:T(8,128)(2,1)S(1)} %get-tuple-element.62.refs_0_, ...), custom_call_target="tpu_custom_call" | custom-call | bytes 4194304 | tf_op jit(solution)/shard_map/inner_sums/pallas_call | solution.py:608
  45.0 0.2 collective-permute-start.17
  45.2 2.2 %collective-permute-start.18 = (bf16[256,128]{1,0:T(8,128)(2,1)S(1)}, bf16[256,128]{1,0:T(8,128)(2,1)S(1)}, u32[]{:S(2)}, u32[]{:S(2)}) collective-permute-start(bf16[256,128]{1,0:T(8,128)(2,1)S(1)} %get-tuple-element.77), channel_id=1, source_target_pairs={{0,8},{1,9},{2,10},{3,11},{4,12},{5,13},{6,14},{7,15},{8,0},{9,1},... | collective-permute-start | bytes 196616 | tf_op jit(solution)/shard_map/ppermute | solution.py:568
  47.4 0.4 collective-permute-start.19
  47.7 0.1 edge_rows.1
  47.8 0.3 collective-permute-start.20
  48.1 7.0 %collective-permute-start.21 = (bf16[32,512]{1,0:T(8,128)(2,1)S(1)}, bf16[32,512]{1,0:T(8,128)(2,1)S(1)}, u32[]{:S(2)}, u32[]{:S(2)}) collective-permute-start(bf16[32,512]{1,0:T(8,128)(2,1)S(1)} %get-tuple-element.80), channel_id=1, source_target_pairs={{1,2},{3,4},{5,6},{7,8},{9,10},{11,12},{13,14},{15,16},{17,18},{19... | collective-permute-start | bytes 98312 | tf_op jit(solution)/shard_map/ppermute | solution.py:630
  55.1 0.0 collective-permute-done.20.refs_8_
  55.1 1.8 %collective-permute-done.21.refs_9_ = bf16[32,512]{1,0:T(8,128)(2,1)S(1)} collective-permute-done((bf16[32,512]{1,0:T(8,128)(2,1)S(1)}, bf16[32,512]{1,0:T(8,128)(2,1)S(1)}, u32[]{:S(2)}, u32[]{:S(2)}) %collective-permute-start.21) | collective-permute-done | bytes 32800 | tf_op jit(solution)/shard_map/ppermute | solution.py:630
  56.9 0.0 collective-permute-done.17.refs_5_
  56.9 0.0 collective-permute-done.18.refs_6_
  56.9 0.0 collective-permute-done.19.refs_7_
  56.9 1.4 %coadd_detect.1 = (f32[128,512]{1,0:T(8,128)}, f32[128,512]{1,0:T(8,128)}) custom-call(bf16[272,128]{1,0:T(8,128)(2,1)S(1)} %get-tuple-element.53.refs_0_, bf16[272,128]{1,0:T(8,128)(2,1)S(1)} %collective-permute-done.7.refs_1_, bf16[272,128]{1,0:T(8,128)(2,1)S(1)} %collective-permute-done.8.refs_2_, bf16[272,128]{1,0:T(8,128)(2,1)S(1)} %collective-permute-done.9.refs_3_, ...), custom_call_target="tpu_custom_call" | custom-call | tf_op jit(solution)/shard_map/coadd_detect/pallas_call | solution.py:634
  (8 shorter events, 0.0 us)
Async XLA Ops:
  0.6 23.1 %copy-start.2 = (f32[2,41]{1,0:T(2,128)S(1)}, f32[2,41]{1,0:T(2,128)}, u32[]{:S(2)}) copy-start(f32[2,41]{1,0:T(2,128)} %taps_ref.1) | copy-start | bytes 988
  7.3 6.4 %collective-permute-start = (bf16[544,128]{1,0:T(8,128)(2,1)}, bf16[544,128]{1,0:T(8,128)(2,1)S(1)}, u32[]{:S(2)}, u32[]{:S(2)}) collective-permute-start(bf16[544,128]{1,0:T(8,128)(2,1)} %get-tuple-element.46), channel_id=1, source_target_pairs={{0,16},{1,17},{2,18},{3,19},{16,0},{17,1},{18,2},{19,3},{4,20},{5,... | collective-permute-start | bytes 417800 | tf_op jit(solution)/shard_map/ppermute | solution.py:561
  7.4 8.1 %collective-permute-start.2 = (bf16[544,128]{1,0:T(8,128)(2,1)}, bf16[544,128]{1,0:T(8,128)(2,1)S(1)}, u32[]{:S(2)}, u32[]{:S(2)}) collective-permute-start(bf16[544,128]{1,0:T(8,128)(2,1)} %get-tuple-element.48), channel_id=1, source_target_pairs={{0,19},{1,18},{2,17},{3,16},{16,3},{17,2},{18,1},{19,0},{4,23},{5,... | collective-permute-start | bytes 417800 | tf_op jit(solution)/shard_map/ppermute | solution.py:561
  11.0 7.2 %collective-permute-start.1 = (bf16[544,128]{1,0:T(8,128)(2,1)}, bf16[544,128]{1,0:T(8,128)(2,1)S(1)}, u32[]{:S(2)}, u32[]{:S(2)}) collective-permute-start(bf16[544,128]{1,0:T(8,128)(2,1)} %get-tuple-element.47), channel_id=1, source_target_pairs={{0,3},{1,2},{2,1},{3,0},{16,19},{17,18},{18,17},{19,16},{4,7},{5,6... | collective-permute-start | bytes 417800 | tf_op jit(solution)/shard_map/ppermute | solution.py:561
  11.1 10.3 %collective-permute-start.3 = (bf16[544,128]{1,0:T(8,128)(2,1)}, bf16[544,128]{1,0:T(8,128)(2,1)S(1)}, u32[]{:S(2)}, u32[]{:S(2)}) collective-permute-start(bf16[544,128]{1,0:T(8,128)(2,1)} %get-tuple-element.49), channel_id=1, source_target_pairs={{0,1},{1,0},{2,3},{3,2},{16,18},{17,19},{18,16},{19,17},{4,5},{5,4... | collective-permute-start | bytes 417800 | tf_op jit(solution)/shard_map/ppermute | solution.py:561
  12.5 14.2 %collective-permute-start.4 = (bf16[544,128]{1,0:T(8,128)(2,1)}, bf16[544,128]{1,0:T(8,128)(2,1)S(1)}, u32[]{:S(2)}, u32[]{:S(2)}) collective-permute-start(bf16[544,128]{1,0:T(8,128)(2,1)} %get-tuple-element.50), channel_id=1, source_target_pairs={{0,2},{1,3},{2,0},{3,1},{16,17},{17,16},{18,19},{19,18},{4,6},{5,7... | collective-permute-start | bytes 417800 | tf_op jit(solution)/shard_map/ppermute | solution.py:561
  13.7 13.0 %collective-permute-start.5 = (bf16[544,128]{1,0:T(8,128)(2,1)}, bf16[544,128]{1,0:T(8,128)(2,1)S(1)}, u32[]{:S(2)}, u32[]{:S(2)}) collective-permute-start(bf16[544,128]{1,0:T(8,128)(2,1)} %get-tuple-element.51), channel_id=1, source_target_pairs={{0,17},{1,16},{2,19},{3,18},{16,2},{17,3},{18,0},{19,1},{4,21},{5,... | collective-permute-start | bytes 417800 | tf_op jit(solution)/shard_map/ppermute | solution.py:561
  15.6 11.1 %collective-permute-start.6 = (bf16[544,128]{1,0:T(8,128)(2,1)}, bf16[544,128]{1,0:T(8,128)(2,1)S(1)}, u32[]{:S(2)}, u32[]{:S(2)}) collective-permute-start(bf16[544,128]{1,0:T(8,128)(2,1)} %get-tuple-element.52), channel_id=1, source_target_pairs={{0,18},{1,19},{2,16},{3,17},{16,1},{17,0},{18,3},{19,2},{4,22},{5,... | collective-permute-start | bytes 417800 | tf_op jit(solution)/shard_map/ppermute | solution.py:561
  18.3 17.1 %collective-permute-start.10 = (bf16[512,128]{1,0:T(8,128)(2,1)}, bf16[512,128]{1,0:T(8,128)(2,1)S(1)}, u32[]{:S(2)}, u32[]{:S(2)}) collective-permute-start(bf16[512,128]{1,0:T(8,128)(2,1)} %get-tuple-element.68), channel_id=1, source_target_pairs={{0,16},{1,17},{2,18},{3,19},{16,0},{17,1},{18,2},{19,3},{4,20},{5,... | collective-permute-start | bytes 393224 | tf_op jit(solution)/shard_map/ppermute | solution.py:561
  21.4 17.1 %collective-permute-start.11 = (bf16[512,128]{1,0:T(8,128)(2,1)}, bf16[512,128]{1,0:T(8,128)(2,1)S(1)}, u32[]{:S(2)}, u32[]{:S(2)}) collective-permute-start(bf16[512,128]{1,0:T(8,128)(2,1)} %get-tuple-element.69), channel_id=1, source_target_pairs={{0,3},{1,2},{2,1},{3,0},{16,19},{17,18},{18,17},{19,16},{4,7},{5,6... | collective-permute-start | bytes 393224 | tf_op jit(solution)/shard_map/ppermute | solution.py:561
  23.7 0.9 %copy-start = (bf16[544,128]{1,0:T(8,128)(2,1)S(1)}, bf16[544,128]{1,0:T(8,128)(2,1)}, u32[]{:S(2)}) copy-start(bf16[544,128]{1,0:T(8,128)(2,1)} %get-tuple-element.43.refs_0_) | copy-start | bytes 417796
  24.6 0.9 %copy-start.1 = (bf16[512,128]{1,0:T(8,128)(2,1)S(1)}, bf16[512,128]{1,0:T(8,128)(2,1)}, u32[]{:S(2)}) copy-start(bf16[512,128]{1,0:T(8,128)(2,1)} %get-tuple-element.44.refs_1_) | copy-start | bytes 393220
  27.3 5.8 %collective-permute-start.7 = (bf16[272,128]{1,0:T(8,128)(2,1)S(1)}, bf16[272,128]{1,0:T(8,128)(2,1)S(1)}, u32[]{:S(2)}, u32[]{:S(2)}) collective-permute-start(bf16[272,128]{1,0:T(8,128)(2,1)S(1)} %get-tuple-element.54), channel_id=1, source_target_pairs={{0,4},{1,5},{2,6},{3,7},{4,0},{5,1},{6,2},{7,3},{8,12},{9,13},{10,... | collective-permute-start | bytes 208904 | tf_op jit(solution)/shard_map/ppermute | solution.py:568
  29.7 5.4 %collective-permute-start.8 = (bf16[272,128]{1,0:T(8,128)(2,1)S(1)}, bf16[272,128]{1,0:T(8,128)(2,1)S(1)}, u32[]{:S(2)}, u32[]{:S(2)}) collective-permute-start(bf16[272,128]{1,0:T(8,128)(2,1)S(1)} %get-tuple-element.55), channel_id=1, source_target_pairs={{0,8},{1,9},{2,10},{3,11},{4,12},{5,13},{6,14},{7,15},{8,0},{9,1},... | collective-permute-start | bytes 208904 | tf_op jit(solution)/shard_map/ppermute | solution.py:568
  30.8 7.7 %collective-permute-start.12 = (bf16[512,128]{1,0:T(8,128)(2,1)}, bf16[512,128]{1,0:T(8,128)(2,1)S(1)}, u32[]{:S(2)}, u32[]{:S(2)}) collective-permute-start(bf16[512,128]{1,0:T(8,128)(2,1)} %get-tuple-element.70), channel_id=1, source_target_pairs={{0,19},{1,18},{2,17},{3,16},{16,3},{17,2},{18,1},{19,0},{4,23},{5,... | collective-permute-start | bytes 393224 | tf_op jit(solution)/shard_map/ppermute | solution.py:561
  33.1 6.0 %collective-permute-start.13 = (bf16[512,128]{1,0:T(8,128)(2,1)}, bf16[512,128]{1,0:T(8,128)(2,1)S(1)}, u32[]{:S(2)}, u32[]{:S(2)}) collective-permute-start(bf16[512,128]{1,0:T(8,128)(2,1)} %get-tuple-element.71), channel_id=1, source_target_pairs={{0,1},{1,0},{2,3},{3,2},{16,18},{17,19},{18,16},{19,17},{4,5},{5,4... | collective-permute-start | bytes 393224 | tf_op jit(solution)/shard_map/ppermute | solution.py:561
  35.1 5.4 %collective-permute-start.14 = (bf16[512,128]{1,0:T(8,128)(2,1)}, bf16[512,128]{1,0:T(8,128)(2,1)S(1)}, u32[]{:S(2)}, u32[]{:S(2)}) collective-permute-start(bf16[512,128]{1,0:T(8,128)(2,1)} %get-tuple-element.72), channel_id=1, source_target_pairs={{0,2},{1,3},{2,0},{3,1},{16,17},{17,16},{18,19},{19,18},{4,6},{5,7... | collective-permute-start | bytes 393224 | tf_op jit(solution)/shard_map/ppermute | solution.py:561
  35.3 6.9 %collective-permute-start.15 = (bf16[512,128]{1,0:T(8,128)(2,1)}, bf16[512,128]{1,0:T(8,128)(2,1)S(1)}, u32[]{:S(2)}, u32[]{:S(2)}) collective-permute-start(bf16[512,128]{1,0:T(8,128)(2,1)} %get-tuple-element.73), channel_id=1, source_target_pairs={{0,17},{1,16},{2,19},{3,18},{16,2},{17,3},{18,0},{19,1},{4,21},{5,... | collective-permute-start | bytes 393224 | tf_op jit(solution)/shard_map/ppermute | solution.py:561
  38.4 6.0 %collective-permute-start.16 = (bf16[512,128]{1,0:T(8,128)(2,1)}, bf16[512,128]{1,0:T(8,128)(2,1)S(1)}, u32[]{:S(2)}, u32[]{:S(2)}) collective-permute-start(bf16[512,128]{1,0:T(8,128)(2,1)} %get-tuple-element.74), channel_id=1, source_target_pairs={{0,18},{1,19},{2,16},{3,17},{16,1},{17,0},{18,3},{19,2},{4,22},{5,... | collective-permute-start | bytes 393224 | tf_op jit(solution)/shard_map/ppermute | solution.py:561
  38.4 9.3 %collective-permute-start.9 = (bf16[272,128]{1,0:T(8,128)(2,1)S(1)}, bf16[272,128]{1,0:T(8,128)(2,1)S(1)}, u32[]{:S(2)}, u32[]{:S(2)}) collective-permute-start(bf16[272,128]{1,0:T(8,128)(2,1)S(1)} %get-tuple-element.60), channel_id=1, source_target_pairs={{0,12},{1,13},{2,14},{3,15},{4,8},{5,9},{6,10},{7,11},{8,4},{9,5},... | collective-permute-start | bytes 208904 | tf_op jit(solution)/shard_map/ppermute | solution.py:568
  45.0 11.9 %collective-permute-start.17 = (bf16[256,128]{1,0:T(8,128)(2,1)S(1)}, bf16[256,128]{1,0:T(8,128)(2,1)S(1)}, u32[]{:S(2)}, u32[]{:S(2)}) collective-permute-start(bf16[256,128]{1,0:T(8,128)(2,1)S(1)} %get-tuple-element.76), channel_id=1, source_target_pairs={{0,4},{1,5},{2,6},{3,7},{4,0},{5,1},{6,2},{7,3},{8,12},{9,13},{10,... | collective-permute-start | bytes 196616 | tf_op jit(solution)/shard_map/ppermute | solution.py:568
  45.2 11.7 %collective-permute-start.18 = (bf16[256,128]{1,0:T(8,128)(2,1)S(1)}, bf16[256,128]{1,0:T(8,128)(2,1)S(1)}, u32[]{:S(2)}, u32[]{:S(2)}) collective-permute-start(bf16[256,128]{1,0:T(8,128)(2,1)S(1)} %get-tuple-element.77), channel_id=1, source_target_pairs={{0,8},{1,9},{2,10},{3,11},{4,12},{5,13},{6,14},{7,15},{8,0},{9,1},... | collective-permute-start | bytes 196616 | tf_op jit(solution)/shard_map/ppermute | solution.py:568
  47.4 9.6 %collective-permute-start.19 = (bf16[256,128]{1,0:T(8,128)(2,1)S(1)}, bf16[256,128]{1,0:T(8,128)(2,1)S(1)}, u32[]{:S(2)}, u32[]{:S(2)}) collective-permute-start(bf16[256,128]{1,0:T(8,128)(2,1)S(1)} %get-tuple-element.78), channel_id=1, source_target_pairs={{0,12},{1,13},{2,14},{3,15},{4,8},{5,9},{6,10},{7,11},{8,4},{9,5},... | collective-permute-start | bytes 196616 | tf_op jit(solution)/shard_map/ppermute | solution.py:568
  47.8 7.3 %collective-permute-start.20 = (bf16[32,512]{1,0:T(8,128)(2,1)S(1)}, bf16[32,512]{1,0:T(8,128)(2,1)S(1)}, u32[]{:S(2)}, u32[]{:S(2)}) collective-permute-start(bf16[32,512]{1,0:T(8,128)(2,1)S(1)} %get-tuple-element.79), channel_id=1, source_target_pairs={{0,1},{2,3},{4,5},{6,7},{8,9},{10,11},{12,13},{14,15},{16,17},{18,... | collective-permute-start | bytes 98312 | tf_op jit(solution)/shard_map/ppermute | solution.py:630
  48.1 8.8 %collective-permute-start.21 = (bf16[32,512]{1,0:T(8,128)(2,1)S(1)}, bf16[32,512]{1,0:T(8,128)(2,1)S(1)}, u32[]{:S(2)}, u32[]{:S(2)}) collective-permute-start(bf16[32,512]{1,0:T(8,128)(2,1)S(1)} %get-tuple-element.80), channel_id=1, source_target_pairs={{1,2},{3,4},{5,6},{7,8},{9,10},{11,12},{13,14},{15,16},{17,18},{19... | collective-permute-start | bytes 98312 | tf_op jit(solution)/shard_map/ppermute | solution.py:630

commit v9 on v8

--- a/solution.py
+++ b/solution.py
@@ -88,7 +88,7 @@
     *rest,
 ):
     nz, pn, ns = split
-    outs, rest = rest[: 2 * ns * pn], rest[2 * ns * pn :]
+    outs, rest = rest[: 2 * ns * pn - 2], rest[2 * ns * pn - 2 :]
     warp_body(
         split,
         (
@@ -319,26 +319,26 @@
             axis=0,
         )
         out_ref[dest, pl.ds(data_rows, fields.shape[0]), :] = fields.astype(jnp.bfloat16)
-    for i, rows_of in enumerate((pl.ds(0, edge_rows), pl.ds(edge_rows, data_rows))):
-        for dest in range(group):
-            copies.append(
-                pltpu.make_async_copy(
-                    out_ref.at[dest, rows_of], outs[i * group + dest], out_sem.at[i, dest]
-                )
-            )
-            copies[-1].start()
+    whole = pl.ds(0, edge_rows + data_rows)
+    pieces = [(k, whole if k in (0, pn) else pl.ds(0, edge_rows)) for k in range(group)]
+    pieces += [(k, pl.ds(edge_rows, data_rows)) for k in range(group) if k not in (0, pn)]
+    for out, (dest, rows_of) in enumerate(pieces):
+        copies.append(
+            pltpu.make_async_copy(out_ref.at[dest, rows_of], outs[out], out_sem.at[out])
+        )
+        copies[-1].start()
     for copy in copies:
         copy.wait()
 
 
-def add_blocks(nz, ins, weight_ref, outs):
+def add_blocks(nz, ins, starts, weight_ref, outs):
     for z in range(nz):
         for place in range(PART // HALO):
             sums = [jnp.zeros((HALO, SIDE), jnp.float32) for _ in range(PATCH_DEV)]
-            for g, ref in enumerate(ins):
+            for g, (ref, start) in enumerate(zip(ins, starts)):
                 for r in range(CAP):
                     at = z * CAP + r
-                    value = ref[pl.ds(at * PART + place * HALO, HALO), :].astype(jnp.float32)
+                    value = ref[pl.ds(start + at * PART + place * HALO, HALO), :].astype(jnp.float32)
                     for j in range(PATCH_DEV):
                         sums[j] = sums[j] + weight_ref[g, j, pl.ds(at, 1), :] * value
             for j in range(PATCH_DEV):
@@ -359,7 +359,7 @@
         )
         for j in range(PATCH_DEV):
             weight_ref[g, j] = jnp.where(slot == float(j), weight, 0.0)
-    add_blocks(nz, ins, weight_ref, outs)
+    add_blocks(nz, ins, [0] * sources, weight_ref, outs)
     for z in range(nz):
         totals = []
         for j in range(PATCH_DEV):
@@ -376,7 +376,9 @@
 
 
 def inner_sum_kernel(nz, sources, weight_ref, *refs):
-    add_blocks(nz, refs[:sources], weight_ref, refs[sources:])
+    after = nz * CAP * (PART + FIELDS)
+    starts = [after, after] + [0] * (sources - 2)
+    add_blocks(nz, refs[:sources], starts, weight_ref, refs[sources:])
 
 
 def totals_of(ins, start):
@@ -437,13 +439,9 @@
 
 
 def prepare_kernel(taps_ref, *refs):
-    owns_hbm, (across_ref, centre_ref, edge_ref), owns = refs[:2], refs[2:5], refs[5:7]
-    band_ref, own_sem = refs[7:]
-    own_copies = [
-        pltpu.make_async_copy(owns_hbm[i], owns[i], own_sem.at[i]) for i in range(len(owns))
-    ]
-    for copy in own_copies:
-        copy.start()
+    own_hbm, across_ref, centre_ref, edge_ref, own_ref, band_ref, own_sem = refs
+    own_copy = pltpu.make_async_copy(own_hbm, own_ref, own_sem)
+    own_copy.start()
     tap_count = taps_ref.shape[1]
     half = tap_count // 2
     across = tap_row(lambda k: taps_ref[1, k], tap_count, SIDE - half, 3 * SIDE, True)
@@ -463,8 +461,7 @@
         ),
     )
     edge_ref[0], edge_ref[1] = two_parts(edge[:, : 2 * HALO])
-    for copy in own_copies:
-        copy.wait()
+    own_copy.wait()
 
 
 def dot_parts(left, across_ref):
@@ -509,10 +506,13 @@
     weights = term_weights.transpose(1, 2, 0)
     send = pl.pallas_call(
         functools.partial(warp_kernel, split),
-        out_shape=[shaped((edge_rows, SIDE), jnp.bfloat16)] * group
-        + [shaped((inner_rows, SIDE), jnp.bfloat16)] * group,
+        out_shape=[
+            shaped((edge_rows + (inner_rows if k in (0, pn) else 0), SIDE), jnp.bfloat16)
+            for k in range(group)
+        ]
+        + [shaped((inner_rows, SIDE), jnp.bfloat16)] * (group - 2),
         in_specs=[hbm] * 11,
-        out_specs=[hbm] * (2 * group),
+        out_specs=[hbm] * (2 * group - 2),
         scratch_shapes=[
             pltpu.SMEM((blocks,), jnp.int32),
             pltpu.SMEM((blocks,), jnp.int32),
@@ -535,7 +535,7 @@
             pltpu.SemaphoreType.DMA,
             pltpu.SemaphoreType.DMA((visits,)),
             pltpu.VMEM((group, edge_rows + inner_rows, SIDE), jnp.bfloat16),
-            pltpu.SemaphoreType.DMA((2, group)),
+            pltpu.SemaphoreType.DMA((2 * group - 2,)),
         ],
         compiler_params=pltpu.CompilerParams(vmem_limit_bytes=60 * 1024 * 1024),
         name="warp",
@@ -571,22 +571,21 @@
     peers = sorted(range(1, group), key=lambda k: (k != pn, -bin(k % pn).count("1"), k))
     edge_blocks = [in_plane(send[k], k) for k in peers]
 
-    across, centre, edge, own_edge, own_inner = pl.pallas_call(
+    across, centre, edge, own = pl.pallas_call(
         prepare_kernel,
         out_shape=(
             shaped((2, width, width), jnp.bfloat16),
             shaped((2, SIDE, SIDE), jnp.bfloat16),
             shaped((2, 2 * HALO, 2 * HALO), jnp.bfloat16),
-            shaped((edge_rows, SIDE), jnp.bfloat16),
-            shaped((inner_rows, SIDE), jnp.bfloat16),
+            shaped((edge_rows + inner_rows, SIDE), jnp.bfloat16),
         ),
-        in_specs=[smem, hbm, hbm],
-        out_specs=(vmem,) * 5,
-        scratch_shapes=[pltpu.VMEM((width, width), jnp.float32), pltpu.SemaphoreType.DMA((2,))],
+        in_specs=[smem, hbm],
+        out_specs=(vmem,) * 4,
+        scratch_shapes=[pltpu.VMEM((width, width), jnp.float32), pltpu.SemaphoreType.DMA],
         compiler_params=params,
         cost_estimate=pl.CostEstimate(flops=0, bytes_accessed=8 << 20, transcendentals=0),
         name="matrices",
-    )(detect_taps, send[0], send[group])
+    )(detect_taps, send[0])
 
     busy = pl.CostEstimate(flops=0, bytes_accessed=4 << 20, transcendentals=0)
     edge_sums = list(pl.pallas_call(
@@ -598,13 +597,34 @@
         compiler_params=params,
         cost_estimate=busy,
         name="edge_sums",
-    )(own_edge, *edge_blocks))
+    )(own, *edge_blocks))
     edges = [edge_sums[0]] + [along_z(edge_sums[d], d) for d in range(1, nz)]
-    count = 2
-    held = lax.optimization_barrier((edge_blocks[TIED], *(send[group + k] for k in peers[:-TAIL])))
-    kept = lax.optimization_barrier((*edges[1:3], *(send[group + k] for k in peers[-TAIL:])))
-    edges[1 : 1 + count], kept = kept[:count], kept[count:]
-    inner_blocks = [in_plane(part, k) for part, k in zip((*held[1:], *kept), peers)]
+    others = [k for k in range(group) if k not in (0, pn)]
+    later = {k: send[group + i] for i, k in enumerate(others)}
+    order = [k for k in peers if k != pn]
+    held = lax.optimization_barrier(
+        (edge_blocks[TIED], across, *(later[k] for k in order[:-TAIL]))
+    )
+    across = held[1]
+    kept = lax.optimization_barrier((*edges[1:], *(later[k] for k in order[-TAIL:])))
+    edges[1 : 1 + (nz - 1)], kept = kept[: (nz - 1)], kept[(nz - 1) :]
+    inner_blocks = [in_plane(part, k) for part, k in zip((*held[2:], *kept), order)]
+    first_rows, second_rows = pl.pallas_call(
+        edges_kernel,
+        out_shape=[shaped((HALO, width), jnp.bfloat16)] * 2,
+        in_specs=[vmem] * nz,
+        out_specs=[vmem] * 2,
+        compiler_params=params,
+        name="edge_rows",
+    )(*edges)
+
+    def swap(rows, start):
+        pairs = [(i, i + 1) for i in range(start, devices - 1, 2)]
+        return lax.ppermute(rows, every, pairs + [(j, i) for i, j in pairs])
+
+    first_rows, second_rows, own = lax.optimization_barrier((first_rows, second_rows, own))
+    first, second = swap(first_rows, 0), swap(second_rows, 1)
+
     inner_sums = pl.pallas_call(
         functools.partial(inner_sum_kernel, nz, group),
         out_shape=[shaped((PATCH_DEV * PART, SIDE), jnp.bfloat16)] * nz,
@@ -613,23 +633,8 @@
         compiler_params=params,
         cost_estimate=busy,
         name="inner_sums",
-    )(edge_sums[nz], own_inner, *inner_blocks)
+    )(edge_sums[nz], own, edge_blocks[0], *inner_blocks)
     inner = [inner_sums[0]] + [along_z(inner_sums[d], d) for d in range(1, nz)]
-
-    first_rows, second_rows = pl.pallas_call(
-        edges_kernel,
-        out_shape=[shaped((HALO, width), jnp.bfloat16)] * 2,
-        in_specs=[vmem] * nz,
-        out_specs=[vmem] * 2,
-        compiler_params=params,
-        name="edge_rows",
-    )(*edges)
-
-    def swap(rows, start):
-        pairs = [(i, i + 1) for i in range(start, devices - 1, 2)]
-        return lax.ppermute(rows, every, pairs + [(j, i) for i, j in pairs])
-
-    first, second = swap(first_rows, 0), swap(second_rows, 1)
 
     coadd, detection = pl.pallas_call(
         functools.partial(detect_kernel, nz),

time: 58.5 us -> 56.6 us (0.968)
  waiting for transfers between devices: 13.6 us -> 9.37 us
  starting transfers between devices: 31.6 us -> 35.3 us
  local copies, waits for them, and re-layouts: 1.81 us -> 0.96 us
    ppermute x14 -> x13, waiting for transfers between devices: 10 us -> 6.19 us  [in_plane(): return lax.ppermute(part, ('sec', 'p'), pairs)]
    ppermute x14 -> x13, starting transfers between devices: 18 us -> 20.5 us  [in_plane(): return lax.ppermute(part, ('sec', 'p'), pairs)]
    ppermute x6, starting transfers between devices: 6.36 us -> 7.3 us  [along_z(): return lax.ppermute(part, every, pairs)]
    unnamed x6 -> x4, local copies, waits for them, and re-layouts: 1.81 us -> 0.96 us
    ppermute x6, waiting for transfers between devices: 1.76 us -> 1.09 us  [along_z(): return lax.ppermute(part, every, pairs)]
  transfers between devices with their start and end apart: 22 -> 21, of which waited for: 9 -> 10; matrix products, arithmetic and copies ran while one was open for 0% -> 0% of each run, Pallas kernels for 4% -> 3%
where the time goes in v9:
time: 56.6 us; the launch traced here: 56.4 us
  starting transfers between devices  35.3 us (62%)
  Pallas kernels  10.2 us (18%)
  waiting for transfers between devices  9.37 us (17%)
  local copies, waits for them, and re-layouts  0.96 us (2%)
  between operations  0.71 us (1%)
    ppermute x13, starting transfers between devices, in_plane(): return lax.ppermute(part, ('sec', 'p'), pairs)  20.5 us
    ppermute x2, starting transfers between devices, swap(): return lax.ppermute(rows, every, pairs + [(j, i) for i, j in pairs])  7.47 us
    ppermute x6, starting transfers between devices, along_z(): return lax.ppermute(part, every, pairs)  7.3 us
    pallas_call x1, Pallas kernels, per_device(): pl.pallas_call(functools.partial(warp_kernel, split), out_shape=[shaped((...  6.64 us
    ppermute x13, waiting for transfers between devices, in_plane(): return lax.ppermute(part, ('sec', 'p'), pairs)  6.19 us
    ppermute x2, waiting for transfers between devices, swap(): return lax.ppermute(rows, every, pairs + [(j, i) for i, j in pairs])  2.09 us
    pallas_call x1, Pallas kernels, per_device(): pl.pallas_call(functools.partial(detect_kernel, nz), out_shape=[shaped((S...  1.38 us
  transfers between devices with their start and end apart: 21, of which 10 were waited for; matrix products, arithmetic and copies ran while one was open for 0% of the time, Pallas kernels for 3%

profile of v9, /device:TPU:1, one launch (start us, length us, event | category | flops | bytes accessed | tf_op | source)
XLA Modules:
  0.0 56.4 jit_solution(10566442232778027776)
XLA Ops:
  0.6 6.6 %warp.1 = (bf16[1056,128]{1,0:T(8,128)(2,1)}, bf16[544,128]{1,0:T(8,128)(2,1)}, bf16[544,128]{1,0:T(8,128)(2,1)}, bf16[544,128]{1,0:T(8,128)(2,1)}, bf16[1056,12...) custom-call(s32[32]{0:T(128)} %bitcast.4, ...), custom_call_target="tpu_custom_call" | custom-call | tf_op jit(solution)/shard_map/warp/pallas_call | solution.py:507
  7.3 3.1 %collective-permute-start.1 = (bf16[544,128]{1,0:T(8,128)(2,1)}, bf16[544,128]{1,0:T(8,128)(2,1)S(1)}, u32[]{:S(2)}, u32[]{:S(2)}) collective-permute-start(bf16[544,128]{1,0:T(8,128)(2,1)} %get-tuple-element.47), channel_id=1, source_target_pairs={{0,3},{1,2},{2,1},{3,0},{16,19},{17,18},{18,17},{19,16},{4,7},{5,6... | collective-permute-start | bytes 417800 | tf_op jit(solution)/shard_map/ppermute | solution.py:561
  10.4 0.6 %collective-permute-start.2 = (bf16[544,128]{1,0:T(8,128)(2,1)}, bf16[544,128]{1,0:T(8,128)(2,1)S(1)}, u32[]{:S(2)}, u32[]{:S(2)}) collective-permute-start(bf16[544,128]{1,0:T(8,128)(2,1)} %get-tuple-element.48), channel_id=1, source_target_pairs={{0,19},{1,18},{2,17},{3,16},{16,3},{17,2},{18,1},{19,0},{4,23},{5,... | collective-permute-start | bytes 417800 | tf_op jit(solution)/shard_map/ppermute | solution.py:561
  11.0 0.3 collective-permute-start
  11.3 1.3 %collective-permute-start.3 = (bf16[544,128]{1,0:T(8,128)(2,1)}, bf16[544,128]{1,0:T(8,128)(2,1)S(1)}, u32[]{:S(2)}, u32[]{:S(2)}) collective-permute-start(bf16[544,128]{1,0:T(8,128)(2,1)} %get-tuple-element.49), channel_id=1, source_target_pairs={{0,1},{1,0},{2,3},{3,2},{16,18},{17,19},{18,16},{19,17},{4,5},{5,4... | collective-permute-start | bytes 417800 | tf_op jit(solution)/shard_map/ppermute | solution.py:561
  12.6 1.2 %collective-permute-start.4 = (bf16[544,128]{1,0:T(8,128)(2,1)}, bf16[544,128]{1,0:T(8,128)(2,1)S(1)}, u32[]{:S(2)}, u32[]{:S(2)}) collective-permute-start(bf16[544,128]{1,0:T(8,128)(2,1)} %get-tuple-element.50), channel_id=1, source_target_pairs={{0,2},{1,3},{2,0},{3,1},{16,17},{17,16},{18,19},{19,18},{4,6},{5,7... | collective-permute-start | bytes 417800 | tf_op jit(solution)/shard_map/ppermute | solution.py:561
  13.8 0.1 collective-permute-done.1.refs_2_
  14.0 3.7 %collective-permute-start.5 = (bf16[544,128]{1,0:T(8,128)(2,1)}, bf16[544,128]{1,0:T(8,128)(2,1)S(1)}, u32[]{:S(2)}, u32[]{:S(2)}) collective-permute-start(bf16[544,128]{1,0:T(8,128)(2,1)} %get-tuple-element.51), channel_id=1, source_target_pairs={{0,17},{1,16},{2,19},{3,18},{16,2},{17,3},{18,0},{19,1},{4,21},{5,... | collective-permute-start | bytes 417800 | tf_op jit(solution)/shard_map/ppermute | solution.py:561
  17.7 0.0 collective-permute-done.2.refs_3_
  17.7 1.1 %collective-permute-start.6 = (bf16[544,128]{1,0:T(8,128)(2,1)}, bf16[544,128]{1,0:T(8,128)(2,1)S(1)}, u32[]{:S(2)}, u32[]{:S(2)}) collective-permute-start(bf16[544,128]{1,0:T(8,128)(2,1)} %get-tuple-element.52), channel_id=1, source_target_pairs={{0,18},{1,19},{2,16},{3,17},{16,1},{17,0},{18,3},{19,2},{4,22},{5,... | collective-permute-start | bytes 417800 | tf_op jit(solution)/shard_map/ppermute | solution.py:561
  18.8 1.0 %copy-done = bf16[1056,128]{1,0:T(8,128)(2,1)S(1)} copy-done((bf16[1056,128]{1,0:T(8,128)(2,1)S(1)}, bf16[1056,128]{1,0:T(8,128)(2,1)}, u32[]{:S(2)}) %copy-start) | copy-done | bytes 270360
  19.8 0.8 %matrices.1 = (bf16[2,512,512]{2,1,0:T(8,128)(2,1)S(1)}, bf16[2,128,128]{2,1,0:T(8,128)(2,1)S(1)}, bf16[2,64,64]{2,1,0:T(8,128)(2,1)S(1)}, bf16[1056,128]{1,0:T(8,128)(2,1)S(1)}) custom-call(f32[2,41]{1,0:T(2,128)S(1)} %copy-done.1, bf16[1056,128]{1,0:T(8,128)(2,1)S(1)} %copy-done), custom_call_target="tpu_custom_call" | custom-call | bytes 8388608 | tf_op jit(solution)/shard_map/matrices/pallas_call | solution.py:574
  20.5 0.1 collective-permute-done.3.refs_4_
  20.7 2.4 %collective-permute-start.10 = (bf16[512,128]{1,0:T(8,128)(2,1)}, bf16[512,128]{1,0:T(8,128)(2,1)S(1)}, u32[]{:S(2)}, u32[]{:S(2)}) collective-permute-start(bf16[512,128]{1,0:T(8,128)(2,1)} %get-tuple-element.71), channel_id=1, source_target_pairs={{0,3},{1,2},{2,1},{3,0},{16,19},{17,18},{18,17},{19,16},{4,7},{5,6... | collective-permute-start | bytes 393224 | tf_op jit(solution)/shard_map/ppermute | solution.py:561
  23.0 0.0 collective-permute-done.4.refs_5_
  23.0 0.5 collective-permute-done.5.refs_6_
  23.6 0.2 collective-permute-done.6.refs_7_
  23.8 0.0 collective-permute-done.refs_1_
  23.8 0.7 %edge_sums.1 = (bf16[272,128]{1,0:T(8,128)(2,1)S(1)}, bf16[272,128]{1,0:T(8,128)(2,1)S(1)}, bf16[272,128]{1,0:T(8,128)(2,1)S(1)}, bf16[272,128]{1,0:T(8,128)(2,1)S(1)}, f32[8,4,8,128]{3,2,1,0:T(8,128)S(1)}) custom-call(bf16[1056,128]{1,0:T(8,128)(2,1)S(1)} %get-tuple-element.65.refs_0_, bf16[1056,128]{1,0:T(8,128)(2,1)S(1)} %collective-permute-done.refs_1_, ...), custom_call_target="tpu_custom_call" | custom-call | bytes 4194304 | tf_op jit(solution)/shard_map/edge_sums/pallas_call | solution.py:591
  24.4 2.6 %collective-permute-start.7 = (bf16[272,128]{1,0:T(8,128)(2,1)S(1)}, bf16[272,128]{1,0:T(8,128)(2,1)S(1)}, u32[]{:S(2)}, u32[]{:S(2)}) collective-permute-start(bf16[272,128]{1,0:T(8,128)(2,1)S(1)} %get-tuple-element.54), channel_id=1, source_target_pairs={{0,4},{1,5},{2,6},{3,7},{4,0},{5,1},{6,2},{7,3},{8,12},{9,13},{10,... | collective-permute-start | bytes 208904 | tf_op jit(solution)/shard_map/ppermute | solution.py:568
  27.0 1.1 %collective-permute-start.8 = (bf16[272,128]{1,0:T(8,128)(2,1)S(1)}, bf16[272,128]{1,0:T(8,128)(2,1)S(1)}, u32[]{:S(2)}, u32[]{:S(2)}) collective-permute-start(bf16[272,128]{1,0:T(8,128)(2,1)S(1)} %get-tuple-element.55), channel_id=1, source_target_pairs={{0,8},{1,9},{2,10},{3,11},{4,12},{5,13},{6,14},{7,15},{8,0},{9,1},... | collective-permute-start | bytes 208904 | tf_op jit(solution)/shard_map/ppermute | solution.py:568
  28.1 0.2 collective-permute-start.9
  28.3 2.3 %collective-permute-start.11 = (bf16[512,128]{1,0:T(8,128)(2,1)}, bf16[512,128]{1,0:T(8,128)(2,1)S(1)}, u32[]{:S(2)}, u32[]{:S(2)}) collective-permute-start(bf16[512,128]{1,0:T(8,128)(2,1)} %get-tuple-element.72), channel_id=1, source_target_pairs={{0,19},{1,18},{2,17},{3,16},{16,3},{17,2},{18,1},{19,0},{4,23},{5,... | collective-permute-start | bytes 393224 | tf_op jit(solution)/shard_map/ppermute | solution.py:561
  30.6 0.0 collective-permute-done.7.refs_1_
  30.6 0.7 %collective-permute-start.12 = (bf16[512,128]{1,0:T(8,128)(2,1)}, bf16[512,128]{1,0:T(8,128)(2,1)S(1)}, u32[]{:S(2)}, u32[]{:S(2)}) collective-permute-start(bf16[512,128]{1,0:T(8,128)(2,1)} %get-tuple-element.73), channel_id=1, source_target_pairs={{0,1},{1,0},{2,3},{3,2},{16,18},{17,19},{18,16},{19,17},{4,5},{5,4... | collective-permute-start | bytes 393224 | tf_op jit(solution)/shard_map/ppermute | solution.py:561
  31.4 1.1 %collective-permute-done.8.refs_2_ = bf16[272,128]{1,0:T(8,128)(2,1)S(1)} collective-permute-done((bf16[272,128]{1,0:T(8,128)(2,1)S(1)}, bf16[272,128]{1,0:T(8,128)(2,1)S(1)}, u32[]{:S(2)}, u32[]{:S(2)}) %collective-permute-start.8) | collective-permute-done | bytes 69664 | tf_op jit(solution)/shard_map/ppermute | solution.py:568
  32.5 0.7 %collective-permute-start.13 = (bf16[512,128]{1,0:T(8,128)(2,1)}, bf16[512,128]{1,0:T(8,128)(2,1)S(1)}, u32[]{:S(2)}, u32[]{:S(2)}) collective-permute-start(bf16[512,128]{1,0:T(8,128)(2,1)} %get-tuple-element.74), channel_id=1, source_target_pairs={{0,2},{1,3},{2,0},{3,1},{16,17},{17,16},{18,19},{19,18},{4,6},{5,7... | collective-permute-start | bytes 393224 | tf_op jit(solution)/shard_map/ppermute | solution.py:561
  33.2 0.0 collective-permute-done.9.refs_3_
  33.2 2.9 %collective-permute-start.14 = (bf16[512,128]{1,0:T(8,128)(2,1)}, bf16[512,128]{1,0:T(8,128)(2,1)S(1)}, u32[]{:S(2)}, u32[]{:S(2)}) collective-permute-start(bf16[512,128]{1,0:T(8,128)(2,1)} %get-tuple-element.75), channel_id=1, source_target_pairs={{0,17},{1,16},{2,19},{3,18},{16,2},{17,3},{18,0},{19,1},{4,21},{5,... | collective-permute-start | bytes 393224 | tf_op jit(solution)/shard_map/ppermute | solution.py:561
  36.0 0.0 collective-permute-done.10.refs_2_
  36.0 0.1 collective-permute-start.15
  36.1 0.1 edge_rows.1
  36.2 0.0 collective-permute-done.11.refs_3_
  36.2 0.7 %collective-permute-done.12.refs_4_ = bf16[512,128]{1,0:T(8,128)(2,1)S(1)} collective-permute-done((bf16[512,128]{1,0:T(8,128)(2,1)}, bf16[512,128]{1,0:T(8,128)(2,1)S(1)}, u32[]{:S(2)}, u32[]{:S(2)}) %collective-permute-start.12) | collective-permute-done | bytes 131104 | tf_op jit(solution)/shard_map/ppermute | solution.py:561
  36.9 1.4 %collective-permute-done.13.refs_5_ = bf16[512,128]{1,0:T(8,128)(2,1)S(1)} collective-permute-done((bf16[512,128]{1,0:T(8,128)(2,1)}, bf16[512,128]{1,0:T(8,128)(2,1)S(1)}, u32[]{:S(2)}, u32[]{:S(2)}) %collective-permute-start.13) | collective-permute-done | bytes 131104 | tf_op jit(solution)/shard_map/ppermute | solution.py:561
  38.3 2.3 %collective-permute-done.14.refs_6_ = bf16[512,128]{1,0:T(8,128)(2,1)S(1)} collective-permute-done((bf16[512,128]{1,0:T(8,128)(2,1)}, bf16[512,128]{1,0:T(8,128)(2,1)S(1)}, u32[]{:S(2)}, u32[]{:S(2)}) %collective-permute-start.14) | collective-permute-done | bytes 131104 | tf_op jit(solution)/shard_map/ppermute | solution.py:561
  40.6 0.8 %collective-permute-done.15.refs_7_ = bf16[512,128]{1,0:T(8,128)(2,1)S(1)} collective-permute-done((bf16[512,128]{1,0:T(8,128)(2,1)}, bf16[512,128]{1,0:T(8,128)(2,1)S(1)}, u32[]{:S(2)}, u32[]{:S(2)}) %collective-permute-start.15) | collective-permute-done | bytes 131104 | tf_op jit(solution)/shard_map/ppermute | solution.py:561
  41.4 0.6 %inner_sums.1 = (bf16[256,128]{1,0:T(8,128)(2,1)S(1)}, bf16[256,128]{1,0:T(8,128)(2,1)S(1)}, bf16[256,128]{1,0:T(8,128)(2,1)S(1)}, bf16[256,128]{1,0:T(8,128)(2,1)S(1)}) custom-call(f32[8,4,8,128]{3,2,1,0:T(8,128)S(1)} %get-tuple-element.62.weight_ref, bf16[1056,128]{1,0:T(8,128)(2,1)S(1)} %get-tuple-element.65.refs_0_, ...), custom_call_target="tpu_custom_call" | custom-call | bytes 4194304 | tf_op jit(solution)/shard_map/inner_sums/pallas_call | solution.py:628
  42.0 1.8 %collective-permute-start.16 = (bf16[256,128]{1,0:T(8,128)(2,1)S(1)}, bf16[256,128]{1,0:T(8,128)(2,1)S(1)}, u32[]{:S(2)}, u32[]{:S(2)}) collective-permute-start(bf16[256,128]{1,0:T(8,128)(2,1)S(1)} %get-tuple-element.78), channel_id=1, source_target_pairs={{0,4},{1,5},{2,6},{3,7},{4,0},{5,1},{6,2},{7,3},{8,12},{9,13},{10,... | collective-permute-start | bytes 196616 | tf_op jit(solution)/shard_map/ppermute | solution.py:568
  43.8 1.4 %collective-permute-start.17 = (bf16[256,128]{1,0:T(8,128)(2,1)S(1)}, bf16[256,128]{1,0:T(8,128)(2,1)S(1)}, u32[]{:S(2)}, u32[]{:S(2)}) collective-permute-start(bf16[256,128]{1,0:T(8,128)(2,1)S(1)} %get-tuple-element.79), channel_id=1, source_target_pairs={{0,8},{1,9},{2,10},{3,11},{4,12},{5,13},{6,14},{7,15},{8,0},{9,1},... | collective-permute-start | bytes 196616 | tf_op jit(solution)/shard_map/ppermute | solution.py:568
  45.3 0.2 collective-permute-start.18
  45.5 0.8 %collective-permute-start.19 = (bf16[32,512]{1,0:T(8,128)(2,1)S(1)}, bf16[32,512]{1,0:T(8,128)(2,1)S(1)}, u32[]{:S(2)}, u32[]{:S(2)}) collective-permute-start(bf16[32,512]{1,0:T(8,128)(2,1)S(1)} %get-tuple-element.81), channel_id=1, source_target_pairs={{0,1},{2,3},{4,5},{6,7},{8,9},{10,11},{12,13},{14,15},{16,17},{18,... | collective-permute-start | bytes 98312 | tf_op jit(solution)/shard_map/ppermute | solution.py:623
  46.2 6.7 %collective-permute-start.20 = (bf16[32,512]{1,0:T(8,128)(2,1)S(1)}, bf16[32,512]{1,0:T(8,128)(2,1)S(1)}, u32[]{:S(2)}, u32[]{:S(2)}) collective-permute-start(bf16[32,512]{1,0:T(8,128)(2,1)S(1)} %get-tuple-element.82), channel_id=1, source_target_pairs={{1,2},{3,4},{5,6},{7,8},{9,10},{11,12},{13,14},{15,16},{17,18},{19... | collective-permute-start | bytes 98312 | tf_op jit(solution)/shard_map/ppermute | solution.py:623
  52.9 0.0 collective-permute-done.19.refs_8_
  53.0 2.1 %collective-permute-done.20.refs_9_ = bf16[32,512]{1,0:T(8,128)(2,1)S(1)} collective-permute-done((bf16[32,512]{1,0:T(8,128)(2,1)S(1)}, bf16[32,512]{1,0:T(8,128)(2,1)S(1)}, u32[]{:S(2)}, u32[]{:S(2)}) %collective-permute-start.20) | collective-permute-done | bytes 32800 | tf_op jit(solution)/shard_map/ppermute | solution.py:623
  55.0 0.0 collective-permute-done.16.refs_5_
  55.1 0.0 collective-permute-done.17.refs_6_
  55.1 1.4 %coadd_detect.1 = (f32[128,512]{1,0:T(8,128)}, f32[128,512]{1,0:T(8,128)}) custom-call(bf16[272,128]{1,0:T(8,128)(2,1)S(1)} %get-tuple-element.53.refs_0_, bf16[272,128]{1,0:T(8,128)(2,1)S(1)} %collective-permute-done.7.refs_1_, bf16[272,128]{1,0:T(8,128)(2,1)S(1)} %collective-permute-done.8.refs_2_, bf16[272,128]{1,0:T(8,128)(2,1)S(1)} %collective-permute-done.9.refs_3_, ...), custom_call_target="tpu_custom_call" | custom-call | tf_op jit(solution)/shard_map/coadd_detect/pallas_call | solution.py:639
  (4 shorter events, 0.0 us)
Async XLA Ops:
  0.6 18.2 %copy-start.1 = (f32[2,41]{1,0:T(2,128)S(1)}, f32[2,41]{1,0:T(2,128)}, u32[]{:S(2)}) copy-start(f32[2,41]{1,0:T(2,128)} %taps_ref.1) | copy-start | bytes 988
  7.3 6.7 %collective-permute-start.1 = (bf16[544,128]{1,0:T(8,128)(2,1)}, bf16[544,128]{1,0:T(8,128)(2,1)S(1)}, u32[]{:S(2)}, u32[]{:S(2)}) collective-permute-start(bf16[544,128]{1,0:T(8,128)(2,1)} %get-tuple-element.47), channel_id=1, source_target_pairs={{0,3},{1,2},{2,1},{3,0},{16,19},{17,18},{18,17},{19,16},{4,7},{5,6... | collective-permute-start | bytes 417800 | tf_op jit(solution)/shard_map/ppermute | solution.py:561
  10.4 7.3 %collective-permute-start.2 = (bf16[544,128]{1,0:T(8,128)(2,1)}, bf16[544,128]{1,0:T(8,128)(2,1)S(1)}, u32[]{:S(2)}, u32[]{:S(2)}) collective-permute-start(bf16[544,128]{1,0:T(8,128)(2,1)} %get-tuple-element.48), channel_id=1, source_target_pairs={{0,19},{1,18},{2,17},{3,16},{16,3},{17,2},{18,1},{19,0},{4,23},{5,... | collective-permute-start | bytes 417800 | tf_op jit(solution)/shard_map/ppermute | solution.py:561
  11.0 12.8 %collective-permute-start = (bf16[1056,128]{1,0:T(8,128)(2,1)}, bf16[1056,128]{1,0:T(8,128)(2,1)S(1)}, u32[]{:S(2)}, u32[]{:S(2)}) collective-permute-start(bf16[1056,128]{1,0:T(8,128)(2,1)} %get-tuple-element.46), channel_id=1, source_target_pairs={{0,16},{1,17},{2,18},{3,19},{16,0},{17,1},{18,2},{19,3},{4,20},{5,... | collective-permute-start | bytes 811016 | tf_op jit(solution)/shard_map/ppermute | solution.py:561
  11.3 9.4 %collective-permute-start.3 = (bf16[544,128]{1,0:T(8,128)(2,1)}, bf16[544,128]{1,0:T(8,128)(2,1)S(1)}, u32[]{:S(2)}, u32[]{:S(2)}) collective-permute-start(bf16[544,128]{1,0:T(8,128)(2,1)} %get-tuple-element.49), channel_id=1, source_target_pairs={{0,1},{1,0},{2,3},{3,2},{16,18},{17,19},{18,16},{19,17},{4,5},{5,4... | collective-permute-start | bytes 417800 | tf_op jit(solution)/shard_map/ppermute | solution.py:561
  12.6 10.4 %collective-permute-start.4 = (bf16[544,128]{1,0:T(8,128)(2,1)}, bf16[544,128]{1,0:T(8,128)(2,1)S(1)}, u32[]{:S(2)}, u32[]{:S(2)}) collective-permute-start(bf16[544,128]{1,0:T(8,128)(2,1)} %get-tuple-element.50), channel_id=1, source_target_pairs={{0,2},{1,3},{2,0},{3,1},{16,17},{17,16},{18,19},{19,18},{4,6},{5,7... | collective-permute-start | bytes 417800 | tf_op jit(solution)/shard_map/ppermute | solution.py:561
  14.0 9.6 %collective-permute-start.5 = (bf16[544,128]{1,0:T(8,128)(2,1)}, bf16[544,128]{1,0:T(8,128)(2,1)S(1)}, u32[]{:S(2)}, u32[]{:S(2)}) collective-permute-start(bf16[544,128]{1,0:T(8,128)(2,1)} %get-tuple-element.51), channel_id=1, source_target_pairs={{0,17},{1,16},{2,19},{3,18},{16,2},{17,3},{18,0},{19,1},{4,21},{5,... | collective-permute-start | bytes 417800 | tf_op jit(solution)/shard_map/ppermute | solution.py:561
  17.7 6.1 %collective-permute-start.6 = (bf16[544,128]{1,0:T(8,128)(2,1)}, bf16[544,128]{1,0:T(8,128)(2,1)S(1)}, u32[]{:S(2)}, u32[]{:S(2)}) collective-permute-start(bf16[544,128]{1,0:T(8,128)(2,1)} %get-tuple-element.52), channel_id=1, source_target_pairs={{0,18},{1,19},{2,16},{3,17},{16,1},{17,0},{18,3},{19,2},{4,22},{5,... | collective-permute-start | bytes 417800 | tf_op jit(solution)/shard_map/ppermute | solution.py:561
  18.8 1.0 %copy-start = (bf16[1056,128]{1,0:T(8,128)(2,1)S(1)}, bf16[1056,128]{1,0:T(8,128)(2,1)}, u32[]{:S(2)}) copy-start(bf16[1056,128]{1,0:T(8,128)(2,1)} %get-tuple-element.44.refs_0_) | copy-start | bytes 811012
  20.7 15.4 %collective-permute-start.10 = (bf16[512,128]{1,0:T(8,128)(2,1)}, bf16[512,128]{1,0:T(8,128)(2,1)S(1)}, u32[]{:S(2)}, u32[]{:S(2)}) collective-permute-start(bf16[512,128]{1,0:T(8,128)(2,1)} %get-tuple-element.71), channel_id=1, source_target_pairs={{0,3},{1,2},{2,1},{3,0},{16,19},{17,18},{18,17},{19,16},{4,7},{5,6... | collective-permute-start | bytes 393224 | tf_op jit(solution)/shard_map/ppermute | solution.py:561
  24.4 6.2 %collective-permute-start.7 = (bf16[272,128]{1,0:T(8,128)(2,1)S(1)}, bf16[272,128]{1,0:T(8,128)(2,1)S(1)}, u32[]{:S(2)}, u32[]{:S(2)}) collective-permute-start(bf16[272,128]{1,0:T(8,128)(2,1)S(1)} %get-tuple-element.54), channel_id=1, source_target_pairs={{0,4},{1,5},{2,6},{3,7},{4,0},{5,1},{6,2},{7,3},{8,12},{9,13},{10,... | collective-permute-start | bytes 208904 | tf_op jit(solution)/shard_map/ppermute | solution.py:568
  27.0 5.4 %collective-permute-start.8 = (bf16[272,128]{1,0:T(8,128)(2,1)S(1)}, bf16[272,128]{1,0:T(8,128)(2,1)S(1)}, u32[]{:S(2)}, u32[]{:S(2)}) collective-permute-start(bf16[272,128]{1,0:T(8,128)(2,1)S(1)} %get-tuple-element.55), channel_id=1, source_target_pairs={{0,8},{1,9},{2,10},{3,11},{4,12},{5,13},{6,14},{7,15},{8,0},{9,1},... | collective-permute-start | bytes 208904 | tf_op jit(solution)/shard_map/ppermute | solution.py:568
  28.1 5.1 %collective-permute-start.9 = (bf16[272,128]{1,0:T(8,128)(2,1)S(1)}, bf16[272,128]{1,0:T(8,128)(2,1)S(1)}, u32[]{:S(2)}, u32[]{:S(2)}) collective-permute-start(bf16[272,128]{1,0:T(8,128)(2,1)S(1)} %get-tuple-element.56), channel_id=1, source_target_pairs={{0,12},{1,13},{2,14},{3,15},{4,8},{5,9},{6,10},{7,11},{8,4},{9,5},... | collective-permute-start | bytes 208904 | tf_op jit(solution)/shard_map/ppermute | solution.py:568
  28.3 7.9 %collective-permute-start.11 = (bf16[512,128]{1,0:T(8,128)(2,1)}, bf16[512,128]{1,0:T(8,128)(2,1)S(1)}, u32[]{:S(2)}, u32[]{:S(2)}) collective-permute-start(bf16[512,128]{1,0:T(8,128)(2,1)} %get-tuple-element.72), channel_id=1, source_target_pairs={{0,19},{1,18},{2,17},{3,16},{16,3},{17,2},{18,1},{19,0},{4,23},{5,... | collective-permute-start | bytes 393224 | tf_op jit(solution)/shard_map/ppermute | solution.py:561
  30.6 6.3 %collective-permute-start.12 = (bf16[512,128]{1,0:T(8,128)(2,1)}, bf16[512,128]{1,0:T(8,128)(2,1)S(1)}, u32[]{:S(2)}, u32[]{:S(2)}) collective-permute-start(bf16[512,128]{1,0:T(8,128)(2,1)} %get-tuple-element.73), channel_id=1, source_target_pairs={{0,1},{1,0},{2,3},{3,2},{16,18},{17,19},{18,16},{19,17},{4,5},{5,4... | collective-permute-start | bytes 393224 | tf_op jit(solution)/shard_map/ppermute | solution.py:561
  32.5 5.9 %collective-permute-start.13 = (bf16[512,128]{1,0:T(8,128)(2,1)}, bf16[512,128]{1,0:T(8,128)(2,1)S(1)}, u32[]{:S(2)}, u32[]{:S(2)}) collective-permute-start(bf16[512,128]{1,0:T(8,128)(2,1)} %get-tuple-element.74), channel_id=1, source_target_pairs={{0,2},{1,3},{2,0},{3,1},{16,17},{17,16},{18,19},{19,18},{4,6},{5,7... | collective-permute-start | bytes 393224 | tf_op jit(solution)/shard_map/ppermute | solution.py:561
  33.2 7.5 %collective-permute-start.14 = (bf16[512,128]{1,0:T(8,128)(2,1)}, bf16[512,128]{1,0:T(8,128)(2,1)S(1)}, u32[]{:S(2)}, u32[]{:S(2)}) collective-permute-start(bf16[512,128]{1,0:T(8,128)(2,1)} %get-tuple-element.75), channel_id=1, source_target_pairs={{0,17},{1,16},{2,19},{3,18},{16,2},{17,3},{18,0},{19,1},{4,21},{5,... | collective-permute-start | bytes 393224 | tf_op jit(solution)/shard_map/ppermute | solution.py:561
  36.0 5.4 %collective-permute-start.15 = (bf16[512,128]{1,0:T(8,128)(2,1)}, bf16[512,128]{1,0:T(8,128)(2,1)S(1)}, u32[]{:S(2)}, u32[]{:S(2)}) collective-permute-start(bf16[512,128]{1,0:T(8,128)(2,1)} %get-tuple-element.76), channel_id=1, source_target_pairs={{0,18},{1,19},{2,16},{3,17},{16,1},{17,0},{18,3},{19,2},{4,22},{5,... | collective-permute-start | bytes 393224 | tf_op jit(solution)/shard_map/ppermute | solution.py:561
  42.0 13.0 %collective-permute-start.16 = (bf16[256,128]{1,0:T(8,128)(2,1)S(1)}, bf16[256,128]{1,0:T(8,128)(2,1)S(1)}, u32[]{:S(2)}, u32[]{:S(2)}) collective-permute-start(bf16[256,128]{1,0:T(8,128)(2,1)S(1)} %get-tuple-element.78), channel_id=1, source_target_pairs={{0,4},{1,5},{2,6},{3,7},{4,0},{5,1},{6,2},{7,3},{8,12},{9,13},{10,... | collective-permute-start | bytes 196616 | tf_op jit(solution)/shard_map/ppermute | solution.py:568
  43.8 11.2 %collective-permute-start.17 = (bf16[256,128]{1,0:T(8,128)(2,1)S(1)}, bf16[256,128]{1,0:T(8,128)(2,1)S(1)}, u32[]{:S(2)}, u32[]{:S(2)}) collective-permute-start(bf16[256,128]{1,0:T(8,128)(2,1)S(1)} %get-tuple-element.79), channel_id=1, source_target_pairs={{0,8},{1,9},{2,10},{3,11},{4,12},{5,13},{6,14},{7,15},{8,0},{9,1},... | collective-permute-start | bytes 196616 | tf_op jit(solution)/shard_map/ppermute | solution.py:568
  45.3 9.8 %collective-permute-start.18 = (bf16[256,128]{1,0:T(8,128)(2,1)S(1)}, bf16[256,128]{1,0:T(8,128)(2,1)S(1)}, u32[]{:S(2)}, u32[]{:S(2)}) collective-permute-start(bf16[256,128]{1,0:T(8,128)(2,1)S(1)} %get-tuple-element.80), channel_id=1, source_target_pairs={{0,12},{1,13},{2,14},{3,15},{4,8},{5,9},{6,10},{7,11},{8,4},{9,5},... | collective-permute-start | bytes 196616 | tf_op jit(solution)/shard_map/ppermute | solution.py:568
  45.5 7.5 %collective-permute-start.19 = (bf16[32,512]{1,0:T(8,128)(2,1)S(1)}, bf16[32,512]{1,0:T(8,128)(2,1)S(1)}, u32[]{:S(2)}, u32[]{:S(2)}) collective-permute-start(bf16[32,512]{1,0:T(8,128)(2,1)S(1)} %get-tuple-element.81), channel_id=1, source_target_pairs={{0,1},{2,3},{4,5},{6,7},{8,9},{10,11},{12,13},{14,15},{16,17},{18,... | collective-permute-start | bytes 98312 | tf_op jit(solution)/shard_map/ppermute | solution.py:623
  46.2 8.8 %collective-permute-start.20 = (bf16[32,512]{1,0:T(8,128)(2,1)S(1)}, bf16[32,512]{1,0:T(8,128)(2,1)S(1)}, u32[]{:S(2)}, u32[]{:S(2)}) collective-permute-start(bf16[32,512]{1,0:T(8,128)(2,1)S(1)} %get-tuple-element.82), channel_id=1, source_target_pairs={{1,2},{3,4},{5,6},{7,8},{9,10},{11,12},{13,14},{15,16},{17,18},{19... | collective-permute-start | bytes 98312 | tf_op jit(solution)/shard_map/ppermute | solution.py:623

commit v10 on v9

--- a/solution.py
+++ b/solution.py
@@ -15,6 +15,7 @@
 HALO = 32
 FIELDS = 4
 TIED = 2
+EARLY = 3
 TAIL = 2
 PART = SIDE // 2
 VMEM_LIMIT = 48 * 1024 * 1024
@@ -609,6 +610,8 @@
     kept = lax.optimization_barrier((*edges[1:], *(later[k] for k in order[-TAIL:])))
     edges[1 : 1 + (nz - 1)], kept = kept[: (nz - 1)], kept[(nz - 1) :]
     inner_blocks = [in_plane(part, k) for part, k in zip((*held[2:], *kept), order)]
+    held = lax.optimization_barrier((*inner_blocks[:EARLY], *edges))
+    inner_blocks[:EARLY], edges = held[:EARLY], list(held[EARLY:])
     first_rows, second_rows = pl.pallas_call(
         edges_kernel,
         out_shape=[shaped((HALO, width), jnp.bfloat16)] * 2,
@@ -622,8 +625,8 @@
         pairs = [(i, i + 1) for i in range(start, devices - 1, 2)]
         return lax.ppermute(rows, every, pairs + [(j, i) for i, j in pairs])
 
-    first_rows, second_rows, own = lax.optimization_barrier((first_rows, second_rows, own))
     first, second = swap(first_rows, 0), swap(second_rows, 1)
+    first, second, own = lax.optimization_barrier((first, second, own))
 
     inner_sums = pl.pallas_call(
         functools.partial(inner_sum_kernel, nz, group),

time: 56.6 us -> 58.7 us (1.037)
  the two profiles are of different devices: /device:TPU:1 before, /device:TPU:0 now
where the time goes in v10:
time: 58.7 us; the launch traced here: 58.6 us
  starting transfers between devices  31.4 us (53%)
  waiting for transfers between devices  15.4 us (26%)
  Pallas kernels  10.2 us (17%)
  local copies, waits for them, and re-layouts  0.96 us (2%)
  between operations  0.7 us (1%)
    ppermute x13, starting transfers between devices, in_plane(): return lax.ppermute(part, ('sec', 'p'), pairs)  17 us
    ppermute x6, starting transfers between devices, along_z(): return lax.ppermute(part, every, pairs)  12.2 us
    ppermute x6, waiting for transfers between devices, along_z(): return lax.ppermute(part, every, pairs)  9.21 us
    pallas_call x1, Pallas kernels, per_device(): pl.pallas_call(functools.partial(warp_kernel, split), out_shape=[shaped((...  6.64 us
    ppermute x13, waiting for transfers between devices, in_plane(): return lax.ppermute(part, ('sec', 'p'), pairs)  4.43 us
    ppermute x2, starting transfers between devices, swap(): return lax.ppermute(rows, every, pairs + [(j, i) for i, j in pairs])  2.24 us
    ppermute x2, waiting for transfers between devices, swap(): return lax.ppermute(rows, every, pairs + [(j, i) for i, j in pairs])  1.73 us
    pallas_call x1, Pallas kernels, per_device(): pl.pallas_call(functools.partial(detect_kernel, nz), out_shape=[shaped((S...  1.39 us
  transfers between devices with their start and end apart: 21, of which 11 were waited for; matrix products, arithmetic and copies ran while one was open for 0% of the time, Pallas kernels for 3%

profile of v10, /device:TPU:0, one launch (start us, length us, event | category | flops | bytes accessed | tf_op | source)
XLA Modules:
  0.0 58.6 jit_solution(15644831773661501403)
XLA Ops:
  0.6 6.6 %warp.1 = (bf16[1056,128]{1,0:T(8,128)(2,1)}, bf16[544,128]{1,0:T(8,128)(2,1)}, bf16[544,128]{1,0:T(8,128)(2,1)}, bf16[544,128]{1,0:T(8,128)(2,1)}, bf16[1056,12...) custom-call(s32[32]{0:T(128)} %bitcast.4, ...), custom_call_target="tpu_custom_call" | custom-call | tf_op jit(solution)/shard_map/warp/pallas_call | solution.py:508
  7.3 3.4 %collective-permute-start = (bf16[544,128]{1,0:T(8,128)(2,1)}, bf16[544,128]{1,0:T(8,128)(2,1)S(1)}, u32[]{:S(2)}, u32[]{:S(2)}) collective-permute-start(bf16[544,128]{1,0:T(8,128)(2,1)} %get-tuple-element.51), channel_id=1, source_target_pairs={{0,19},{1,18},{2,17},{3,16},{16,3},{17,2},{18,1},{19,0},{4,23},{5,... | collective-permute-start | bytes 417800 | tf_op jit(solution)/shard_map/ppermute | solution.py:562
  10.7 0.6 %collective-permute-start.5 = (bf16[544,128]{1,0:T(8,128)(2,1)}, bf16[544,128]{1,0:T(8,128)(2,1)S(1)}, u32[]{:S(2)}, u32[]{:S(2)}) collective-permute-start(bf16[544,128]{1,0:T(8,128)(2,1)} %get-tuple-element.63), channel_id=1, source_target_pairs={{0,3},{1,2},{2,1},{3,0},{16,19},{17,18},{18,17},{19,16},{4,7},{5,6... | collective-permute-start | bytes 417800 | tf_op jit(solution)/shard_map/ppermute | solution.py:562
  11.3 0.0 collective-permute-start.4
  11.4 1.7 %collective-permute-start.6 = (bf16[544,128]{1,0:T(8,128)(2,1)}, bf16[544,128]{1,0:T(8,128)(2,1)S(1)}, u32[]{:S(2)}, u32[]{:S(2)}) collective-permute-start(bf16[544,128]{1,0:T(8,128)(2,1)} %get-tuple-element.64), channel_id=1, source_target_pairs={{0,1},{1,0},{2,3},{3,2},{16,18},{17,19},{18,16},{19,17},{4,5},{5,4... | collective-permute-start | bytes 417800 | tf_op jit(solution)/shard_map/ppermute | solution.py:562
  13.1 1.5 %collective-permute-start.7 = (bf16[544,128]{1,0:T(8,128)(2,1)}, bf16[544,128]{1,0:T(8,128)(2,1)S(1)}, u32[]{:S(2)}, u32[]{:S(2)}) collective-permute-start(bf16[544,128]{1,0:T(8,128)(2,1)} %get-tuple-element.65), channel_id=1, source_target_pairs={{0,2},{1,3},{2,0},{3,1},{16,17},{17,16},{18,19},{19,18},{4,6},{5,7... | collective-permute-start | bytes 417800 | tf_op jit(solution)/shard_map/ppermute | solution.py:562
  14.6 0.5 collective-permute-done.refs_3_
  15.1 2.0 %collective-permute-start.8 = (bf16[544,128]{1,0:T(8,128)(2,1)}, bf16[544,128]{1,0:T(8,128)(2,1)S(1)}, u32[]{:S(2)}, u32[]{:S(2)}) collective-permute-start(bf16[544,128]{1,0:T(8,128)(2,1)} %get-tuple-element.66), channel_id=1, source_target_pairs={{0,17},{1,16},{2,19},{3,18},{16,2},{17,3},{18,0},{19,1},{4,21},{5,... | collective-permute-start | bytes 417800 | tf_op jit(solution)/shard_map/ppermute | solution.py:562
  17.1 1.3 %collective-permute-done.5.refs_2_ = bf16[544,128]{1,0:T(8,128)(2,1)S(1)} collective-permute-done((bf16[544,128]{1,0:T(8,128)(2,1)}, bf16[544,128]{1,0:T(8,128)(2,1)S(1)}, u32[]{:S(2)}, u32[]{:S(2)}) %collective-permute-start.5) | collective-permute-done | bytes 139296 | tf_op jit(solution)/shard_map/ppermute | solution.py:562
  18.4 1.7 %collective-permute-start.9 = (bf16[544,128]{1,0:T(8,128)(2,1)}, bf16[544,128]{1,0:T(8,128)(2,1)S(1)}, u32[]{:S(2)}, u32[]{:S(2)}) collective-permute-start(bf16[544,128]{1,0:T(8,128)(2,1)} %get-tuple-element.67), channel_id=1, source_target_pairs={{0,18},{1,19},{2,16},{3,17},{16,1},{17,0},{18,3},{19,2},{4,22},{5,... | collective-permute-start | bytes 417800 | tf_op jit(solution)/shard_map/ppermute | solution.py:562
  20.1 1.0 %copy-done = bf16[1056,128]{1,0:T(8,128)(2,1)S(1)} copy-done((bf16[1056,128]{1,0:T(8,128)(2,1)S(1)}, bf16[1056,128]{1,0:T(8,128)(2,1)}, u32[]{:S(2)}) %copy-start) | copy-done | bytes 270360
  21.1 0.8 %matrices.1 = (bf16[2,512,512]{2,1,0:T(8,128)(2,1)S(1)}, bf16[2,128,128]{2,1,0:T(8,128)(2,1)S(1)}, bf16[2,64,64]{2,1,0:T(8,128)(2,1)S(1)}, bf16[1056,128]{1,0:T(8,128)(2,1)S(1)}) custom-call(f32[2,41]{1,0:T(2,128)S(1)} %copy-done.1, bf16[1056,128]{1,0:T(8,128)(2,1)S(1)} %copy-done), custom_call_target="tpu_custom_call" | custom-call | bytes 8388608 | tf_op jit(solution)/shard_map/matrices/pallas_call | solution.py:575
  21.8 0.2 collective-permute-done.6.refs_4_
  22.0 1.4 %collective-permute-start.1 = (bf16[512,128]{1,0:T(8,128)(2,1)}, bf16[512,128]{1,0:T(8,128)(2,1)S(1)}, u32[]{:S(2)}, u32[]{:S(2)}) collective-permute-start(bf16[512,128]{1,0:T(8,128)(2,1)} %get-tuple-element.58), channel_id=1, source_target_pairs={{0,3},{1,2},{2,1},{3,0},{16,19},{17,18},{18,17},{19,16},{4,7},{5,6... | collective-permute-start | bytes 393224 | tf_op jit(solution)/shard_map/ppermute | solution.py:562
  23.4 0.0 collective-permute-done.7.refs_5_
  23.4 0.4 collective-permute-done.8.refs_6_
  23.8 1.1 %collective-permute-done.9.refs_7_ = bf16[544,128]{1,0:T(8,128)(2,1)S(1)} collective-permute-done((bf16[544,128]{1,0:T(8,128)(2,1)}, bf16[544,128]{1,0:T(8,128)(2,1)S(1)}, u32[]{:S(2)}, u32[]{:S(2)}) %collective-permute-start.9) | collective-permute-done | bytes 139296 | tf_op jit(solution)/shard_map/ppermute | solution.py:562
  24.9 0.0 collective-permute-done.4.refs_1_
  24.9 0.7 %edge_sums.1 = (bf16[272,128]{1,0:T(8,128)(2,1)S(1)}, bf16[272,128]{1,0:T(8,128)(2,1)S(1)}, bf16[272,128]{1,0:T(8,128)(2,1)S(1)}, bf16[272,128]{1,0:T(8,128)(2,1)S(1)}, f32[8,4,8,128]{3,2,1,0:T(8,128)S(1)}) custom-call(bf16[1056,128]{1,0:T(8,128)(2,1)S(1)} %get-tuple-element.84.refs_0_, bf16[1056,128]{1,0:T(8,128)(2,1)S(1)} %collective-permute-done.4.refs_1_, ...), custom_call_target="tpu_custom_call" | custom-call | bytes 4194304 | tf_op jit(solution)/shard_map/edge_sums/pallas_call | solution.py:592
  25.6 1.7 %collective-permute-start.10 = (bf16[272,128]{1,0:T(8,128)(2,1)S(1)}, bf16[272,128]{1,0:T(8,128)(2,1)S(1)}, u32[]{:S(2)}, u32[]{:S(2)}) collective-permute-start(bf16[272,128]{1,0:T(8,128)(2,1)S(1)} %get-tuple-element.69), channel_id=1, source_target_pairs={{0,4},{1,5},{2,6},{3,7},{4,0},{5,1},{6,2},{7,3},{8,12},{9,13},{10,... | collective-permute-start | bytes 208904 | tf_op jit(solution)/shard_map/ppermute | solution.py:569
  27.3 2.6 %collective-permute-start.11 = (bf16[272,128]{1,0:T(8,128)(2,1)S(1)}, bf16[272,128]{1,0:T(8,128)(2,1)S(1)}, u32[]{:S(2)}, u32[]{:S(2)}) collective-permute-start(bf16[272,128]{1,0:T(8,128)(2,1)S(1)} %get-tuple-element.70), channel_id=1, source_target_pairs={{0,8},{1,9},{2,10},{3,11},{4,12},{5,13},{6,14},{7,15},{8,0},{9,1},... | collective-permute-start | bytes 208904 | tf_op jit(solution)/shard_map/ppermute | solution.py:569
  29.9 0.2 collective-permute-start.12
  30.0 1.0 %collective-permute-start.2 = (bf16[512,128]{1,0:T(8,128)(2,1)}, bf16[512,128]{1,0:T(8,128)(2,1)S(1)}, u32[]{:S(2)}, u32[]{:S(2)}) collective-permute-start(bf16[512,128]{1,0:T(8,128)(2,1)} %get-tuple-element.59), channel_id=1, source_target_pairs={{0,19},{1,18},{2,17},{3,16},{16,3},{17,2},{18,1},{19,0},{4,23},{5,... | collective-permute-start | bytes 393224 | tf_op jit(solution)/shard_map/ppermute | solution.py:562
  31.1 0.0 collective-permute-done.10.refs_1_
  31.1 1.1 %collective-permute-start.3 = (bf16[512,128]{1,0:T(8,128)(2,1)}, bf16[512,128]{1,0:T(8,128)(2,1)S(1)}, u32[]{:S(2)}, u32[]{:S(2)}) collective-permute-start(bf16[512,128]{1,0:T(8,128)(2,1)} %get-tuple-element.60), channel_id=1, source_target_pairs={{0,1},{1,0},{2,3},{3,2},{16,18},{17,19},{18,16},{19,17},{4,5},{5,4... | collective-permute-start | bytes 393224 | tf_op jit(solution)/shard_map/ppermute | solution.py:562
  32.2 2.4 %collective-permute-done.11.refs_2_ = bf16[272,128]{1,0:T(8,128)(2,1)S(1)} collective-permute-done((bf16[272,128]{1,0:T(8,128)(2,1)S(1)}, bf16[272,128]{1,0:T(8,128)(2,1)S(1)}, u32[]{:S(2)}, u32[]{:S(2)}) %collective-permute-start.11) | collective-permute-done | bytes 69664 | tf_op jit(solution)/shard_map/ppermute | solution.py:569
  34.6 0.7 %collective-permute-start.15 = (bf16[512,128]{1,0:T(8,128)(2,1)}, bf16[512,128]{1,0:T(8,128)(2,1)S(1)}, u32[]{:S(2)}, u32[]{:S(2)}) collective-permute-start(bf16[512,128]{1,0:T(8,128)(2,1)} %get-tuple-element.88), channel_id=1, source_target_pairs={{0,2},{1,3},{2,0},{3,1},{16,17},{17,16},{18,19},{19,18},{4,6},{5,7... | collective-permute-start | bytes 393224 | tf_op jit(solution)/shard_map/ppermute | solution.py:562
  35.3 0.8 %collective-permute-done.12.refs_3_ = bf16[272,128]{1,0:T(8,128)(2,1)S(1)} collective-permute-done((bf16[272,128]{1,0:T(8,128)(2,1)S(1)}, bf16[272,128]{1,0:T(8,128)(2,1)S(1)}, u32[]{:S(2)}, u32[]{:S(2)}) %collective-permute-start.12) | collective-permute-done | bytes 69664 | tf_op jit(solution)/shard_map/ppermute | solution.py:569
  36.1 0.0 collective-permute-start.16
  36.1 0.0 collective-permute-done.1.refs_2_
  36.1 1.7 %collective-permute-start.17 = (bf16[512,128]{1,0:T(8,128)(2,1)}, bf16[512,128]{1,0:T(8,128)(2,1)S(1)}, u32[]{:S(2)}, u32[]{:S(2)}) collective-permute-start(bf16[512,128]{1,0:T(8,128)(2,1)} %get-tuple-element.90), channel_id=1, source_target_pairs={{0,18},{1,19},{2,16},{3,17},{16,1},{17,0},{18,3},{19,2},{4,22},{5,... | collective-permute-start | bytes 393224 | tf_op jit(solution)/shard_map/ppermute | solution.py:562
  37.8 0.0 collective-permute-done.2.refs_3_
  37.9 0.9 %collective-permute-done.3.refs_4_ = bf16[512,128]{1,0:T(8,128)(2,1)S(1)} collective-permute-done((bf16[512,128]{1,0:T(8,128)(2,1)}, bf16[512,128]{1,0:T(8,128)(2,1)S(1)}, u32[]{:S(2)}, u32[]{:S(2)}) %collective-permute-start.3) | collective-permute-done | bytes 131104 | tf_op jit(solution)/shard_map/ppermute | solution.py:562
  38.8 0.1 edge_rows.1
  38.9 1.6 %collective-permute-start.13 = (bf16[32,512]{1,0:T(8,128)(2,1)S(1)}, bf16[32,512]{1,0:T(8,128)(2,1)S(1)}, u32[]{:S(2)}, u32[]{:S(2)}) collective-permute-start(bf16[32,512]{1,0:T(8,128)(2,1)S(1)} %get-tuple-element.82), channel_id=1, source_target_pairs={{0,1},{2,3},{4,5},{6,7},{8,9},{10,11},{12,13},{14,15},{16,17},{18,... | collective-permute-start | bytes 98312 | tf_op jit(solution)/shard_map/ppermute | solution.py:626
  40.5 0.7 %collective-permute-start.14 = (bf16[32,512]{1,0:T(8,128)(2,1)S(1)}, bf16[32,512]{1,0:T(8,128)(2,1)S(1)}, u32[]{:S(2)}, u32[]{:S(2)}) collective-permute-start(bf16[32,512]{1,0:T(8,128)(2,1)S(1)} %get-tuple-element.83), channel_id=1, source_target_pairs={{1,2},{3,4},{5,6},{7,8},{9,10},{11,12},{13,14},{15,16},{17,18},{19... | collective-permute-start | bytes 98312 | tf_op jit(solution)/shard_map/ppermute | solution.py:626
  41.1 1.7 %collective-permute-done.13.refs_8_ = bf16[32,512]{1,0:T(8,128)(2,1)S(1)} collective-permute-done((bf16[32,512]{1,0:T(8,128)(2,1)S(1)}, bf16[32,512]{1,0:T(8,128)(2,1)S(1)}, u32[]{:S(2)}, u32[]{:S(2)}) %collective-permute-start.13) | collective-permute-done | bytes 32800 | tf_op jit(solution)/shard_map/ppermute | solution.py:626
  42.8 0.0 collective-permute-done.14.refs_9_
  42.8 0.0 collective-permute-done.15.refs_5_
  42.8 0.0 collective-permute-done.16.refs_6_
  42.9 0.6 %inner_sums.1 = (bf16[256,128]{1,0:T(8,128)(2,1)S(1)}, bf16[256,128]{1,0:T(8,128)(2,1)S(1)}, bf16[256,128]{1,0:T(8,128)(2,1)S(1)}, bf16[256,128]{1,0:T(8,128)(2,1)S(1)}) custom-call(f32[8,4,8,128]{3,2,1,0:T(8,128)S(1)} %get-tuple-element.81.weight_ref, bf16[1056,128]{1,0:T(8,128)(2,1)S(1)} %get-tuple-element.84.refs_0_, ...), custom_call_target="tpu_custom_call" | custom-call | bytes 4194304 | tf_op jit(solution)/shard_map/inner_sums/pallas_call | solution.py:631
  43.5 5.3 %collective-permute-start.18 = (bf16[256,128]{1,0:T(8,128)(2,1)S(1)}, bf16[256,128]{1,0:T(8,128)(2,1)S(1)}, u32[]{:S(2)}, u32[]{:S(2)}) collective-permute-start(bf16[256,128]{1,0:T(8,128)(2,1)S(1)} %get-tuple-element.92), channel_id=1, source_target_pairs={{0,4},{1,5},{2,6},{3,7},{4,0},{5,1},{6,2},{7,3},{8,12},{9,13},{10,... | collective-permute-start | bytes 196616 | tf_op jit(solution)/shard_map/ppermute | solution.py:569
  48.8 2.2 %collective-permute-start.19 = (bf16[256,128]{1,0:T(8,128)(2,1)S(1)}, bf16[256,128]{1,0:T(8,128)(2,1)S(1)}, u32[]{:S(2)}, u32[]{:S(2)}) collective-permute-start(bf16[256,128]{1,0:T(8,128)(2,1)S(1)} %get-tuple-element.93), channel_id=1, source_target_pairs={{0,8},{1,9},{2,10},{3,11},{4,12},{5,13},{6,14},{7,15},{8,0},{9,1},... | collective-permute-start | bytes 196616 | tf_op jit(solution)/shard_map/ppermute | solution.py:569
  51.0 0.2 collective-permute-start.20
  51.2 0.0 collective-permute-done.18.refs_5_
  51.2 4.6 %collective-permute-done.19.refs_6_ = bf16[256,128]{1,0:T(8,128)(2,1)S(1)} collective-permute-done((bf16[256,128]{1,0:T(8,128)(2,1)S(1)}, bf16[256,128]{1,0:T(8,128)(2,1)S(1)}, u32[]{:S(2)}, u32[]{:S(2)}) %collective-permute-start.19) | collective-permute-done | bytes 65568 | tf_op jit(solution)/shard_map/ppermute | solution.py:569
  55.8 1.4 %collective-permute-done.20.refs_7_ = bf16[256,128]{1,0:T(8,128)(2,1)S(1)} collective-permute-done((bf16[256,128]{1,0:T(8,128)(2,1)S(1)}, bf16[256,128]{1,0:T(8,128)(2,1)S(1)}, u32[]{:S(2)}, u32[]{:S(2)}) %collective-permute-start.20) | collective-permute-done | bytes 65568 | tf_op jit(solution)/shard_map/ppermute | solution.py:569
  57.2 1.4 %coadd_detect.1 = (f32[128,512]{1,0:T(8,128)}, f32[128,512]{1,0:T(8,128)}) custom-call(bf16[272,128]{1,0:T(8,128)(2,1)S(1)} %get-tuple-element.77.refs_0_, bf16[272,128]{1,0:T(8,128)(2,1)S(1)} %collective-permute-done.10.refs_1_, bf16[272,128]{1,0:T(8,128)(2,1)S(1)} %collective-permute-done.11.refs_2_, bf16[272,128]{1,0:T(8,128)(2,1)S(1)} %collective-permute-done.12.refs_3_, ...), custom_call_target="tpu_custom_call" | custom-call | tf_op jit(solution)/shard_map/coadd_detect/pallas_call | solution.py:642
  (4 shorter events, 0.0 us)
Async XLA Ops:
  0.6 19.5 %copy-start.1 = (f32[2,41]{1,0:T(2,128)S(1)}, f32[2,41]{1,0:T(2,128)}, u32[]{:S(2)}) copy-start(f32[2,41]{1,0:T(2,128)} %taps_ref.1) | copy-start | bytes 988
  7.3 7.8 %collective-permute-start = (bf16[544,128]{1,0:T(8,128)(2,1)}, bf16[544,128]{1,0:T(8,128)(2,1)S(1)}, u32[]{:S(2)}, u32[]{:S(2)}) collective-permute-start(bf16[544,128]{1,0:T(8,128)(2,1)} %get-tuple-element.51), channel_id=1, source_target_pairs={{0,19},{1,18},{2,17},{3,16},{16,3},{17,2},{18,1},{19,0},{4,23},{5,... | collective-permute-start | bytes 417800 | tf_op jit(solution)/shard_map/ppermute | solution.py:562
  10.7 7.7 %collective-permute-start.5 = (bf16[544,128]{1,0:T(8,128)(2,1)}, bf16[544,128]{1,0:T(8,128)(2,1)S(1)}, u32[]{:S(2)}, u32[]{:S(2)}) collective-permute-start(bf16[544,128]{1,0:T(8,128)(2,1)} %get-tuple-element.63), channel_id=1, source_target_pairs={{0,3},{1,2},{2,1},{3,0},{16,19},{17,18},{18,17},{19,16},{4,7},{5,6... | collective-permute-start | bytes 417800 | tf_op jit(solution)/shard_map/ppermute | solution.py:562
  11.3 13.6 %collective-permute-start.4 = (bf16[1056,128]{1,0:T(8,128)(2,1)}, bf16[1056,128]{1,0:T(8,128)(2,1)S(1)}, u32[]{:S(2)}, u32[]{:S(2)}) collective-permute-start(bf16[1056,128]{1,0:T(8,128)(2,1)} %get-tuple-element.62), channel_id=1, source_target_pairs={{0,16},{1,17},{2,18},{3,19},{16,0},{17,1},{18,2},{19,3},{4,20},{5,... | collective-permute-start | bytes 811016 | tf_op jit(solution)/shard_map/ppermute | solution.py:562
  11.4 10.6 %collective-permute-start.6 = (bf16[544,128]{1,0:T(8,128)(2,1)}, bf16[544,128]{1,0:T(8,128)(2,1)S(1)}, u32[]{:S(2)}, u32[]{:S(2)}) collective-permute-start(bf16[544,128]{1,0:T(8,128)(2,1)} %get-tuple-element.64), channel_id=1, source_target_pairs={{0,1},{1,0},{2,3},{3,2},{16,18},{17,19},{18,16},{19,17},{4,5},{5,4... | collective-permute-start | bytes 417800 | tf_op jit(solution)/shard_map/ppermute | solution.py:562
  13.1 10.3 %collective-permute-start.7 = (bf16[544,128]{1,0:T(8,128)(2,1)}, bf16[544,128]{1,0:T(8,128)(2,1)S(1)}, u32[]{:S(2)}, u32[]{:S(2)}) collective-permute-start(bf16[544,128]{1,0:T(8,128)(2,1)} %get-tuple-element.65), channel_id=1, source_target_pairs={{0,2},{1,3},{2,0},{3,1},{16,17},{17,16},{18,19},{19,18},{4,6},{5,7... | collective-permute-start | bytes 417800 | tf_op jit(solution)/shard_map/ppermute | solution.py:562
  15.1 8.7 %collective-permute-start.8 = (bf16[544,128]{1,0:T(8,128)(2,1)}, bf16[544,128]{1,0:T(8,128)(2,1)S(1)}, u32[]{:S(2)}, u32[]{:S(2)}) collective-permute-start(bf16[544,128]{1,0:T(8,128)(2,1)} %get-tuple-element.66), channel_id=1, source_target_pairs={{0,17},{1,16},{2,19},{3,18},{16,2},{17,3},{18,0},{19,1},{4,21},{5,... | collective-permute-start | bytes 417800 | tf_op jit(solution)/shard_map/ppermute | solution.py:562
  18.4 6.5 %collective-permute-start.9 = (bf16[544,128]{1,0:T(8,128)(2,1)}, bf16[544,128]{1,0:T(8,128)(2,1)S(1)}, u32[]{:S(2)}, u32[]{:S(2)}) collective-permute-start(bf16[544,128]{1,0:T(8,128)(2,1)} %get-tuple-element.67), channel_id=1, source_target_pairs={{0,18},{1,19},{2,16},{3,17},{16,1},{17,0},{18,3},{19,2},{4,22},{5,... | collective-permute-start | bytes 417800 | tf_op jit(solution)/shard_map/ppermute | solution.py:562
  20.1 1.0 %copy-start = (bf16[1056,128]{1,0:T(8,128)(2,1)S(1)}, bf16[1056,128]{1,0:T(8,128)(2,1)}, u32[]{:S(2)}) copy-start(bf16[1056,128]{1,0:T(8,128)(2,1)} %get-tuple-element.52.refs_0_) | copy-start | bytes 811012
  22.0 14.1 %collective-permute-start.1 = (bf16[512,128]{1,0:T(8,128)(2,1)}, bf16[512,128]{1,0:T(8,128)(2,1)S(1)}, u32[]{:S(2)}, u32[]{:S(2)}) collective-permute-start(bf16[512,128]{1,0:T(8,128)(2,1)} %get-tuple-element.58), channel_id=1, source_target_pairs={{0,3},{1,2},{2,1},{3,0},{16,19},{17,18},{18,17},{19,16},{4,7},{5,6... | collective-permute-start | bytes 393224 | tf_op jit(solution)/shard_map/ppermute | solution.py:562
  25.6 5.5 %collective-permute-start.10 = (bf16[272,128]{1,0:T(8,128)(2,1)S(1)}, bf16[272,128]{1,0:T(8,128)(2,1)S(1)}, u32[]{:S(2)}, u32[]{:S(2)}) collective-permute-start(bf16[272,128]{1,0:T(8,128)(2,1)S(1)} %get-tuple-element.69), channel_id=1, source_target_pairs={{0,4},{1,5},{2,6},{3,7},{4,0},{5,1},{6,2},{7,3},{8,12},{9,13},{10,... | collective-permute-start | bytes 208904 | tf_op jit(solution)/shard_map/ppermute | solution.py:569
  27.3 7.3 %collective-permute-start.11 = (bf16[272,128]{1,0:T(8,128)(2,1)S(1)}, bf16[272,128]{1,0:T(8,128)(2,1)S(1)}, u32[]{:S(2)}, u32[]{:S(2)}) collective-permute-start(bf16[272,128]{1,0:T(8,128)(2,1)S(1)} %get-tuple-element.70), channel_id=1, source_target_pairs={{0,8},{1,9},{2,10},{3,11},{4,12},{5,13},{6,14},{7,15},{8,0},{9,1},... | collective-permute-start | bytes 208904 | tf_op jit(solution)/shard_map/ppermute | solution.py:569
  29.9 6.2 %collective-permute-start.12 = (bf16[272,128]{1,0:T(8,128)(2,1)S(1)}, bf16[272,128]{1,0:T(8,128)(2,1)S(1)}, u32[]{:S(2)}, u32[]{:S(2)}) collective-permute-start(bf16[272,128]{1,0:T(8,128)(2,1)S(1)} %get-tuple-element.71), channel_id=1, source_target_pairs={{0,12},{1,13},{2,14},{3,15},{4,8},{5,9},{6,10},{7,11},{8,4},{9,5},... | collective-permute-start | bytes 208904 | tf_op jit(solution)/shard_map/ppermute | solution.py:569
  30.0 7.8 %collective-permute-start.2 = (bf16[512,128]{1,0:T(8,128)(2,1)}, bf16[512,128]{1,0:T(8,128)(2,1)S(1)}, u32[]{:S(2)}, u32[]{:S(2)}) collective-permute-start(bf16[512,128]{1,0:T(8,128)(2,1)} %get-tuple-element.59), channel_id=1, source_target_pairs={{0,19},{1,18},{2,17},{3,16},{16,3},{17,2},{18,1},{19,0},{4,23},{5,... | collective-permute-start | bytes 393224 | tf_op jit(solution)/shard_map/ppermute | solution.py:562
  31.1 7.7 %collective-permute-start.3 = (bf16[512,128]{1,0:T(8,128)(2,1)}, bf16[512,128]{1,0:T(8,128)(2,1)S(1)}, u32[]{:S(2)}, u32[]{:S(2)}) collective-permute-start(bf16[512,128]{1,0:T(8,128)(2,1)} %get-tuple-element.60), channel_id=1, source_target_pairs={{0,1},{1,0},{2,3},{3,2},{16,18},{17,19},{18,16},{19,17},{4,5},{5,4... | collective-permute-start | bytes 393224 | tf_op jit(solution)/shard_map/ppermute | solution.py:562
  34.6 8.2 %collective-permute-start.15 = (bf16[512,128]{1,0:T(8,128)(2,1)}, bf16[512,128]{1,0:T(8,128)(2,1)S(1)}, u32[]{:S(2)}, u32[]{:S(2)}) collective-permute-start(bf16[512,128]{1,0:T(8,128)(2,1)} %get-tuple-element.88), channel_id=1, source_target_pairs={{0,2},{1,3},{2,0},{3,1},{16,17},{17,16},{18,19},{19,18},{4,6},{5,7... | collective-permute-start | bytes 393224 | tf_op jit(solution)/shard_map/ppermute | solution.py:562
  36.1 6.7 %collective-permute-start.16 = (bf16[512,128]{1,0:T(8,128)(2,1)}, bf16[512,128]{1,0:T(8,128)(2,1)S(1)}, u32[]{:S(2)}, u32[]{:S(2)}) collective-permute-start(bf16[512,128]{1,0:T(8,128)(2,1)} %get-tuple-element.89), channel_id=1, source_target_pairs={{0,17},{1,16},{2,19},{3,18},{16,2},{17,3},{18,0},{19,1},{4,21},{5,... | collective-permute-start | bytes 393224 | tf_op jit(solution)/shard_map/ppermute | solution.py:562
  36.1 6.7 %collective-permute-start.17 = (bf16[512,128]{1,0:T(8,128)(2,1)}, bf16[512,128]{1,0:T(8,128)(2,1)S(1)}, u32[]{:S(2)}, u32[]{:S(2)}) collective-permute-start(bf16[512,128]{1,0:T(8,128)(2,1)} %get-tuple-element.90), channel_id=1, source_target_pairs={{0,18},{1,19},{2,16},{3,17},{16,1},{17,0},{18,3},{19,2},{4,22},{5,... | collective-permute-start | bytes 393224 | tf_op jit(solution)/shard_map/ppermute | solution.py:562
  38.9 4.0 %collective-permute-start.13 = (bf16[32,512]{1,0:T(8,128)(2,1)S(1)}, bf16[32,512]{1,0:T(8,128)(2,1)S(1)}, u32[]{:S(2)}, u32[]{:S(2)}) collective-permute-start(bf16[32,512]{1,0:T(8,128)(2,1)S(1)} %get-tuple-element.82), channel_id=1, source_target_pairs={{0,1},{2,3},{4,5},{6,7},{8,9},{10,11},{12,13},{14,15},{16,17},{18,... | collective-permute-start | bytes 98312 | tf_op jit(solution)/shard_map/ppermute | solution.py:626
  40.5 2.4 %collective-permute-start.14 = (bf16[32,512]{1,0:T(8,128)(2,1)S(1)}, bf16[32,512]{1,0:T(8,128)(2,1)S(1)}, u32[]{:S(2)}, u32[]{:S(2)}) collective-permute-start(bf16[32,512]{1,0:T(8,128)(2,1)S(1)} %get-tuple-element.83), channel_id=1, source_target_pairs={{1,2},{3,4},{5,6},{7,8},{9,10},{11,12},{13,14},{15,16},{17,18},{19... | collective-permute-start | bytes 98312 | tf_op jit(solution)/shard_map/ppermute | solution.py:626
  43.5 7.7 %collective-permute-start.18 = (bf16[256,128]{1,0:T(8,128)(2,1)S(1)}, bf16[256,128]{1,0:T(8,128)(2,1)S(1)}, u32[]{:S(2)}, u32[]{:S(2)}) collective-permute-start(bf16[256,128]{1,0:T(8,128)(2,1)S(1)} %get-tuple-element.92), channel_id=1, source_target_pairs={{0,4},{1,5},{2,6},{3,7},{4,0},{5,1},{6,2},{7,3},{8,12},{9,13},{10,... | collective-permute-start | bytes 196616 | tf_op jit(solution)/shard_map/ppermute | solution.py:569
  48.8 7.0 %collective-permute-start.19 = (bf16[256,128]{1,0:T(8,128)(2,1)S(1)}, bf16[256,128]{1,0:T(8,128)(2,1)S(1)}, u32[]{:S(2)}, u32[]{:S(2)}) collective-permute-start(bf16[256,128]{1,0:T(8,128)(2,1)S(1)} %get-tuple-element.93), channel_id=1, source_target_pairs={{0,8},{1,9},{2,10},{3,11},{4,12},{5,13},{6,14},{7,15},{8,0},{9,1},... | collective-permute-start | bytes 196616 | tf_op jit(solution)/shard_map/ppermute | solution.py:569
  51.0 6.2 %collective-permute-start.20 = (bf16[256,128]{1,0:T(8,128)(2,1)S(1)}, bf16[256,128]{1,0:T(8,128)(2,1)S(1)}, u32[]{:S(2)}, u32[]{:S(2)}) collective-permute-start(bf16[256,128]{1,0:T(8,128)(2,1)S(1)} %get-tuple-element.94), channel_id=1, source_target_pairs={{0,12},{1,13},{2,14},{3,15},{4,8},{5,9},{6,10},{7,11},{8,4},{9,5},... | collective-permute-start | bytes 196616 | tf_op jit(solution)/shard_map/ppermute | solution.py:569

commit v11 on v9

--- a/solution.py
+++ b/solution.py
@@ -603,12 +603,12 @@
     later = {k: send[group + i] for i, k in enumerate(others)}
     order = [k for k in peers if k != pn]
     held = lax.optimization_barrier(
-        (edge_blocks[TIED], across, *(later[k] for k in order[:-TAIL]))
-    )
-    across = held[1]
+        (edge_blocks[0], edge_blocks[TIED], across, *(later[k] for k in order[:-TAIL]))
+    )
+    edge_blocks[0], edge_blocks[TIED], across = held[:3]
     kept = lax.optimization_barrier((*edges[1:], *(later[k] for k in order[-TAIL:])))
     edges[1 : 1 + (nz - 1)], kept = kept[: (nz - 1)], kept[(nz - 1) :]
-    inner_blocks = [in_plane(part, k) for part, k in zip((*held[2:], *kept), order)]
+    inner_blocks = [in_plane(part, k) for part, k in zip((*held[3:], *kept), order)]
     first_rows, second_rows = pl.pallas_call(
         edges_kernel,
         out_shape=[shaped((HALO, width), jnp.bfloat16)] * 2,

time: 56.6 us -> 57.9 us (1.023)
  waiting for transfers between devices: 9.37 us -> 12.5 us
  starting transfers between devices: 35.3 us -> 33.5 us
    ppermute x13, waiting for transfers between devices: 6.19 us -> 9.85 us  [in_plane(): return lax.ppermute(part, ('sec', 'p'), pairs)]
    ppermute x13, starting transfers between devices: 20.5 us -> 18.2 us  [in_plane(): return lax.ppermute(part, ('sec', 'p'), pairs)]
  transfers between devices with their start and end apart: 21 -> 21, of which waited for: 10 -> 7; matrix products, arithmetic and copies ran while one was open for 0% -> 0% of each run, Pallas kernels for 3% -> 3%
where the time goes in v11:
time: 57.9 us; the launch traced here: 57.7 us
  starting transfers between devices  33.5 us (58%)
  waiting for transfers between devices  12.5 us (22%)
  Pallas kernels  10.1 us (17%)
  local copies, waits for them, and re-layouts  0.96 us (2%)
  between operations  0.72 us (1%)
    ppermute x13, starting transfers between devices, in_plane(): return lax.ppermute(part, ('sec', 'p'), pairs)  18.2 us
    ppermute x13, waiting for transfers between devices, in_plane(): return lax.ppermute(part, ('sec', 'p'), pairs)  9.85 us
    ppermute x2, starting transfers between devices, swap(): return lax.ppermute(rows, every, pairs + [(j, i) for i, j in pairs])  7.95 us
    ppermute x6, starting transfers between devices, along_z(): return lax.ppermute(part, every, pairs)  7.3 us
    pallas_call x1, Pallas kernels, per_device(): pl.pallas_call(functools.partial(warp_kernel, split), out_shape=[shaped((...  6.64 us
    ppermute x2, waiting for transfers between devices, swap(): return lax.ppermute(rows, every, pairs + [(j, i) for i, j in pairs])  1.91 us
    pallas_call x1, Pallas kernels, per_device(): pl.pallas_call(functools.partial(detect_kernel, nz), out_shape=[shaped((S...  1.38 us
  transfers between devices with their start and end apart: 21, of which 7 were waited for; matrix products, arithmetic and copies ran while one was open for 0% of the time, Pallas kernels for 3%

profile of v11, /device:TPU:1, one launch (start us, length us, event | category | flops | bytes accessed | tf_op | source)
XLA Modules:
  0.0 57.7 jit_solution(6650021480901743441)
XLA Ops:
  0.6 6.6 %warp.1 = (bf16[1056,128]{1,0:T(8,128)(2,1)}, bf16[544,128]{1,0:T(8,128)(2,1)}, bf16[544,128]{1,0:T(8,128)(2,1)}, bf16[544,128]{1,0:T(8,128)(2,1)}, bf16[1056,12...) custom-call(s32[32]{0:T(128)} %bitcast.4, ...), custom_call_target="tpu_custom_call" | custom-call | tf_op jit(solution)/shard_map/warp/pallas_call | solution.py:507
  7.3 0.1 collective-permute-start
  7.4 3.6 %collective-permute-start.2 = (bf16[544,128]{1,0:T(8,128)(2,1)}, bf16[544,128]{1,0:T(8,128)(2,1)S(1)}, u32[]{:S(2)}, u32[]{:S(2)}) collective-permute-start(bf16[544,128]{1,0:T(8,128)(2,1)} %get-tuple-element.49), channel_id=1, source_target_pairs={{0,19},{1,18},{2,17},{3,16},{16,3},{17,2},{18,1},{19,0},{4,23},{5,... | collective-permute-start | bytes 417800 | tf_op jit(solution)/shard_map/ppermute | solution.py:561
  11.0 0.1 collective-permute-start.1
  11.1 1.4 %collective-permute-start.3 = (bf16[544,128]{1,0:T(8,128)(2,1)}, bf16[544,128]{1,0:T(8,128)(2,1)S(1)}, u32[]{:S(2)}, u32[]{:S(2)}) collective-permute-start(bf16[544,128]{1,0:T(8,128)(2,1)} %get-tuple-element.50), channel_id=1, source_target_pairs={{0,1},{1,0},{2,3},{3,2},{16,18},{17,19},{18,16},{19,17},{4,5},{5,4... | collective-permute-start | bytes 417800 | tf_op jit(solution)/shard_map/ppermute | solution.py:561
  12.4 1.2 %collective-permute-start.4 = (bf16[544,128]{1,0:T(8,128)(2,1)}, bf16[544,128]{1,0:T(8,128)(2,1)S(1)}, u32[]{:S(2)}, u32[]{:S(2)}) collective-permute-start(bf16[544,128]{1,0:T(8,128)(2,1)} %get-tuple-element.51), channel_id=1, source_target_pairs={{0,2},{1,3},{2,0},{3,1},{16,17},{17,16},{18,19},{19,18},{4,6},{5,7... | collective-permute-start | bytes 417800 | tf_op jit(solution)/shard_map/ppermute | solution.py:561
  13.6 1.9 %collective-permute-done.2.refs_3_ = bf16[544,128]{1,0:T(8,128)(2,1)S(1)} collective-permute-done((bf16[544,128]{1,0:T(8,128)(2,1)}, bf16[544,128]{1,0:T(8,128)(2,1)S(1)}, u32[]{:S(2)}, u32[]{:S(2)}) %collective-permute-start.2) | collective-permute-done | bytes 139296 | tf_op jit(solution)/shard_map/ppermute | solution.py:561
  15.5 1.1 %collective-permute-start.5 = (bf16[544,128]{1,0:T(8,128)(2,1)}, bf16[544,128]{1,0:T(8,128)(2,1)S(1)}, u32[]{:S(2)}, u32[]{:S(2)}) collective-permute-start(bf16[544,128]{1,0:T(8,128)(2,1)} %get-tuple-element.52), channel_id=1, source_target_pairs={{0,17},{1,16},{2,19},{3,18},{16,2},{17,3},{18,0},{19,1},{4,21},{5,... | collective-permute-start | bytes 417800 | tf_op jit(solution)/shard_map/ppermute | solution.py:561
  16.7 0.0 collective-permute-done.refs_1_
  16.7 0.6 %collective-permute-start.6 = (bf16[544,128]{1,0:T(8,128)(2,1)}, bf16[544,128]{1,0:T(8,128)(2,1)S(1)}, u32[]{:S(2)}, u32[]{:S(2)}) collective-permute-start(bf16[544,128]{1,0:T(8,128)(2,1)} %get-tuple-element.53), channel_id=1, source_target_pairs={{0,18},{1,19},{2,16},{3,17},{16,1},{17,0},{18,3},{19,2},{4,22},{5,... | collective-permute-start | bytes 417800 | tf_op jit(solution)/shard_map/ppermute | solution.py:561
  17.3 1.0 %copy-done = bf16[1056,128]{1,0:T(8,128)(2,1)S(1)} copy-done((bf16[1056,128]{1,0:T(8,128)(2,1)S(1)}, bf16[1056,128]{1,0:T(8,128)(2,1)}, u32[]{:S(2)}) %copy-start) | copy-done | bytes 270360
  18.2 0.8 %matrices.1 = (bf16[2,512,512]{2,1,0:T(8,128)(2,1)S(1)}, bf16[2,128,128]{2,1,0:T(8,128)(2,1)S(1)}, bf16[2,64,64]{2,1,0:T(8,128)(2,1)S(1)}, bf16[1056,128]{1,0:T(8,128)(2,1)S(1)}) custom-call(f32[2,41]{1,0:T(2,128)S(1)} %copy-done.1, bf16[1056,128]{1,0:T(8,128)(2,1)S(1)} %copy-done), custom_call_target="tpu_custom_call" | custom-call | bytes 8388608 | tf_op jit(solution)/shard_map/matrices/pallas_call | solution.py:574
  19.0 0.0 collective-permute-done.1.refs_2_
  19.0 2.7 %collective-permute-start.10 = (bf16[512,128]{1,0:T(8,128)(2,1)}, bf16[512,128]{1,0:T(8,128)(2,1)S(1)}, u32[]{:S(2)}, u32[]{:S(2)}) collective-permute-start(bf16[512,128]{1,0:T(8,128)(2,1)} %get-tuple-element.73), channel_id=1, source_target_pairs={{0,3},{1,2},{2,1},{3,0},{16,19},{17,18},{18,17},{19,16},{4,7},{5,6... | collective-permute-start | bytes 393224 | tf_op jit(solution)/shard_map/ppermute | solution.py:561
  21.7 0.0 collective-permute-done.3.refs_4_
  21.7 0.0 collective-permute-done.4.refs_5_
  21.7 3.5 %collective-permute-done.5.refs_6_ = bf16[544,128]{1,0:T(8,128)(2,1)S(1)} collective-permute-done((bf16[544,128]{1,0:T(8,128)(2,1)}, bf16[544,128]{1,0:T(8,128)(2,1)S(1)}, u32[]{:S(2)}, u32[]{:S(2)}) %collective-permute-start.5) | collective-permute-done | bytes 139296 | tf_op jit(solution)/shard_map/ppermute | solution.py:561
  25.3 0.0 collective-permute-done.6.refs_7_
  25.3 0.7 %edge_sums.1 = (bf16[272,128]{1,0:T(8,128)(2,1)S(1)}, bf16[272,128]{1,0:T(8,128)(2,1)S(1)}, bf16[272,128]{1,0:T(8,128)(2,1)S(1)}, bf16[272,128]{1,0:T(8,128)(2,1)S(1)}, f32[8,4,8,128]{3,2,1,0:T(8,128)S(1)}) custom-call(bf16[1056,128]{1,0:T(8,128)(2,1)S(1)} %get-tuple-element.66.refs_0_, bf16[1056,128]{1,0:T(8,128)(2,1)S(1)} %collective-permute-done.refs_1_, ...), custom_call_target="tpu_custom_call" | custom-call | bytes 4194304 | tf_op jit(solution)/shard_map/edge_sums/pallas_call | solution.py:591
  25.9 2.4 %collective-permute-start.7 = (bf16[272,128]{1,0:T(8,128)(2,1)S(1)}, bf16[272,128]{1,0:T(8,128)(2,1)S(1)}, u32[]{:S(2)}, u32[]{:S(2)}) collective-permute-start(bf16[272,128]{1,0:T(8,128)(2,1)S(1)} %get-tuple-element.55), channel_id=1, source_target_pairs={{0,4},{1,5},{2,6},{3,7},{4,0},{5,1},{6,2},{7,3},{8,12},{9,13},{10,... | collective-permute-start | bytes 208904 | tf_op jit(solution)/shard_map/ppermute | solution.py:568
  28.3 1.1 %collective-permute-start.8 = (bf16[272,128]{1,0:T(8,128)(2,1)S(1)}, bf16[272,128]{1,0:T(8,128)(2,1)S(1)}, u32[]{:S(2)}, u32[]{:S(2)}) collective-permute-start(bf16[272,128]{1,0:T(8,128)(2,1)S(1)} %get-tuple-element.56), channel_id=1, source_target_pairs={{0,8},{1,9},{2,10},{3,11},{4,12},{5,13},{6,14},{7,15},{8,0},{9,1},... | collective-permute-start | bytes 208904 | tf_op jit(solution)/shard_map/ppermute | solution.py:568
  29.4 0.2 collective-permute-start.9
  29.7 2.8 %collective-permute-start.11 = (bf16[512,128]{1,0:T(8,128)(2,1)}, bf16[512,128]{1,0:T(8,128)(2,1)S(1)}, u32[]{:S(2)}, u32[]{:S(2)}) collective-permute-start(bf16[512,128]{1,0:T(8,128)(2,1)} %get-tuple-element.74), channel_id=1, source_target_pairs={{0,19},{1,18},{2,17},{3,16},{16,3},{17,2},{18,1},{19,0},{4,23},{5,... | collective-permute-start | bytes 393224 | tf_op jit(solution)/shard_map/ppermute | solution.py:561
  32.5 0.0 collective-permute-done.7.refs_1_
  32.5 0.2 collective-permute-start.12
  32.7 0.7 %collective-permute-done.8.refs_2_ = bf16[272,128]{1,0:T(8,128)(2,1)S(1)} collective-permute-done((bf16[272,128]{1,0:T(8,128)(2,1)S(1)}, bf16[272,128]{1,0:T(8,128)(2,1)S(1)}, u32[]{:S(2)}, u32[]{:S(2)}) %collective-permute-start.8) | collective-permute-done | bytes 69664 | tf_op jit(solution)/shard_map/ppermute | solution.py:568
  33.4 1.2 %collective-permute-start.13 = (bf16[512,128]{1,0:T(8,128)(2,1)}, bf16[512,128]{1,0:T(8,128)(2,1)S(1)}, u32[]{:S(2)}, u32[]{:S(2)}) collective-permute-start(bf16[512,128]{1,0:T(8,128)(2,1)} %get-tuple-element.76), channel_id=1, source_target_pairs={{0,2},{1,3},{2,0},{3,1},{16,17},{17,16},{18,19},{19,18},{4,6},{5,7... | collective-permute-start | bytes 393224 | tf_op jit(solution)/shard_map/ppermute | solution.py:561
  34.6 0.0 collective-permute-done.9.refs_3_
  34.6 3.0 %collective-permute-start.14 = (bf16[512,128]{1,0:T(8,128)(2,1)}, bf16[512,128]{1,0:T(8,128)(2,1)S(1)}, u32[]{:S(2)}, u32[]{:S(2)}) collective-permute-start(bf16[512,128]{1,0:T(8,128)(2,1)} %get-tuple-element.77), channel_id=1, source_target_pairs={{0,17},{1,16},{2,19},{3,18},{16,2},{17,3},{18,0},{19,1},{4,21},{5,... | collective-permute-start | bytes 393224 | tf_op jit(solution)/shard_map/ppermute | solution.py:561
  37.6 0.0 collective-permute-done.10.refs_2_
  37.6 0.1 collective-permute-start.15
  37.8 0.1 edge_rows.1
  37.8 0.0 collective-permute-done.11.refs_3_
  37.8 0.0 collective-permute-done.12.refs_4_
  37.8 1.6 %collective-permute-done.13.refs_5_ = bf16[512,128]{1,0:T(8,128)(2,1)S(1)} collective-permute-done((bf16[512,128]{1,0:T(8,128)(2,1)}, bf16[512,128]{1,0:T(8,128)(2,1)S(1)}, u32[]{:S(2)}, u32[]{:S(2)}) %collective-permute-start.13) | collective-permute-done | bytes 131104 | tf_op jit(solution)/shard_map/ppermute | solution.py:561
  39.4 2.1 %collective-permute-done.14.refs_6_ = bf16[512,128]{1,0:T(8,128)(2,1)S(1)} collective-permute-done((bf16[512,128]{1,0:T(8,128)(2,1)}, bf16[512,128]{1,0:T(8,128)(2,1)S(1)}, u32[]{:S(2)}, u32[]{:S(2)}) %collective-permute-start.14) | collective-permute-done | bytes 131104 | tf_op jit(solution)/shard_map/ppermute | solution.py:561
  41.5 0.8 %collective-permute-done.15.refs_7_ = bf16[512,128]{1,0:T(8,128)(2,1)S(1)} collective-permute-done((bf16[512,128]{1,0:T(8,128)(2,1)}, bf16[512,128]{1,0:T(8,128)(2,1)S(1)}, u32[]{:S(2)}, u32[]{:S(2)}) %collective-permute-start.15) | collective-permute-done | bytes 131104 | tf_op jit(solution)/shard_map/ppermute | solution.py:561
  42.3 0.6 %inner_sums.1 = (bf16[256,128]{1,0:T(8,128)(2,1)S(1)}, bf16[256,128]{1,0:T(8,128)(2,1)S(1)}, bf16[256,128]{1,0:T(8,128)(2,1)S(1)}, bf16[256,128]{1,0:T(8,128)(2,1)S(1)}) custom-call(f32[8,4,8,128]{3,2,1,0:T(8,128)S(1)} %get-tuple-element.63.weight_ref, bf16[1056,128]{1,0:T(8,128)(2,1)S(1)} %get-tuple-element.66.refs_0_, ...), custom_call_target="tpu_custom_call" | custom-call | bytes 4194304 | tf_op jit(solution)/shard_map/inner_sums/pallas_call | solution.py:628
  42.9 2.7 %collective-permute-start.16 = (bf16[256,128]{1,0:T(8,128)(2,1)S(1)}, bf16[256,128]{1,0:T(8,128)(2,1)S(1)}, u32[]{:S(2)}, u32[]{:S(2)}) collective-permute-start(bf16[256,128]{1,0:T(8,128)(2,1)S(1)} %get-tuple-element.80), channel_id=1, source_target_pairs={{0,4},{1,5},{2,6},{3,7},{4,0},{5,1},{6,2},{7,3},{8,12},{9,13},{10,... | collective-permute-start | bytes 196616 | tf_op jit(solution)/shard_map/ppermute | solution.py:568
  45.6 0.7 %collective-permute-start.17 = (bf16[256,128]{1,0:T(8,128)(2,1)S(1)}, bf16[256,128]{1,0:T(8,128)(2,1)S(1)}, u32[]{:S(2)}, u32[]{:S(2)}) collective-permute-start(bf16[256,128]{1,0:T(8,128)(2,1)S(1)} %get-tuple-element.81), channel_id=1, source_target_pairs={{0,8},{1,9},{2,10},{3,11},{4,12},{5,13},{6,14},{7,15},{8,0},{9,1},... | collective-permute-start | bytes 196616 | tf_op jit(solution)/shard_map/ppermute | solution.py:568
  46.3 0.2 collective-permute-start.18
  46.5 1.1 %collective-permute-start.19 = (bf16[32,512]{1,0:T(8,128)(2,1)S(1)}, bf16[32,512]{1,0:T(8,128)(2,1)S(1)}, u32[]{:S(2)}, u32[]{:S(2)}) collective-permute-start(bf16[32,512]{1,0:T(8,128)(2,1)S(1)} %get-tuple-element.83), channel_id=1, source_target_pairs={{0,1},{2,3},{4,5},{6,7},{8,9},{10,11},{12,13},{14,15},{16,17},{18,... | collective-permute-start | bytes 98312 | tf_op jit(solution)/shard_map/ppermute | solution.py:623
  47.5 6.9 %collective-permute-start.20 = (bf16[32,512]{1,0:T(8,128)(2,1)S(1)}, bf16[32,512]{1,0:T(8,128)(2,1)S(1)}, u32[]{:S(2)}, u32[]{:S(2)}) collective-permute-start(bf16[32,512]{1,0:T(8,128)(2,1)S(1)} %get-tuple-element.84), channel_id=1, source_target_pairs={{1,2},{3,4},{5,6},{7,8},{9,10},{11,12},{13,14},{15,16},{17,18},{19... | collective-permute-start | bytes 98312 | tf_op jit(solution)/shard_map/ppermute | solution.py:623
  54.4 0.0 collective-permute-done.19.refs_8_
  54.4 1.9 %collective-permute-done.20.refs_9_ = bf16[32,512]{1,0:T(8,128)(2,1)S(1)} collective-permute-done((bf16[32,512]{1,0:T(8,128)(2,1)S(1)}, bf16[32,512]{1,0:T(8,128)(2,1)S(1)}, u32[]{:S(2)}, u32[]{:S(2)}) %collective-permute-start.20) | collective-permute-done | bytes 32800 | tf_op jit(solution)/shard_map/ppermute | solution.py:623
  56.3 0.0 collective-permute-done.16.refs_5_
  56.4 0.0 collective-permute-done.17.refs_6_
  56.4 1.4 %coadd_detect.1 = (f32[128,512]{1,0:T(8,128)}, f32[128,512]{1,0:T(8,128)}) custom-call(bf16[272,128]{1,0:T(8,128)(2,1)S(1)} %get-tuple-element.54.refs_0_, bf16[272,128]{1,0:T(8,128)(2,1)S(1)} %collective-permute-done.7.refs_1_, bf16[272,128]{1,0:T(8,128)(2,1)S(1)} %collective-permute-done.8.refs_2_, bf16[272,128]{1,0:T(8,128)(2,1)S(1)} %collective-permute-done.9.refs_3_, ...), custom_call_target="tpu_custom_call" | custom-call | tf_op jit(solution)/shard_map/coadd_detect/pallas_call | solution.py:639
  (4 shorter events, 0.0 us)
Async XLA Ops:
  0.6 16.7 %copy-start.1 = (f32[2,41]{1,0:T(2,128)S(1)}, f32[2,41]{1,0:T(2,128)}, u32[]{:S(2)}) copy-start(f32[2,41]{1,0:T(2,128)} %taps_ref.1) | copy-start | bytes 988
  7.3 9.4 %collective-permute-start = (bf16[1056,128]{1,0:T(8,128)(2,1)}, bf16[1056,128]{1,0:T(8,128)(2,1)S(1)}, u32[]{:S(2)}, u32[]{:S(2)}) collective-permute-start(bf16[1056,128]{1,0:T(8,128)(2,1)} %get-tuple-element.47), channel_id=1, source_target_pairs={{0,16},{1,17},{2,18},{3,19},{16,0},{17,1},{18,2},{19,3},{4,20},{5,... | collective-permute-start | bytes 811016 | tf_op jit(solution)/shard_map/ppermute | solution.py:561
  7.4 8.1 %collective-permute-start.2 = (bf16[544,128]{1,0:T(8,128)(2,1)}, bf16[544,128]{1,0:T(8,128)(2,1)S(1)}, u32[]{:S(2)}, u32[]{:S(2)}) collective-permute-start(bf16[544,128]{1,0:T(8,128)(2,1)} %get-tuple-element.49), channel_id=1, source_target_pairs={{0,19},{1,18},{2,17},{3,16},{16,3},{17,2},{18,1},{19,0},{4,23},{5,... | collective-permute-start | bytes 417800 | tf_op jit(solution)/shard_map/ppermute | solution.py:561
  11.0 8.0 %collective-permute-start.1 = (bf16[544,128]{1,0:T(8,128)(2,1)}, bf16[544,128]{1,0:T(8,128)(2,1)S(1)}, u32[]{:S(2)}, u32[]{:S(2)}) collective-permute-start(bf16[544,128]{1,0:T(8,128)(2,1)} %get-tuple-element.48), channel_id=1, source_target_pairs={{0,3},{1,2},{2,1},{3,0},{16,19},{17,18},{18,17},{19,16},{4,7},{5,6... | collective-permute-start | bytes 417800 | tf_op jit(solution)/shard_map/ppermute | solution.py:561
  11.1 10.7 %collective-permute-start.3 = (bf16[544,128]{1,0:T(8,128)(2,1)}, bf16[544,128]{1,0:T(8,128)(2,1)S(1)}, u32[]{:S(2)}, u32[]{:S(2)}) collective-permute-start(bf16[544,128]{1,0:T(8,128)(2,1)} %get-tuple-element.50), channel_id=1, source_target_pairs={{0,1},{1,0},{2,3},{3,2},{16,18},{17,19},{18,16},{19,17},{4,5},{5,4... | collective-permute-start | bytes 417800 | tf_op jit(solution)/shard_map/ppermute | solution.py:561
  12.4 9.3 %collective-permute-start.4 = (bf16[544,128]{1,0:T(8,128)(2,1)}, bf16[544,128]{1,0:T(8,128)(2,1)S(1)}, u32[]{:S(2)}, u32[]{:S(2)}) collective-permute-start(bf16[544,128]{1,0:T(8,128)(2,1)} %get-tuple-element.51), channel_id=1, source_target_pairs={{0,2},{1,3},{2,0},{3,1},{16,17},{17,16},{18,19},{19,18},{4,6},{5,7... | collective-permute-start | bytes 417800 | tf_op jit(solution)/shard_map/ppermute | solution.py:561
  15.5 9.7 %collective-permute-start.5 = (bf16[544,128]{1,0:T(8,128)(2,1)}, bf16[544,128]{1,0:T(8,128)(2,1)S(1)}, u32[]{:S(2)}, u32[]{:S(2)}) collective-permute-start(bf16[544,128]{1,0:T(8,128)(2,1)} %get-tuple-element.52), channel_id=1, source_target_pairs={{0,17},{1,16},{2,19},{3,18},{16,2},{17,3},{18,0},{19,1},{4,21},{5,... | collective-permute-start | bytes 417800 | tf_op jit(solution)/shard_map/ppermute | solution.py:561
  16.7 8.6 %collective-permute-start.6 = (bf16[544,128]{1,0:T(8,128)(2,1)}, bf16[544,128]{1,0:T(8,128)(2,1)S(1)}, u32[]{:S(2)}, u32[]{:S(2)}) collective-permute-start(bf16[544,128]{1,0:T(8,128)(2,1)} %get-tuple-element.53), channel_id=1, source_target_pairs={{0,18},{1,19},{2,16},{3,17},{16,1},{17,0},{18,3},{19,2},{4,22},{5,... | collective-permute-start | bytes 417800 | tf_op jit(solution)/shard_map/ppermute | solution.py:561
  17.3 1.0 %copy-start = (bf16[1056,128]{1,0:T(8,128)(2,1)S(1)}, bf16[1056,128]{1,0:T(8,128)(2,1)}, u32[]{:S(2)}) copy-start(bf16[1056,128]{1,0:T(8,128)(2,1)} %get-tuple-element.45.refs_0_) | copy-start | bytes 811012
  19.0 18.6 %collective-permute-start.10 = (bf16[512,128]{1,0:T(8,128)(2,1)}, bf16[512,128]{1,0:T(8,128)(2,1)S(1)}, u32[]{:S(2)}, u32[]{:S(2)}) collective-permute-start(bf16[512,128]{1,0:T(8,128)(2,1)} %get-tuple-element.73), channel_id=1, source_target_pairs={{0,3},{1,2},{2,1},{3,0},{16,19},{17,18},{18,17},{19,16},{4,7},{5,6... | collective-permute-start | bytes 393224 | tf_op jit(solution)/shard_map/ppermute | solution.py:561
  25.9 6.6 %collective-permute-start.7 = (bf16[272,128]{1,0:T(8,128)(2,1)S(1)}, bf16[272,128]{1,0:T(8,128)(2,1)S(1)}, u32[]{:S(2)}, u32[]{:S(2)}) collective-permute-start(bf16[272,128]{1,0:T(8,128)(2,1)S(1)} %get-tuple-element.55), channel_id=1, source_target_pairs={{0,4},{1,5},{2,6},{3,7},{4,0},{5,1},{6,2},{7,3},{8,12},{9,13},{10,... | collective-permute-start | bytes 208904 | tf_op jit(solution)/shard_map/ppermute | solution.py:568
  28.3 5.1 %collective-permute-start.8 = (bf16[272,128]{1,0:T(8,128)(2,1)S(1)}, bf16[272,128]{1,0:T(8,128)(2,1)S(1)}, u32[]{:S(2)}, u32[]{:S(2)}) collective-permute-start(bf16[272,128]{1,0:T(8,128)(2,1)S(1)} %get-tuple-element.56), channel_id=1, source_target_pairs={{0,8},{1,9},{2,10},{3,11},{4,12},{5,13},{6,14},{7,15},{8,0},{9,1},... | collective-permute-start | bytes 208904 | tf_op jit(solution)/shard_map/ppermute | solution.py:568
  29.4 5.2 %collective-permute-start.9 = (bf16[272,128]{1,0:T(8,128)(2,1)S(1)}, bf16[272,128]{1,0:T(8,128)(2,1)S(1)}, u32[]{:S(2)}, u32[]{:S(2)}) collective-permute-start(bf16[272,128]{1,0:T(8,128)(2,1)S(1)} %get-tuple-element.57), channel_id=1, source_target_pairs={{0,12},{1,13},{2,14},{3,15},{4,8},{5,9},{6,10},{7,11},{8,4},{9,5},... | collective-permute-start | bytes 208904 | tf_op jit(solution)/shard_map/ppermute | solution.py:568
  29.7 8.2 %collective-permute-start.11 = (bf16[512,128]{1,0:T(8,128)(2,1)}, bf16[512,128]{1,0:T(8,128)(2,1)S(1)}, u32[]{:S(2)}, u32[]{:S(2)}) collective-permute-start(bf16[512,128]{1,0:T(8,128)(2,1)} %get-tuple-element.74), channel_id=1, source_target_pairs={{0,19},{1,18},{2,17},{3,16},{16,3},{17,2},{18,1},{19,0},{4,23},{5,... | collective-permute-start | bytes 393224 | tf_op jit(solution)/shard_map/ppermute | solution.py:561
  32.5 5.3 %collective-permute-start.12 = (bf16[512,128]{1,0:T(8,128)(2,1)}, bf16[512,128]{1,0:T(8,128)(2,1)S(1)}, u32[]{:S(2)}, u32[]{:S(2)}) collective-permute-start(bf16[512,128]{1,0:T(8,128)(2,1)} %get-tuple-element.75), channel_id=1, source_target_pairs={{0,1},{1,0},{2,3},{3,2},{16,18},{17,19},{18,16},{19,17},{4,5},{5,4... | collective-permute-start | bytes 393224 | tf_op jit(solution)/shard_map/ppermute | solution.py:561
  33.4 6.0 %collective-permute-start.13 = (bf16[512,128]{1,0:T(8,128)(2,1)}, bf16[512,128]{1,0:T(8,128)(2,1)S(1)}, u32[]{:S(2)}, u32[]{:S(2)}) collective-permute-start(bf16[512,128]{1,0:T(8,128)(2,1)} %get-tuple-element.76), channel_id=1, source_target_pairs={{0,2},{1,3},{2,0},{3,1},{16,17},{17,16},{18,19},{19,18},{4,6},{5,7... | collective-permute-start | bytes 393224 | tf_op jit(solution)/shard_map/ppermute | solution.py:561
  34.6 6.8 %collective-permute-start.14 = (bf16[512,128]{1,0:T(8,128)(2,1)}, bf16[512,128]{1,0:T(8,128)(2,1)S(1)}, u32[]{:S(2)}, u32[]{:S(2)}) collective-permute-start(bf16[512,128]{1,0:T(8,128)(2,1)} %get-tuple-element.77), channel_id=1, source_target_pairs={{0,17},{1,16},{2,19},{3,18},{16,2},{17,3},{18,0},{19,1},{4,21},{5,... | collective-permute-start | bytes 393224 | tf_op jit(solution)/shard_map/ppermute | solution.py:561
  37.6 4.6 %collective-permute-start.15 = (bf16[512,128]{1,0:T(8,128)(2,1)}, bf16[512,128]{1,0:T(8,128)(2,1)S(1)}, u32[]{:S(2)}, u32[]{:S(2)}) collective-permute-start(bf16[512,128]{1,0:T(8,128)(2,1)} %get-tuple-element.78), channel_id=1, source_target_pairs={{0,18},{1,19},{2,16},{3,17},{16,1},{17,0},{18,3},{19,2},{4,22},{5,... | collective-permute-start | bytes 393224 | tf_op jit(solution)/shard_map/ppermute | solution.py:561
  42.9 13.5 %collective-permute-start.16 = (bf16[256,128]{1,0:T(8,128)(2,1)S(1)}, bf16[256,128]{1,0:T(8,128)(2,1)S(1)}, u32[]{:S(2)}, u32[]{:S(2)}) collective-permute-start(bf16[256,128]{1,0:T(8,128)(2,1)S(1)} %get-tuple-element.80), channel_id=1, source_target_pairs={{0,4},{1,5},{2,6},{3,7},{4,0},{5,1},{6,2},{7,3},{8,12},{9,13},{10,... | collective-permute-start | bytes 196616 | tf_op jit(solution)/shard_map/ppermute | solution.py:568
  45.6 10.8 %collective-permute-start.17 = (bf16[256,128]{1,0:T(8,128)(2,1)S(1)}, bf16[256,128]{1,0:T(8,128)(2,1)S(1)}, u32[]{:S(2)}, u32[]{:S(2)}) collective-permute-start(bf16[256,128]{1,0:T(8,128)(2,1)S(1)} %get-tuple-element.81), channel_id=1, source_target_pairs={{0,8},{1,9},{2,10},{3,11},{4,12},{5,13},{6,14},{7,15},{8,0},{9,1},... | collective-permute-start | bytes 196616 | tf_op jit(solution)/shard_map/ppermute | solution.py:568
  46.3 10.1 %collective-permute-start.18 = (bf16[256,128]{1,0:T(8,128)(2,1)S(1)}, bf16[256,128]{1,0:T(8,128)(2,1)S(1)}, u32[]{:S(2)}, u32[]{:S(2)}) collective-permute-start(bf16[256,128]{1,0:T(8,128)(2,1)S(1)} %get-tuple-element.82), channel_id=1, source_target_pairs={{0,12},{1,13},{2,14},{3,15},{4,8},{5,9},{6,10},{7,11},{8,4},{9,5},... | collective-permute-start | bytes 196616 | tf_op jit(solution)/shard_map/ppermute | solution.py:568
  46.5 8.0 %collective-permute-start.19 = (bf16[32,512]{1,0:T(8,128)(2,1)S(1)}, bf16[32,512]{1,0:T(8,128)(2,1)S(1)}, u32[]{:S(2)}, u32[]{:S(2)}) collective-permute-start(bf16[32,512]{1,0:T(8,128)(2,1)S(1)} %get-tuple-element.83), channel_id=1, source_target_pairs={{0,1},{2,3},{4,5},{6,7},{8,9},{10,11},{12,13},{14,15},{16,17},{18,... | collective-permute-start | bytes 98312 | tf_op jit(solution)/shard_map/ppermute | solution.py:623
  47.5 8.8 %collective-permute-start.20 = (bf16[32,512]{1,0:T(8,128)(2,1)S(1)}, bf16[32,512]{1,0:T(8,128)(2,1)S(1)}, u32[]{:S(2)}, u32[]{:S(2)}) collective-permute-start(bf16[32,512]{1,0:T(8,128)(2,1)S(1)} %get-tuple-element.84), channel_id=1, source_target_pairs={{1,2},{3,4},{5,6},{7,8},{9,10},{11,12},{13,14},{15,16},{17,18},{19... | collective-permute-start | bytes 98312 | tf_op jit(solution)/shard_map/ppermute | solution.py:623

commit v12 on v9

--- a/solution.py
+++ b/solution.py
@@ -412,7 +412,7 @@
 
 def detect_kernel(nz, *refs):
     edges, inner = refs[:nz], refs[nz : 2 * nz]
-    first_ref, second_ref, across_ref, centre_ref, edge_ref = refs[2 * nz : 2 * nz + 5]
+    second_ref, first_ref, across_ref, centre_ref, edge_ref = refs[2 * nz : 2 * nz + 5]
     coadd_ref, out_ref, halo_ref = refs[2 * nz + 5 :]
     odd = lax.axis_index("p") % 2
     halo_ref[pl.ds(pl.multiple_of((1 - odd) * HALO, HALO), HALO)] = first_ref[...]
@@ -623,7 +623,8 @@
         return lax.ppermute(rows, every, pairs + [(j, i) for i, j in pairs])
 
     first_rows, second_rows, own = lax.optimization_barrier((first_rows, second_rows, own))
-    first, second = swap(first_rows, 0), swap(second_rows, 1)
+    second = swap(second_rows, 1)
+    first = swap(first_rows, 0)
 
     inner_sums = pl.pallas_call(
         functools.partial(inner_sum_kernel, nz, group),
@@ -644,7 +645,7 @@
         scratch_shapes=[pltpu.VMEM((2 * HALO, width), jnp.bfloat16)],
         compiler_params=params,
         name="coadd_detect",
-    )(*edges, *inner, first, second, across, centre, edge)
+    )(*edges, *inner, second, first, across, centre, edge)
     return coadd, detection
 
 

time: 56.6 us -> 56.8 us (level)
  waiting for transfers between devices: 9.37 us -> 10 us
    ppermute x2, waiting for transfers between devices: 2.09 us -> 2.75 us  [swap(): return lax.ppermute(rows, every, pairs + [(j, i) for i, j in pairs])]
  transfers between devices with their start and end apart: 21 -> 21, of which waited for: 10 -> 11; matrix products, arithmetic and copies ran while one was open for 0% -> 0% of each run, Pallas kernels for 3% -> 3%
where the time goes in v12:
time: 56.8 us; the launch traced here: 56.6 us
  starting transfers between devices  34.8 us (61%)
  Pallas kernels  10.2 us (18%)
  waiting for transfers between devices  10 us (18%)
  local copies, waits for them, and re-layouts  0.96 us (2%)
  between operations  0.71 us (1%)
    ppermute x13, starting transfers between devices, in_plane(): return lax.ppermute(part, ('sec', 'p'), pairs)  20.5 us
    ppermute x6, starting transfers between devices, along_z(): return lax.ppermute(part, every, pairs)  7.3 us
    ppermute x2, starting transfers between devices, swap(): return lax.ppermute(rows, every, pairs + [(j, i) for i, j in pairs])  6.97 us
    pallas_call x1, Pallas kernels, per_device(): pl.pallas_call(functools.partial(warp_kernel, split), out_shape=[shaped((...  6.64 us
    ppermute x13, waiting for transfers between devices, in_plane(): return lax.ppermute(part, ('sec', 'p'), pairs)  6.19 us
    ppermute x2, waiting for transfers between devices, swap(): return lax.ppermute(rows, every, pairs + [(j, i) for i, j in pairs])  2.75 us
    pallas_call x1, Pallas kernels, per_device(): pl.pallas_call(functools.partial(detect_kernel, nz), out_shape=[shaped((S...  1.38 us
  transfers between devices with their start and end apart: 21, of which 11 were waited for; matrix products, arithmetic and copies ran while one was open for 0% of the time, Pallas kernels for 3%

profile of v12, /device:TPU:1, one launch (start us, length us, event | category | flops | bytes accessed | tf_op | source)
XLA Modules:
  0.0 56.6 jit_solution(12291174045858631362)
XLA Ops:
  0.6 6.6 %warp.1 = (bf16[1056,128]{1,0:T(8,128)(2,1)}, bf16[544,128]{1,0:T(8,128)(2,1)}, bf16[544,128]{1,0:T(8,128)(2,1)}, bf16[544,128]{1,0:T(8,128)(2,1)}, bf16[1056,12...) custom-call(s32[32]{0:T(128)} %bitcast.4, ...), custom_call_target="tpu_custom_call" | custom-call | tf_op jit(solution)/shard_map/warp/pallas_call | solution.py:507
  7.3 3.1 %collective-permute-start.1 = (bf16[544,128]{1,0:T(8,128)(2,1)}, bf16[544,128]{1,0:T(8,128)(2,1)S(1)}, u32[]{:S(2)}, u32[]{:S(2)}) collective-permute-start(bf16[544,128]{1,0:T(8,128)(2,1)} %get-tuple-element.47), channel_id=1, source_target_pairs={{0,3},{1,2},{2,1},{3,0},{16,19},{17,18},{18,17},{19,16},{4,7},{5,6... | collective-permute-start | bytes 417800 | tf_op jit(solution)/shard_map/ppermute | solution.py:561
  10.4 0.6 %collective-permute-start.2 = (bf16[544,128]{1,0:T(8,128)(2,1)}, bf16[544,128]{1,0:T(8,128)(2,1)S(1)}, u32[]{:S(2)}, u32[]{:S(2)}) collective-permute-start(bf16[544,128]{1,0:T(8,128)(2,1)} %get-tuple-element.48), channel_id=1, source_target_pairs={{0,19},{1,18},{2,17},{3,16},{16,3},{17,2},{18,1},{19,0},{4,23},{5,... | collective-permute-start | bytes 417800 | tf_op jit(solution)/shard_map/ppermute | solution.py:561
  11.0 0.3 collective-permute-start
  11.3 1.3 %collective-permute-start.3 = (bf16[544,128]{1,0:T(8,128)(2,1)}, bf16[544,128]{1,0:T(8,128)(2,1)S(1)}, u32[]{:S(2)}, u32[]{:S(2)}) collective-permute-start(bf16[544,128]{1,0:T(8,128)(2,1)} %get-tuple-element.49), channel_id=1, source_target_pairs={{0,1},{1,0},{2,3},{3,2},{16,18},{17,19},{18,16},{19,17},{4,5},{5,4... | collective-permute-start | bytes 417800 | tf_op jit(solution)/shard_map/ppermute | solution.py:561
  12.6 1.2 %collective-permute-start.4 = (bf16[544,128]{1,0:T(8,128)(2,1)}, bf16[544,128]{1,0:T(8,128)(2,1)S(1)}, u32[]{:S(2)}, u32[]{:S(2)}) collective-permute-start(bf16[544,128]{1,0:T(8,128)(2,1)} %get-tuple-element.50), channel_id=1, source_target_pairs={{0,2},{1,3},{2,0},{3,1},{16,17},{17,16},{18,19},{19,18},{4,6},{5,7... | collective-permute-start | bytes 417800 | tf_op jit(solution)/shard_map/ppermute | solution.py:561
  13.8 0.1 collective-permute-done.1.refs_2_
  14.0 3.7 %collective-permute-start.5 = (bf16[544,128]{1,0:T(8,128)(2,1)}, bf16[544,128]{1,0:T(8,128)(2,1)S(1)}, u32[]{:S(2)}, u32[]{:S(2)}) collective-permute-start(bf16[544,128]{1,0:T(8,128)(2,1)} %get-tuple-element.51), channel_id=1, source_target_pairs={{0,17},{1,16},{2,19},{3,18},{16,2},{17,3},{18,0},{19,1},{4,21},{5,... | collective-permute-start | bytes 417800 | tf_op jit(solution)/shard_map/ppermute | solution.py:561
  17.7 0.0 collective-permute-done.2.refs_3_
  17.7 1.1 %collective-permute-start.6 = (bf16[544,128]{1,0:T(8,128)(2,1)}, bf16[544,128]{1,0:T(8,128)(2,1)S(1)}, u32[]{:S(2)}, u32[]{:S(2)}) collective-permute-start(bf16[544,128]{1,0:T(8,128)(2,1)} %get-tuple-element.52), channel_id=1, source_target_pairs={{0,18},{1,19},{2,16},{3,17},{16,1},{17,0},{18,3},{19,2},{4,22},{5,... | collective-permute-start | bytes 417800 | tf_op jit(solution)/shard_map/ppermute | solution.py:561
  18.8 1.0 %copy-done = bf16[1056,128]{1,0:T(8,128)(2,1)S(1)} copy-done((bf16[1056,128]{1,0:T(8,128)(2,1)S(1)}, bf16[1056,128]{1,0:T(8,128)(2,1)}, u32[]{:S(2)}) %copy-start) | copy-done | bytes 270360
  19.8 0.8 %matrices.1 = (bf16[2,512,512]{2,1,0:T(8,128)(2,1)S(1)}, bf16[2,128,128]{2,1,0:T(8,128)(2,1)S(1)}, bf16[2,64,64]{2,1,0:T(8,128)(2,1)S(1)}, bf16[1056,128]{1,0:T(8,128)(2,1)S(1)}) custom-call(f32[2,41]{1,0:T(2,128)S(1)} %copy-done.1, bf16[1056,128]{1,0:T(8,128)(2,1)S(1)} %copy-done), custom_call_target="tpu_custom_call" | custom-call | bytes 8388608 | tf_op jit(solution)/shard_map/matrices/pallas_call | solution.py:574
  20.5 0.1 collective-permute-done.3.refs_4_
  20.7 2.4 %collective-permute-start.10 = (bf16[512,128]{1,0:T(8,128)(2,1)}, bf16[512,128]{1,0:T(8,128)(2,1)S(1)}, u32[]{:S(2)}, u32[]{:S(2)}) collective-permute-start(bf16[512,128]{1,0:T(8,128)(2,1)} %get-tuple-element.71), channel_id=1, source_target_pairs={{0,3},{1,2},{2,1},{3,0},{16,19},{17,18},{18,17},{19,16},{4,7},{5,6... | collective-permute-start | bytes 393224 | tf_op jit(solution)/shard_map/ppermute | solution.py:561
  23.0 0.0 collective-permute-done.4.refs_5_
  23.0 0.5 collective-permute-done.5.refs_6_
  23.6 0.2 collective-permute-done.6.refs_7_
  23.8 0.0 collective-permute-done.refs_1_
  23.8 0.7 %edge_sums.1 = (bf16[272,128]{1,0:T(8,128)(2,1)S(1)}, bf16[272,128]{1,0:T(8,128)(2,1)S(1)}, bf16[272,128]{1,0:T(8,128)(2,1)S(1)}, bf16[272,128]{1,0:T(8,128)(2,1)S(1)}, f32[8,4,8,128]{3,2,1,0:T(8,128)S(1)}) custom-call(bf16[1056,128]{1,0:T(8,128)(2,1)S(1)} %get-tuple-element.65.refs_0_, bf16[1056,128]{1,0:T(8,128)(2,1)S(1)} %collective-permute-done.refs_1_, ...), custom_call_target="tpu_custom_call" | custom-call | bytes 4194304 | tf_op jit(solution)/shard_map/edge_sums/pallas_call | solution.py:591
  24.4 2.6 %collective-permute-start.7 = (bf16[272,128]{1,0:T(8,128)(2,1)S(1)}, bf16[272,128]{1,0:T(8,128)(2,1)S(1)}, u32[]{:S(2)}, u32[]{:S(2)}) collective-permute-start(bf16[272,128]{1,0:T(8,128)(2,1)S(1)} %get-tuple-element.54), channel_id=1, source_target_pairs={{0,4},{1,5},{2,6},{3,7},{4,0},{5,1},{6,2},{7,3},{8,12},{9,13},{10,... | collective-permute-start | bytes 208904 | tf_op jit(solution)/shard_map/ppermute | solution.py:568
  27.0 1.1 %collective-permute-start.8 = (bf16[272,128]{1,0:T(8,128)(2,1)S(1)}, bf16[272,128]{1,0:T(8,128)(2,1)S(1)}, u32[]{:S(2)}, u32[]{:S(2)}) collective-permute-start(bf16[272,128]{1,0:T(8,128)(2,1)S(1)} %get-tuple-element.55), channel_id=1, source_target_pairs={{0,8},{1,9},{2,10},{3,11},{4,12},{5,13},{6,14},{7,15},{8,0},{9,1},... | collective-permute-start | bytes 208904 | tf_op jit(solution)/shard_map/ppermute | solution.py:568
  28.1 0.2 collective-permute-start.9
  28.3 2.3 %collective-permute-start.11 = (bf16[512,128]{1,0:T(8,128)(2,1)}, bf16[512,128]{1,0:T(8,128)(2,1)S(1)}, u32[]{:S(2)}, u32[]{:S(2)}) collective-permute-start(bf16[512,128]{1,0:T(8,128)(2,1)} %get-tuple-element.72), channel_id=1, source_target_pairs={{0,19},{1,18},{2,17},{3,16},{16,3},{17,2},{18,1},{19,0},{4,23},{5,... | collective-permute-start | bytes 393224 | tf_op jit(solution)/shard_map/ppermute | solution.py:561
  30.6 0.0 collective-permute-done.7.refs_1_
  30.6 0.7 %collective-permute-start.12 = (bf16[512,128]{1,0:T(8,128)(2,1)}, bf16[512,128]{1,0:T(8,128)(2,1)S(1)}, u32[]{:S(2)}, u32[]{:S(2)}) collective-permute-start(bf16[512,128]{1,0:T(8,128)(2,1)} %get-tuple-element.73), channel_id=1, source_target_pairs={{0,1},{1,0},{2,3},{3,2},{16,18},{17,19},{18,16},{19,17},{4,5},{5,4... | collective-permute-start | bytes 393224 | tf_op jit(solution)/shard_map/ppermute | solution.py:561
  31.4 1.1 %collective-permute-done.8.refs_2_ = bf16[272,128]{1,0:T(8,128)(2,1)S(1)} collective-permute-done((bf16[272,128]{1,0:T(8,128)(2,1)S(1)}, bf16[272,128]{1,0:T(8,128)(2,1)S(1)}, u32[]{:S(2)}, u32[]{:S(2)}) %collective-permute-start.8) | collective-permute-done | bytes 69664 | tf_op jit(solution)/shard_map/ppermute | solution.py:568
  32.5 0.7 %collective-permute-start.13 = (bf16[512,128]{1,0:T(8,128)(2,1)}, bf16[512,128]{1,0:T(8,128)(2,1)S(1)}, u32[]{:S(2)}, u32[]{:S(2)}) collective-permute-start(bf16[512,128]{1,0:T(8,128)(2,1)} %get-tuple-element.74), channel_id=1, source_target_pairs={{0,2},{1,3},{2,0},{3,1},{16,17},{17,16},{18,19},{19,18},{4,6},{5,7... | collective-permute-start | bytes 393224 | tf_op jit(solution)/shard_map/ppermute | solution.py:561
  33.2 0.0 collective-permute-done.9.refs_3_
  33.2 2.9 %collective-permute-start.14 = (bf16[512,128]{1,0:T(8,128)(2,1)}, bf16[512,128]{1,0:T(8,128)(2,1)S(1)}, u32[]{:S(2)}, u32[]{:S(2)}) collective-permute-start(bf16[512,128]{1,0:T(8,128)(2,1)} %get-tuple-element.75), channel_id=1, source_target_pairs={{0,17},{1,16},{2,19},{3,18},{16,2},{17,3},{18,0},{19,1},{4,21},{5,... | collective-permute-start | bytes 393224 | tf_op jit(solution)/shard_map/ppermute | solution.py:561
  36.0 0.0 collective-permute-done.10.refs_2_
  36.0 0.1 collective-permute-start.15
  36.1 0.1 edge_rows.1
  36.2 0.0 collective-permute-done.11.refs_3_
  36.2 0.7 %collective-permute-done.12.refs_4_ = bf16[512,128]{1,0:T(8,128)(2,1)S(1)} collective-permute-done((bf16[512,128]{1,0:T(8,128)(2,1)}, bf16[512,128]{1,0:T(8,128)(2,1)S(1)}, u32[]{:S(2)}, u32[]{:S(2)}) %collective-permute-start.12) | collective-permute-done | bytes 131104 | tf_op jit(solution)/shard_map/ppermute | solution.py:561
  36.9 1.4 %collective-permute-done.13.refs_5_ = bf16[512,128]{1,0:T(8,128)(2,1)S(1)} collective-permute-done((bf16[512,128]{1,0:T(8,128)(2,1)}, bf16[512,128]{1,0:T(8,128)(2,1)S(1)}, u32[]{:S(2)}, u32[]{:S(2)}) %collective-permute-start.13) | collective-permute-done | bytes 131104 | tf_op jit(solution)/shard_map/ppermute | solution.py:561
  38.3 2.3 %collective-permute-done.14.refs_6_ = bf16[512,128]{1,0:T(8,128)(2,1)S(1)} collective-permute-done((bf16[512,128]{1,0:T(8,128)(2,1)}, bf16[512,128]{1,0:T(8,128)(2,1)S(1)}, u32[]{:S(2)}, u32[]{:S(2)}) %collective-permute-start.14) | collective-permute-done | bytes 131104 | tf_op jit(solution)/shard_map/ppermute | solution.py:561
  40.6 0.8 %collective-permute-done.15.refs_7_ = bf16[512,128]{1,0:T(8,128)(2,1)S(1)} collective-permute-done((bf16[512,128]{1,0:T(8,128)(2,1)}, bf16[512,128]{1,0:T(8,128)(2,1)S(1)}, u32[]{:S(2)}, u32[]{:S(2)}) %collective-permute-start.15) | collective-permute-done | bytes 131104 | tf_op jit(solution)/shard_map/ppermute | solution.py:561
  41.4 0.6 %inner_sums.1 = (bf16[256,128]{1,0:T(8,128)(2,1)S(1)}, bf16[256,128]{1,0:T(8,128)(2,1)S(1)}, bf16[256,128]{1,0:T(8,128)(2,1)S(1)}, bf16[256,128]{1,0:T(8,128)(2,1)S(1)}) custom-call(f32[8,4,8,128]{3,2,1,0:T(8,128)S(1)} %get-tuple-element.62.weight_ref, bf16[1056,128]{1,0:T(8,128)(2,1)S(1)} %get-tuple-element.65.refs_0_, ...), custom_call_target="tpu_custom_call" | custom-call | bytes 4194304 | tf_op jit(solution)/shard_map/inner_sums/pallas_call | solution.py:629
  42.0 1.8 %collective-permute-start.16 = (bf16[256,128]{1,0:T(8,128)(2,1)S(1)}, bf16[256,128]{1,0:T(8,128)(2,1)S(1)}, u32[]{:S(2)}, u32[]{:S(2)}) collective-permute-start(bf16[256,128]{1,0:T(8,128)(2,1)S(1)} %get-tuple-element.78), channel_id=1, source_target_pairs={{0,4},{1,5},{2,6},{3,7},{4,0},{5,1},{6,2},{7,3},{8,12},{9,13},{10,... | collective-permute-start | bytes 196616 | tf_op jit(solution)/shard_map/ppermute | solution.py:568
  43.8 1.4 %collective-permute-start.17 = (bf16[256,128]{1,0:T(8,128)(2,1)S(1)}, bf16[256,128]{1,0:T(8,128)(2,1)S(1)}, u32[]{:S(2)}, u32[]{:S(2)}) collective-permute-start(bf16[256,128]{1,0:T(8,128)(2,1)S(1)} %get-tuple-element.79), channel_id=1, source_target_pairs={{0,8},{1,9},{2,10},{3,11},{4,12},{5,13},{6,14},{7,15},{8,0},{9,1},... | collective-permute-start | bytes 196616 | tf_op jit(solution)/shard_map/ppermute | solution.py:568
  45.3 0.2 collective-permute-start.18
  45.5 6.9 %collective-permute-start.19 = (bf16[32,512]{1,0:T(8,128)(2,1)S(1)}, bf16[32,512]{1,0:T(8,128)(2,1)S(1)}, u32[]{:S(2)}, u32[]{:S(2)}) collective-permute-start(bf16[32,512]{1,0:T(8,128)(2,1)S(1)} %get-tuple-element.81), channel_id=1, source_target_pairs={{1,2},{3,4},{5,6},{7,8},{9,10},{11,12},{13,14},{15,16},{17,18},{19... | collective-permute-start | bytes 98312 | tf_op jit(solution)/shard_map/ppermute | solution.py:623
  52.4 0.1 collective-permute-start.20
  52.5 1.8 %collective-permute-done.19.refs_8_ = bf16[32,512]{1,0:T(8,128)(2,1)S(1)} collective-permute-done((bf16[32,512]{1,0:T(8,128)(2,1)S(1)}, bf16[32,512]{1,0:T(8,128)(2,1)S(1)}, u32[]{:S(2)}, u32[]{:S(2)}) %collective-permute-start.19) | collective-permute-done | bytes 32800 | tf_op jit(solution)/shard_map/ppermute | solution.py:623
  54.3 0.9 %collective-permute-done.20.refs_9_ = bf16[32,512]{1,0:T(8,128)(2,1)S(1)} collective-permute-done((bf16[32,512]{1,0:T(8,128)(2,1)S(1)}, bf16[32,512]{1,0:T(8,128)(2,1)S(1)}, u32[]{:S(2)}, u32[]{:S(2)}) %collective-permute-start.20) | collective-permute-done | bytes 32800 | tf_op jit(solution)/shard_map/ppermute | solution.py:623
  55.2 0.0 collective-permute-done.16.refs_5_
  55.2 0.0 collective-permute-done.17.refs_6_
  55.2 1.4 %coadd_detect.1 = (f32[128,512]{1,0:T(8,128)}, f32[128,512]{1,0:T(8,128)}) custom-call(bf16[272,128]{1,0:T(8,128)(2,1)S(1)} %get-tuple-element.53.refs_0_, bf16[272,128]{1,0:T(8,128)(2,1)S(1)} %collective-permute-done.7.refs_1_, bf16[272,128]{1,0:T(8,128)(2,1)S(1)} %collective-permute-done.8.refs_2_, bf16[272,128]{1,0:T(8,128)(2,1)S(1)} %collective-permute-done.9.refs_3_, ...), custom_call_target="tpu_custom_call" | custom-call | tf_op jit(solution)/shard_map/coadd_detect/pallas_call | solution.py:640
  (4 shorter events, 0.0 us)
Async XLA Ops:
  0.6 18.2 %copy-start.1 = (f32[2,41]{1,0:T(2,128)S(1)}, f32[2,41]{1,0:T(2,128)}, u32[]{:S(2)}) copy-start(f32[2,41]{1,0:T(2,128)} %taps_ref.1) | copy-start | bytes 988
  7.3 6.7 %collective-permute-start.1 = (bf16[544,128]{1,0:T(8,128)(2,1)}, bf16[544,128]{1,0:T(8,128)(2,1)S(1)}, u32[]{:S(2)}, u32[]{:S(2)}) collective-permute-start(bf16[544,128]{1,0:T(8,128)(2,1)} %get-tuple-element.47), channel_id=1, source_target_pairs={{0,3},{1,2},{2,1},{3,0},{16,19},{17,18},{18,17},{19,16},{4,7},{5,6... | collective-permute-start | bytes 417800 | tf_op jit(solution)/shard_map/ppermute | solution.py:561
  10.4 7.3 %collective-permute-start.2 = (bf16[544,128]{1,0:T(8,128)(2,1)}, bf16[544,128]{1,0:T(8,128)(2,1)S(1)}, u32[]{:S(2)}, u32[]{:S(2)}) collective-permute-start(bf16[544,128]{1,0:T(8,128)(2,1)} %get-tuple-element.48), channel_id=1, source_target_pairs={{0,19},{1,18},{2,17},{3,16},{16,3},{17,2},{18,1},{19,0},{4,23},{5,... | collective-permute-start | bytes 417800 | tf_op jit(solution)/shard_map/ppermute | solution.py:561
  11.0 12.8 %collective-permute-start = (bf16[1056,128]{1,0:T(8,128)(2,1)}, bf16[1056,128]{1,0:T(8,128)(2,1)S(1)}, u32[]{:S(2)}, u32[]{:S(2)}) collective-permute-start(bf16[1056,128]{1,0:T(8,128)(2,1)} %get-tuple-element.46), channel_id=1, source_target_pairs={{0,16},{1,17},{2,18},{3,19},{16,0},{17,1},{18,2},{19,3},{4,20},{5,... | collective-permute-start | bytes 811016 | tf_op jit(solution)/shard_map/ppermute | solution.py:561
  11.3 9.4 %collective-permute-start.3 = (bf16[544,128]{1,0:T(8,128)(2,1)}, bf16[544,128]{1,0:T(8,128)(2,1)S(1)}, u32[]{:S(2)}, u32[]{:S(2)}) collective-permute-start(bf16[544,128]{1,0:T(8,128)(2,1)} %get-tuple-element.49), channel_id=1, source_target_pairs={{0,1},{1,0},{2,3},{3,2},{16,18},{17,19},{18,16},{19,17},{4,5},{5,4... | collective-permute-start | bytes 417800 | tf_op jit(solution)/shard_map/ppermute | solution.py:561
  12.6 10.4 %collective-permute-start.4 = (bf16[544,128]{1,0:T(8,128)(2,1)}, bf16[544,128]{1,0:T(8,128)(2,1)S(1)}, u32[]{:S(2)}, u32[]{:S(2)}) collective-permute-start(bf16[544,128]{1,0:T(8,128)(2,1)} %get-tuple-element.50), channel_id=1, source_target_pairs={{0,2},{1,3},{2,0},{3,1},{16,17},{17,16},{18,19},{19,18},{4,6},{5,7... | collective-permute-start | bytes 417800 | tf_op jit(solution)/shard_map/ppermute | solution.py:561
  14.0 9.6 %collective-permute-start.5 = (bf16[544,128]{1,0:T(8,128)(2,1)}, bf16[544,128]{1,0:T(8,128)(2,1)S(1)}, u32[]{:S(2)}, u32[]{:S(2)}) collective-permute-start(bf16[544,128]{1,0:T(8,128)(2,1)} %get-tuple-element.51), channel_id=1, source_target_pairs={{0,17},{1,16},{2,19},{3,18},{16,2},{17,3},{18,0},{19,1},{4,21},{5,... | collective-permute-start | bytes 417800 | tf_op jit(solution)/shard_map/ppermute | solution.py:561
  17.7 6.1 %collective-permute-start.6 = (bf16[544,128]{1,0:T(8,128)(2,1)}, bf16[544,128]{1,0:T(8,128)(2,1)S(1)}, u32[]{:S(2)}, u32[]{:S(2)}) collective-permute-start(bf16[544,128]{1,0:T(8,128)(2,1)} %get-tuple-element.52), channel_id=1, source_target_pairs={{0,18},{1,19},{2,16},{3,17},{16,1},{17,0},{18,3},{19,2},{4,22},{5,... | collective-permute-start | bytes 417800 | tf_op jit(solution)/shard_map/ppermute | solution.py:561
  18.8 1.0 %copy-start = (bf16[1056,128]{1,0:T(8,128)(2,1)S(1)}, bf16[1056,128]{1,0:T(8,128)(2,1)}, u32[]{:S(2)}) copy-start(bf16[1056,128]{1,0:T(8,128)(2,1)} %get-tuple-element.44.refs_0_) | copy-start | bytes 811012
  20.7 15.4 %collective-permute-start.10 = (bf16[512,128]{1,0:T(8,128)(2,1)}, bf16[512,128]{1,0:T(8,128)(2,1)S(1)}, u32[]{:S(2)}, u32[]{:S(2)}) collective-permute-start(bf16[512,128]{1,0:T(8,128)(2,1)} %get-tuple-element.71), channel_id=1, source_target_pairs={{0,3},{1,2},{2,1},{3,0},{16,19},{17,18},{18,17},{19,16},{4,7},{5,6... | collective-permute-start | bytes 393224 | tf_op jit(solution)/shard_map/ppermute | solution.py:561
  24.4 6.2 %collective-permute-start.7 = (bf16[272,128]{1,0:T(8,128)(2,1)S(1)}, bf16[272,128]{1,0:T(8,128)(2,1)S(1)}, u32[]{:S(2)}, u32[]{:S(2)}) collective-permute-start(bf16[272,128]{1,0:T(8,128)(2,1)S(1)} %get-tuple-element.54), channel_id=1, source_target_pairs={{0,4},{1,5},{2,6},{3,7},{4,0},{5,1},{6,2},{7,3},{8,12},{9,13},{10,... | collective-permute-start | bytes 208904 | tf_op jit(solution)/shard_map/ppermute | solution.py:568
  27.0 5.4 %collective-permute-start.8 = (bf16[272,128]{1,0:T(8,128)(2,1)S(1)}, bf16[272,128]{1,0:T(8,128)(2,1)S(1)}, u32[]{:S(2)}, u32[]{:S(2)}) collective-permute-start(bf16[272,128]{1,0:T(8,128)(2,1)S(1)} %get-tuple-element.55), channel_id=1, source_target_pairs={{0,8},{1,9},{2,10},{3,11},{4,12},{5,13},{6,14},{7,15},{8,0},{9,1},... | collective-permute-start | bytes 208904 | tf_op jit(solution)/shard_map/ppermute | solution.py:568
  28.1 5.1 %collective-permute-start.9 = (bf16[272,128]{1,0:T(8,128)(2,1)S(1)}, bf16[272,128]{1,0:T(8,128)(2,1)S(1)}, u32[]{:S(2)}, u32[]{:S(2)}) collective-permute-start(bf16[272,128]{1,0:T(8,128)(2,1)S(1)} %get-tuple-element.56), channel_id=1, source_target_pairs={{0,12},{1,13},{2,14},{3,15},{4,8},{5,9},{6,10},{7,11},{8,4},{9,5},... | collective-permute-start | bytes 208904 | tf_op jit(solution)/shard_map/ppermute | solution.py:568
  28.3 7.9 %collective-permute-start.11 = (bf16[512,128]{1,0:T(8,128)(2,1)}, bf16[512,128]{1,0:T(8,128)(2,1)S(1)}, u32[]{:S(2)}, u32[]{:S(2)}) collective-permute-start(bf16[512,128]{1,0:T(8,128)(2,1)} %get-tuple-element.72), channel_id=1, source_target_pairs={{0,19},{1,18},{2,17},{3,16},{16,3},{17,2},{18,1},{19,0},{4,23},{5,... | collective-permute-start | bytes 393224 | tf_op jit(solution)/shard_map/ppermute | solution.py:561
  30.6 6.3 %collective-permute-start.12 = (bf16[512,128]{1,0:T(8,128)(2,1)}, bf16[512,128]{1,0:T(8,128)(2,1)S(1)}, u32[]{:S(2)}, u32[]{:S(2)}) collective-permute-start(bf16[512,128]{1,0:T(8,128)(2,1)} %get-tuple-element.73), channel_id=1, source_target_pairs={{0,1},{1,0},{2,3},{3,2},{16,18},{17,19},{18,16},{19,17},{4,5},{5,4... | collective-permute-start | bytes 393224 | tf_op jit(solution)/shard_map/ppermute | solution.py:561
  32.5 5.9 %collective-permute-start.13 = (bf16[512,128]{1,0:T(8,128)(2,1)}, bf16[512,128]{1,0:T(8,128)(2,1)S(1)}, u32[]{:S(2)}, u32[]{:S(2)}) collective-permute-start(bf16[512,128]{1,0:T(8,128)(2,1)} %get-tuple-element.74), channel_id=1, source_target_pairs={{0,2},{1,3},{2,0},{3,1},{16,17},{17,16},{18,19},{19,18},{4,6},{5,7... | collective-permute-start | bytes 393224 | tf_op jit(solution)/shard_map/ppermute | solution.py:561
  33.2 7.5 %collective-permute-start.14 = (bf16[512,128]{1,0:T(8,128)(2,1)}, bf16[512,128]{1,0:T(8,128)(2,1)S(1)}, u32[]{:S(2)}, u32[]{:S(2)}) collective-permute-start(bf16[512,128]{1,0:T(8,128)(2,1)} %get-tuple-element.75), channel_id=1, source_target_pairs={{0,17},{1,16},{2,19},{3,18},{16,2},{17,3},{18,0},{19,1},{4,21},{5,... | collective-permute-start | bytes 393224 | tf_op jit(solution)/shard_map/ppermute | solution.py:561
  36.0 5.4 %collective-permute-start.15 = (bf16[512,128]{1,0:T(8,128)(2,1)}, bf16[512,128]{1,0:T(8,128)(2,1)S(1)}, u32[]{:S(2)}, u32[]{:S(2)}) collective-permute-start(bf16[512,128]{1,0:T(8,128)(2,1)} %get-tuple-element.76), channel_id=1, source_target_pairs={{0,18},{1,19},{2,16},{3,17},{16,1},{17,0},{18,3},{19,2},{4,22},{5,... | collective-permute-start | bytes 393224 | tf_op jit(solution)/shard_map/ppermute | solution.py:561
  42.0 13.2 %collective-permute-start.16 = (bf16[256,128]{1,0:T(8,128)(2,1)S(1)}, bf16[256,128]{1,0:T(8,128)(2,1)S(1)}, u32[]{:S(2)}, u32[]{:S(2)}) collective-permute-start(bf16[256,128]{1,0:T(8,128)(2,1)S(1)} %get-tuple-element.78), channel_id=1, source_target_pairs={{0,4},{1,5},{2,6},{3,7},{4,0},{5,1},{6,2},{7,3},{8,12},{9,13},{10,... | collective-permute-start | bytes 196616 | tf_op jit(solution)/shard_map/ppermute | solution.py:568
  43.8 11.4 %collective-permute-start.17 = (bf16[256,128]{1,0:T(8,128)(2,1)S(1)}, bf16[256,128]{1,0:T(8,128)(2,1)S(1)}, u32[]{:S(2)}, u32[]{:S(2)}) collective-permute-start(bf16[256,128]{1,0:T(8,128)(2,1)S(1)} %get-tuple-element.79), channel_id=1, source_target_pairs={{0,8},{1,9},{2,10},{3,11},{4,12},{5,13},{6,14},{7,15},{8,0},{9,1},... | collective-permute-start | bytes 196616 | tf_op jit(solution)/shard_map/ppermute | solution.py:568
  45.3 10.0 %collective-permute-start.18 = (bf16[256,128]{1,0:T(8,128)(2,1)S(1)}, bf16[256,128]{1,0:T(8,128)(2,1)S(1)}, u32[]{:S(2)}, u32[]{:S(2)}) collective-permute-start(bf16[256,128]{1,0:T(8,128)(2,1)S(1)} %get-tuple-element.80), channel_id=1, source_target_pairs={{0,12},{1,13},{2,14},{3,15},{4,8},{5,9},{6,10},{7,11},{8,4},{9,5},... | collective-permute-start | bytes 196616 | tf_op jit(solution)/shard_map/ppermute | solution.py:568
  45.5 8.8 %collective-permute-start.19 = (bf16[32,512]{1,0:T(8,128)(2,1)S(1)}, bf16[32,512]{1,0:T(8,128)(2,1)S(1)}, u32[]{:S(2)}, u32[]{:S(2)}) collective-permute-start(bf16[32,512]{1,0:T(8,128)(2,1)S(1)} %get-tuple-element.81), channel_id=1, source_target_pairs={{1,2},{3,4},{5,6},{7,8},{9,10},{11,12},{13,14},{15,16},{17,18},{19... | collective-permute-start | bytes 98312 | tf_op jit(solution)/shard_map/ppermute | solution.py:623
  52.4 2.8 %collective-permute-start.20 = (bf16[32,512]{1,0:T(8,128)(2,1)S(1)}, bf16[32,512]{1,0:T(8,128)(2,1)S(1)}, u32[]{:S(2)}, u32[]{:S(2)}) collective-permute-start(bf16[32,512]{1,0:T(8,128)(2,1)S(1)} %get-tuple-element.82), channel_id=1, source_target_pairs={{0,1},{2,3},{4,5},{6,7},{8,9},{10,11},{12,13},{14,15},{16,17},{18,... | collective-permute-start | bytes 98312 | tf_op jit(solution)/shard_map/ppermute | solution.py:623

commit v13 on v9

--- a/solution.py
+++ b/solution.py
@@ -606,8 +606,8 @@
         (edge_blocks[TIED], across, *(later[k] for k in order[:-TAIL]))
     )
     across = held[1]
-    kept = lax.optimization_barrier((*edges[1:], *(later[k] for k in order[-TAIL:])))
-    edges[1 : 1 + (nz - 1)], kept = kept[: (nz - 1)], kept[(nz - 1) :]
+    kept = lax.optimization_barrier((*edges[1:3], *(later[k] for k in order[-TAIL:])))
+    edges[1 : 1 + 2], kept = kept[: 2], kept[2 :]
     inner_blocks = [in_plane(part, k) for part, k in zip((*held[2:], *kept), order)]
     first_rows, second_rows = pl.pallas_call(
         edges_kernel,

time: 56.6 us -> 56.6 us (level)
  no operation moved by 1% of the time
where the time goes in v13:
time: 56.6 us; the launch traced here: 56.4 us
  starting transfers between devices  35.2 us (62%)
  Pallas kernels  10.2 us (18%)
  waiting for transfers between devices  9.38 us (17%)
  local copies, waits for them, and re-layouts  0.96 us (2%)
  between operations  0.71 us (1%)
    ppermute x13, starting transfers between devices, in_plane(): return lax.ppermute(part, ('sec', 'p'), pairs)  20.5 us
    ppermute x2, starting transfers between devices, swap(): return lax.ppermute(rows, every, pairs + [(j, i) for i, j in pairs])  7.47 us
    ppermute x6, starting transfers between devices, along_z(): return lax.ppermute(part, every, pairs)  7.3 us
    pallas_call x1, Pallas kernels, per_device(): pl.pallas_call(functools.partial(warp_kernel, split), out_shape=[shaped((...  6.64 us
    ppermute x13, waiting for transfers between devices, in_plane(): return lax.ppermute(part, ('sec', 'p'), pairs)  6.2 us
    ppermute x2, waiting for transfers between devices, swap(): return lax.ppermute(rows, every, pairs + [(j, i) for i, j in pairs])  2.1 us
    pallas_call x1, Pallas kernels, per_device(): pl.pallas_call(functools.partial(detect_kernel, nz), out_shape=[shaped((S...  1.38 us
  transfers between devices with their start and end apart: 21, of which 10 were waited for; matrix products, arithmetic and copies ran while one was open for 0% of the time, Pallas kernels for 3%

profile of v13, /device:TPU:1, one launch (start us, length us, event | category | flops | bytes accessed | tf_op | source)
XLA Modules:
  0.0 56.4 jit_solution(5543841638708846190)
XLA Ops:
  0.6 6.6 %warp.1 = (bf16[1056,128]{1,0:T(8,128)(2,1)}, bf16[544,128]{1,0:T(8,128)(2,1)}, bf16[544,128]{1,0:T(8,128)(2,1)}, bf16[544,128]{1,0:T(8,128)(2,1)}, bf16[1056,12...) custom-call(s32[32]{0:T(128)} %bitcast.4, ...), custom_call_target="tpu_custom_call" | custom-call | tf_op jit(solution)/shard_map/warp/pallas_call | solution.py:507
  7.3 3.1 %collective-permute-start.1 = (bf16[544,128]{1,0:T(8,128)(2,1)}, bf16[544,128]{1,0:T(8,128)(2,1)S(1)}, u32[]{:S(2)}, u32[]{:S(2)}) collective-permute-start(bf16[544,128]{1,0:T(8,128)(2,1)} %get-tuple-element.46), channel_id=1, source_target_pairs={{0,3},{1,2},{2,1},{3,0},{16,19},{17,18},{18,17},{19,16},{4,7},{5,6... | collective-permute-start | bytes 417800 | tf_op jit(solution)/shard_map/ppermute | solution.py:561
  10.4 0.6 %collective-permute-start.2 = (bf16[544,128]{1,0:T(8,128)(2,1)}, bf16[544,128]{1,0:T(8,128)(2,1)S(1)}, u32[]{:S(2)}, u32[]{:S(2)}) collective-permute-start(bf16[544,128]{1,0:T(8,128)(2,1)} %get-tuple-element.47), channel_id=1, source_target_pairs={{0,19},{1,18},{2,17},{3,16},{16,3},{17,2},{18,1},{19,0},{4,23},{5,... | collective-permute-start | bytes 417800 | tf_op jit(solution)/shard_map/ppermute | solution.py:561
  11.0 0.3 collective-permute-start
  11.3 1.3 %collective-permute-start.3 = (bf16[544,128]{1,0:T(8,128)(2,1)}, bf16[544,128]{1,0:T(8,128)(2,1)S(1)}, u32[]{:S(2)}, u32[]{:S(2)}) collective-permute-start(bf16[544,128]{1,0:T(8,128)(2,1)} %get-tuple-element.48), channel_id=1, source_target_pairs={{0,1},{1,0},{2,3},{3,2},{16,18},{17,19},{18,16},{19,17},{4,5},{5,4... | collective-permute-start | bytes 417800 | tf_op jit(solution)/shard_map/ppermute | solution.py:561
  12.6 1.2 %collective-permute-start.4 = (bf16[544,128]{1,0:T(8,128)(2,1)}, bf16[544,128]{1,0:T(8,128)(2,1)S(1)}, u32[]{:S(2)}, u32[]{:S(2)}) collective-permute-start(bf16[544,128]{1,0:T(8,128)(2,1)} %get-tuple-element.49), channel_id=1, source_target_pairs={{0,2},{1,3},{2,0},{3,1},{16,17},{17,16},{18,19},{19,18},{4,6},{5,7... | collective-permute-start | bytes 417800 | tf_op jit(solution)/shard_map/ppermute | solution.py:561
  13.8 0.1 collective-permute-done.1.refs_2_
  14.0 3.7 %collective-permute-start.5 = (bf16[544,128]{1,0:T(8,128)(2,1)}, bf16[544,128]{1,0:T(8,128)(2,1)S(1)}, u32[]{:S(2)}, u32[]{:S(2)}) collective-permute-start(bf16[544,128]{1,0:T(8,128)(2,1)} %get-tuple-element.50), channel_id=1, source_target_pairs={{0,17},{1,16},{2,19},{3,18},{16,2},{17,3},{18,0},{19,1},{4,21},{5,... | collective-permute-start | bytes 417800 | tf_op jit(solution)/shard_map/ppermute | solution.py:561
  17.7 0.0 collective-permute-done.2.refs_3_
  17.7 1.1 %collective-permute-start.6 = (bf16[544,128]{1,0:T(8,128)(2,1)}, bf16[544,128]{1,0:T(8,128)(2,1)S(1)}, u32[]{:S(2)}, u32[]{:S(2)}) collective-permute-start(bf16[544,128]{1,0:T(8,128)(2,1)} %get-tuple-element.51), channel_id=1, source_target_pairs={{0,18},{1,19},{2,16},{3,17},{16,1},{17,0},{18,3},{19,2},{4,22},{5,... | collective-permute-start | bytes 417800 | tf_op jit(solution)/shard_map/ppermute | solution.py:561
  18.8 1.0 %copy-done = bf16[1056,128]{1,0:T(8,128)(2,1)S(1)} copy-done((bf16[1056,128]{1,0:T(8,128)(2,1)S(1)}, bf16[1056,128]{1,0:T(8,128)(2,1)}, u32[]{:S(2)}) %copy-start) | copy-done | bytes 270360
  19.8 0.8 %matrices.1 = (bf16[2,512,512]{2,1,0:T(8,128)(2,1)S(1)}, bf16[2,128,128]{2,1,0:T(8,128)(2,1)S(1)}, bf16[2,64,64]{2,1,0:T(8,128)(2,1)S(1)}, bf16[1056,128]{1,0:T(8,128)(2,1)S(1)}) custom-call(f32[2,41]{1,0:T(2,128)S(1)} %copy-done.1, bf16[1056,128]{1,0:T(8,128)(2,1)S(1)} %copy-done), custom_call_target="tpu_custom_call" | custom-call | bytes 8388608 | tf_op jit(solution)/shard_map/matrices/pallas_call | solution.py:574
  20.5 0.1 collective-permute-done.3.refs_4_
  20.7 2.4 %collective-permute-start.10 = (bf16[512,128]{1,0:T(8,128)(2,1)}, bf16[512,128]{1,0:T(8,128)(2,1)S(1)}, u32[]{:S(2)}, u32[]{:S(2)}) collective-permute-start(bf16[512,128]{1,0:T(8,128)(2,1)} %get-tuple-element.69), channel_id=1, source_target_pairs={{0,3},{1,2},{2,1},{3,0},{16,19},{17,18},{18,17},{19,16},{4,7},{5,6... | collective-permute-start | bytes 393224 | tf_op jit(solution)/shard_map/ppermute | solution.py:561
  23.0 0.0 collective-permute-done.4.refs_5_
  23.0 0.5 collective-permute-done.5.refs_6_
  23.6 0.2 collective-permute-done.6.refs_7_
  23.8 0.0 collective-permute-done.refs_1_
  23.8 0.7 %edge_sums.1 = (bf16[272,128]{1,0:T(8,128)(2,1)S(1)}, bf16[272,128]{1,0:T(8,128)(2,1)S(1)}, bf16[272,128]{1,0:T(8,128)(2,1)S(1)}, bf16[272,128]{1,0:T(8,128)(2,1)S(1)}, f32[8,4,8,128]{3,2,1,0:T(8,128)S(1)}) custom-call(bf16[1056,128]{1,0:T(8,128)(2,1)S(1)} %get-tuple-element.63.refs_0_, bf16[1056,128]{1,0:T(8,128)(2,1)S(1)} %collective-permute-done.refs_1_, ...), custom_call_target="tpu_custom_call" | custom-call | bytes 4194304 | tf_op jit(solution)/shard_map/edge_sums/pallas_call | solution.py:591
  24.4 2.6 %collective-permute-start.7 = (bf16[272,128]{1,0:T(8,128)(2,1)S(1)}, bf16[272,128]{1,0:T(8,128)(2,1)S(1)}, u32[]{:S(2)}, u32[]{:S(2)}) collective-permute-start(bf16[272,128]{1,0:T(8,128)(2,1)S(1)} %get-tuple-element.53), channel_id=1, source_target_pairs={{0,4},{1,5},{2,6},{3,7},{4,0},{5,1},{6,2},{7,3},{8,12},{9,13},{10,... | collective-permute-start | bytes 208904 | tf_op jit(solution)/shard_map/ppermute | solution.py:568
  27.0 1.1 %collective-permute-start.8 = (bf16[272,128]{1,0:T(8,128)(2,1)S(1)}, bf16[272,128]{1,0:T(8,128)(2,1)S(1)}, u32[]{:S(2)}, u32[]{:S(2)}) collective-permute-start(bf16[272,128]{1,0:T(8,128)(2,1)S(1)} %get-tuple-element.54), channel_id=1, source_target_pairs={{0,8},{1,9},{2,10},{3,11},{4,12},{5,13},{6,14},{7,15},{8,0},{9,1},... | collective-permute-start | bytes 208904 | tf_op jit(solution)/shard_map/ppermute | solution.py:568
  28.1 0.2 collective-permute-start.9
  28.3 2.3 %collective-permute-start.11 = (bf16[512,128]{1,0:T(8,128)(2,1)}, bf16[512,128]{1,0:T(8,128)(2,1)S(1)}, u32[]{:S(2)}, u32[]{:S(2)}) collective-permute-start(bf16[512,128]{1,0:T(8,128)(2,1)} %get-tuple-element.70), channel_id=1, source_target_pairs={{0,19},{1,18},{2,17},{3,16},{16,3},{17,2},{18,1},{19,0},{4,23},{5,... | collective-permute-start | bytes 393224 | tf_op jit(solution)/shard_map/ppermute | solution.py:561
  30.6 0.0 collective-permute-done.7.refs_1_
  30.6 0.7 %collective-permute-start.12 = (bf16[512,128]{1,0:T(8,128)(2,1)}, bf16[512,128]{1,0:T(8,128)(2,1)S(1)}, u32[]{:S(2)}, u32[]{:S(2)}) collective-permute-start(bf16[512,128]{1,0:T(8,128)(2,1)} %get-tuple-element.71), channel_id=1, source_target_pairs={{0,1},{1,0},{2,3},{3,2},{16,18},{17,19},{18,16},{19,17},{4,5},{5,4... | collective-permute-start | bytes 393224 | tf_op jit(solution)/shard_map/ppermute | solution.py:561
  31.4 1.1 %collective-permute-done.8.refs_2_ = bf16[272,128]{1,0:T(8,128)(2,1)S(1)} collective-permute-done((bf16[272,128]{1,0:T(8,128)(2,1)S(1)}, bf16[272,128]{1,0:T(8,128)(2,1)S(1)}, u32[]{:S(2)}, u32[]{:S(2)}) %collective-permute-start.8) | collective-permute-done | bytes 69664 | tf_op jit(solution)/shard_map/ppermute | solution.py:568
  32.5 0.7 %collective-permute-start.13 = (bf16[512,128]{1,0:T(8,128)(2,1)}, bf16[512,128]{1,0:T(8,128)(2,1)S(1)}, u32[]{:S(2)}, u32[]{:S(2)}) collective-permute-start(bf16[512,128]{1,0:T(8,128)(2,1)} %get-tuple-element.72), channel_id=1, source_target_pairs={{0,2},{1,3},{2,0},{3,1},{16,17},{17,16},{18,19},{19,18},{4,6},{5,7... | collective-permute-start | bytes 393224 | tf_op jit(solution)/shard_map/ppermute | solution.py:561
  33.2 0.0 collective-permute-done.10.refs_2_
  33.2 2.6 %collective-permute-start.14 = (bf16[512,128]{1,0:T(8,128)(2,1)}, bf16[512,128]{1,0:T(8,128)(2,1)S(1)}, u32[]{:S(2)}, u32[]{:S(2)}) collective-permute-start(bf16[512,128]{1,0:T(8,128)(2,1)} %get-tuple-element.73), channel_id=1, source_target_pairs={{0,17},{1,16},{2,19},{3,18},{16,2},{17,3},{18,0},{19,1},{4,21},{5,... | collective-permute-start | bytes 393224 | tf_op jit(solution)/shard_map/ppermute | solution.py:561
  35.8 0.0 collective-permute-done.9.refs_3_
  35.8 0.4 collective-permute-start.15
  36.1 0.1 edge_rows.1
  36.2 0.0 collective-permute-done.11.refs_3_
  36.2 0.7 %collective-permute-done.12.refs_4_ = bf16[512,128]{1,0:T(8,128)(2,1)S(1)} collective-permute-done((bf16[512,128]{1,0:T(8,128)(2,1)}, bf16[512,128]{1,0:T(8,128)(2,1)S(1)}, u32[]{:S(2)}, u32[]{:S(2)}) %collective-permute-start.12) | collective-permute-done | bytes 131104 | tf_op jit(solution)/shard_map/ppermute | solution.py:561
  36.9 1.4 %collective-permute-done.13.refs_5_ = bf16[512,128]{1,0:T(8,128)(2,1)S(1)} collective-permute-done((bf16[512,128]{1,0:T(8,128)(2,1)}, bf16[512,128]{1,0:T(8,128)(2,1)S(1)}, u32[]{:S(2)}, u32[]{:S(2)}) %collective-permute-start.13) | collective-permute-done | bytes 131104 | tf_op jit(solution)/shard_map/ppermute | solution.py:561
  38.3 2.3 %collective-permute-done.14.refs_6_ = bf16[512,128]{1,0:T(8,128)(2,1)S(1)} collective-permute-done((bf16[512,128]{1,0:T(8,128)(2,1)}, bf16[512,128]{1,0:T(8,128)(2,1)S(1)}, u32[]{:S(2)}, u32[]{:S(2)}) %collective-permute-start.14) | collective-permute-done | bytes 131104 | tf_op jit(solution)/shard_map/ppermute | solution.py:561
  40.6 0.8 %collective-permute-done.15.refs_7_ = bf16[512,128]{1,0:T(8,128)(2,1)S(1)} collective-permute-done((bf16[512,128]{1,0:T(8,128)(2,1)}, bf16[512,128]{1,0:T(8,128)(2,1)S(1)}, u32[]{:S(2)}, u32[]{:S(2)}) %collective-permute-start.15) | collective-permute-done | bytes 131104 | tf_op jit(solution)/shard_map/ppermute | solution.py:561
  41.4 0.6 %inner_sums.1 = (bf16[256,128]{1,0:T(8,128)(2,1)S(1)}, bf16[256,128]{1,0:T(8,128)(2,1)S(1)}, bf16[256,128]{1,0:T(8,128)(2,1)S(1)}, bf16[256,128]{1,0:T(8,128)(2,1)S(1)}) custom-call(f32[8,4,8,128]{3,2,1,0:T(8,128)S(1)} %get-tuple-element.60.weight_ref, bf16[1056,128]{1,0:T(8,128)(2,1)S(1)} %get-tuple-element.63.refs_0_, ...), custom_call_target="tpu_custom_call" | custom-call | bytes 4194304 | tf_op jit(solution)/shard_map/inner_sums/pallas_call | solution.py:628
  42.0 1.8 %collective-permute-start.16 = (bf16[256,128]{1,0:T(8,128)(2,1)S(1)}, bf16[256,128]{1,0:T(8,128)(2,1)S(1)}, u32[]{:S(2)}, u32[]{:S(2)}) collective-permute-start(bf16[256,128]{1,0:T(8,128)(2,1)S(1)} %get-tuple-element.76), channel_id=1, source_target_pairs={{0,4},{1,5},{2,6},{3,7},{4,0},{5,1},{6,2},{7,3},{8,12},{9,13},{10,... | collective-permute-start | bytes 196616 | tf_op jit(solution)/shard_map/ppermute | solution.py:568
  43.8 1.4 %collective-permute-start.17 = (bf16[256,128]{1,0:T(8,128)(2,1)S(1)}, bf16[256,128]{1,0:T(8,128)(2,1)S(1)}, u32[]{:S(2)}, u32[]{:S(2)}) collective-permute-start(bf16[256,128]{1,0:T(8,128)(2,1)S(1)} %get-tuple-element.77), channel_id=1, source_target_pairs={{0,8},{1,9},{2,10},{3,11},{4,12},{5,13},{6,14},{7,15},{8,0},{9,1},... | collective-permute-start | bytes 196616 | tf_op jit(solution)/shard_map/ppermute | solution.py:568
  45.3 0.2 collective-permute-start.18
  45.5 0.8 %collective-permute-start.19 = (bf16[32,512]{1,0:T(8,128)(2,1)S(1)}, bf16[32,512]{1,0:T(8,128)(2,1)S(1)}, u32[]{:S(2)}, u32[]{:S(2)}) collective-permute-start(bf16[32,512]{1,0:T(8,128)(2,1)S(1)} %get-tuple-element.79), channel_id=1, source_target_pairs={{0,1},{2,3},{4,5},{6,7},{8,9},{10,11},{12,13},{14,15},{16,17},{18,... | collective-permute-start | bytes 98312 | tf_op jit(solution)/shard_map/ppermute | solution.py:623
  46.2 6.7 %collective-permute-start.20 = (bf16[32,512]{1,0:T(8,128)(2,1)S(1)}, bf16[32,512]{1,0:T(8,128)(2,1)S(1)}, u32[]{:S(2)}, u32[]{:S(2)}) collective-permute-start(bf16[32,512]{1,0:T(8,128)(2,1)S(1)} %get-tuple-element.80), channel_id=1, source_target_pairs={{1,2},{3,4},{5,6},{7,8},{9,10},{11,12},{13,14},{15,16},{17,18},{19... | collective-permute-start | bytes 98312 | tf_op jit(solution)/shard_map/ppermute | solution.py:623
  52.9 0.0 collective-permute-done.19.refs_8_
  53.0 2.1 %collective-permute-done.20.refs_9_ = bf16[32,512]{1,0:T(8,128)(2,1)S(1)} collective-permute-done((bf16[32,512]{1,0:T(8,128)(2,1)S(1)}, bf16[32,512]{1,0:T(8,128)(2,1)S(1)}, u32[]{:S(2)}, u32[]{:S(2)}) %collective-permute-start.20) | collective-permute-done | bytes 32800 | tf_op jit(solution)/shard_map/ppermute | solution.py:623
  55.0 0.0 collective-permute-done.16.refs_5_
  55.1 0.0 collective-permute-done.18.refs_7_
  55.1 1.4 %coadd_detect.1 = (f32[128,512]{1,0:T(8,128)}, f32[128,512]{1,0:T(8,128)}) custom-call(bf16[272,128]{1,0:T(8,128)(2,1)S(1)} %get-tuple-element.52.refs_0_, bf16[272,128]{1,0:T(8,128)(2,1)S(1)} %collective-permute-done.7.refs_1_, bf16[272,128]{1,0:T(8,128)(2,1)S(1)} %collective-permute-done.8.refs_2_, bf16[272,128]{1,0:T(8,128)(2,1)S(1)} %collective-permute-done.9.refs_3_, ...), custom_call_target="tpu_custom_call" | custom-call | tf_op jit(solution)/shard_map/coadd_detect/pallas_call | solution.py:639
  (4 shorter events, 0.0 us)
Async XLA Ops:
  0.6 18.2 %copy-start.1 = (f32[2,41]{1,0:T(2,128)S(1)}, f32[2,41]{1,0:T(2,128)}, u32[]{:S(2)}) copy-start(f32[2,41]{1,0:T(2,128)} %taps_ref.1) | copy-start | bytes 988
  7.3 6.7 %collective-permute-start.1 = (bf16[544,128]{1,0:T(8,128)(2,1)}, bf16[544,128]{1,0:T(8,128)(2,1)S(1)}, u32[]{:S(2)}, u32[]{:S(2)}) collective-permute-start(bf16[544,128]{1,0:T(8,128)(2,1)} %get-tuple-element.46), channel_id=1, source_target_pairs={{0,3},{1,2},{2,1},{3,0},{16,19},{17,18},{18,17},{19,16},{4,7},{5,6... | collective-permute-start | bytes 417800 | tf_op jit(solution)/shard_map/ppermute | solution.py:561
  10.4 7.3 %collective-permute-start.2 = (bf16[544,128]{1,0:T(8,128)(2,1)}, bf16[544,128]{1,0:T(8,128)(2,1)S(1)}, u32[]{:S(2)}, u32[]{:S(2)}) collective-permute-start(bf16[544,128]{1,0:T(8,128)(2,1)} %get-tuple-element.47), channel_id=1, source_target_pairs={{0,19},{1,18},{2,17},{3,16},{16,3},{17,2},{18,1},{19,0},{4,23},{5,... | collective-permute-start | bytes 417800 | tf_op jit(solution)/shard_map/ppermute | solution.py:561
  11.0 12.8 %collective-permute-start = (bf16[1056,128]{1,0:T(8,128)(2,1)}, bf16[1056,128]{1,0:T(8,128)(2,1)S(1)}, u32[]{:S(2)}, u32[]{:S(2)}) collective-permute-start(bf16[1056,128]{1,0:T(8,128)(2,1)} %get-tuple-element.45), channel_id=1, source_target_pairs={{0,16},{1,17},{2,18},{3,19},{16,0},{17,1},{18,2},{19,3},{4,20},{5,... | collective-permute-start | bytes 811016 | tf_op jit(solution)/shard_map/ppermute | solution.py:561
  11.3 9.4 %collective-permute-start.3 = (bf16[544,128]{1,0:T(8,128)(2,1)}, bf16[544,128]{1,0:T(8,128)(2,1)S(1)}, u32[]{:S(2)}, u32[]{:S(2)}) collective-permute-start(bf16[544,128]{1,0:T(8,128)(2,1)} %get-tuple-element.48), channel_id=1, source_target_pairs={{0,1},{1,0},{2,3},{3,2},{16,18},{17,19},{18,16},{19,17},{4,5},{5,4... | collective-permute-start | bytes 417800 | tf_op jit(solution)/shard_map/ppermute | solution.py:561
  12.6 10.4 %collective-permute-start.4 = (bf16[544,128]{1,0:T(8,128)(2,1)}, bf16[544,128]{1,0:T(8,128)(2,1)S(1)}, u32[]{:S(2)}, u32[]{:S(2)}) collective-permute-start(bf16[544,128]{1,0:T(8,128)(2,1)} %get-tuple-element.49), channel_id=1, source_target_pairs={{0,2},{1,3},{2,0},{3,1},{16,17},{17,16},{18,19},{19,18},{4,6},{5,7... | collective-permute-start | bytes 417800 | tf_op jit(solution)/shard_map/ppermute | solution.py:561
  14.0 9.6 %collective-permute-start.5 = (bf16[544,128]{1,0:T(8,128)(2,1)}, bf16[544,128]{1,0:T(8,128)(2,1)S(1)}, u32[]{:S(2)}, u32[]{:S(2)}) collective-permute-start(bf16[544,128]{1,0:T(8,128)(2,1)} %get-tuple-element.50), channel_id=1, source_target_pairs={{0,17},{1,16},{2,19},{3,18},{16,2},{17,3},{18,0},{19,1},{4,21},{5,... | collective-permute-start | bytes 417800 | tf_op jit(solution)/shard_map/ppermute | solution.py:561
  17.7 6.1 %collective-permute-start.6 = (bf16[544,128]{1,0:T(8,128)(2,1)}, bf16[544,128]{1,0:T(8,128)(2,1)S(1)}, u32[]{:S(2)}, u32[]{:S(2)}) collective-permute-start(bf16[544,128]{1,0:T(8,128)(2,1)} %get-tuple-element.51), channel_id=1, source_target_pairs={{0,18},{1,19},{2,16},{3,17},{16,1},{17,0},{18,3},{19,2},{4,22},{5,... | collective-permute-start | bytes 417800 | tf_op jit(solution)/shard_map/ppermute | solution.py:561
  18.8 1.0 %copy-start = (bf16[1056,128]{1,0:T(8,128)(2,1)S(1)}, bf16[1056,128]{1,0:T(8,128)(2,1)}, u32[]{:S(2)}) copy-start(bf16[1056,128]{1,0:T(8,128)(2,1)} %get-tuple-element.43.refs_0_) | copy-start | bytes 811012
  20.7 12.5 %collective-permute-start.10 = (bf16[512,128]{1,0:T(8,128)(2,1)}, bf16[512,128]{1,0:T(8,128)(2,1)S(1)}, u32[]{:S(2)}, u32[]{:S(2)}) collective-permute-start(bf16[512,128]{1,0:T(8,128)(2,1)} %get-tuple-element.69), channel_id=1, source_target_pairs={{0,3},{1,2},{2,1},{3,0},{16,19},{17,18},{18,17},{19,16},{4,7},{5,6... | collective-permute-start | bytes 393224 | tf_op jit(solution)/shard_map/ppermute | solution.py:561
  24.4 6.2 %collective-permute-start.7 = (bf16[272,128]{1,0:T(8,128)(2,1)S(1)}, bf16[272,128]{1,0:T(8,128)(2,1)S(1)}, u32[]{:S(2)}, u32[]{:S(2)}) collective-permute-start(bf16[272,128]{1,0:T(8,128)(2,1)S(1)} %get-tuple-element.53), channel_id=1, source_target_pairs={{0,4},{1,5},{2,6},{3,7},{4,0},{5,1},{6,2},{7,3},{8,12},{9,13},{10,... | collective-permute-start | bytes 208904 | tf_op jit(solution)/shard_map/ppermute | solution.py:568
  27.0 5.4 %collective-permute-start.8 = (bf16[272,128]{1,0:T(8,128)(2,1)S(1)}, bf16[272,128]{1,0:T(8,128)(2,1)S(1)}, u32[]{:S(2)}, u32[]{:S(2)}) collective-permute-start(bf16[272,128]{1,0:T(8,128)(2,1)S(1)} %get-tuple-element.54), channel_id=1, source_target_pairs={{0,8},{1,9},{2,10},{3,11},{4,12},{5,13},{6,14},{7,15},{8,0},{9,1},... | collective-permute-start | bytes 208904 | tf_op jit(solution)/shard_map/ppermute | solution.py:568
  28.1 7.6 %collective-permute-start.9 = (bf16[272,128]{1,0:T(8,128)(2,1)S(1)}, bf16[272,128]{1,0:T(8,128)(2,1)S(1)}, u32[]{:S(2)}, u32[]{:S(2)}) collective-permute-start(bf16[272,128]{1,0:T(8,128)(2,1)S(1)} %get-tuple-element.59), channel_id=1, source_target_pairs={{0,12},{1,13},{2,14},{3,15},{4,8},{5,9},{6,10},{7,11},{8,4},{9,5},... | collective-permute-start | bytes 208904 | tf_op jit(solution)/shard_map/ppermute | solution.py:568
  28.3 7.9 %collective-permute-start.11 = (bf16[512,128]{1,0:T(8,128)(2,1)}, bf16[512,128]{1,0:T(8,128)(2,1)S(1)}, u32[]{:S(2)}, u32[]{:S(2)}) collective-permute-start(bf16[512,128]{1,0:T(8,128)(2,1)} %get-tuple-element.70), channel_id=1, source_target_pairs={{0,19},{1,18},{2,17},{3,16},{16,3},{17,2},{18,1},{19,0},{4,23},{5,... | collective-permute-start | bytes 393224 | tf_op jit(solution)/shard_map/ppermute | solution.py:561
  30.6 6.3 %collective-permute-start.12 = (bf16[512,128]{1,0:T(8,128)(2,1)}, bf16[512,128]{1,0:T(8,128)(2,1)S(1)}, u32[]{:S(2)}, u32[]{:S(2)}) collective-permute-start(bf16[512,128]{1,0:T(8,128)(2,1)} %get-tuple-element.71), channel_id=1, source_target_pairs={{0,1},{1,0},{2,3},{3,2},{16,18},{17,19},{18,16},{19,17},{4,5},{5,4... | collective-permute-start | bytes 393224 | tf_op jit(solution)/shard_map/ppermute | solution.py:561
  32.5 5.9 %collective-permute-start.13 = (bf16[512,128]{1,0:T(8,128)(2,1)}, bf16[512,128]{1,0:T(8,128)(2,1)S(1)}, u32[]{:S(2)}, u32[]{:S(2)}) collective-permute-start(bf16[512,128]{1,0:T(8,128)(2,1)} %get-tuple-element.72), channel_id=1, source_target_pairs={{0,2},{1,3},{2,0},{3,1},{16,17},{17,16},{18,19},{19,18},{4,6},{5,7... | collective-permute-start | bytes 393224 | tf_op jit(solution)/shard_map/ppermute | solution.py:561
  33.2 7.5 %collective-permute-start.14 = (bf16[512,128]{1,0:T(8,128)(2,1)}, bf16[512,128]{1,0:T(8,128)(2,1)S(1)}, u32[]{:S(2)}, u32[]{:S(2)}) collective-permute-start(bf16[512,128]{1,0:T(8,128)(2,1)} %get-tuple-element.73), channel_id=1, source_target_pairs={{0,17},{1,16},{2,19},{3,18},{16,2},{17,3},{18,0},{19,1},{4,21},{5,... | collective-permute-start | bytes 393224 | tf_op jit(solution)/shard_map/ppermute | solution.py:561
  35.8 5.7 %collective-permute-start.15 = (bf16[512,128]{1,0:T(8,128)(2,1)}, bf16[512,128]{1,0:T(8,128)(2,1)S(1)}, u32[]{:S(2)}, u32[]{:S(2)}) collective-permute-start(bf16[512,128]{1,0:T(8,128)(2,1)} %get-tuple-element.74), channel_id=1, source_target_pairs={{0,18},{1,19},{2,16},{3,17},{16,1},{17,0},{18,3},{19,2},{4,22},{5,... | collective-permute-start | bytes 393224 | tf_op jit(solution)/shard_map/ppermute | solution.py:561
  42.0 13.0 %collective-permute-start.16 = (bf16[256,128]{1,0:T(8,128)(2,1)S(1)}, bf16[256,128]{1,0:T(8,128)(2,1)S(1)}, u32[]{:S(2)}, u32[]{:S(2)}) collective-permute-start(bf16[256,128]{1,0:T(8,128)(2,1)S(1)} %get-tuple-element.76), channel_id=1, source_target_pairs={{0,4},{1,5},{2,6},{3,7},{4,0},{5,1},{6,2},{7,3},{8,12},{9,13},{10,... | collective-permute-start | bytes 196616 | tf_op jit(solution)/shard_map/ppermute | solution.py:568
  43.8 11.2 %collective-permute-start.17 = (bf16[256,128]{1,0:T(8,128)(2,1)S(1)}, bf16[256,128]{1,0:T(8,128)(2,1)S(1)}, u32[]{:S(2)}, u32[]{:S(2)}) collective-permute-start(bf16[256,128]{1,0:T(8,128)(2,1)S(1)} %get-tuple-element.77), channel_id=1, source_target_pairs={{0,8},{1,9},{2,10},{3,11},{4,12},{5,13},{6,14},{7,15},{8,0},{9,1},... | collective-permute-start | bytes 196616 | tf_op jit(solution)/shard_map/ppermute | solution.py:568
  45.3 9.8 %collective-permute-start.18 = (bf16[256,128]{1,0:T(8,128)(2,1)S(1)}, bf16[256,128]{1,0:T(8,128)(2,1)S(1)}, u32[]{:S(2)}, u32[]{:S(2)}) collective-permute-start(bf16[256,128]{1,0:T(8,128)(2,1)S(1)} %get-tuple-element.78), channel_id=1, source_target_pairs={{0,12},{1,13},{2,14},{3,15},{4,8},{5,9},{6,10},{7,11},{8,4},{9,5},... | collective-permute-start | bytes 196616 | tf_op jit(solution)/shard_map/ppermute | solution.py:568
  45.5 7.5 %collective-permute-start.19 = (bf16[32,512]{1,0:T(8,128)(2,1)S(1)}, bf16[32,512]{1,0:T(8,128)(2,1)S(1)}, u32[]{:S(2)}, u32[]{:S(2)}) collective-permute-start(bf16[32,512]{1,0:T(8,128)(2,1)S(1)} %get-tuple-element.79), channel_id=1, source_target_pairs={{0,1},{2,3},{4,5},{6,7},{8,9},{10,11},{12,13},{14,15},{16,17},{18,... | collective-permute-start | bytes 98312 | tf_op jit(solution)/shard_map/ppermute | solution.py:623
  46.2 8.8 %collective-permute-start.20 = (bf16[32,512]{1,0:T(8,128)(2,1)S(1)}, bf16[32,512]{1,0:T(8,128)(2,1)S(1)}, u32[]{:S(2)}, u32[]{:S(2)}) collective-permute-start(bf16[32,512]{1,0:T(8,128)(2,1)S(1)} %get-tuple-element.80), channel_id=1, source_target_pairs={{1,2},{3,4},{5,6},{7,8},{9,10},{11,12},{13,14},{15,16},{17,18},{19... | collective-permute-start | bytes 98312 | tf_op jit(solution)/shard_map/ppermute | solution.py:623
